TPU v7x, 32 devices: a whole 2x2x4 slice. The times are simulated.
32 devices in a mesh: blk: 8 (over y, x, core), fsdp: 4 (over z).
Axes of the slice: x: 2, y: 2, z: 4, core: 2. Of those that a mesh axis runs over, the one named last changes fastest.
Arguments:
- tokens: bfloat16 [4096, 2048], P('blk'), may hold values from -6 to 6
- span_order: int32 [16], replicated, may hold values from 0 to 15, as said below
- input_gain: bfloat16 [2048], P('blk'), may hold values from 0.25 to 1.75
- query_weight: bfloat16 [2048, 2048], P('blk', 'fsdp'), may hold values from -0.125 to 0.125
- key_weight: bfloat16 [2048, 1024], P('blk', 'fsdp'), may hold values from -0.125 to 0.125
- value_weight: bfloat16 [2048, 1024], P('blk', 'fsdp'), may hold values from -0.125 to 0.125
- query_gain: bfloat16 [128], P('blk'), may hold values from 0.25 to 1.75
- key_gain: bfloat16 [128], P('blk'), may hold values from 0.25 to 1.75
- output_weight: bfloat16 [2048, 2048], P('fsdp', 'blk'), may hold values from -1 to 1
- post_gain: bfloat16 [2048], P('blk'), may hold values from 0.25 to 1.75
- gate_weight: bfloat16 [2048, 6144], P('blk', 'fsdp'), may hold values from -0.125 to 0.125
- up_weight: bfloat16 [2048, 6144], P('blk', 'fsdp'), may hold values from -0.125 to 0.125
- down_weight: bfloat16 [6144, 2048], P('fsdp', 'blk'), may hold values from -0.078125 to 0.078125
- cotangent: bfloat16 [4096, 2048], P('blk'), may hold values from -6 to 6
Outputs:
- layer_out: bfloat16 [4096, 2048], P('blk')
- tokens_gradient: float32 [4096, 2048], P('blk')
- input_gain_gradient: float32 [2048], P('blk')
- query_weight_gradient: float32 [2048, 2048], P('blk', 'fsdp')
- key_weight_gradient: float32 [2048, 1024], P('blk', 'fsdp')
- value_weight_gradient: float32 [2048, 1024], P('blk', 'fsdp')
- query_gain_gradient: float32 [128], P('blk')
- key_gain_gradient: float32 [128], P('blk')
- output_weight_gradient: float32 [2048, 2048], P('fsdp', 'blk')
- post_gain_gradient: float32 [2048], P('blk')
- gate_weight_gradient: float32 [2048, 6144], P('blk', 'fsdp')
- up_weight_gradient: float32 [2048, 6144], P('blk', 'fsdp')
- down_weight_gradient: float32 [6144, 2048], P('fsdp', 'blk')
Inputs may be any that keep to these rules, and one draw needn't show every extreme that they name: Each span number appears once, and the two spans of one index d of blk, span_order[2 d] and span_order[2 d + 1], sum to 15, in either order.
All inputs are finite; a program needn't handle non-finite values.
Results may differ from a plain program's by a relative error of at most 0.025.
Values may be sent and summed in bfloat16 or wider, within the bound.
No kernel may reach another device: no remote copies, remote signals or barrier semaphores. Data moves between devices by JAX's collectives and lax.ppermute only.
A program may use at most 192 MiB of HBM per device.

v0:
```python
import jax
import jax.numpy as jnp
from jax import lax
from jax.sharding import PartitionSpec as P

HD = 128


EPS = 1e-06
THETA = 1000000.0
NEG = -1e30


def passed_along(block, axis, distance):
    devices = range(lax.axis_size(axis))
    route = [((i - distance) % len(devices), i) for i in devices]
    return lax.ppermute(block, axis, route)


def row_norm(values, gain):
    scale = lax.rsqrt(jnp.mean(values * values, axis=-1, keepdims=True) + EPS)
    return (values * scale * gain, scale)


def norm_back(values, scale, gain, upstream):
    weighted = upstream * gain
    inner = jnp.mean(weighted * values, axis=-1, keepdims=True)
    return (scale * (weighted - values * scale * scale * inner), upstream * values * scale)


def rope_tables(places, width):
    half = width // 2
    freqs = THETA ** (-jnp.arange(half, dtype=jnp.float32) * 2.0 / width)
    angles = places.astype(jnp.float32)[:, None] * freqs[None, :]
    angles = jnp.concatenate([angles, angles], axis=1)
    return (jnp.cos(angles), jnp.sin(angles))


def rotate(values, cosine, sine):
    half = values.shape[-1] // 2
    turned = jnp.concatenate([-values[..., half:], values[..., :half]], axis=-1)
    return values * cosine[:, None, :] + turned * sine[:, None, :]


def rotate_back(grads, cosine, sine):
    half = grads.shape[-1] // 2
    twisted = grads * sine[:, None, :]
    turned = jnp.concatenate([twisted[..., half:], -twisted[..., :half]], axis=-1)
    return grads * cosine[:, None, :] + turned


def span_places(span_order, device, span_rows):
    pair = lax.dynamic_slice_in_dim(span_order, 2 * device, 2)
    return (pair[:, None] * span_rows + jnp.arange(span_rows, dtype=jnp.int32)[None, :]).reshape(-1)


def shards(
    tokens,
    span_order,
    input_gain,
    query_weight,
    key_weight,
    value_weight,
    query_gain,
    key_gain,
    output_weight,
    post_gain,
    gate_weight,
    up_weight,
    down_weight,
    cotangent,
):
    f32 = jnp.float32
    bf16 = jnp.bfloat16
    (
        gain_input,
        w_query,
        w_key,
        w_value,
        gain_query,
        gain_key,
        w_out,
        gain_post,
        w_gate,
        w_up,
        w_down,
    ) = (
        lax.all_gather(input_gain, "blk", axis=0, tiled=True),
        lax.all_gather(query_weight, "blk", axis=0, tiled=True),
        lax.all_gather(key_weight, "blk", axis=0, tiled=True),
        lax.all_gather(value_weight, "blk", axis=0, tiled=True),
        lax.all_gather(query_gain, "blk", axis=0, tiled=True),
        lax.all_gather(key_gain, "blk", axis=0, tiled=True),
        lax.all_gather(output_weight, "blk", axis=1, tiled=True),
        lax.all_gather(post_gain, "blk", axis=0, tiled=True),
        lax.all_gather(gate_weight, "blk", axis=0, tiled=True),
        lax.all_gather(up_weight, "blk", axis=0, tiled=True),
        lax.all_gather(down_weight, "blk", axis=1, tiled=True),
    )
    rows = tokens.shape[0]
    span_rows = rows // 2
    heads_local = w_query.shape[1] // HD
    kv_local = w_key.shape[1] // HD
    group = heads_local // kv_local
    devices = lax.axis_size("blk")
    myself = lax.axis_index("blk")
    factor = HD ** (-0.5)
    inputs = tokens.astype(f32)
    normed, scale_in = row_norm(inputs, gain_input.astype(f32))
    normed_low = normed.astype(bf16)
    q_proj = jnp.dot(normed_low, w_query, preferred_element_type=f32).reshape(rows, heads_local, HD)
    k_proj = jnp.dot(normed_low, w_key, preferred_element_type=f32).reshape(rows, kv_local, HD)
    v_proj = jnp.dot(normed_low, w_value, preferred_element_type=f32)
    places = span_places(span_order, myself, span_rows)
    cosine, sine = rope_tables(places, HD)
    q_normed, q_scale = row_norm(q_proj, gain_query.astype(f32))
    queries = rotate(q_normed, cosine, sine).astype(bf16).reshape(rows, kv_local, group, HD)
    k_normed, k_scale = row_norm(k_proj, gain_key.astype(f32))
    keys = rotate(k_normed, cosine, sine).astype(bf16)
    values = v_proj.astype(bf16).reshape(rows, kv_local, HD)
    q_spans = (queries[:span_rows], queries[span_rows:])
    p_spans = (places[:span_rows], places[span_rows:])

    def attend_span(state, q_index, key_span, value_span, k_places):
        query_span = q_spans[q_index]
        q_places = p_spans[q_index]

        def attend_compute(state):
            most, total, summed = state
            scores = (
                jnp.einsum("qhgd,khd->hgqk", query_span, key_span, preferred_element_type=f32)
                * factor
            )
            allowed = q_places[:, None] >= k_places[None, :]
            scores = jnp.where(allowed, scores, NEG)
            new_most = jnp.maximum(most, jnp.max(scores, axis=-1))
            weights = jnp.where(allowed, jnp.exp(scores - new_most[..., None]), 0.0)
            carried = jnp.exp(most - new_most)
            total = total * carried + jnp.sum(weights, axis=-1)
            summed = summed * carried[..., None] + jnp.einsum(
                "hgqk,khd->hgqd", weights.astype(bf16), value_span, preferred_element_type=f32
            )
            return (new_most, total, summed)

        return lax.cond(q_places[0] >= k_places[0], attend_compute, lambda kept: kept, state)

    def forward_block(states, key_block, value_block, key_places):
        result = []
        for q_index in range(2):
            current = states[q_index]
            for k_index in range(2):
                lower = k_index * span_rows
                upper = lower + span_rows
                current = attend_span(
                    current,
                    q_index,
                    key_block[lower:upper],
                    value_block[lower:upper],
                    key_places[lower:upper],
                )
            result.append(current)
        return tuple(result)

    def empty_state():
        return (
            jnp.full((kv_local, group, span_rows), NEG, f32),
            jnp.zeros((kv_local, group, span_rows), f32),
            jnp.zeros((kv_local, group, span_rows, HD), f32),
        )

    states = (empty_state(), empty_state())
    states = forward_block(states, keys, values, places)

    def forward_turn(turn, carry):
        key_block, value_block, states = carry
        key_block, value_block = passed_along((key_block, value_block), "blk", 1)
        source = (myself - turn) % devices
        states = forward_block(
            states, key_block, value_block, span_places(span_order, source, span_rows)
        )
        return (key_block, value_block, states)

    unused_keys, unused_values, states = lax.fori_loop(
        1, devices, forward_turn, (keys, values, states)
    )
    most = jnp.concatenate([states[0][0], states[1][0]], axis=2)
    total = jnp.concatenate([states[0][1], states[1][1]], axis=2)
    summed = jnp.concatenate([states[0][2], states[1][2]], axis=2)
    context = summed / total[..., None]
    log_total = most + jnp.log(total)
    context_low = context.transpose(2, 0, 1, 3).reshape(rows, heads_local * HD).astype(bf16)
    attn = lax.psum(
        jnp.dot(context_low, w_out, preferred_element_type=f32).astype(jnp.bfloat16), "fsdp"
    ).astype(jnp.float32)
    hidden = inputs + attn
    post_normed, scale_post = row_norm(hidden, gain_post.astype(f32))
    post_low = post_normed.astype(bf16)
    gate = jnp.dot(post_low, w_gate, preferred_element_type=f32)
    up_vals = jnp.dot(post_low, w_up, preferred_element_type=f32)
    silu_gate = jax.nn.silu(gate)
    act = (silu_gate * up_vals).astype(bf16)
    mlp = lax.psum(
        jnp.dot(act, w_down, preferred_element_type=f32).astype(jnp.bfloat16), "fsdp"
    ).astype(jnp.float32)
    layer_out = (hidden + mlp).astype(bf16)
    (
        gain_input,
        w_query,
        w_key,
        w_value,
        gain_query,
        gain_key,
        w_out,
        gain_post,
        w_gate,
        w_up,
        w_down,
    ) = (
        lax.all_gather(input_gain, "blk", axis=0, tiled=True),
        lax.all_gather(query_weight, "blk", axis=0, tiled=True),
        lax.all_gather(key_weight, "blk", axis=0, tiled=True),
        lax.all_gather(value_weight, "blk", axis=0, tiled=True),
        lax.all_gather(query_gain, "blk", axis=0, tiled=True),
        lax.all_gather(key_gain, "blk", axis=0, tiled=True),
        lax.all_gather(output_weight, "blk", axis=1, tiled=True),
        lax.all_gather(post_gain, "blk", axis=0, tiled=True),
        lax.all_gather(gate_weight, "blk", axis=0, tiled=True),
        lax.all_gather(up_weight, "blk", axis=0, tiled=True),
        lax.all_gather(down_weight, "blk", axis=1, tiled=True),
    )
    grad_act = jnp.einsum("td,fd->tf", cotangent, w_down, preferred_element_type=f32)
    down_grad = jnp.einsum("tf,td->fd", act, cotangent, preferred_element_type=f32)
    sigma = jax.nn.sigmoid(gate)
    grad_up = (grad_act * silu_gate).astype(bf16)
    grad_gate = (grad_act * up_vals * sigma * (1.0 + gate * (1.0 - sigma))).astype(bf16)
    gate_grad = jnp.einsum("td,tf->df", post_low, grad_gate, preferred_element_type=f32)
    up_grad = jnp.einsum("td,tf->df", post_low, grad_up, preferred_element_type=f32)
    post_part = jnp.einsum("tf,df->td", grad_gate, w_gate, preferred_element_type=f32) + jnp.einsum(
        "tf,df->td", grad_up, w_up, preferred_element_type=f32
    )
    grad_post = lax.psum(post_part.astype(jnp.bfloat16), "fsdp").astype(jnp.float32)
    back_hidden, post_terms = norm_back(hidden, scale_post, gain_post.astype(f32), grad_post)
    post_gain_grad = jnp.sum(post_terms, axis=0)
    grad_hidden = cotangent.astype(f32) + back_hidden
    hidden_low = grad_hidden.astype(bf16)
    out_grad = jnp.einsum("tc,td->cd", context_low, hidden_low, preferred_element_type=f32)
    grad_context = jnp.einsum("td,cd->tc", hidden_low, w_out, preferred_element_type=f32).astype(
        bf16
    )
    grad_low = grad_context.reshape(rows, kv_local, group, HD).transpose(1, 2, 0, 3)
    delta = jnp.sum(grad_low.astype(f32) * context, axis=-1)
    grad_halves = (grad_low[:, :, :span_rows], grad_low[:, :, span_rows:])
    log_halves = (log_total[:, :, :span_rows], log_total[:, :, span_rows:])
    delta_halves = (delta[:, :, :span_rows], delta[:, :, span_rows:])

    def back_span(carry, q_index, key_span, value_span, k_places):
        query_span = q_spans[q_index]
        q_places = p_spans[q_index]
        grad_span = grad_halves[q_index]

        def back_compute(carry):
            grad_q, grad_k, grad_v = carry
            scores = (
                jnp.einsum("qhgd,khd->hgqk", query_span, key_span, preferred_element_type=f32)
                * factor
            )
            allowed = q_places[:, None] >= k_places[None, :]
            probs = jnp.where(allowed, jnp.exp(scores - log_halves[q_index][..., None]), 0.0)
            grad_v = grad_v + jnp.einsum(
                "hgqk,hgqd->khd", probs.astype(bf16), grad_span, preferred_element_type=f32
            )
            grad_probs = jnp.einsum(
                "hgqd,khd->hgqk", grad_span, value_span, preferred_element_type=f32
            )
            grad_scores = (probs * (grad_probs - delta_halves[q_index][..., None])).astype(bf16)
            grad_q = (
                grad_q
                + jnp.einsum("hgqk,khd->hgqd", grad_scores, key_span, preferred_element_type=f32)
                * factor
            )
            grad_k = (
                grad_k
                + jnp.einsum("hgqk,qhgd->khd", grad_scores, query_span, preferred_element_type=f32)
                * factor
            )
            return (grad_q, grad_k, grad_v)

        return lax.cond(q_places[0] >= k_places[0], back_compute, lambda kept: kept, carry)

    def backward_block(grad_qs, key_block, value_block, grad_k, grad_v, key_places):
        grad_list = list(grad_qs)
        key_parts = []
        value_parts = []
        for k_index in range(2):
            lower = k_index * span_rows
            upper = lower + span_rows
            key_piece = grad_k[lower:upper]
            value_piece = grad_v[lower:upper]
            for q_index in range(2):
                grad_list[q_index], key_piece, value_piece = back_span(
                    (grad_list[q_index], key_piece, value_piece),
                    q_index,
                    key_block[lower:upper],
                    value_block[lower:upper],
                    key_places[lower:upper],
                )
            key_parts.append(key_piece)
            value_parts.append(value_piece)
        return (
            tuple(grad_list),
            jnp.concatenate(key_parts, axis=0),
            jnp.concatenate(value_parts, axis=0),
        )

    grad_qs = (
        jnp.zeros((kv_local, group, span_rows, HD), f32),
        jnp.zeros((kv_local, group, span_rows, HD), f32),
    )
    grad_qs, grad_k, grad_v = backward_block(
        grad_qs,
        keys,
        values,
        jnp.zeros((rows, kv_local, HD), f32),
        jnp.zeros((rows, kv_local, HD), f32),
        places,
    )

    def backward_turn(turn, carry):
        key_block, value_block, grad_k, grad_v, grad_qs = carry
        key_block, value_block, grad_k, grad_v = (
            passed_along(key_block, "blk", -1),
            passed_along(value_block, "blk", -1),
            passed_along(grad_k.astype(jnp.bfloat16), "blk", -1).astype(grad_k.dtype),
            passed_along(grad_v.astype(jnp.bfloat16), "blk", -1).astype(grad_v.dtype),
        )
        source = (myself + turn) % devices
        grad_qs, grad_k, grad_v = backward_block(
            grad_qs,
            key_block,
            value_block,
            grad_k,
            grad_v,
            span_places(span_order, source, span_rows),
        )
        return (key_block, value_block, grad_k, grad_v, grad_qs)

    unused_keys, unused_values, grad_k, grad_v, grad_qs = lax.fori_loop(
        1, devices, backward_turn, (keys, values, grad_k, grad_v, grad_qs)
    )
    grad_k, grad_v = (
        passed_along(grad_k.astype(jnp.bfloat16), "blk", -1).astype(grad_k.dtype),
        passed_along(grad_v.astype(jnp.bfloat16), "blk", -1).astype(grad_v.dtype),
    )
    grad_q = jnp.concatenate([grad_qs[0], grad_qs[1]], axis=2)
    grad_qr = grad_q.transpose(2, 0, 1, 3).reshape(rows, heads_local, HD)
    back_q, q_terms = norm_back(
        q_proj, q_scale, gain_query.astype(f32), rotate_back(grad_qr, cosine, sine)
    )
    back_k, k_terms = norm_back(
        k_proj, k_scale, gain_key.astype(f32), rotate_back(grad_k, cosine, sine)
    )
    q_gain_part = jnp.sum(q_terms, axis=(0, 1))
    k_gain_part = jnp.sum(k_terms, axis=(0, 1))
    grad_q_low = back_q.reshape(rows, heads_local * HD).astype(bf16)
    grad_k_low = back_k.reshape(rows, kv_local * HD).astype(bf16)
    grad_v_low = grad_v.reshape(rows, kv_local * HD).astype(bf16)
    query_grad = jnp.einsum("td,tc->dc", normed_low, grad_q_low, preferred_element_type=f32)
    key_grad = jnp.einsum("td,tc->dc", normed_low, grad_k_low, preferred_element_type=f32)
    value_grad = jnp.einsum("td,tc->dc", normed_low, grad_v_low, preferred_element_type=f32)
    normed_part = (
        jnp.einsum("tc,dc->td", grad_q_low, w_query, preferred_element_type=f32)
        + jnp.einsum("tc,dc->td", grad_k_low, w_key, preferred_element_type=f32)
        + jnp.einsum("tc,dc->td", grad_v_low, w_value, preferred_element_type=f32)
    )
    grad_normed, q_gain_grad, k_gain_grad = (
        lax.psum(normed_part.astype(jnp.bfloat16), "fsdp").astype(jnp.float32),
        lax.psum(q_gain_part.astype(jnp.bfloat16), "fsdp").astype(jnp.float32),
        lax.psum(k_gain_part.astype(jnp.bfloat16), "fsdp").astype(jnp.float32),
    )
    back_input, input_terms = norm_back(inputs, scale_in, gain_input.astype(f32), grad_normed)
    input_gain_grad = jnp.sum(input_terms, axis=0)
    tokens_grad = grad_hidden + back_input
    (
        input_gain_sum,
        query_sum,
        key_sum,
        value_sum,
        q_gain_sum,
        k_gain_sum,
        out_sum,
        post_gain_sum,
        gate_sum,
        up_sum,
        down_sum,
    ) = (
        lax.psum_scatter(
            input_gain_grad.astype(jnp.bfloat16), "blk", scatter_dimension=0, tiled=True
        ).astype(jnp.float32),
        lax.psum_scatter(
            query_grad.astype(jnp.bfloat16), "blk", scatter_dimension=0, tiled=True
        ).astype(jnp.float32),
        lax.psum_scatter(
            key_grad.astype(jnp.bfloat16), "blk", scatter_dimension=0, tiled=True
        ).astype(jnp.float32),
        lax.psum_scatter(
            value_grad.astype(jnp.bfloat16), "blk", scatter_dimension=0, tiled=True
        ).astype(jnp.float32),
        lax.psum_scatter(
            q_gain_grad.astype(jnp.bfloat16), "blk", scatter_dimension=0, tiled=True
        ).astype(jnp.float32),
        lax.psum_scatter(
            k_gain_grad.astype(jnp.bfloat16), "blk", scatter_dimension=0, tiled=True
        ).astype(jnp.float32),
        lax.psum_scatter(
            out_grad.astype(jnp.bfloat16), "blk", scatter_dimension=1, tiled=True
        ).astype(jnp.float32),
        lax.psum_scatter(
            post_gain_grad.astype(jnp.bfloat16), "blk", scatter_dimension=0, tiled=True
        ).astype(jnp.float32),
        lax.psum_scatter(
            gate_grad.astype(jnp.bfloat16), "blk", scatter_dimension=0, tiled=True
        ).astype(jnp.float32),
        lax.psum_scatter(
            up_grad.astype(jnp.bfloat16), "blk", scatter_dimension=0, tiled=True
        ).astype(jnp.float32),
        lax.psum_scatter(
            down_grad.astype(jnp.bfloat16), "blk", scatter_dimension=1, tiled=True
        ).astype(jnp.float32),
    )
    return (
        layer_out,
        tokens_grad,
        input_gain_sum,
        query_sum,
        key_sum,
        value_sum,
        q_gain_sum,
        k_gain_sum,
        out_sum,
        post_gain_sum,
        gate_sum,
        up_sum,
        down_sum,
    )


def solution(mesh):
    placed = (
        P("blk", None),
        P(),
        P("blk"),
        P("blk", "fsdp"),
        P("blk", "fsdp"),
        P("blk", "fsdp"),
        P("blk"),
        P("blk"),
        P("fsdp", "blk"),
        P("blk"),
        P("blk", "fsdp"),
        P("blk", "fsdp"),
        P("fsdp", "blk"),
        P("blk", None),
    )
    return jax.shard_map(
        shards,
        mesh=mesh,
        in_specs=placed,
        out_specs=(
            P("blk", None),
            P("blk", None),
            P("blk"),
            P("blk", "fsdp"),
            P("blk", "fsdp"),
            P("blk", "fsdp"),
            P("blk"),
            P("blk"),
            P("fsdp", "blk"),
            P("blk"),
            P("blk", "fsdp"),
            P("blk", "fsdp"),
            P("fsdp", "blk"),
        ),
        check_vma=False,
    )
```

profile of v0, /device:TPU:0, one launch (start us, length us, event | category | flops | bytes accessed | tf_op | source)
XLA Modules:
  0.0 1410.6 jit_solution(7878932336239235766)
XLA Ops:
  14.7 10.3 all-gather
  30.8 13.2 all-reduce.7
  56.3 5.3 all-gather.12.cloned.1.call-done
  66.9 24.5 %all-gather.14.cloned.1.call-done = bf16[2048,512]{1,0:T(8,128)(2,1)} async-done(((bf16[256,512]{1,0:T(8,128)(2,1)}), bf16[2048,512]{1,0:T(8,128)(2,1)}) %all-gather.14.cloned.1.call-update) | async-done | bytes 2097168 | tf_op jit(solution)/shard_map/all_gather | solution.py:89
  109.6 4.5 conditional.12
  114.1 172.8 %while.54 = (s32[]{:T(128)}, bf16[512,2,128]{2,0,1:T(8,128)(2,1)}, bf16[512,2,128]{2,0,1:T(8,128)(2,1)}, f32[2,2,256]{2,1,0:T(2,128)S(1)}, f32[2,2,256]{2,1,0:T(...) while((s32[]{:T(128)}, bf16[512,2,128]{2,0,1:T(8,128)(2,1)}, ...), condition=%wide.region_32.33_spmd, body=%wide.region_15.32_spmd.sunk | while | flops 547627520 | bytes 24394712 | solution.py:183
  127.7 4.1 conditional.26
  131.8 5.0 conditional.24
  151.7 5.0 conditional.24
  156.7 4.9 conditional.25
  176.4 5.0 conditional.24
  181.4 4.9 conditional.25
  201.2 5.0 conditional.24
  206.2 4.9 conditional.25
  225.9 5.0 conditional.24
  230.9 4.9 conditional.25
  250.6 5.0 conditional.24
  255.6 4.9 conditional.25
  275.4 3.2 conditional.27
  278.6 4.9 conditional.25
  292.5 4.4 convolution_convert_fusion.6
  299.0 9.6 all-gather.1
  308.6 76.9 %all-reduce.14.cloned.1.call-done = bf16[512,2048]{1,0:T(8,128)(2,1)} async-done(((bf16[512,2048]{1,0:T(8,128)(2,1)}), bf16[512,2048]{1,0:T(8,128)(2,1)}) %all-reduce.14.cloned.1.call-update) | async-done | bytes 2097168 | tf_op jit(solution)/shard_map/psum | solution.py:192
  390.4 41.5 %all-gather.18.cloned.1.call-done = bf16[2048,1536]{1,0:T(8,128)(2,1)} async-done(((bf16[256,1536]{1,0:T(8,128)(2,1)}), bf16[2048,1536]{1,0:T(8,128)(2,1)}) %all-gather.18.cloned.1.call-update) | async-done | bytes 6291472 | tf_op jit(solution)/shard_map/all_gather | solution.py:96
  432.0 8.5 fusion.278
  440.5 39.1 %all-gather.20.cloned.1.call-done = bf16[2048,1536]{1,0:T(8,128)(2,1)} async-done(((bf16[256,1536]{1,0:T(8,128)(2,1)}), bf16[2048,1536]{1,0:T(8,128)(2,1)}) %all-gather.20.cloned.1.call-update) | async-done | bytes 6291472 | tf_op jit(solution)/shard_map/all_gather | solution.py:97
  479.6 8.5 fusion.279
  488.1 40.2 %all-gather.22.cloned.1.call-done = bf16[1536,2048]{1,0:T(8,128)(2,1)} async-done(((bf16[1536,256]{1,0:T(8,128)(2,1)}), bf16[1536,2048]{1,0:T(8,128)(2,1)}) %all-gather.22.cloned.1.call-update) | async-done | bytes 6291472 | tf_op jit(solution)/shard_map/all_gather | solution.py:98
  528.3 11.0 multiply_convert_fusion.1
  539.3 6.7 fusion.280
  546.1 4.6 add_convert_fusion.1
  551.2 86.2 %all-reduce.16.cloned.1.call-done = bf16[512,2048]{1,0:T(8,128)(2,1)} async-done(((bf16[512,2048]{1,0:T(8,128)(2,1)}), bf16[512,2048]{1,0:T(8,128)(2,1)}) %all-reduce.16.cloned.1.call-update) | async-done | bytes 2097168 | tf_op jit(solution)/shard_map/psum | solution.py:241
  637.4 4.5 fusion.167
  664.4 208.4 %while.55 = (s32[]{:T(128)}, bf16[512,2,128]{2,0,1:T(8,128)(2,1)}, bf16[512,2,128]{2,0,1:T(8,128)(2,1)}, bf16[512,2,128]{2,0,1:T(8,128)(2,1)}, bf16[512,2,128]{2...) while((s32[]{:T(128)}, bf16[512,2,128]{2,0,1:T(8,128)(2,1)}, ...), condition=%wide.region_52.53_spmd, body=%wide.region_43.52_spmd.sunk | while | flops 1352663552 | bytes 43564244 | solution.py:347
  664.4 4.4 collective-permute-start.2
  694.8 3.6 collective-permute-start.2
  713.7 4.1 conditional.28
  717.8 3.2 conditional.30
  742.3 4.1 conditional.28
  746.4 3.2 conditional.30
  771.9 4.1 conditional.28
  775.9 3.2 conditional.30
  801.4 4.1 conditional.28
  830.9 4.1 conditional.28
  835.0 3.2 conditional.30
  860.4 4.1 conditional.28
  864.5 4.1 conditional.29
  874.7 4.2 collective-permute-done.6
  888.8 3.9 collective-permute-done.7
  908.9 8.3 convolution_convert_fusion.5
  922.9 4.8 convolution_convert_fusion.3
  928.0 8.2 convolution_convert_fusion.2
  936.3 8.2 convolution_convert_fusion.1
  944.6 8.1 convolution_convert_fusion
  955.7 4.1 reduce-scatter.12.cloned.1.call-done
  961.4 42.7 %reduce-scatter.8.cloned.1.call-done = bf16[256,512]{1,0:T(8,128)(2,1)} async-done(((bf16[2048,512]{1,0:T(8,128)(2,1)}), bf16[256,512]{1,0:T(8,128)(2,1)}) %reduce-scatter.8.cloned.1.call-update) | async-done | bytes 262160 | tf_op jit(solution)/shard_map/reduce_scatter | solution.py:399
  1006.0 156.1 %all-reduce.18.cloned.1.call-done = (bf16[512,2048]{1,0:T(8,128)(2,1)}, bf16[512,2048]{1,0:T(8,128)(2,1)}) async-done(((bf16[512,2048]{1,0:T(8,128)(2,1)}, bf16[512,2048]{1,0:T(8,128)(2,1)}), (bf16[512,2048]{1,0:T(8,128)(2,1)}, bf16[512,2048]{1,0:T(8,128)(2,1)})) %all-reduce.18.cloned.1.call-update) | async-done | bytes 4194320 | tf_op jit(solution)/shard_map/psum | solution.py:202
  1165.3 14.2 %all-reduce.6 = (bf16[2048]{0:T(1024)(128)(2,1)S(1)}, bf16[128]{0:T(256)(128)(2,1)S(1)}, bf16[128]{0:T(256)(128)(2,1)S(1)}, bf16[2048]{0:T(1024)(128)(2,1)S(1)}) all-reduce(bf16[2048]{0:T(1024)(128)(2,1)S(1)} %get-tuple-element.1634, bf16[128]{0:T(256)(128)(2,1)S(1)} %bitcast_reduce_fusion, ...), channel_id=2, replica_groups=mesh['blk'=8,'fsdp'=4] {'blk'}, use_global_device_ids=true, to_apply=%region_58.59.clone | all-reduce | flops 4352 | bytes 17408
  1179.6 25.9 %reduce-scatter.14.cloned.1.call-done = bf16[512,256]{1,0:T(8,128)(2,1)} async-done(((bf16[512,2048]{1,0:T(8,128)(2,1)}), bf16[512,256]{1,0:T(8,128)(2,1)}) %reduce-scatter.14.cloned.1.call-update) | async-done | bytes 262160 | tf_op jit(solution)/shard_map/reduce_scatter | solution.py:414
  1207.3 11.7 all-reduce.8
  1221.3 7.7 fusion.162
  1229.0 41.9 %reduce-scatter.16.cloned.1.call-done = bf16[256,1536]{1,0:T(8,128)(2,1)} async-done(((bf16[2048,1536]{1,0:T(8,128)(2,1)}), bf16[256,1536]{1,0:T(8,128)(2,1)}) %reduce-scatter.16.cloned.1.call-update) | async-done | bytes 786448 | tf_op jit(solution)/shard_map/reduce_scatter | solution.py:420
  1273.4 62.5 %reduce-scatter.18.cloned.1.call-done = bf16[256,1536]{1,0:T(8,128)(2,1)} async-done(((bf16[2048,1536]{1,0:T(8,128)(2,1)}), bf16[256,1536]{1,0:T(8,128)(2,1)}) %reduce-scatter.18.cloned.1.call-update) | async-done | bytes 786448 | tf_op jit(solution)/shard_map/reduce_scatter | solution.py:423
  1338.3 62.9 %reduce-scatter.20.cloned.1.call-done = bf16[1536,256]{1,0:T(8,128)(2,1)} async-done(((bf16[1536,2048]{1,0:T(8,128)(2,1)}), bf16[1536,256]{1,0:T(8,128)(2,1)}) %reduce-scatter.20.cloned.1.call-update) | async-done | bytes 786448 | tf_op jit(solution)/shard_map/reduce_scatter | solution.py:426
  (785 shorter events, 449.5 us)
Async XLA Ops:
  7.2 41.1 %all-gather.10.cloned.1.call-start = ((), (), s32[]{:S(2)}) async-start(), calls=%async_computation.7 | async-start | bytes 1179648 | tf_op jit(solution)/shard_map/all_gather | solution.py:90
  7.9 53.7 %all-gather.12.cloned.1.call-start = ((), (), s32[]{:S(2)}) async-start(), calls=%async_computation.8 | async-start | bytes 1179648 | tf_op jit(solution)/shard_map/all_gather | solution.py:91
  8.7 82.7 %all-gather.14.cloned.1.call-start = ((), (), s32[]{:S(2)}) async-start(), calls=%async_computation.9 | async-start | bytes 2359296 | tf_op jit(solution)/shard_map/all_gather | solution.py:89
  9.4 283.1 %all-gather.16.cloned.1.call-start = ((), (), s32[]{:S(2)}) async-start(), calls=%async_computation.10 | async-start | bytes 2359296 | tf_op jit(solution)/shard_map/all_gather | solution.py:94
  10.0 375.6 %all-reduce.14.cloned.1.call-start = ((), (), s32[]{:S(2)}) async-start(), calls=%async_computation.11 | async-start | bytes 4194304 | tf_op jit(solution)/shard_map/psum | solution.py:192
  25.0 66.4 %copy-start.60 = (f32[8,1,256]{2,1,0:T(1,128)}, f32[8,1,256]{2,1,0:T(1,128)S(1)}, u32[]{:S(2)}) copy-start(f32[8,1,256]{2,1,0:T(1,128)S(1)} %convert_element_type.482) | copy-start | bytes 24580
  46.0 48.8 %copy-start.17 = (f32[512,128]{0,1:T(8,128)}, f32[512,128]{0,1:T(8,128)S(1)}, u32[]{:S(2)}) copy-start(f32[512,128]{0,1:T(8,128)S(1)} %copy.187) | copy-start | bytes 786436
  114.1 9.1 collective-permute-start
  114.4 11.7 collective-permute-start.1
  140.2 8.2 collective-permute-start
  140.2 9.8 collective-permute-start.1
  164.9 8.9 collective-permute-start
  165.5 9.2 collective-permute-start.1
  189.7 8.5 collective-permute-start
  189.7 9.8 collective-permute-start.1
  214.4 8.2 collective-permute-start
  214.4 9.8 collective-permute-start.1
  239.2 8.2 collective-permute-start
  239.2 9.8 collective-permute-start.1
  263.9 8.2 collective-permute-start
  263.9 9.8 collective-permute-start.1
  296.9 135.1 %all-gather.18.cloned.1.call-start = ((), (), s32[]{:S(2)}) async-start(), calls=%async_computation.12 | async-start | bytes 7077888 | tf_op jit(solution)/shard_map/all_gather | solution.py:96
  297.5 182.1 %all-gather.20.cloned.1.call-start = ((), (), s32[]{:S(2)}) async-start(), calls=%async_computation.13 | async-start | bytes 7077888 | tf_op jit(solution)/shard_map/all_gather | solution.py:97
  298.2 230.1 %all-gather.22.cloned.1.call-start = ((), (), s32[]{:S(2)}) async-start(), calls=%async_computation.14 | async-start | bytes 7077888 | tf_op jit(solution)/shard_map/all_gather | solution.py:98
  299.0 338.4 %all-reduce.16.cloned.1.call-start = ((), (), s32[]{:S(2)}) async-start(), calls=%async_computation.15 | async-start | bytes 4194304 | tf_op jit(solution)/shard_map/psum | solution.py:241
  550.7 403.3 %reduce-scatter.10.cloned.1.call-start = ((), (), s32[]{:S(2)}) async-start(), calls=%async_computation.17 | async-start | bytes 1179648 | tf_op jit(solution)/shard_map/reduce_scatter | solution.py:402
  664.4 17.1 %collective-permute-start.2 = (bf16[512,2,128]{2,0,1:T(8,128)(2,1)}, bf16[512,2,128]{2,0,1:T(8,128)(2,1)}, u32[]{:S(2)}, u32[]{:S(2)}) collective-permute-start(bf16[512,2,128]{2,0,1:T(8,128)(2,1)} %get-tuple-element.2275), channel_id=1, source_target_pairs={{4,0},{8,4},{12,8},{16,12},{20,16},{24,20},{28,24},{0,28},{5,1},{9... | collective-permute-start | bytes 786440 | tf_op jit(solution)/shard_map/while/body/eval_jaxpr/ppermute | solution.py:17
  668.8 13.7 collective-permute-start.3
  669.5 9.2 collective-permute-start.4
  669.5 11.9 collective-permute-start.5
  694.8 16.2 %collective-permute-start.2 = (bf16[512,2,128]{2,0,1:T(8,128)(2,1)}, bf16[512,2,128]{2,0,1:T(8,128)(2,1)}, u32[]{:S(2)}, u32[]{:S(2)}) collective-permute-start(bf16[512,2,128]{2,0,1:T(8,128)(2,1)} %get-tuple-element.2275), channel_id=1, source_target_pairs={{4,0},{8,4},{12,8},{16,12},{20,16},{24,20},{28,24},{0,28},{5,1},{9... | collective-permute-start | bytes 786440 | tf_op jit(solution)/shard_map/while/body/eval_jaxpr/ppermute | solution.py:17
  698.3 13.7 collective-permute-start.3
  698.4 9.8 collective-permute-start.4
  698.4 12.6 collective-permute-start.5
  725.2 14.4 %collective-permute-start.2 = (bf16[512,2,128]{2,0,1:T(8,128)(2,1)}, bf16[512,2,128]{2,0,1:T(8,128)(2,1)}, u32[]{:S(2)}, u32[]{:S(2)}) collective-permute-start(bf16[512,2,128]{2,0,1:T(8,128)(2,1)} %get-tuple-element.2275), channel_id=1, source_target_pairs={{4,0},{8,4},{12,8},{16,12},{20,16},{24,20},{28,24},{0,28},{5,1},{9... | collective-permute-start | bytes 786440 | tf_op jit(solution)/shard_map/while/body/eval_jaxpr/ppermute | solution.py:17
  727.0 13.7 collective-permute-start.3
  727.0 9.8 collective-permute-start.4
  727.7 11.9 collective-permute-start.5
  753.9 15.3 %collective-permute-start.2 = (bf16[512,2,128]{2,0,1:T(8,128)(2,1)}, bf16[512,2,128]{2,0,1:T(8,128)(2,1)}, u32[]{:S(2)}, u32[]{:S(2)}) collective-permute-start(bf16[512,2,128]{2,0,1:T(8,128)(2,1)} %get-tuple-element.2275), channel_id=1, source_target_pairs={{4,0},{8,4},{12,8},{16,12},{20,16},{24,20},{28,24},{0,28},{5,1},{9... | collective-permute-start | bytes 786440 | tf_op jit(solution)/shard_map/while/body/eval_jaxpr/ppermute | solution.py:17
  756.5 13.7 collective-permute-start.3
  756.5 9.8 collective-permute-start.4
  756.6 12.6 collective-permute-start.5
  783.4 15.3 %collective-permute-start.2 = (bf16[512,2,128]{2,0,1:T(8,128)(2,1)}, bf16[512,2,128]{2,0,1:T(8,128)(2,1)}, u32[]{:S(2)}, u32[]{:S(2)}) collective-permute-start(bf16[512,2,128]{2,0,1:T(8,128)(2,1)} %get-tuple-element.2275), channel_id=1, source_target_pairs={{4,0},{8,4},{12,8},{16,12},{20,16},{24,20},{28,24},{0,28},{5,1},{9... | collective-permute-start | bytes 786440 | tf_op jit(solution)/shard_map/while/body/eval_jaxpr/ppermute | solution.py:17
  786.0 13.7 collective-permute-start.3
  786.1 9.8 collective-permute-start.4
  786.1 12.6 collective-permute-start.5
  812.9 15.3 %collective-permute-start.2 = (bf16[512,2,128]{2,0,1:T(8,128)(2,1)}, bf16[512,2,128]{2,0,1:T(8,128)(2,1)}, u32[]{:S(2)}, u32[]{:S(2)}) collective-permute-start(bf16[512,2,128]{2,0,1:T(8,128)(2,1)} %get-tuple-element.2275), channel_id=1, source_target_pairs={{4,0},{8,4},{12,8},{16,12},{20,16},{24,20},{28,24},{0,28},{5,1},{9... | collective-permute-start | bytes 786440 | tf_op jit(solution)/shard_map/while/body/eval_jaxpr/ppermute | solution.py:17
  815.6 13.7 collective-permute-start.3
  815.6 9.8 collective-permute-start.4
  815.6 12.6 collective-permute-start.5
  842.4 15.3 %collective-permute-start.2 = (bf16[512,2,128]{2,0,1:T(8,128)(2,1)}, bf16[512,2,128]{2,0,1:T(8,128)(2,1)}, u32[]{:S(2)}, u32[]{:S(2)}) collective-permute-start(bf16[512,2,128]{2,0,1:T(8,128)(2,1)} %get-tuple-element.2275), channel_id=1, source_target_pairs={{4,0},{8,4},{12,8},{16,12},{20,16},{24,20},{28,24},{0,28},{5,1},{9... | collective-permute-start | bytes 786440 | tf_op jit(solution)/shard_map/while/body/eval_jaxpr/ppermute | solution.py:17
  845.1 13.7 collective-permute-start.3
  845.1 9.8 collective-permute-start.4
  845.1 12.6 collective-permute-start.5
  872.9 6.0 collective-permute-start.6
  884.9 75.0 %reduce-scatter.12.cloned.1.call-start = ((), (), s32[]{:S(2)}) async-start(), calls=%async_computation.18 | async-start | bytes 1179648 | tf_op jit(solution)/shard_map/reduce_scatter | solution.py:405
  886.0 6.6 collective-permute-start.7
  895.3 108.8 %reduce-scatter.8.cloned.1.call-start = ((), (), s32[]{:S(2)}) async-start(), calls=%async_computation.16 | async-start | bytes 2359296 | tf_op jit(solution)/shard_map/reduce_scatter | solution.py:399
  908.8 253.3 %all-reduce.18.cloned.1.call-start = ((), (), s32[]{:S(2)}) async-start(), calls=%async_computation.23 | async-start | bytes 8388608 | tf_op jit(solution)/shard_map/psum | solution.py:202
  921.9 283.6 %reduce-scatter.14.cloned.1.call-start = ((), (), s32[]{:S(2)}) async-start(), calls=%async_computation.19 | async-start | bytes 2359296 | tf_op jit(solution)/shard_map/reduce_scatter | solution.py:414
  927.7 343.2 %reduce-scatter.16.cloned.1.call-start = ((), (), s32[]{:S(2)}) async-start(), calls=%async_computation.20 | async-start | bytes 7077888 | tf_op jit(solution)/shard_map/reduce_scatter | solution.py:420
  936.2 399.7 %reduce-scatter.18.cloned.1.call-start = ((), (), s32[]{:S(2)}) async-start(), calls=%async_computation.21 | async-start | bytes 7077888 | tf_op jit(solution)/shard_map/reduce_scatter | solution.py:423
  944.5 456.8 %reduce-scatter.20.cloned.1.call-start = ((), (), s32[]{:S(2)}) async-start(), calls=%async_computation.22 | async-start | bytes 7077888 | tf_op jit(solution)/shard_map/reduce_scatter | solution.py:426
  952.7 212.6 %copy-start.64 = (bf16[2048]{0:T(1024)(128)(2,1)S(1)}, bf16[2048]{0:T(1024)(128)(2,1)}, u32[]{:S(2)}) copy-start(bf16[2048]{0:T(1024)(128)(2,1)} %get-tuple-element.1632) | copy-start | bytes 12292
  (72 other events, 435.0 us)
Sparse Core Ops, SparseCore 0:
  9.9 26.1 all-gather.9
  38.0 23.5 all-gather.11
  63.5 27.8 all-gather.13
  93.1 28.7 all-gather.15
  297.0 88.4 all-reduce.13
  387.5 44.4 all-gather.17
  434.0 45.5 all-gather.19
  481.6 46.6 all-gather.21
  550.9 86.5 all-reduce.15
  885.0 35.5 reduce-scatter.9
  923.8 36.0 reduce-scatter.11
  963.0 41.1 reduce-scatter.7
  1006.7 155.3 all-reduce.17
  1165.2 40.2 reduce-scatter.13
  1209.1 61.7 reduce-scatter.15
  1274.1 61.7 reduce-scatter.17
  1339.5 61.7 reduce-scatter.19
where the time goes:
time: 1420 us; the launch traced here: 1410 us
  waiting for transfers between devices  756 us (53%)
  matrix products  197 us (14%)
  local copies, waits for them, and re-layouts  148 us (10%)
  other arithmetic  125 us (9%)
  loops' own time  75.1 us (5%)
  blocking collectives  58.9 us (4%)
  starting transfers between devices  30.3 us (2%)
  between operations  20.1 us (1%)
    psum x1, waiting for transfers between devices, shards(): lax.psum(jnp.dot(act, w_down, preferred_element_type=f32).astype(jnp.bflo...  156 us
    psum x1, waiting for transfers between devices, shards(): lax.psum(post_part.astype(jnp.bfloat16), 'fsdp').astype(jnp.float32)  86.2 us
    psum x1, waiting for transfers between devices, shards(): lax.psum(jnp.dot(context_low, w_out, preferred_element_type=f32).astype(j...  76.9 us
    reduce_scatter x1, waiting for transfers between devices, shards(): lax.psum_scatter(down_grad.astype(jnp.bfloat16), 'blk', scatter_dimension...  62.9 us
    reduce_scatter x1, waiting for transfers between devices, shards(): lax.psum_scatter(up_grad.astype(jnp.bfloat16), 'blk', scatter_dimension=0...  62.5 us
    while x28, local copies, waits for them, and re-layouts  46.7 us
    reduce_scatter x1, waiting for transfers between devices, shards(): lax.psum_scatter(query_grad.astype(jnp.bfloat16), 'blk', scatter_dimensio...  42.7 us
    reduce_scatter x1, waiting for transfers between devices, shards(): lax.psum_scatter(gate_grad.astype(jnp.bfloat16), 'blk', scatter_dimension...  41.9 us
  transfers between devices with their start and end apart: 61, of which 37 were waited for; matrix products, arithmetic and copies ran while one was open for 22% of the time, Pallas kernels for 0%

commit v1 on v0

v1 whole, which is shorter than its diff:
```python
import functools
import math

import jax
import jax.numpy as jnp
from jax import lax
from jax.experimental import pallas as pl
from jax.experimental.pallas import tpu as pltpu
from jax.sharding import PartitionSpec as P

HD = 128
EPS = 1e-06
THETA = 1000000.0
LOG2E = math.log2(math.e)
LN2 = math.log(2.0)
MIB = 1024 * 1024

F32 = jnp.float32
BF16 = jnp.bfloat16


def dims(lhs, rhs, left, right):
    return lax.dot_general(lhs, rhs, (((left,), (right,)), ((), ())), preferred_element_type=F32)


def mask_order(n):
    return [2 * i for i in range(n // 2)] + [2 * i + 1 for i in range(n // 2)]


def high_bits(n):
    return [1 << i for i in range(1, n.bit_length() - 1)]


def exchange(block, bit):
    n = lax.axis_size("blk")
    return lax.ppermute(block, "blk", [(i, i ^ bit) for i in range(n)])


def gather_rows(piece, bits):
    rows = piece.shape[0]
    held = {0: piece}
    for bit in bits:
        masks = sorted(held)
        sent = [held[m] for m in masks]
        got = exchange(sent[0] if len(sent) == 1 else jnp.concatenate(sent, axis=0), bit)
        for i, m in enumerate(masks):
            held[m | bit] = got[i * rows : (i + 1) * rows]
    own = jnp.concatenate([held[m] for m in sorted(held)], axis=0)
    return own, exchange(own, 1)


def add_low(a, b):
    return (a.astype(F32) + b.astype(F32)).astype(BF16)


def scatter_sum(own, got, bits):
    count = 2 ** len(bits)
    rows = own.shape[0] // count
    held = {}
    for i in range(count):
        part = slice(i * rows, (i + 1) * rows)
        held[2 * i] = (own[part], got[part])
    for bit in bits:
        leave = [m for m in sorted(held) if m & bit]
        stay = [m for m in sorted(held) if not m & bit]
        sent = [add_low(*held[m]) for m in leave]
        back = exchange(sent[0] if len(sent) == 1 else jnp.concatenate(sent, axis=0), bit)
        held = {
            m: (add_low(*held[m]), back[i * rows : (i + 1) * rows]) for i, m in enumerate(stay)
        }
    return held[0][0].astype(F32) + held[0][1].astype(F32)


def row_norm(values, gain):
    scale = lax.rsqrt(jnp.mean(values * values, axis=-1, keepdims=True) + EPS)
    return (values * scale * gain, scale)


def norm_back(values, scale, weighted):
    inner = jnp.mean(weighted * values, axis=-1, keepdims=True)
    return scale * (weighted - values * scale * scale * inner)


def rope_tables(places, width):
    half = width // 2
    freqs = THETA ** (-jnp.arange(half, dtype=F32) * 2.0 / width)
    angles = places.astype(F32)[:, None] * freqs[None, :]
    sine = jnp.sin(angles)
    cosine = jnp.cos(angles)
    return (jnp.concatenate([cosine, cosine], axis=1), jnp.concatenate([-sine, sine], axis=1))


def turned(values):
    half = values.shape[-1] // 2
    return jnp.concatenate([values[..., half:], values[..., :half]], axis=-1)


def attend_kernel(span, sc, q_ref, k0, k1, v0, v1, ctx_ref, lse_ref, k_s, v_s, acc_s, sum_s):
    half = k0.shape[0]
    k_s[:half] = k0[...]
    k_s[half:] = k1[...]
    v_s[:half] = v0[...]
    v_s[half:] = v1[...]
    group = q_ref.shape[1] // HD
    rows = span * group
    for s in range(2):
        top = slice(s * span, (s + 1) * span)
        q = jnp.concatenate([q_ref[top, g * HD : (g + 1) * HD] for g in range(group)], axis=0)
        acc_s[...] = jnp.zeros_like(acc_s)
        sum_s[...] = jnp.zeros_like(sum_s)

        def step(p, masked):
            at = pl.ds(pl.multiple_of(sc[2 + p] * span, span), span)
            e = jnp.exp2(dims(q, k_s[at, :], 1, 1))
            if masked:
                row = lax.broadcasted_iota(jnp.int32, (rows, span), 0) % span
                col = lax.broadcasted_iota(jnp.int32, (rows, span), 1)
                e = jnp.where(row >= col, e, 0.0)
            part = e[:, :HD]
            for c in range(HD, span, HD):
                part = part + e[:, c : c + HD]
            sum_s[...] += part
            acc_s[...] += dims(e.astype(BF16), v_s[at, :], 1, 0)

        pl.loop(0, sc[s])(lambda p: step(p, False))
        step(sc[s], True)
        total = jnp.sum(sum_s[...], axis=1, keepdims=True)
        ctx = (acc_s[...] / total).astype(BF16)
        for g in range(group):
            ctx_ref[top, g * HD : (g + 1) * HD] = ctx[g * span : (g + 1) * span]
        wide = jnp.broadcast_to(jnp.log2(total), (rows, HD))
        lse_ref[0, s : s + 1, :] = wide.T[0:1]


def attend_back_kernel(
    span, sc, q_ref, do_ref, ctx_ref, lse_ref, k0, k1, v0, v1, dq_ref, dk0, dk1, dv0, dv1, k_s, v_s, dk_s, dv_s, dq_s
):
    half = k0.shape[0]
    k_s[:half] = k0[...]
    k_s[half:] = k1[...]
    v_s[:half] = v0[...]
    v_s[half:] = v1[...]
    dk_s[...] = jnp.zeros_like(dk_s)
    dv_s[...] = jnp.zeros_like(dv_s)
    group = q_ref.shape[1] // HD
    rows = span * group
    for s in range(2):
        top = slice(s * span, (s + 1) * span)

        def stacked(ref):
            return jnp.concatenate([ref[top, g * HD : (g + 1) * HD] for g in range(group)], axis=0)

        q = stacked(q_ref)
        do = stacked(do_ref)
        q_t = q.T
        do_t = do.T
        product = do.astype(F32) * stacked(ctx_ref).astype(F32)
        delta = jnp.sum(product.T, axis=0, keepdims=True)
        lse = lse_ref[0, s : s + 1, :]
        dq_s[...] = jnp.zeros_like(dq_s)

        def step(p, masked):
            at = pl.ds(pl.multiple_of(sc[2 + p] * span, span), span)
            k = k_s[at, :]
            probs = jnp.exp2(dims(k, q_t, 1, 0) - lse)
            if masked:
                key = lax.broadcasted_iota(jnp.int32, (span, rows), 0)
                query = lax.broadcasted_iota(jnp.int32, (span, rows), 1) % span
                probs = jnp.where(query >= key, probs, 0.0)
            dv_s[at, :] += dims(probs.astype(BF16), do, 1, 0)
            grad = (probs * (dims(v_s[at, :], do_t, 1, 0) - delta)).astype(BF16)
            dk_s[at, :] += dims(grad, q, 1, 0)
            dq_s[...] += dims(grad, k, 0, 0)

        pl.loop(0, sc[s])(lambda p: step(p, False))
        step(sc[s], True)
        dq = dq_s[...] * (HD**-0.5)
        for g in range(group):
            dq_ref[top, g * HD : (g + 1) * HD] = dq[g * span : (g + 1) * span]
    dk0[...] = (dk_s[:half] * LN2).astype(BF16)
    dk1[...] = (dk_s[half:] * LN2).astype(BF16)
    dv0[...] = dv_s[:half].astype(BF16)
    dv1[...] = dv_s[half:].astype(BF16)


def attend(scalars, queries, keys, values, span):
    rows, width = queries.shape
    kv_local = keys[0].shape[1] // HD
    across = width // kv_local
    half = keys[0].shape[0]
    wide = pl.BlockSpec((rows, across), lambda h, sc: (0, h))
    slots = pl.Buffered(2 if half <= 4096 else 1)
    tall = pl.BlockSpec((half, HD), lambda h, sc: (0, h))
    read = pl.BlockSpec((half, HD), lambda h, sc: (0, h), pipeline_mode=slots)
    stacked = across // HD * span
    flops = 4 * rows * half * width
    return pl.pallas_call(
        functools.partial(attend_kernel, span),
        grid_spec=pltpu.PrefetchScalarGridSpec(
            num_scalar_prefetch=1,
            grid=(kv_local,),
            in_specs=[wide, read, read, read, read],
            out_specs=[wide, pl.BlockSpec((1, 2, stacked), lambda h, sc: (h, 0, 0))],
            scratch_shapes=[
                pltpu.VMEM((2 * half, HD), BF16),
                pltpu.VMEM((2 * half, HD), BF16),
                pltpu.VMEM((stacked, HD), F32),
                pltpu.VMEM((stacked, HD), F32),
            ],
        ),
        out_shape=[
            jax.ShapeDtypeStruct((rows, width), BF16),
            jax.ShapeDtypeStruct((kv_local, 2, stacked), F32),
        ],
        compiler_params=pltpu.CompilerParams(vmem_limit_bytes=min(60 * MIB, 16 * MIB + 44 * HD * half)),
        cost_estimate=pl.CostEstimate(
            flops=4 * flops, bytes_accessed=16 * half * HD, transcendentals=rows * half
        ),
        name="attend",
    )(scalars, queries, *keys, *values)


def attend_back(scalars, queries, grad_context, context, lse, keys, values, span):
    rows, width = queries.shape
    kv_local = keys[0].shape[1] // HD
    across = width // kv_local
    half = keys[0].shape[0]
    wide = pl.BlockSpec((rows, across), lambda h, sc: (0, h))
    slots = pl.Buffered(2 if half <= 4096 else 1)
    tall = pl.BlockSpec((half, HD), lambda h, sc: (0, h))
    read = pl.BlockSpec((half, HD), lambda h, sc: (0, h), pipeline_mode=slots)
    stacked = across // HD * span
    flops = 10 * rows * half * width
    grads = jax.ShapeDtypeStruct(keys[0].shape, BF16)
    return pl.pallas_call(
        functools.partial(attend_back_kernel, span),
        grid_spec=pltpu.PrefetchScalarGridSpec(
            num_scalar_prefetch=1,
            grid=(kv_local,),
            in_specs=[wide, wide, wide, pl.BlockSpec((1, 2, stacked), lambda h, sc: (h, 0, 0))]
            + [read] * 4,
            out_specs=[wide] + [tall] * 4,
            scratch_shapes=[
                pltpu.VMEM((2 * half, HD), BF16),
                pltpu.VMEM((2 * half, HD), BF16),
                pltpu.VMEM((2 * half, HD), F32),
                pltpu.VMEM((2 * half, HD), F32),
                pltpu.VMEM((stacked, HD), F32),
            ],
        ),
        out_shape=[jax.ShapeDtypeStruct((rows, width), F32)] + [grads] * 4,
        compiler_params=pltpu.CompilerParams(vmem_limit_bytes=min(60 * MIB, 16 * MIB + 44 * HD * half)),
        cost_estimate=pl.CostEstimate(
            flops=4 * flops, bytes_accessed=32 * half * HD, transcendentals=rows * half
        ),
        name="attend_back",
    )(scalars, queries, grad_context, context, lse, *keys, *values)


def shards(
    tokens,
    span_order,
    input_gain,
    query_weight,
    key_weight,
    value_weight,
    query_gain,
    key_gain,
    output_weight,
    post_gain,
    gate_weight,
    up_weight,
    down_weight,
    cotangent,
):
    n = lax.axis_size("blk")
    me = lax.axis_index("blk")
    bits = high_bits(n)
    flipped = bits[::-1]
    masks = mask_order(n)
    rows, width = tokens.shape
    block = width // n
    split = width // 2
    span = rows // 2
    q_cols = query_weight.shape[1]
    kv_cols = key_weight.shape[1]
    heads = q_cols // HD
    kv_heads = kv_cols // HD
    units = gate_weight.shape[1]
    o_cols = output_weight.shape[0]

    def in_masks(array):
        return jnp.concatenate(
            [lax.dynamic_slice_in_dim(array, (me ^ m) * block, block, 1) for m in masks], axis=1
        )

    def in_blocks(array):
        places = [((me ^ j) >> 1) + ((me ^ j) & 1) * (n // 2) for j in range(n)]
        return jnp.concatenate(
            [lax.dynamic_slice_in_dim(array, p * block, block, 1) for p in places], axis=1
        )

    gains = jnp.concatenate([input_gain, post_gain, query_gain, key_gain]).reshape(1, -1)
    gains = jnp.concatenate(gather_rows(gains, bits), axis=0).astype(F32)
    wq = gather_rows(query_weight, bits)
    wkv = gather_rows(jnp.concatenate([key_weight, value_weight], axis=1), flipped)
    gain_input = gains[:, :block].reshape(1, width)
    gain_post = gains[:, block : 2 * block].reshape(1, width)
    chosen = (me ^ jnp.arange(n))[:, None] == jnp.array(masks)[None, :]
    head_gains = jnp.sum(jnp.where(chosen[:, :, None], gains[None, :, 2 * block :], 0.0), axis=1)
    part = head_gains.shape[1] // 2
    gain_query = head_gains[:, :part].reshape(HD)
    gain_key = head_gains[:, part:].reshape(HD)

    tokens = in_masks(tokens)
    cotangent = in_masks(cotangent)
    inputs = tokens.astype(F32)
    normed, scale_in = row_norm(inputs, gain_input)
    normed_low = normed.astype(BF16)

    def project(left, pair):
        return dims(left[:, :split], pair[0], 1, 0) + dims(left[:, split:], pair[1], 1, 0)

    q_proj = project(normed_low, wq).reshape(rows, heads, HD)
    kv_proj = project(normed_low, wkv)
    k_proj = kv_proj[:, :kv_cols].reshape(rows, kv_heads, HD)

    spans = span_order.reshape(n, 2)
    chunk_ids = jnp.sum(
        jnp.where(
            (me ^ jnp.array(masks))[:, None, None] == jnp.arange(n)[None, :, None], spans[None], 0
        ),
        axis=1,
    ).reshape(-1)
    count = 2 * n
    positions = jnp.sum(
        jnp.where(
            chunk_ids[None, :] == jnp.arange(count)[:, None], jnp.arange(count)[None, :], 0
        ),
        axis=1,
    )
    scalars = jnp.concatenate([chunk_ids[:2], positions]).astype(jnp.int32)
    places = (chunk_ids[:2, None] * span + jnp.arange(span)[None, :]).reshape(-1)
    cosine, sine = rope_tables(places, HD)
    cosine, sine = cosine[:, None, :], sine[:, None, :]

    def rotate(values):
        return values * cosine + turned(values) * sine

    def rotate_back(grads):
        return grads * cosine + turned(grads * sine)

    q_normed, q_scale = row_norm(q_proj, gain_query)
    queries = (rotate(q_normed) * (HD**-0.5 * LOG2E)).astype(BF16).reshape(rows, q_cols)
    k_normed, k_scale = row_norm(k_proj, gain_key)
    keys = rotate(k_normed).astype(BF16).reshape(rows, kv_cols)
    values = kv_proj[:, kv_cols:].astype(BF16)
    all_keys = gather_rows(keys, bits)
    all_values = gather_rows(values, flipped)

    down_t = down_weight.T
    cut = (units - o_cols) // 2
    side_a = jnp.concatenate([output_weight.T, down_t[:, :cut]], axis=1)
    side_b = down_t[:, cut:]
    side_a, side_b, _ = lax.optimization_barrier((side_a, side_b, wkv[1]))
    side_a = gather_rows(side_a, bits)
    side_b = gather_rows(side_b, flipped)
    wo = [w[:, :o_cols] for w in side_a]
    wd_a = [w[:, o_cols:] for w in side_a]
    wd_b = side_b
    wg = gather_rows(gate_weight, bits)
    wu = gather_rows(up_weight, flipped)

    context, lse = attend(scalars, queries, all_keys, all_values, span)

    attn_part = jnp.concatenate([dims(context, w, 1, 1) for w in wo], axis=1).astype(BF16)
    attn = lax.psum(attn_part, "fsdp").astype(F32)
    hidden = inputs + attn
    post, scale_post = row_norm(hidden, gain_post)
    post_low = post.astype(BF16)
    grad_act = jnp.concatenate([project(cotangent, wd_a), project(cotangent, wd_b)], axis=1)
    gate = project(post_low, wg)
    up = project(post_low, wu)
    sigma = jax.nn.sigmoid(gate)
    silu = gate * sigma
    act = (silu * up).astype(BF16)
    grad_up = (grad_act * silu).astype(BF16)
    grad_gate = (grad_act * up * sigma * (1.0 + gate * (1.0 - sigma))).astype(BF16)
    post_part = jnp.concatenate(
        [dims(grad_gate, g, 1, 1) + dims(grad_up, u, 1, 1) for g, u in zip(wg, wu)], axis=1
    ).astype(BF16)
    grad_post = lax.psum(post_part, "fsdp").astype(F32)
    mlp_part = jnp.concatenate(
        [dims(act[:, :cut], a, 1, 1) + dims(act[:, cut:], b, 1, 1) for a, b in zip(wd_a, wd_b)],
        axis=1,
    ).astype(BF16)
    mlp_part, grad_post = lax.optimization_barrier((mlp_part, grad_post))
    mlp = lax.psum(mlp_part, "fsdp").astype(F32)
    layer_out = in_blocks((hidden + mlp).astype(BF16))

    def weight_grad(left, right, order):
        away = dims(left[:, split:], right, 0, 0).astype(BF16)
        home = dims(left[:, :split], right, 0, 0).astype(BF16)
        return scatter_sum(home, exchange(away, 1), order)

    middle = units // 2
    down_a = weight_grad(cotangent, act[:, :middle], bits)
    down_b = weight_grad(cotangent, act[:, middle:], flipped)
    gate_sum = weight_grad(post_low, grad_gate, bits)
    up_sum = weight_grad(post_low, grad_up, flipped)
    down_sum = jnp.concatenate([down_a, down_b], axis=1).T

    grad_hidden = cotangent.astype(F32) + norm_back(hidden, scale_post, grad_post * gain_post)
    hidden_low = grad_hidden.astype(BF16)
    grad_context = (
        dims(hidden_low[:, :split], wo[0], 1, 0) + dims(hidden_low[:, split:], wo[1], 1, 0)
    ).astype(BF16)
    dq, dk_own, dk_other, dv_own, dv_other = attend_back(
        scalars, queries, grad_context, context, lse, all_keys, all_values, span
    )
    grad_k = scatter_sum(dk_own, exchange(dk_other, 1), bits).reshape(rows, kv_heads, HD)
    grad_v = scatter_sum(dv_own, exchange(dv_other, 1), flipped)

    rotated_q = rotate_back(dq.reshape(rows, heads, HD))
    q_gain_part = jnp.sum(rotated_q * q_proj * q_scale, axis=(0, 1))
    grad_q_low = norm_back(q_proj, q_scale, rotated_q * gain_query)
    grad_q_low = grad_q_low.astype(BF16).reshape(rows, q_cols)
    rotated_k = rotate_back(grad_k)
    k_gain_part = jnp.sum(rotated_k * k_proj * k_scale, axis=(0, 1))
    grad_k_low = norm_back(k_proj, k_scale, rotated_k * gain_key).astype(BF16)
    grad_kv_low = jnp.concatenate(
        [grad_k_low.reshape(rows, kv_cols), grad_v.astype(BF16)], axis=1
    )
    normed_part = jnp.concatenate(
        [dims(grad_q_low, q, 1, 1) + dims(grad_kv_low, kv, 1, 1) for q, kv in zip(wq, wkv)],
        axis=1,
    ).astype(BF16)
    grad_normed = lax.psum(normed_part, "fsdp").astype(F32)

    o_half = o_cols // 2
    qo = weight_grad_two(
        (normed_low, grad_q_low), (hidden_low, context[:, :o_half]), split, bits
    )
    kvo = weight_grad_two(
        (normed_low, grad_kv_low), (hidden_low, context[:, o_half:]), split, flipped
    )
    query_sum = qo[:, :q_cols]
    key_sum = kvo[:, :kv_cols]
    value_sum = kvo[:, kv_cols : 2 * kv_cols]
    out_sum = jnp.concatenate([qo[:, q_cols:], kvo[:, 2 * kv_cols :]], axis=1).T

    def along_rows(weight, grad):
        return jnp.sum(weight.astype(F32) * grad, axis=1)

    input_gain_part = (
        along_rows(query_weight, query_sum)
        + along_rows(key_weight, key_sum)
        + along_rows(value_weight, value_sum)
    ) / input_gain.astype(F32)
    post_gain_part = (
        along_rows(gate_weight, gate_sum) + along_rows(up_weight, up_sum)
    ) / post_gain.astype(F32)
    mine = (jnp.arange(n) == me)[:, None]
    widths = jnp.concatenate([input_gain_part, post_gain_part])[None, :]
    small = jnp.concatenate(
        [
            jnp.where(mine, widths, 0.0),
            jnp.concatenate([q_gain_part.reshape(n, -1), k_gain_part.reshape(n, -1)], axis=1),
        ],
        axis=1,
    )
    small = lax.dynamic_slice_in_dim(lax.psum(small, ("blk", "fsdp")), me, 1, 0)[0]
    head = HD // n

    tokens_grad = in_blocks(grad_hidden + norm_back(inputs, scale_in, grad_normed * gain_input))
    return (
        layer_out,
        tokens_grad,
        small[:block],
        query_sum,
        key_sum,
        value_sum,
        small[2 * block : 2 * block + head],
        small[2 * block + head :],
        out_sum,
        small[block : 2 * block],
        gate_sum,
        up_sum,
        down_sum,
    )


def weight_grad_two(first, second, split, order):
    def side(columns):
        return jnp.concatenate(
            [dims(left[:, columns], right, 0, 0) for left, right in (first, second)], axis=1
        ).astype(BF16)

    away = side(slice(split, None))
    home = side(slice(0, split))
    return scatter_sum(home, exchange(away, 1), order)


def solution(mesh):
    placed = (
        P("blk", None),
        P(),
        P("blk"),
        P("blk", "fsdp"),
        P("blk", "fsdp"),
        P("blk", "fsdp"),
        P("blk"),
        P("blk"),
        P("fsdp", "blk"),
        P("blk"),
        P("blk", "fsdp"),
        P("blk", "fsdp"),
        P("fsdp", "blk"),
        P("blk", None),
    )
    return jax.shard_map(
        shards,
        mesh=mesh,
        in_specs=placed,
        out_specs=(
            P("blk", None),
            P("blk", None),
            P("blk"),
            P("blk", "fsdp"),
            P("blk", "fsdp"),
            P("blk", "fsdp"),
            P("blk"),
            P("blk"),
            P("fsdp", "blk"),
            P("blk"),
            P("blk", "fsdp"),
            P("blk", "fsdp"),
            P("fsdp", "blk"),
        ),
        check_vma=False,
    )
```

time: 1420 us -> 774 us (0.55)
  waiting for transfers between devices: 756 us -> 310 us
  matrix products: 197 us -> 98.4 us
  loops' own time: 75.1 us -> 0 us
  local copies, waits for them, and re-layouts: 148 us -> 86.8 us
  Pallas kernels: 0 us -> 44.5 us
  blocking collectives: 58.9 us -> 41.9 us
    reduce_scatter x7 -> x0, waiting for transfers between devices: 240 us -> none  [the longest x1 62.9 us: shards(): lax.psum_scatter(down_grad.astype(jnp.bfloat16), 'blk', scatter_dimension...]
    psum x3, waiting for transfers between devices: 319 us -> 167 us  [the longest x1 64.2 us: shards(): attn = lax.psum(attn_part, 'fsdp').astype(F32)]
    all_gather x7 -> x0, waiting for transfers between devices: 151 us -> none  [the longest x1 41.5 us: shards(): lax.all_gather(gate_weight, 'blk', axis=0, tiled=True)]
    ppermute x44 -> x51, waiting for transfers between devices: 41.1 us -> 144 us  [exchange(): return lax.ppermute(block, 'blk', [(i, i ^ bit) for i in range(n)])]
    dot_general x138 -> x44, matrix products: 197 us -> 98.4 us  [dims(): lax.dot_general(lhs, rhs, (((left,), (right,)), ((), ())), preferred_elem...]
    another operation x62 -> x0, loops' own time: 75.1 us -> none  [the longest x1 36.9 us: shards(): lax.fori_loop(1, devices, forward_turn, (keys, values, states))]
    slice x107 -> x18, local copies, waits for them, and re-layouts: 72.1 us -> 10.3 us  [the longest x4 2.75 us: gather_rows(): held[m | bit] = got[i * rows:(i + 1) * rows]]
    while x30 -> x0, local copies, waits for them, and re-layouts: 48.7 us -> none
  transfers between devices with their start and end apart: 61 -> 54, of which waited for: 37 -> 20; matrix products, arithmetic and copies ran while one was open for 22% -> 34% of each run, Pallas kernels for 0% -> 6%
where the time goes in v1:
time: 774 us; the launch traced here: 765 us
  waiting for transfers between devices  310 us (40%)
  other arithmetic  124 us (16%)
  matrix products  98.4 us (13%)
  local copies, waits for them, and re-layouts  86.8 us (11%)
  Pallas kernels  44.5 us (6%)
  starting transfers between devices  42.9 us (6%)
  blocking collectives  41.9 us (5%)
  between operations  16.6 us (2%)
    ppermute x51, waiting for transfers between devices, exchange(): return lax.ppermute(block, 'blk', [(i, i ^ bit) for i in range(n)])  144 us
    dot_general x44, matrix products, dims(): lax.dot_general(lhs, rhs, (((left,), (right,)), ((), ())), preferred_elem...  98.4 us
    psum x1, waiting for transfers between devices, shards(): attn = lax.psum(attn_part, 'fsdp').astype(F32)  64.2 us
    unnamed x334, local copies, waits for them, and re-layouts  60.6 us
    psum x1, waiting for transfers between devices, shards(): grad_post = lax.psum(post_part, 'fsdp').astype(F32)  57.4 us
    psum x1, waiting for transfers between devices, shards(): mlp = lax.psum(mlp_part, 'fsdp').astype(F32)  45 us
    ppermute x51, starting transfers between devices, exchange(): return lax.ppermute(block, 'blk', [(i, i ^ bit) for i in range(n)])  42.4 us
    psum x1, blocking collectives, shards(): lax.psum(small, ('blk', 'fsdp'))  41.9 us
  transfers between devices with their start and end apart: 54, of which 20 were waited for; matrix products, arithmetic and copies ran while one was open for 34% of the time, Pallas kernels for 6%

profile of v1, /device:TPU:0, one launch (start us, length us, event | category | flops | bytes accessed | tf_op | source)
XLA Modules:
  0.0 765.4 jit_solution(1706959898084735444)
XLA Ops:
  9.1 3.0 collective-permute-start.6
  20.5 2.1 constant_dynamic-update-slice_fusion.10
  59.5 2.6 fusion.2
  67.3 10.3 %collective-permute-done.7 = bf16[512,512]{1,0:T(8,128)(2,1)S(1)} collective-permute-done((bf16[512,512]{1,0:T(8,128)(2,1)S(1)}, bf16[512,512]{1,0:T(8,128)(2,1)S(1)}, u32[]{:S(2)}, u32[]{:S(2)}) %collective-permute-start.7) | collective-permute-done | bytes 524320 | tf_op jit(solution)/shard_map/ppermute | solution.py:36
  77.7 2.2 pad_maximum_fusion.13
  84.1 2.4 pad_maximum_fusion.8
  86.8 2.5 pad_maximum_fusion.7
  111.0 3.4 collective-permute-done.12
  116.0 19.3 %collective-permute-done.15 = bf16[256,1024]{0,1:T(8,128)(2,1)} collective-permute-done((bf16[256,1024]{0,1:T(8,128)(2,1)}, bf16[256,1024]{0,1:T(8,128)(2,1)}, u32[]{:S(2)}, u32[]{:S(2)}) %collective-permute-start.15) | collective-permute-done | bytes 524320 | tf_op jit(solution)/shard_map/ppermute | solution.py:36
  138.2 2.8 collective-permute-done.9
  146.6 5.5 collective-permute-done.13
  153.3 17.9 %collective-permute-done.10 = bf16[1024,256]{1,0:T(8,128)(2,1)S(1)} collective-permute-done((bf16[1024,256]{1,0:T(8,128)(2,1)S(1)}, bf16[1024,256]{1,0:T(8,128)(2,1)S(1)}, u32[]{:S(2)}, u32[]{:S(2)}) %collective-permute-start.10) | collective-permute-done | bytes 524320 | tf_op jit(solution)/shard_map/ppermute | solution.py:36
  176.6 2.6 fusion.83
  179.3 3.2 pad_maximum_fusion.3
  182.6 16.1 %attend.1 = (bf16[512,512]{1,0:T(8,128)(2,1)S(1)}, f32[2,2,512]{2,1,0:T(2,128)S(1)}) custom-call(s32[18]{0:T(128)S(1)} %pad_add_fusion.sc, bf16[512,512]{1,0:T(8,128)(2,1)S(1)} %fusion.15.q_ref, bf16[2048,256]{1,0:T(8,128)(2,1)S(1)} %pad_maximum_fusion.14.k0, bf16[2048,256]{1,0:T(8,128)(2,1)S(1)} %collective-permute-done.11.k1, ...), custom_call_target="tpu_custom_call" | custom-call | flops 8589934592 | bytes 4194304 | tf_op jit(solution)/shard_map/attend/pallas_call | solution.py:197
  203.1 3.0 pad_maximum_fusion
  206.7 2.1 constant_dynamic-update-slice_fusion.9
  208.8 3.0 collective-permute-done.19
  211.8 2.7 constant_dynamic-update-slice_fusion.8
  214.5 3.1 fusion.81
  221.2 3.8 convolution_add_fusion.2
  225.0 64.2 %all-reduce.5.cloned.1.call-done = bf16[512,2048]{1,0:T(8,128)(2,1)} async-done(((bf16[512,2048]{1,0:T(8,128)(2,1)}), bf16[512,2048]{1,0:T(8,128)(2,1)}) %all-reduce.5.cloned.1.call-update) | async-done | bytes 2097168 | tf_op jit(solution)/shard_map/psum | solution.py:377
  289.2 3.1 multiply_reduce_fusion.1
  293.8 4.4 fusion.43
  298.2 3.7 convolution_add_fusion
  301.9 3.8 fusion.45
  305.8 5.5 multiply_convert_fusion.2
  311.4 2.7 convolution_convert_fusion.6
  314.1 2.2 convolution_convert_fusion.4
  316.3 3.7 fusion.94
  320.0 3.5 convolution_convert_fusion
  324.0 3.5 convolution_convert_fusion.2
  327.5 3.7 add_convert_fusion.4
  331.2 3.7 fusion.95
  335.0 3.7 add_convert_fusion.3
  340.7 2.9 fusion.22
  345.0 3.1 fusion.20
  353.8 3.5 convolution_convert_fusion.1
  357.3 3.5 convolution_convert_fusion.3
  368.4 57.4 %all-reduce.7.cloned.1.call-done = bf16[512,2048]{1,0:T(8,128)(2,1)} async-done(((bf16[512,2048]{1,0:T(8,128)(2,1)}), bf16[512,2048]{1,0:T(8,128)(2,1)}) %all-reduce.7.cloned.1.call-update) | async-done | bytes 2097168 | tf_op jit(solution)/shard_map/psum | solution.py:392
  425.8 2.3 convert_element_type.620
  431.8 2.5 fusion.82
  440.7 28.3 %attend_back.1 = (f32[512,512]{1,0:T(8,128)S(1)}, bf16[2048,256]{1,0:T(8,128)(2,1)S(1)}, bf16[2048,256]{1,0:T(8,128)(2,1)}, bf16[2048,256]{1,0:T(8,128)(2,1)S(1)}, bf16[2048,256]{1,0:T(8,128)(2,1)S(1)}) custom-call(s32[18]{0:T(128)S(1)} %pad_add_fusion.sc, bf16[512,512]{1,0:T(8,128)(2,1)S(1)} %copy-done.5, bf16[512,512]{1,0:T(8,128)(2,1)S(1)} %fusion.10.do_ref, ...), custom_call_target="tpu_custom_call" | custom-call | flops 21474836480 | bytes 8388608 | tf_op jit(solution)/shard_map/attend_back/pallas_call | solution.py:235
  489.7 2.4 pad_maximum_fusion.9
  492.1 4.7 collective-permute-done.47
  502.3 3.1 copy.84
  518.4 3.0 collective-permute-done.28
  525.0 2.2 collective-permute-start.34
  529.1 33.7 %collective-permute-done.29 = bf16[512,256]{1,0:T(8,128)(2,1)S(1)} collective-permute-done((bf16[512,256]{1,0:T(8,128)(2,1)S(1)}, bf16[512,256]{1,0:T(8,128)(2,1)S(1)}, u32[]{:S(2)}, u32[]{:S(2)}) %collective-permute-start.29) | collective-permute-done | bytes 262176 | tf_op jit(solution)/shard_map/ppermute | solution.py:36
  564.7 2.2 reshape.243
  571.7 5.6 collective-permute-done.32
  581.0 3.1 fusion.80
  584.9 2.9 add_convert_fusion.2
  596.2 2.8 add_convert_fusion.7
  600.5 2.8 add_convert_fusion.13
  612.1 6.8 collective-permute-done.44
  618.9 3.5 multiply_reduce_fusion.2
  622.4 18.8 %collective-permute-done.37 = bf16[512,768]{0,1:T(8,128)(2,1)} collective-permute-done((bf16[512,768]{0,1:T(8,128)(2,1)}, bf16[512,768]{0,1:T(8,128)(2,1)}, u32[]{:S(2)}, u32[]{:S(2)}) %collective-permute-start.37) | collective-permute-done | bytes 786464 | tf_op jit(solution)/shard_map/ppermute | solution.py:36
  644.0 3.5 multiply_reduce_fusion.3
  647.6 5.6 collective-permute-done.38
  656.6 41.9 %psum.39 = f32[8,544]{1,0:T(8,128)S(1)} all-reduce(f32[8,544]{1,0:T(8,128)S(1)} %pad_maximum_fusion.38), channel_id=1, replica_groups=mesh['blk'=8,'fsdp'=4] {'blk','fsdp'}, use_global_device_ids=true, to_apply=%region_24.25 | all-reduce | flops 4352 | bytes 34816 | tf_op jit(solution)/shard_map/psum | solution.py:472
  700.5 45.0 %all-reduce.9.cloned.1.call-done = (bf16[512,2048]{1,0:T(8,128)(2,1)}, bf16[512,2048]{1,0:T(8,128)(2,1)}) async-done(((bf16[512,2048]{1,0:T(8,128)(2,1)}, bf16[512,2048]{1,0:T(8,128)(2,1)}), (bf16[512,2048]{1,0:T(8,128)(2,1)}, bf16[512,2048]{1,0:T(8,128)(2,1)})) %all-reduce.9.cloned.1.call-update) | async-done | bytes 4194320 | tf_op jit(solution)/shard_map/psum | solution.py:398
  745.6 2.5 fusion.8
  748.4 6.4 fusion.6
  (589 shorter events, 217.8 us)
Async XLA Ops:
  7.2 282.1 %all-reduce.5.cloned.1.call-start = ((), (), s32[]{:S(2)}) async-start(), calls=%async_computation | async-start | bytes 4194304 | tf_op jit(solution)/shard_map/psum | solution.py:377
  9.1 53.1 %copy-start.69 = (bf16[256,512]{1,0:T(8,128)(2,1)}, bf16[256,512]{1,0:T(8,128)(2,1)S(1)}, u32[]{:S(2)}) copy-start(bf16[256,512]{1,0:T(8,128)(2,1)S(1)} %constant_dynamic-update-slice_fusion.3) | copy-start | bytes 786436
  9.1 53.1 %collective-permute-start.6 = (bf16[256,512]{1,0:T(8,128)(2,1)S(1)}, bf16[256,512]{1,0:T(8,128)(2,1)}, u32[]{:S(2)}, u32[]{:S(2)}) collective-permute-start(bf16[256,512]{1,0:T(8,128)(2,1)S(1)} %constant_dynamic-update-slice_fusion.3), channel_id=1, source_target_pairs={{0,16},{4,20},{8,24},{12,28},{16,0},{20,4},{24,8},{28,12},{1,17},{... | collective-permute-start | bytes 786440 | tf_op jit(solution)/shard_map/ppermute | solution.py:36
  12.9 37.4 %collective-permute-start = (bf16[1,544]{1,0:T(2,128)(2,1)S(1)}, bf16[1,544]{1,0:T(2,128)(2,1)S(1)}, u32[]{:S(2)}, u32[]{:S(2)}) collective-permute-start(bf16[1,544]{1,0:T(2,128)(2,1)S(1)} %reshape.239), channel_id=1, source_target_pairs={{0,8},{4,12},{8,0},{12,4},{16,24},{20,28},{24,16},{28,20},{1,9},{5... | collective-permute-start | bytes 3272 | tf_op jit(solution)/shard_map/ppermute | solution.py:36
  14.4 49.1 %collective-permute-start.3 = (bf16[256,512]{1,0:T(8,128)(2,1)}, bf16[256,512]{1,0:T(8,128)(2,1)}, u32[]{:S(2)}, u32[]{:S(2)}) collective-permute-start(bf16[256,512]{1,0:T(8,128)(2,1)} %param.19), channel_id=1, source_target_pairs={{0,8},{4,12},{8,0},{12,4},{16,24},{20,28},{24,16},{28,20},{1,9},{5... | collective-permute-start | bytes 786440 | tf_op jit(solution)/shard_map/ppermute | solution.py:36
  15.0 71.9 %collective-permute-start.18 = (bf16[256,1536]{1,0:T(8,128)(2,1)}, bf16[256,1536]{1,0:T(8,128)(2,1)}, u32[]{:S(2)}, u32[]{:S(2)}) collective-permute-start(bf16[256,1536]{1,0:T(8,128)(2,1)} %param.26), channel_id=1, source_target_pairs={{0,8},{4,12},{8,0},{12,4},{16,24},{20,28},{24,16},{28,20},{1,9},{5... | collective-permute-start | bytes 2359304 | tf_op jit(solution)/shard_map/ppermute | solution.py:36
  16.4 67.7 %collective-permute-start.21 = (bf16[256,1536]{1,0:T(8,128)(2,1)}, bf16[256,1536]{1,0:T(8,128)(2,1)}, u32[]{:S(2)}, u32[]{:S(2)}) collective-permute-start(bf16[256,1536]{1,0:T(8,128)(2,1)} %param.27), channel_id=1, source_target_pairs={{0,16},{4,20},{8,24},{12,28},{16,0},{20,4},{24,8},{28,12},{1,17},{... | collective-permute-start | bytes 2359304 | tf_op jit(solution)/shard_map/ppermute | solution.py:36
  50.2 59.1 %copy-start.39 = (f32[512,128]{1,0:T(8,128)}, f32[512,128]{1,0:T(8,128)S(1)}, u32[]{:S(2)}) copy-start(f32[512,128]{1,0:T(8,128)S(1)} %get-tuple-element.171) | copy-start | bytes 786436
  50.4 3.7 collective-permute-start.1
  54.0 5.3 collective-permute-start.2
  63.2 14.4 %collective-permute-start.7 = (bf16[512,512]{1,0:T(8,128)(2,1)S(1)}, bf16[512,512]{1,0:T(8,128)(2,1)S(1)}, u32[]{:S(2)}, u32[]{:S(2)}) collective-permute-start(bf16[512,512]{1,0:T(8,128)(2,1)S(1)} %pad_maximum_fusion.26), channel_id=1, source_target_pairs={{0,8},{4,12},{8,0},{12,4},{16,24},{20,28},{24,16},{28,20},{1,9},{5... | collective-permute-start | bytes 1572872 | tf_op jit(solution)/shard_map/ppermute | solution.py:36
  63.5 34.7 %copy-start.127 = (f32[128]{0:T(128)}, f32[128]{0:T(128)S(1)}, u32[]{:S(2)}) copy-start(f32[128]{0:T(128)S(1)} %mul.567) | copy-start | bytes 1540
  63.5 38.1 %copy-start.129 = (f32[256]{0:T(256)}, f32[256]{0:T(256)S(1)}, u32[]{:S(2)}) copy-start(f32[256]{0:T(256)S(1)} %broadcast_bitcast_fusion.1) | copy-start | bytes 3076
  65.3 16.3 %collective-permute-start.4 = (bf16[512,512]{1,0:T(8,128)(2,1)}, bf16[512,512]{1,0:T(8,128)(2,1)}, u32[]{:S(2)}, u32[]{:S(2)}) collective-permute-start(bf16[512,512]{1,0:T(8,128)(2,1)} %pad_maximum_fusion.25), channel_id=1, source_target_pairs={{0,16},{4,20},{8,24},{12,28},{16,0},{20,4},{24,8},{28,12},{1,17},{... | collective-permute-start | bytes 1572872 | tf_op jit(solution)/shard_map/ppermute | solution.py:36
  79.9 9.5 %collective-permute-start.8 = (bf16[1024,512]{1,0:T(8,128)(2,1)}, bf16[1024,512]{1,0:T(8,128)(2,1)S(1)}, u32[]{:S(2)}, u32[]{:S(2)}) collective-permute-start(bf16[1024,512]{1,0:T(8,128)(2,1)} %pad_maximum_fusion.13), channel_id=1, source_target_pairs={{0,4},{4,0},{8,12},{12,8},{16,20},{20,16},{24,28},{28,24},{1,5},{5... | collective-permute-start | bytes 3145736 | tf_op jit(solution)/shard_map/ppermute | solution.py:36
  83.6 18.9 %collective-permute-start.5 = (bf16[1024,512]{1,0:T(8,128)(2,1)}, bf16[1024,512]{1,0:T(8,128)(2,1)}, u32[]{:S(2)}, u32[]{:S(2)}) collective-permute-start(bf16[1024,512]{1,0:T(8,128)(2,1)} %constant_dynamic-update-slice_fusion), channel_id=1, source_target_pairs={{0,4},{4,0},{8,12},{12,8},{16,20},{20,16},{24,28},{28,24},{1,5},{5... | collective-permute-start | bytes 3145736 | tf_op jit(solution)/shard_map/ppermute | solution.py:36
  86.5 88.5 %collective-permute-start.22 = (bf16[512,1536]{1,0:T(8,128)(2,1)}, bf16[512,1536]{1,0:T(8,128)(2,1)}, u32[]{:S(2)}, u32[]{:S(2)}) collective-permute-start(bf16[512,1536]{1,0:T(8,128)(2,1)} %pad_maximum_fusion.8), channel_id=1, source_target_pairs={{0,8},{4,12},{8,0},{12,4},{16,24},{20,28},{24,16},{28,20},{1,9},{5... | collective-permute-start | bytes 4718600 | tf_op jit(solution)/shard_map/ppermute | solution.py:36
  93.6 41.7 %collective-permute-start.15 = (bf16[256,1024]{0,1:T(8,128)(2,1)}, bf16[256,1024]{0,1:T(8,128)(2,1)}, u32[]{:S(2)}, u32[]{:S(2)}) collective-permute-start(bf16[256,1024]{0,1:T(8,128)(2,1)} %pad_maximum_fusion.29), channel_id=1, source_target_pairs={{0,8},{4,12},{8,0},{12,4},{16,24},{20,28},{24,16},{28,20},{1,9},{5... | collective-permute-start | bytes 1572872 | tf_op jit(solution)/shard_map/ppermute | solution.py:36
  95.3 48.4 %collective-permute-start.24 = (bf16[256,1024]{0,1:T(8,128)(2,1)}, bf16[256,1024]{0,1:T(8,128)(2,1)}, u32[]{:S(2)}, u32[]{:S(2)}) collective-permute-start(bf16[256,1024]{0,1:T(8,128)(2,1)} %slice.604), channel_id=1, source_target_pairs={{0,16},{4,20},{8,24},{12,28},{16,0},{20,4},{24,8},{28,12},{1,17},{... | collective-permute-start | bytes 1572872 | tf_op jit(solution)/shard_map/ppermute | solution.py:36
  96.8 17.7 %collective-permute-start.12 = (bf16[512,256]{1,0:T(8,128)(2,1)}, bf16[512,256]{1,0:T(8,128)(2,1)}, u32[]{:S(2)}, u32[]{:S(2)}) collective-permute-start(bf16[512,256]{1,0:T(8,128)(2,1)} %slice.919), channel_id=1, source_target_pairs={{0,16},{4,20},{8,24},{12,28},{16,0},{20,4},{24,8},{28,12},{1,17},{... | collective-permute-start | bytes 786440 | tf_op jit(solution)/shard_map/ppermute | solution.py:36
  102.5 38.4 %collective-permute-start.9 = (bf16[512,256]{1,0:T(8,128)(2,1)}, bf16[512,256]{1,0:T(8,128)(2,1)}, u32[]{:S(2)}, u32[]{:S(2)}) collective-permute-start(bf16[512,256]{1,0:T(8,128)(2,1)} %fusion.64), channel_id=1, source_target_pairs={{0,8},{4,12},{8,0},{12,4},{16,24},{20,28},{24,16},{28,20},{1,9},{5... | collective-permute-start | bytes 786440 | tf_op jit(solution)/shard_map/ppermute | solution.py:36
  106.9 67.1 %copy-start.25 = (f32[512,512]{1,0:T(8,128)}, f32[512,512]{1,0:T(8,128)S(1)}, u32[]{:S(2)}) copy-start(f32[512,512]{1,0:T(8,128)S(1)} %convolution_add_fusion.6) | copy-start | bytes 3145732
  115.5 36.5 %collective-permute-start.13 = (bf16[1024,256]{1,0:T(8,128)(2,1)S(1)}, bf16[1024,256]{1,0:T(8,128)(2,1)S(1)}, u32[]{:S(2)}, u32[]{:S(2)}) collective-permute-start(bf16[1024,256]{1,0:T(8,128)(2,1)S(1)} %pad_maximum_fusion.28), channel_id=1, source_target_pairs={{0,8},{4,12},{8,0},{12,4},{16,24},{20,28},{24,16},{28,20},{1,9},{5... | collective-permute-start | bytes 1572872 | tf_op jit(solution)/shard_map/ppermute | solution.py:36
  136.6 35.8 %collective-permute-start.16 = (bf16[512,1024]{0,1:T(8,128)(2,1)S(1)}, bf16[512,1024]{0,1:T(8,128)(2,1)S(1)}, u32[]{:S(2)}, u32[]{:S(2)}) collective-permute-start(bf16[512,1024]{0,1:T(8,128)(2,1)S(1)} %pad_maximum_fusion.16), channel_id=1, source_target_pairs={{0,16},{4,20},{8,24},{12,28},{16,0},{20,4},{24,8},{28,12},{1,17},{... | collective-permute-start | bytes 3145736 | tf_op jit(solution)/shard_map/ppermute | solution.py:36
  142.0 29.2 %collective-permute-start.10 = (bf16[1024,256]{1,0:T(8,128)(2,1)S(1)}, bf16[1024,256]{1,0:T(8,128)(2,1)S(1)}, u32[]{:S(2)}, u32[]{:S(2)}) collective-permute-start(bf16[1024,256]{1,0:T(8,128)(2,1)S(1)} %pad_maximum_fusion.27), channel_id=1, source_target_pairs={{0,16},{4,20},{8,24},{12,28},{16,0},{20,4},{24,8},{28,12},{1,17},{... | collective-permute-start | bytes 1572872 | tf_op jit(solution)/shard_map/ppermute | solution.py:36
  144.9 34.3 %collective-permute-start.25 = (bf16[512,1024]{0,1:T(8,128)(2,1)S(1)}, bf16[512,1024]{0,1:T(8,128)(2,1)S(1)}, u32[]{:S(2)}, u32[]{:S(2)}) collective-permute-start(bf16[512,1024]{0,1:T(8,128)(2,1)S(1)} %pad_maximum_fusion.17), channel_id=1, source_target_pairs={{0,8},{4,12},{8,0},{12,4},{16,24},{20,28},{24,16},{28,20},{1,9},{5... | collective-permute-start | bytes 3145736 | tf_op jit(solution)/shard_map/ppermute | solution.py:36
  153.2 29.3 %collective-permute-start.14 = (bf16[2048,256]{1,0:T(8,128)(2,1)S(1)}, bf16[2048,256]{1,0:T(8,128)(2,1)S(1)}, u32[]{:S(2)}, u32[]{:S(2)}) collective-permute-start(bf16[2048,256]{1,0:T(8,128)(2,1)S(1)} %pad_maximum_fusion.15.v0), channel_id=1, source_target_pairs={{0,4},{4,0},{8,12},{12,8},{16,20},{20,16},{24,28},{28,24},{1,5},{5... | collective-permute-start | bytes 3145736 | tf_op jit(solution)/shard_map/ppermute | solution.py:36
  172.3 10.2 %collective-permute-start.11 = (bf16[2048,256]{1,0:T(8,128)(2,1)S(1)}, bf16[2048,256]{1,0:T(8,128)(2,1)S(1)}, u32[]{:S(2)}, u32[]{:S(2)}) collective-permute-start(bf16[2048,256]{1,0:T(8,128)(2,1)S(1)} %pad_maximum_fusion.14.k0), channel_id=1, source_target_pairs={{0,4},{4,0},{8,12},{12,8},{16,20},{20,16},{24,28},{28,24},{1,5},{5... | collective-permute-start | bytes 3145736 | tf_op jit(solution)/shard_map/ppermute | solution.py:36
  172.6 26.9 %collective-permute-start.17 = (bf16[1024,1024]{0,1:T(8,128)(2,1)S(1)}, bf16[1024,1024]{0,1:T(8,128)(2,1)S(1)}, u32[]{:S(2)}, u32[]{:S(2)}) collective-permute-start(bf16[1024,1024]{0,1:T(8,128)(2,1)S(1)} %constant_dynamic-update-slice_fusion.5), channel_id=1, source_target_pairs={{0,4},{4,0},{8,12},{12,8},{16,20},{20,16},{24,28},{28,24},{1,5},{5... | collective-permute-start | bytes 6291464 | tf_op jit(solution)/shard_map/ppermute | solution.py:36
  175.0 36.7 %collective-permute-start.19 = (bf16[512,1536]{1,0:T(8,128)(2,1)}, bf16[512,1536]{1,0:T(8,128)(2,1)}, u32[]{:S(2)}, u32[]{:S(2)}) collective-permute-start(bf16[512,1536]{1,0:T(8,128)(2,1)} %pad_maximum_fusion.7), channel_id=1, source_target_pairs={{0,16},{4,20},{8,24},{12,28},{16,0},{20,4},{24,8},{28,12},{1,17},{... | collective-permute-start | bytes 4718600 | tf_op jit(solution)/shard_map/ppermute | solution.py:36
  182.5 32.0 %collective-permute-start.26 = (bf16[1024,1024]{0,1:T(8,128)(2,1)}, bf16[1024,1024]{0,1:T(8,128)(2,1)}, u32[]{:S(2)}, u32[]{:S(2)}) collective-permute-start(bf16[1024,1024]{0,1:T(8,128)(2,1)} %pad_maximum_fusion.3), channel_id=1, source_target_pairs={{0,4},{4,0},{8,12},{12,8},{16,20},{20,16},{24,28},{28,24},{1,5},{5... | collective-permute-start | bytes 6291464 | tf_op jit(solution)/shard_map/ppermute | solution.py:36
  198.7 236.9 %copy-start.12 = (bf16[512,512]{1,0:T(8,128)(2,1)}, bf16[512,512]{1,0:T(8,128)(2,1)S(1)}, u32[]{:S(2)}) copy-start(bf16[512,512]{1,0:T(8,128)(2,1)S(1)} %get-tuple-element.24.ctx_ref) | copy-start | bytes 1572868
  203.1 222.8 %all-reduce.7.cloned.1.call-start = ((), (), s32[]{:S(2)}) async-start(), calls=%async_computation.1 | async-start | bytes 4194304 | tf_op jit(solution)/shard_map/psum | solution.py:392
  206.2 87.6 %collective-permute-start.23 = (bf16[1024,1536]{1,0:T(8,128)(2,1)}, bf16[1024,1536]{1,0:T(8,128)(2,1)}, u32[]{:S(2)}, u32[]{:S(2)}) collective-permute-start(bf16[1024,1536]{1,0:T(8,128)(2,1)} %pad_maximum_fusion), channel_id=1, source_target_pairs={{0,4},{4,0},{8,12},{12,8},{16,20},{20,16},{24,28},{28,24},{1,5},{5... | collective-permute-start | bytes 9437192 | tf_op jit(solution)/shard_map/ppermute | solution.py:36
  214.5 87.5 %collective-permute-start.20 = (bf16[1024,1536]{1,0:T(8,128)(2,1)}, bf16[1024,1536]{1,0:T(8,128)(2,1)}, u32[]{:S(2)}, u32[]{:S(2)}) collective-permute-start(bf16[1024,1536]{1,0:T(8,128)(2,1)} %constant_dynamic-update-slice_fusion.8), channel_id=1, source_target_pairs={{0,4},{4,0},{8,12},{12,8},{16,20},{20,16},{24,28},{28,24},{1,5},{5... | collective-permute-start | bytes 9437192 | tf_op jit(solution)/shard_map/ppermute | solution.py:36
  323.5 37.3 %collective-permute-start.45 = (bf16[1024,768]{1,0:T(8,128)(2,1)}, bf16[1024,768]{1,0:T(8,128)(2,1)}, u32[]{:S(2)}, u32[]{:S(2)}) collective-permute-start(bf16[1024,768]{1,0:T(8,128)(2,1)} %convolution_convert_fusion.6), channel_id=1, source_target_pairs={{0,4},{4,0},{8,12},{12,8},{16,20},{20,16},{24,28},{28,24},{1,5},{5... | collective-permute-start | bytes 4718600 | tf_op jit(solution)/shard_map/ppermute | solution.py:36
  323.5 41.2 %collective-permute-start.48 = (bf16[1024,768]{1,0:T(8,128)(2,1)}, bf16[1024,768]{1,0:T(8,128)(2,1)}, u32[]{:S(2)}, u32[]{:S(2)}) collective-permute-start(bf16[1024,768]{1,0:T(8,128)(2,1)} %convolution_convert_fusion.4), channel_id=1, source_target_pairs={{0,4},{4,0},{8,12},{12,8},{16,20},{20,16},{24,28},{28,24},{1,5},{5... | collective-permute-start | bytes 4718600 | tf_op jit(solution)/shard_map/ppermute | solution.py:36
  340.2 405.3 %all-reduce.9.cloned.1.call-start = ((), (), s32[]{:S(2)}) async-start(), calls=%async_computation.2 | async-start | bytes 8388608 | tf_op jit(solution)/shard_map/psum | solution.py:398
  344.4 165.9 %collective-permute-start.42 = (bf16[1024,1536]{1,0:T(8,128)(2,1)}, bf16[1024,1536]{1,0:T(8,128)(2,1)}, u32[]{:S(2)}, u32[]{:S(2)}) collective-permute-start(bf16[1024,1536]{1,0:T(8,128)(2,1)} %convolution_convert_fusion), channel_id=1, source_target_pairs={{0,4},{4,0},{8,12},{12,8},{16,20},{20,16},{24,28},{28,24},{1,5},{5... | collective-permute-start | bytes 9437192 | tf_op jit(solution)/shard_map/ppermute | solution.py:36
  344.5 170.0 %collective-permute-start.39 = (bf16[1024,1536]{1,0:T(8,128)(2,1)}, bf16[1024,1536]{1,0:T(8,128)(2,1)}, u32[]{:S(2)}, u32[]{:S(2)}) collective-permute-start(bf16[1024,1536]{1,0:T(8,128)(2,1)} %convolution_convert_fusion.2), channel_id=1, source_target_pairs={{0,4},{4,0},{8,12},{12,8},{16,20},{20,16},{24,28},{28,24},{1,5},{5... | collective-permute-start | bytes 9437192 | tf_op jit(solution)/shard_map/ppermute | solution.py:36
  363.1 120.8 %collective-permute-start.46 = (bf16[512,768]{1,0:T(8,128)(2,1)}, bf16[512,768]{1,0:T(8,128)(2,1)}, u32[]{:S(2)}, u32[]{:S(2)}) collective-permute-start(bf16[512,768]{1,0:T(8,128)(2,1)} %pad_maximum_fusion.23), channel_id=1, source_target_pairs={{0,8},{4,12},{8,0},{12,4},{16,24},{20,28},{24,16},{28,20},{1,9},{5... | collective-permute-start | bytes 2359304 | tf_op jit(solution)/shard_map/ppermute | solution.py:36
  367.0 119.9 %collective-permute-start.49 = (bf16[512,768]{1,0:T(8,128)(2,1)}, bf16[512,768]{1,0:T(8,128)(2,1)}, u32[]{:S(2)}, u32[]{:S(2)}) collective-permute-start(bf16[512,768]{1,0:T(8,128)(2,1)} %pad_maximum_fusion.24), channel_id=1, source_target_pairs={{0,16},{4,20},{8,24},{12,28},{16,0},{20,4},{24,8},{28,12},{1,17},{... | collective-permute-start | bytes 2359304 | tf_op jit(solution)/shard_map/ppermute | solution.py:36
  482.0 23.4 %collective-permute-start.27 = (bf16[2048,256]{1,0:T(8,128)(2,1)}, bf16[2048,256]{1,0:T(8,128)(2,1)}, u32[]{:S(2)}, u32[]{:S(2)}) collective-permute-start(bf16[2048,256]{1,0:T(8,128)(2,1)} %get-tuple-element.32), channel_id=1, source_target_pairs={{0,4},{4,0},{8,12},{12,8},{16,20},{20,16},{24,28},{28,24},{1,5},{5... | collective-permute-start | bytes 3145736 | tf_op jit(solution)/shard_map/ppermute | solution.py:36
  485.3 11.6 %collective-permute-start.47 = (bf16[256,768]{1,0:T(8,128)(2,1)S(1)}, bf16[256,768]{1,0:T(8,128)(2,1)S(1)}, u32[]{:S(2)}, u32[]{:S(2)}) collective-permute-start(bf16[256,768]{1,0:T(8,128)(2,1)S(1)} %add_convert_fusion.25), channel_id=1, source_target_pairs={{0,16},{4,20},{8,24},{12,28},{16,0},{20,4},{24,8},{28,12},{1,17},{... | collective-permute-start | bytes 1179656 | tf_op jit(solution)/shard_map/ppermute | solution.py:36
  488.2 11.3 %collective-permute-start.50 = (bf16[256,768]{1,0:T(8,128)(2,1)S(1)}, bf16[256,768]{1,0:T(8,128)(2,1)S(1)}, u32[]{:S(2)}, u32[]{:S(2)}) collective-permute-start(bf16[256,768]{1,0:T(8,128)(2,1)S(1)} %add_convert_fusion.19), channel_id=1, source_target_pairs={{0,8},{4,12},{8,0},{12,4},{16,24},{20,28},{24,16},{28,20},{1,9},{5... | collective-permute-start | bytes 1179656 | tf_op jit(solution)/shard_map/ppermute | solution.py:36
  496.9 11.3 %collective-permute-start.30 = (bf16[2048,256]{1,0:T(8,128)(2,1)S(1)}, bf16[2048,256]{1,0:T(8,128)(2,1)}, u32[]{:S(2)}, u32[]{:S(2)}) collective-permute-start(bf16[2048,256]{1,0:T(8,128)(2,1)S(1)} %copy-done.11), channel_id=1, source_target_pairs={{0,4},{4,0},{8,12},{12,8},{16,20},{20,16},{24,28},{28,24},{1,5},{5... | collective-permute-start | bytes 3145736 | tf_op jit(solution)/shard_map/ppermute | solution.py:36
  499.5 23.2 %collective-permute-start.33 = (bf16[1024,768]{0,1:T(8,128)(2,1)}, bf16[1024,768]{0,1:T(8,128)(2,1)}, u32[]{:S(2)}, u32[]{:S(2)}) collective-permute-start(bf16[1024,768]{0,1:T(8,128)(2,1)} %pad_maximum_fusion.9), channel_id=1, source_target_pairs={{0,4},{4,0},{8,12},{12,8},{16,20},{20,16},{24,28},{28,24},{1,5},{5... | collective-permute-start | bytes 4718600 | tf_op jit(solution)/shard_map/ppermute | solution.py:36
  506.6 14.8 %collective-permute-start.28 = (bf16[1024,256]{1,0:T(8,128)(2,1)S(1)}, bf16[1024,256]{1,0:T(8,128)(2,1)S(1)}, u32[]{:S(2)}, u32[]{:S(2)}) collective-permute-start(bf16[1024,256]{1,0:T(8,128)(2,1)S(1)} %pad_maximum_fusion.30), channel_id=1, source_target_pairs={{0,8},{4,12},{8,0},{12,4},{16,24},{20,28},{24,16},{28,20},{1,9},{5... | collective-permute-start | bytes 1572872 | tf_op jit(solution)/shard_map/ppermute | solution.py:36
  509.4 17.8 %collective-permute-start.31 = (bf16[1024,256]{1,0:T(8,128)(2,1)S(1)}, bf16[1024,256]{1,0:T(8,128)(2,1)S(1)}, u32[]{:S(2)}, u32[]{:S(2)}) collective-permute-start(bf16[1024,256]{1,0:T(8,128)(2,1)S(1)} %pad_maximum_fusion.32), channel_id=1, source_target_pairs={{0,16},{4,20},{8,24},{12,28},{16,0},{20,4},{24,8},{28,12},{1,17},{... | collective-permute-start | bytes 1572872 | tf_op jit(solution)/shard_map/ppermute | solution.py:36
  513.3 82.9 %collective-permute-start.43 = (bf16[512,1536]{1,0:T(8,128)(2,1)}, bf16[512,1536]{1,0:T(8,128)(2,1)}, u32[]{:S(2)}, u32[]{:S(2)}) collective-permute-start(bf16[512,1536]{1,0:T(8,128)(2,1)} %pad_maximum_fusion.12), channel_id=1, source_target_pairs={{0,16},{4,20},{8,24},{12,28},{16,0},{20,4},{24,8},{28,12},{1,17},{... | collective-permute-start | bytes 4718600 | tf_op jit(solution)/shard_map/ppermute | solution.py:36
  517.6 82.9 %collective-permute-start.40 = (bf16[512,1536]{1,0:T(8,128)(2,1)}, bf16[512,1536]{1,0:T(8,128)(2,1)}, u32[]{:S(2)}, u32[]{:S(2)}) collective-permute-start(bf16[512,1536]{1,0:T(8,128)(2,1)} %pad_maximum_fusion.11), channel_id=1, source_target_pairs={{0,8},{4,12},{8,0},{12,4},{16,24},{20,28},{24,16},{28,20},{1,9},{5... | collective-permute-start | bytes 4718600 | tf_op jit(solution)/shard_map/ppermute | solution.py:36
  522.5 40.4 %collective-permute-start.29 = (bf16[512,256]{1,0:T(8,128)(2,1)S(1)}, bf16[512,256]{1,0:T(8,128)(2,1)S(1)}, u32[]{:S(2)}, u32[]{:S(2)}) collective-permute-start(bf16[512,256]{1,0:T(8,128)(2,1)S(1)} %add_convert_fusion.50), channel_id=1, source_target_pairs={{0,16},{4,20},{8,24},{12,28},{16,0},{20,4},{24,8},{28,12},{1,17},{... | collective-permute-start | bytes 786440 | tf_op jit(solution)/shard_map/ppermute | solution.py:36
  525.0 69.3 %collective-permute-start.34 = (bf16[512,768]{0,1:T(8,128)(2,1)}, bf16[512,768]{0,1:T(8,128)(2,1)}, u32[]{:S(2)}, u32[]{:S(2)}) collective-permute-start(bf16[512,768]{0,1:T(8,128)(2,1)} %pad_maximum_fusion.21), channel_id=1, source_target_pairs={{0,8},{4,12},{8,0},{12,4},{16,24},{20,28},{24,16},{28,20},{1,9},{5... | collective-permute-start | bytes 2359304 | tf_op jit(solution)/shard_map/ppermute | solution.py:36
  527.2 35.7 %copy-start.93 = (bf16[1024,256]{1,0:T(8,128)(2,1)}, bf16[1024,256]{1,0:T(8,128)(2,1)S(1)}, u32[]{:S(2)}) copy-start(bf16[1024,256]{1,0:T(8,128)(2,1)S(1)} %collective-permute-done.31) | copy-start | bytes 1572868
  529.1 48.2 %collective-permute-start.32 = (bf16[512,256]{1,0:T(8,128)(2,1)}, bf16[512,256]{1,0:T(8,128)(2,1)}, u32[]{:S(2)}, u32[]{:S(2)}) collective-permute-start(bf16[512,256]{1,0:T(8,128)(2,1)} %add_convert_fusion.44), channel_id=1, source_target_pairs={{0,8},{4,12},{8,0},{12,4},{16,24},{20,28},{24,16},{28,20},{1,9},{5... | collective-permute-start | bytes 786440 | tf_op jit(solution)/shard_map/ppermute | solution.py:36
  581.0 23.9 %collective-permute-start.36 = (bf16[1024,768]{0,1:T(8,128)(2,1)}, bf16[1024,768]{0,1:T(8,128)(2,1)}, u32[]{:S(2)}, u32[]{:S(2)}) collective-permute-start(bf16[1024,768]{0,1:T(8,128)(2,1)} %pad_maximum_fusion.10), channel_id=1, source_target_pairs={{0,4},{4,0},{8,12},{12,8},{16,20},{20,16},{24,28},{28,24},{1,5},{5... | collective-permute-start | bytes 4718600 | tf_op jit(solution)/shard_map/ppermute | solution.py:36
  595.8 12.0 %collective-permute-start.35 = (bf16[256,768]{0,1:T(8,128)(2,1)S(1)}, bf16[256,768]{0,1:T(8,128)(2,1)S(1)}, u32[]{:S(2)}, u32[]{:S(2)}) collective-permute-start(bf16[256,768]{0,1:T(8,128)(2,1)S(1)} %add_convert_fusion.37), channel_id=1, source_target_pairs={{0,16},{4,20},{8,24},{12,28},{16,0},{20,4},{24,8},{28,12},{1,17},{... | collective-permute-start | bytes 1179656 | tf_op jit(solution)/shard_map/ppermute | solution.py:36
  599.0 19.9 %collective-permute-start.44 = (bf16[256,1536]{1,0:T(8,128)(2,1)}, bf16[256,1536]{1,0:T(8,128)(2,1)}, u32[]{:S(2)}, u32[]{:S(2)}) collective-permute-start(bf16[256,1536]{1,0:T(8,128)(2,1)} %add_convert_fusion.7), channel_id=1, source_target_pairs={{0,8},{4,12},{8,0},{12,4},{16,24},{20,28},{24,16},{28,20},{1,9},{5... | collective-permute-start | bytes 2359304 | tf_op jit(solution)/shard_map/ppermute | solution.py:36
  603.3 40.7 %collective-permute-start.41 = (bf16[256,1536]{1,0:T(8,128)(2,1)}, bf16[256,1536]{1,0:T(8,128)(2,1)}, u32[]{:S(2)}, u32[]{:S(2)}) collective-permute-start(bf16[256,1536]{1,0:T(8,128)(2,1)} %add_convert_fusion.13), channel_id=1, source_target_pairs={{0,16},{4,20},{8,24},{12,28},{16,0},{20,4},{24,8},{28,12},{1,17},{... | collective-permute-start | bytes 2359304 | tf_op jit(solution)/shard_map/ppermute | solution.py:36
  607.2 34.0 %collective-permute-start.37 = (bf16[512,768]{0,1:T(8,128)(2,1)}, bf16[512,768]{0,1:T(8,128)(2,1)}, u32[]{:S(2)}, u32[]{:S(2)}) collective-permute-start(bf16[512,768]{0,1:T(8,128)(2,1)} %pad_maximum_fusion.22), channel_id=1, source_target_pairs={{0,16},{4,20},{8,24},{12,28},{16,0},{20,4},{24,8},{28,12},{1,17},{... | collective-permute-start | bytes 2359304 | tf_op jit(solution)/shard_map/ppermute | solution.py:36
  642.5 10.7 %collective-permute-start.38 = (bf16[256,768]{0,1:T(8,128)(2,1)S(1)}, bf16[256,768]{0,1:T(8,128)(2,1)S(1)}, u32[]{:S(2)}, u32[]{:S(2)}) collective-permute-start(bf16[256,768]{0,1:T(8,128)(2,1)S(1)} %add_convert_fusion.31), channel_id=1, source_target_pairs={{0,8},{4,12},{8,0},{12,4},{16,24},{20,28},{24,16},{28,20},{1,9},{5... | collective-permute-start | bytes 1179656 | tf_op jit(solution)/shard_map/ppermute | solution.py:36
  654.6 45.1 %slice-start = ((f32[256,768]{0,1:T(8,128)}), f32[256,256]{0,1:T(8,128)S(1)}, s32[]{:S(2)}) async-start(f32[256,768]{0,1:T(8,128)} %copy-done.57), calls=%async_computation.3 | async-start | bytes 524288 | tf_op jit(solution)/shard_map/slice | solution.py:450
  654.6 91.0 %copy-start.18 = (bf16[512,2048]{1,0:T(8,128)(2,1)S(1)}, bf16[512,2048]{1,0:T(8,128)(2,1)}, u32[]{:S(2)}) copy-start(bf16[512,2048]{1,0:T(8,128)(2,1)} %copy-done.15) | copy-start | bytes 6291460
  654.6 90.9 %copy-start.117 = (f32[1,2,8,128]{3,1,2,0:T(2,128)S(1)}, f32[1,2,8,128]{3,1,2,0:T(2,128)}, u32[]{:S(2)}) copy-start(f32[1,2,8,128]{3,1,2,0:T(2,128)} %copy-done.116) | copy-start | bytes 24580
  (135 other events, 704.8 us)
Sparse Core Ops, SparseCore 0:
  203.2 85.9 all-reduce.4
  340.3 85.4 all-reduce.6
  591.4 154.0 all-reduce.8

commit v2 on v1

--- a/solution.py
+++ b/solution.py
@@ -36,44 +36,90 @@
     return lax.ppermute(block, "blk", [(i, i ^ bit) for i in range(n)])
 
 
-def gather_rows(piece, bits):
-    rows = piece.shape[0]
-    held = {0: piece}
-    for bit in bits:
-        masks = sorted(held)
-        sent = [held[m] for m in masks]
-        got = exchange(sent[0] if len(sent) == 1 else jnp.concatenate(sent, axis=0), bit)
-        for i, m in enumerate(masks):
-            held[m | bit] = got[i * rows : (i + 1) * rows]
-    own = jnp.concatenate([held[m] for m in sorted(held)], axis=0)
-    return own, exchange(own, 1)
+def together(values, others=()):
+    return lax.optimization_barrier((*values, *others))[: len(values)]
+
+
+def after(value, *others):
+    return lax.optimization_barrier((value,) + others)[0]
+
+
+def gather_rows(pieces, orders, before=(), beside=(), closing=()):
+    count = len(pieces)
+    held = [{0: piece} for piece in pieces]
+    gots = []
+    for step in range(len(orders[0])):
+        sent = []
+        for have in held:
+            one = [have[m] for m in sorted(have)]
+            sent.append(one[0] if len(one) == 1 else jnp.concatenate(one, axis=0))
+        sent = together(sent, before[step] if step < len(before) else ())
+        got = [exchange(x, order[step]) for x, order in zip(sent, orders)]
+        gots.append(got)
+        last = step == len(orders[0]) - 1
+        got = together(got, (beside[step] if step < len(beside) else ()) + (tuple(closing) if last else ()))
+        for have, brought, order in zip(held, got, orders):
+            rows = have[0].shape[0]
+            for i, m in enumerate(sorted(have)):
+                have[m | order[step]] = brought[i * rows : (i + 1) * rows]
+    own = [jnp.concatenate([have[m] for m in sorted(have)], axis=0) for have in held]
+    return [(x, exchange(x, 1)) for x in own], gots
 
 
 def add_low(a, b):
     return (a.astype(F32) + b.astype(F32)).astype(BF16)
 
 
-def scatter_sum(own, got, bits):
-    count = 2 ** len(bits)
-    rows = own.shape[0] // count
-    held = {}
-    for i in range(count):
-        part = slice(i * rows, (i + 1) * rows)
-        held[2 * i] = (own[part], got[part])
-    for bit in bits:
-        leave = [m for m in sorted(held) if m & bit]
-        stay = [m for m in sorted(held) if not m & bit]
-        sent = [add_low(*held[m]) for m in leave]
-        back = exchange(sent[0] if len(sent) == 1 else jnp.concatenate(sent, axis=0), bit)
-        held = {
-            m: (add_low(*held[m]), back[i * rows : (i + 1) * rows]) for i, m in enumerate(stay)
-        }
-    return held[0][0].astype(F32) + held[0][1].astype(F32)
-
-
-def row_norm(values, gain):
-    scale = lax.rsqrt(jnp.mean(values * values, axis=-1, keepdims=True) + EPS)
-    return (values * scale * gain, scale)
+def scatter_terms(parts, orders):
+    held = []
+    sent = [part[0] for part in parts]
+    for (leave, stay), order in zip(parts, orders):
+        masks = [m for m in range(0, 4 * stay.shape[0], 2) if not m & order[0]][: 2 ** (len(order) - 1)]
+        rows = stay.shape[0] // len(masks)
+        held.append({m: stay[i * rows : (i + 1) * rows] for i, m in enumerate(masks)})
+    sends, gots = [], []
+    for step in range(len(orders[0])):
+        if step:
+            sent = []
+            for have, order in zip(held, orders):
+                leave = [add_low(*have.pop(m)) for m in sorted(have) if m & order[step]]
+                sent.append(leave[0] if len(leave) == 1 else jnp.concatenate(leave, axis=0))
+                for m in have:
+                    have[m] = add_low(*have[m])
+        sent = together(sent)
+        sends.append(sent)
+        got = together([exchange(x, order[step]) for x, order in zip(sent, orders)])
+        gots.append(got)
+        for have, back in zip(held, got):
+            rows = back.shape[0] // len(have)
+            for i, m in enumerate(sorted(have)):
+                have[m] = (have[m], back[i * rows : (i + 1) * rows])
+    return [have[0] for have in held], sends, gots
+
+
+def scatter_sums(parts, orders):
+    terms, sends, gots = scatter_terms(parts, orders)
+    return [a.astype(F32) + b.astype(F32) for a, b in terms], sends, gots
+
+
+def leaving_first(n, bit):
+    masks = [2 * i for i in range(n // 2)]
+    return [i for i, m in enumerate(masks) if m & bit] + [i for i, m in enumerate(masks) if not m & bit]
+
+
+def split_sum(own, got, n, bit):
+    rows = own.shape[0] // (n // 2)
+    at = leaving_first(n, bit)
+
+    def part(array, which):
+        return jnp.concatenate([array[i * rows : (i + 1) * rows] for i in which], axis=0)
+
+    half = len(at) // 2
+    return tuple(add_low(part(own, w), part(got, w)) for w in (at[:half], at[half:]))
+
+
+def norm_scale(values):
+    return lax.rsqrt(jnp.mean(values * values, axis=-1, keepdims=True) + EPS)
 
 
 def norm_back(values, scale, weighted):
@@ -91,8 +137,452 @@
 
 
 def turned(values):
-    half = values.shape[-1] // 2
-    return jnp.concatenate([values[..., half:], values[..., :half]], axis=-1)
+    return pltpu.roll(values, HD // 2, 1)
+
+
+def call(kernel, name, grid, in_specs, out_specs, out_shape, args, flops, scratch=(), scalars=None):
+    if scalars is None:
+        spec = {"grid": grid, "in_specs": in_specs, "out_specs": out_specs, "scratch_shapes": scratch}
+    else:
+        spec = {
+            "grid_spec": pltpu.PrefetchScalarGridSpec(
+                num_scalar_prefetch=1,
+                grid=grid,
+                in_specs=in_specs,
+                out_specs=out_specs,
+                scratch_shapes=scratch,
+            )
+        }
+        args = (scalars,) + tuple(args)
+    return pl.pallas_call(
+        kernel,
+        out_shape=out_shape,
+        compiler_params=pltpu.CompilerParams(vmem_limit_bytes=28 * MIB),
+        cost_estimate=pl.CostEstimate(flops=0, bytes_accessed=0, transcendentals=0),
+        name=name,
+        **spec,
+    )(*args)
+
+
+def shape(dims_, dtype):
+    return jax.ShapeDtypeStruct(dims_, dtype)
+
+
+def picked(array, order):
+    n = order.shape[0]
+    block = array.shape[1] // n
+    return jnp.concatenate(
+        [lax.dynamic_slice_in_dim(array, order[i] * block, block, 1) for i in range(n)], axis=1
+    )
+
+
+def enter_kernel(sc, a_ref, b_ref, a_out, b_out):
+    a_out[...] = a_ref[...]
+    b_out[...] = b_ref[...]
+
+
+def enter(order, first, second):
+    rows, width = first.shape
+    n = order.shape[0]
+    block = width // n
+    if block % 128:
+        return picked(first, order), picked(second, order)
+    source = pl.BlockSpec((rows, block), lambda p, sc: (0, sc[p]))
+    target = pl.BlockSpec((rows, block), lambda p, sc: (0, p))
+    return call(
+        enter_kernel,
+        "enter",
+        (n,),
+        [source, source],
+        [target, target],
+        [shape(first.shape, first.dtype), shape(second.shape, second.dtype)],
+        (first, second),
+        0,
+        scalars=order,
+    )
+
+
+def leave_blocks(sc, out_ref, result):
+    width = result.shape[1]
+    n = sc.shape[0]
+    block = width // n
+    if block % 128:
+        out_ref[...] = result.astype(out_ref.dtype)
+        return
+    for p in range(n):
+        at = pl.ds(pl.multiple_of(sc[p] * block, 128), block)
+        out_ref[:, at] = result[:, p * block : (p + 1) * block].astype(out_ref.dtype)
+
+
+def leave_kernel(sc, *refs):
+    count = len(refs) // 2
+    for value_ref, out_ref in zip(refs[:count], refs[count:]):
+        leave_blocks(sc, out_ref, value_ref[...])
+
+
+def leave(name, order, value, dtype):
+    rows, width = value.shape
+    n = order.shape[0]
+    height = rows // 4
+    spec = pl.BlockSpec((height, width), lambda i, sc: (i, 0))
+    result = call(
+        leave_kernel, name, (4,), [spec], [spec], [shape((rows, width), dtype)], (value,), 0, scalars=order
+    )[0]
+    if width // n % 128:
+        index = jnp.arange(n)
+        back = jnp.sum(jnp.where(order[None, :] == index[:, None], index[None, :], 0), axis=1)
+        return picked(result, back)
+    return result
+
+
+def post_kernel(tokens_ref, attn_ref, gain_ref, out_ref):
+    hidden = tokens_ref[...].astype(F32) + attn_ref[...].astype(F32)
+    out_ref[...] = (hidden * norm_scale(hidden) * gain_ref[...]).astype(BF16)
+
+
+def layer_out_kernel(tokens_ref, attn_ref, mlp_ref, out_ref):
+    hidden = tokens_ref[...].astype(F32) + attn_ref[...].astype(F32)
+    out_ref[...] = (hidden + mlp_ref[...].astype(F32)).astype(BF16)
+
+
+def grad_hidden_kernel(tokens_ref, attn_ref, cotangent_ref, grad_ref, gain_ref, out_ref, low_ref):
+    hidden = tokens_ref[...].astype(F32) + attn_ref[...].astype(F32)
+    weighted = grad_ref[...].astype(F32) * gain_ref[...]
+    grad = cotangent_ref[...].astype(F32) + norm_back(hidden, norm_scale(hidden), weighted)
+    out_ref[...] = grad
+    low_ref[...] = grad.astype(BF16)
+
+
+def tokens_grad_kernel(tokens_ref, hidden_ref, grad_ref, gain_ref, out_ref):
+    inputs = tokens_ref[...].astype(F32)
+    weighted = grad_ref[...].astype(F32) * gain_ref[...]
+    back = norm_back(inputs, norm_scale(inputs), weighted)
+    out_ref[...] = (hidden_ref[...] + back).astype(BF16)
+
+
+def on_quarter(kernel, name, arrays, gains, dtypes):
+    rows, width = arrays[0].shape
+    spec = pl.BlockSpec((rows, width), lambda i: (0, 0))
+    full = [pl.BlockSpec(g.shape, lambda i: (0, 0)) for g in gains]
+    return call(
+        kernel,
+        name,
+        (1,),
+        [spec] * len(arrays) + full,
+        [spec] * len(dtypes),
+        [shape((rows, width), dtype) for dtype in dtypes],
+        tuple(arrays) + tuple(gains),
+        0,
+    )
+
+
+def project_kernel(
+    q_steps, split, tokens_ref, gain_ref, wq0, wq1, wkv0, wkv1, cos_ref, sin_ref, gq_ref, gk_ref,
+    normed_ref, q_proj, k_proj, queries, keys, values,
+):
+    j = pl.program_id(0)
+
+    @pl.when(j == 0)
+    def _():
+        inputs = tokens_ref[...].astype(F32)
+        normed_ref[...] = (inputs * norm_scale(inputs) * gain_ref[...]).astype(BF16)
+
+    def product(w0, w1):
+        return dims(normed_ref[:, :split], w0[...], 1, 0) + dims(normed_ref[:, split:], w1[...], 1, 0)
+
+    def heads(proj, proj_ref, out_ref, gain, factor):
+        proj_ref[...] = proj
+        for h in range(proj.shape[1] // HD):
+            one = slice(h * HD, (h + 1) * HD)
+            u = proj[:, one]
+            u = u * norm_scale(u) * gain
+            u = u * cos_ref[...] + turned(u) * sin_ref[...]
+            out_ref[:, one] = (u * factor if factor else u).astype(BF16)
+
+    @pl.when(j < q_steps)
+    def _():
+        heads(product(wq0, wq1), q_proj, queries, gq_ref[...], HD**-0.5 * LOG2E)
+
+    @pl.when(j == q_steps)
+    def _():
+        heads(product(wkv0, wkv1), k_proj, keys, gk_ref[...], None)
+
+    @pl.when(j == q_steps + 1)
+    def _():
+        values[...] = product(wkv0, wkv1).astype(BF16)
+
+
+def projections(tokens, gain, wq, wkv, cosine, sine, gain_query, gain_key):
+    rows, width = tokens.shape
+    q_cols = wq[0].shape[1]
+    kv_cols = wkv[0].shape[1] // 2
+    steps = q_cols // kv_cols
+    split = width // 2
+
+    def whole(array):
+        return pl.BlockSpec(array.shape, lambda j: (0, 0))
+
+    q_tile = pl.BlockSpec((split, kv_cols), lambda j: (0, jnp.minimum(j, steps - 1)))
+    kv_tile = pl.BlockSpec((split, kv_cols), lambda j: (0, jnp.maximum(j - steps, 0)))
+    q_out = pl.BlockSpec((rows, kv_cols), lambda j: (0, jnp.minimum(j, steps - 1)))
+    kv_out = pl.BlockSpec((rows, kv_cols), lambda j: (0, 0))
+    small = [cosine, sine, gain_query, gain_key]
+    return call(
+        functools.partial(project_kernel, steps, split),
+        "projections",
+        (steps + 2,),
+        [whole(tokens), whole(gain), q_tile, q_tile, kv_tile, kv_tile] + [whole(a) for a in small],
+        [whole(tokens), q_out, kv_out, q_out, kv_out, kv_out],
+        [
+            shape((rows, width), BF16),
+            shape((rows, q_cols), F32),
+            shape((rows, kv_cols), F32),
+            shape((rows, q_cols), BF16),
+            shape((rows, kv_cols), BF16),
+            shape((rows, kv_cols), BF16),
+        ],
+        (tokens, gain, *wq, *wkv, *small),
+        2 * rows * width * (q_cols + 2 * kv_cols),
+    )
+
+
+def to_width_kernel(count, half, *refs):
+    i = pl.program_id(0)
+    lefts = refs[:count]
+    rights = refs[count : 3 * count]
+    out_ref = refs[-1]
+    for parity, here in ((0, i < half), (1, i >= half)):
+
+        @pl.when(here)
+        def _(parity=parity):
+            total = None
+            for left, pair in zip(lefts, zip(rights[::2], rights[1::2])):
+                term = dims(left[...], pair[parity][...], 1, 1)
+                total = term if total is None else total + term
+            out_ref[...] = total.astype(out_ref.dtype)
+
+
+def to_width(name, *terms, tile=256):
+    rows = terms[0][0].shape[0]
+    split = terms[0][2][0].shape[0]
+    half = split // tile
+    in_specs = []
+    for left, at, pair, where, columns in terms:
+        in_specs.append(pl.BlockSpec((rows, columns), lambda i, at=at: (0, at)))
+    args = [t[0] for t in terms]
+    flops = 0
+    for left, at, pair, where, columns in terms:
+        in_specs.append(
+            pl.BlockSpec((tile, columns), lambda i, w=where: (jnp.minimum(i, half - 1), w))
+        )
+        in_specs.append(
+            pl.BlockSpec((tile, columns), lambda i, w=where: (jnp.maximum(i - half, 0), w))
+        )
+        args += list(pair)
+        flops += 4 * rows * split * columns
+    return call(
+        functools.partial(to_width_kernel, len(terms), half),
+        name,
+        (2 * half,),
+        in_specs,
+        [pl.BlockSpec((rows, tile), lambda i: (0, i))],
+        [shape((rows, 2 * split), BF16)],
+        tuple(args),
+        flops,
+    )[0]
+
+
+def from_width_kernel(split, bounds, left_ref, *refs):
+    out_ref = refs[-1]
+    j = pl.program_id(0)
+    for k in range(len(bounds) - 1):
+
+        @pl.when((j >= bounds[k]) & (j < bounds[k + 1]))
+        def _(w0=refs[2 * k], w1=refs[2 * k + 1]):
+            product = dims(left_ref[:, :split], w0[...], 1, 0) + dims(left_ref[:, split:], w1[...], 1, 0)
+            out_ref[...] = product.astype(out_ref.dtype)
+
+
+def from_width(name, left, *sides, tile=256):
+    rows, width = left.shape
+    split = width // 2
+    bounds = [0]
+    specs, args = [], [left]
+    for pair, start, columns in sides:
+        low, high = bounds[-1], bounds[-1] + columns // tile
+        bounds.append(high)
+        specs += [
+            pl.BlockSpec(
+                (split, tile),
+                lambda j, low=low, high=high, first=start // tile: (0, first + jnp.clip(j, low, high - 1) - low),
+            )
+        ] * 2
+        args += list(pair)
+    return call(
+        functools.partial(from_width_kernel, split, tuple(bounds)),
+        name,
+        (bounds[-1],),
+        [pl.BlockSpec((rows, width), lambda j: (0, 0))] + specs,
+        [pl.BlockSpec((rows, tile), lambda j: (0, j))],
+        [shape((rows, bounds[-1] * tile), BF16)],
+        tuple(args),
+        2 * rows * width * bounds[-1] * tile,
+    )[0]
+
+
+def units_kernel(split, post_ref, wg0, wg1, wu0, wu1, grad_ref, act_ref, gate_out, up_out):
+    def product(w0, w1):
+        return dims(post_ref[:, :split], w0[...], 1, 0) + dims(post_ref[:, split:], w1[...], 1, 0)
+
+    gate = product(wg0, wg1)
+    up = product(wu0, wu1)
+    grad_act = grad_ref[...].astype(F32)
+    sigma = jax.nn.sigmoid(gate)
+    silu = gate * sigma
+    act_ref[...] = (silu * up).astype(BF16)
+    up_out[...] = (grad_act * silu).astype(BF16)
+    gate_out[...] = (grad_act * up * sigma * (1.0 + gate * (1.0 - sigma))).astype(BF16)
+
+
+def hidden_units(post, wg, wu, grad_act, tile=256):
+    rows, width = post.shape
+    units = grad_act.shape[1]
+    split = width // 2
+    side = pl.BlockSpec((split, tile), lambda j: (0, j))
+    part = pl.BlockSpec((rows, tile), lambda j: (0, j))
+    unit = shape((rows, units), BF16)
+    return call(
+        functools.partial(units_kernel, split),
+        "hidden_units",
+        (units // tile,),
+        [pl.BlockSpec(post.shape, lambda j: (0, 0)), side, side, side, side, part],
+        [part, part, part],
+        [unit, unit, unit],
+        (post, *wg, *wu, grad_act),
+        4 * rows * width * units,
+    )
+
+
+def away_kernel(count, *refs):
+    out_ref = refs[-1]
+    start = 0
+    for left, right in zip(refs[:count], refs[count : 2 * count]):
+        columns = right.shape[1]
+        out_ref[:, start : start + columns] = dims(left[...].T, right[...], 1, 0).astype(BF16)
+        start += columns
+
+
+def home_kernel(count, leaving, sc, *refs):
+    got_ref, leave_ref, stay_ref = refs[2 * count :]
+    step = pl.program_id(0)
+    for out_ref, here in ((leave_ref, step < leaving), (stay_ref, step >= leaving)):
+
+        @pl.when(here)
+        def _(out_ref=out_ref):
+            start = 0
+            for left, right in zip(refs[:count], refs[count : 2 * count]):
+                columns = right.shape[1]
+                at = slice(start, start + columns)
+                term = dims(left[...].T, right[...], 1, 0) + got_ref[:, at].astype(F32)
+                out_ref[:, at] = term.astype(BF16)
+                start += columns
+
+
+def weight_grad(name, n, bit, *pairs):
+    rows, width = pairs[0][0].shape
+    split = width // 2
+    total = sum(p[3] for p in pairs)
+    flops = rows * width * total
+    right_specs = [(p[2], p[3]) for p in pairs]
+    lefts = [p[0] for p in pairs]
+    rights = [p[1] for p in pairs]
+    tile = 256
+    tiles = split // tile
+    away = call(
+        functools.partial(away_kernel, len(pairs)),
+        name + "_away",
+        (tiles,),
+        [pl.BlockSpec((rows, tile), lambda i: (0, tiles + i))] * len(pairs)
+        + [pl.BlockSpec((rows, c), lambda i, w=w: (0, w)) for w, c in right_specs],
+        [pl.BlockSpec((tile, total), lambda i: (i, 0))],
+        [shape((split, total), BF16)],
+        (*lefts, *rights),
+        flops,
+    )[0]
+    got = exchange(away, 1)
+    block = width // n
+    order = leaving_first(n, bit)
+    leaving = len(order) // 2
+    if block % 128:
+        home = call(
+            functools.partial(away_kernel, len(pairs)),
+            name,
+            (tiles,),
+            [pl.BlockSpec((rows, tile), lambda i: (0, i))] * len(pairs)
+            + [pl.BlockSpec((rows, c), lambda i, w=w: (0, w)) for w, c in right_specs],
+            [pl.BlockSpec((tile, total), lambda i: (i, 0))],
+            [shape((split, total), BF16)],
+            (*lefts, *rights),
+            flops,
+        )[0]
+        return split_sum(home, got, n, bit)
+    return call(
+        functools.partial(home_kernel, len(pairs), leaving),
+        name,
+        (len(order),),
+        [pl.BlockSpec((rows, block), lambda i, sc: (0, sc[i]))] * len(pairs)
+        + [pl.BlockSpec((rows, c), lambda i, sc, w=w: (0, w)) for w, c in right_specs]
+        + [pl.BlockSpec((block, total), lambda i, sc: (sc[i], 0))],
+        [
+            pl.BlockSpec((block, total), lambda i, sc: (jnp.minimum(i, leaving - 1), 0)),
+            pl.BlockSpec((block, total), lambda i, sc: (jnp.maximum(i - leaving, 0), 0)),
+        ],
+        [shape((split // 2, total), BF16)] * 2,
+        (*lefts, *rights, got),
+        flops,
+        scalars=jnp.array(order, jnp.int32),
+    )
+
+
+def heads_back_kernel(terms, passed, *refs):
+    grads, refs = refs[:terms], refs[terms:]
+    others, refs = refs[:passed], refs[passed:]
+    proj_ref, cos_ref, sin_ref, gain_ref, out_ref, sum_ref = refs
+    columns = proj_ref.shape[1]
+    total = None
+    for h in range(columns // HD):
+        one = slice(h * HD, (h + 1) * HD)
+        grad = grads[0][:, one].astype(F32)
+        for more in grads[1:]:
+            grad = grad + more[:, one].astype(F32)
+        grad = grad * cos_ref[...] + turned(grad * sin_ref[...])
+        u = proj_ref[:, one]
+        scale = norm_scale(u)
+        term = jnp.sum((grad * u * scale).reshape(-1, 8, HD), axis=0)
+        total = term if total is None else total + term
+        out_ref[:, one] = norm_back(u, scale, grad * gain_ref[...]).astype(BF16)
+    sum_ref[...] = total
+    if passed:
+        other = others[0][...].astype(F32)
+        for more in others[1:]:
+            other = other + more[...].astype(F32)
+        out_ref[:, columns:] = other.astype(BF16)
+
+
+def heads_back(name, grads, others, proj, cosine, sine, gain):
+    rows, columns = proj.shape
+    args = (*grads, *others, proj, cosine, sine, gain)
+    total = columns + (others[0].shape[1] if others else 0)
+    return call(
+        functools.partial(heads_back_kernel, len(grads), len(others)),
+        name,
+        (1,),
+        [pl.BlockSpec(a.shape, lambda i: (0, 0)) for a in args],
+        [pl.BlockSpec((rows, total), lambda i: (0, 0)), pl.BlockSpec((8, HD), lambda i: (0, 0))],
+        [shape((rows, total), BF16), shape((8, HD), F32)],
+        args,
+        20 * rows * columns,
+    )
 
 
 def attend_kernel(span, sc, q_ref, k0, k1, v0, v1, ctx_ref, lse_ref, k_s, v_s, acc_s, sum_s):
@@ -257,6 +747,14 @@
     )(scalars, queries, grad_context, context, lse, *keys, *values)
 
 
+def sum_of_parts(part):
+    return lax.psum_scatter(part, "fsdp", scatter_dimension=0, tiled=True)
+
+
+def all_parts(mine):
+    return lax.all_gather(mine, "fsdp", axis=0, tiled=True)
+
+
 def shards(
     tokens,
     span_order,
@@ -289,47 +787,13 @@
     units = gate_weight.shape[1]
     o_cols = output_weight.shape[0]
 
-    def in_masks(array):
-        return jnp.concatenate(
-            [lax.dynamic_slice_in_dim(array, (me ^ m) * block, block, 1) for m in masks], axis=1
-        )
-
-    def in_blocks(array):
-        places = [((me ^ j) >> 1) + ((me ^ j) & 1) * (n // 2) for j in range(n)]
-        return jnp.concatenate(
-            [lax.dynamic_slice_in_dim(array, p * block, block, 1) for p in places], axis=1
-        )
-
-    gains = jnp.concatenate([input_gain, post_gain, query_gain, key_gain]).reshape(1, -1)
-    gains = jnp.concatenate(gather_rows(gains, bits), axis=0).astype(F32)
-    wq = gather_rows(query_weight, bits)
-    wkv = gather_rows(jnp.concatenate([key_weight, value_weight], axis=1), flipped)
-    gain_input = gains[:, :block].reshape(1, width)
-    gain_post = gains[:, block : 2 * block].reshape(1, width)
-    chosen = (me ^ jnp.arange(n))[:, None] == jnp.array(masks)[None, :]
-    head_gains = jnp.sum(jnp.where(chosen[:, :, None], gains[None, :, 2 * block :], 0.0), axis=1)
-    part = head_gains.shape[1] // 2
-    gain_query = head_gains[:, :part].reshape(HD)
-    gain_key = head_gains[:, part:].reshape(HD)
-
-    tokens = in_masks(tokens)
-    cotangent = in_masks(cotangent)
-    inputs = tokens.astype(F32)
-    normed, scale_in = row_norm(inputs, gain_input)
-    normed_low = normed.astype(BF16)
-
-    def project(left, pair):
-        return dims(left[:, :split], pair[0], 1, 0) + dims(left[:, split:], pair[1], 1, 0)
-
-    q_proj = project(normed_low, wq).reshape(rows, heads, HD)
-    kv_proj = project(normed_low, wkv)
-    k_proj = kv_proj[:, :kv_cols].reshape(rows, kv_heads, HD)
+    mask_list = jnp.array(masks, jnp.int32)
+    order = me ^ mask_list
+    pair = [bits, flipped]
 
     spans = span_order.reshape(n, 2)
     chunk_ids = jnp.sum(
-        jnp.where(
-            (me ^ jnp.array(masks))[:, None, None] == jnp.arange(n)[None, :, None], spans[None], 0
-        ),
+        jnp.where(order[:, None, None] == jnp.arange(n)[None, :, None], spans[None], 0),
         axis=1,
     ).reshape(-1)
     count = 2 * n
@@ -342,112 +806,136 @@
     scalars = jnp.concatenate([chunk_ids[:2], positions]).astype(jnp.int32)
     places = (chunk_ids[:2, None] * span + jnp.arange(span)[None, :]).reshape(-1)
     cosine, sine = rope_tables(places, HD)
-    cosine, sine = cosine[:, None, :], sine[:, None, :]
-
-    def rotate(values):
-        return values * cosine + turned(values) * sine
-
-    def rotate_back(grads):
-        return grads * cosine + turned(grads * sine)
-
-    q_normed, q_scale = row_norm(q_proj, gain_query)
-    queries = (rotate(q_normed) * (HD**-0.5 * LOG2E)).astype(BF16).reshape(rows, q_cols)
-    k_normed, k_scale = row_norm(k_proj, gain_key)
-    keys = rotate(k_normed).astype(BF16).reshape(rows, kv_cols)
-    values = kv_proj[:, kv_cols:].astype(BF16)
-    all_keys = gather_rows(keys, bits)
-    all_values = gather_rows(values, flipped)
-
+
+    parts = lax.axis_size("fsdp")
+    quarter = rows // parts
+    my_part = lax.axis_index("fsdp") * quarter
+
+    def mine(array):
+        return lax.dynamic_slice_in_dim(array, my_part, quarter, 0)
+
+    tokens, cotangent = enter(order, tokens, cotangent)
+    my_tokens = mine(tokens)
+    my_cotangent = mine(cotangent)
     down_t = down_weight.T
     cut = (units - o_cols) // 2
     side_a = jnp.concatenate([output_weight.T, down_t[:, :cut]], axis=1)
     side_b = down_t[:, cut:]
-    side_a, side_b, _ = lax.optimization_barrier((side_a, side_b, wkv[1]))
-    side_a = gather_rows(side_a, bits)
-    side_b = gather_rows(side_b, flipped)
-    wo = [w[:, :o_cols] for w in side_a]
-    wd_a = [w[:, o_cols:] for w in side_a]
-    wd_b = side_b
-    wg = gather_rows(gate_weight, bits)
-    wu = gather_rows(up_weight, flipped)
-
+    gains = jnp.concatenate([input_gain, post_gain, query_gain, key_gain]).reshape(1, -1)
+    (wq, wkv, gains), _ = gather_rows(
+        [query_weight, jnp.concatenate([key_weight, value_weight], axis=1), gains],
+        [bits, flipped, bits],
+        beside=((tokens, cotangent), (side_a, side_b, cosine, sine, scalars)),
+    )
+    gains = jnp.concatenate(gains, axis=0).astype(F32)
+    gain_input = gains[:, :block].reshape(1, width)
+    gain_post = gains[:, block : 2 * block].reshape(1, width)
+    chosen = (me ^ jnp.arange(n))[:, None] == mask_list[None, :]
+    head_gains = jnp.sum(jnp.where(chosen[:, :, None], gains[None, :, 2 * block :], 0.0), axis=1)
+    part = head_gains.shape[1] // 2
+    gain_query = head_gains[:, :part].reshape(1, HD)
+    gain_key = head_gains[:, part:].reshape(1, HD)
+
+    normed_low, q_proj, k_proj, queries, keys, values = projections(
+        tokens, gain_input, wq, wkv, cosine, sine, gain_query, gain_key
+    )
+    (all_keys, all_values), key_gots = gather_rows([keys, values], pair)
     context, lse = attend(scalars, queries, all_keys, all_values, span)
 
-    attn_part = jnp.concatenate([dims(context, w, 1, 1) for w in wo], axis=1).astype(BF16)
-    attn = lax.psum(attn_part, "fsdp").astype(F32)
-    hidden = inputs + attn
-    post, scale_post = row_norm(hidden, gain_post)
-    post_low = post.astype(BF16)
-    grad_act = jnp.concatenate([project(cotangent, wd_a), project(cotangent, wd_b)], axis=1)
-    gate = project(post_low, wg)
-    up = project(post_low, wu)
-    sigma = jax.nn.sigmoid(gate)
-    silu = gate * sigma
-    act = (silu * up).astype(BF16)
-    grad_up = (grad_act * silu).astype(BF16)
-    grad_gate = (grad_act * up * sigma * (1.0 + gate * (1.0 - sigma))).astype(BF16)
-    post_part = jnp.concatenate(
-        [dims(grad_gate, g, 1, 1) + dims(grad_up, u, 1, 1) for g, u in zip(wg, wu)], axis=1
-    ).astype(BF16)
-    grad_post = lax.psum(post_part, "fsdp").astype(F32)
-    mlp_part = jnp.concatenate(
-        [dims(act[:, :cut], a, 1, 1) + dims(act[:, cut:], b, 1, 1) for a, b in zip(wd_a, wd_b)],
-        axis=1,
-    ).astype(BF16)
-    mlp_part, grad_post = lax.optimization_barrier((mlp_part, grad_post))
-    mlp = lax.psum(mlp_part, "fsdp").astype(F32)
-    layer_out = in_blocks((hidden + mlp).astype(BF16))
-
-    def weight_grad(left, right, order):
-        away = dims(left[:, split:], right, 0, 0).astype(BF16)
-        home = dims(left[:, :split], right, 0, 0).astype(BF16)
-        return scatter_sum(home, exchange(away, 1), order)
-
+    (side_a, side_b), _ = gather_rows(
+        [side_a, side_b], pair, before=(tuple(wq[:1]), tuple(key_gots[-1])), closing=[context]
+    )
+    (wg, wu), _ = gather_rows([gate_weight, up_weight], pair, before=((context,),))
+
+    attn_part = to_width("attention_out", (context, 0, side_a, 0, o_cols))
+    my_attn = sum_of_parts(attn_part)
+    my_post = on_quarter(post_kernel, "post", (my_tokens, my_attn), (gain_post,), (BF16,))[0]
+    post_low = all_parts(my_post)
+    grad_act = from_width("grad_act", cotangent, (side_a, o_cols, cut), (side_b, 0, units - cut))
+    act, grad_gate, grad_up = hidden_units(post_low, wg, wu, grad_act)
+    post_part = to_width("grad_post", (grad_gate, 0, wg, 0, units), (grad_up, 0, wu, 0, units))
+    my_grad_post = sum_of_parts(post_part)
+
+    act_later = after(act, post_part)
+    gate_later = after(grad_gate, post_part)
+    up_later = after(grad_up, post_part)
     middle = units // 2
-    down_a = weight_grad(cotangent, act[:, :middle], bits)
-    down_b = weight_grad(cotangent, act[:, middle:], flipped)
-    gate_sum = weight_grad(post_low, grad_gate, bits)
-    up_sum = weight_grad(post_low, grad_up, flipped)
+    down_a = weight_grad("down_a", n, bits[0], (cotangent, act_later, 0, middle))
+    down_b = weight_grad("down_b", n, flipped[0], (cotangent, act_later, 1, middle))
+    gate_terms = weight_grad("gate_grad", n, bits[0], (post_low, gate_later, 0, units))
+    up_terms = weight_grad("up_grad", n, flipped[0], (post_low, up_later, 0, units))
+    (gate_sum, up_sum), sends, gots = scatter_sums([gate_terms, up_terms], pair)
+    (down_a, down_b), _, _ = scatter_sums([down_a, down_b], pair)
     down_sum = jnp.concatenate([down_a, down_b], axis=1).T
 
-    grad_hidden = cotangent.astype(F32) + norm_back(hidden, scale_post, grad_post * gain_post)
-    hidden_low = grad_hidden.astype(BF16)
-    grad_context = (
-        dims(hidden_low[:, :split], wo[0], 1, 0) + dims(hidden_low[:, split:], wo[1], 1, 0)
-    ).astype(BF16)
+    mlp_part = to_width(
+        "units_out",
+        (act_later, 0, side_a, 1, cut),
+        (act_later, 1, side_b, 0, cut),
+        (act_later, 2, side_b, 1, cut),
+    )
+    my_grad_hidden, my_hidden_low = on_quarter(
+        grad_hidden_kernel,
+        "grad_hidden",
+        (my_tokens, my_attn, my_cotangent, my_grad_post),
+        (gain_post,),
+        (F32, BF16),
+    )
+    hidden_low = all_parts(my_hidden_low)
+    mlp_part, hidden_low = together((mlp_part, hidden_low), tuple(gots[0]))
+    my_mlp = sum_of_parts(mlp_part)
+    my_layer_out = on_quarter(
+        layer_out_kernel, "layer_out_rows", (my_tokens, my_attn, my_mlp), (), (BF16,)
+    )[0]
+
+    grad_context = from_width("grad_context", hidden_low, (side_a, 0, o_cols))
+    grad_context = after(grad_context, *gots[-1])
     dq, dk_own, dk_other, dv_own, dv_other = attend_back(
         scalars, queries, grad_context, context, lse, all_keys, all_values, span
     )
-    grad_k = scatter_sum(dk_own, exchange(dk_other, 1), bits).reshape(rows, kv_heads, HD)
-    grad_v = scatter_sum(dv_own, exchange(dv_other, 1), flipped)
-
-    rotated_q = rotate_back(dq.reshape(rows, heads, HD))
-    q_gain_part = jnp.sum(rotated_q * q_proj * q_scale, axis=(0, 1))
-    grad_q_low = norm_back(q_proj, q_scale, rotated_q * gain_query)
-    grad_q_low = grad_q_low.astype(BF16).reshape(rows, q_cols)
-    rotated_k = rotate_back(grad_k)
-    k_gain_part = jnp.sum(rotated_k * k_proj * k_scale, axis=(0, 1))
-    grad_k_low = norm_back(k_proj, k_scale, rotated_k * gain_key).astype(BF16)
-    grad_kv_low = jnp.concatenate(
-        [grad_k_low.reshape(rows, kv_cols), grad_v.astype(BF16)], axis=1
-    )
-    normed_part = jnp.concatenate(
-        [dims(grad_q_low, q, 1, 1) + dims(grad_kv_low, kv, 1, 1) for q, kv in zip(wq, wkv)],
-        axis=1,
-    ).astype(BF16)
-    grad_normed = lax.psum(normed_part, "fsdp").astype(F32)
+    dk_got, dv_got = together((exchange(dk_other, 1), exchange(dv_other, 1)))
+    key_sums = split_sum(dk_own, dk_got, n, bits[0])
+    value_sums = split_sum(dv_own, dv_got, n, flipped[0])
+    (key_terms, value_terms), sends, _ = scatter_terms([key_sums, value_sums], pair)
+    dq, hidden_later = together((dq, hidden_low), tuple(sends[0]))
+    grad_q_low, q_gain_part = heads_back("queries_back", [dq], [], q_proj, cosine, sine, gain_query)
+    grad_kv_low, k_gain_part = heads_back(
+        "keys_back", key_terms, value_terms, k_proj, cosine, sine, gain_key
+    )
+    normed_part = to_width(
+        "grad_normed", (grad_q_low, 0, wq, 0, q_cols), (grad_kv_low, 0, wkv, 0, 2 * kv_cols)
+    )
+    my_grad_normed = sum_of_parts(after(normed_part, my_mlp))
+    my_tokens_grad = on_quarter(
+        tokens_grad_kernel,
+        "tokens_grad_rows",
+        (my_tokens, my_grad_hidden, my_grad_normed),
+        (gain_input,),
+        (BF16,),
+    )[0]
 
     o_half = o_cols // 2
-    qo = weight_grad_two(
-        (normed_low, grad_q_low), (hidden_low, context[:, :o_half]), split, bits
-    )
-    kvo = weight_grad_two(
-        (normed_low, grad_kv_low), (hidden_low, context[:, o_half:]), split, flipped
-    )
+    qo = weight_grad(
+        "query_grad", n, bits[0], (normed_low, grad_q_low, 0, q_cols), (hidden_later, context, 0, o_half)
+    )
+    kvo = weight_grad(
+        "key_value_grad",
+        n,
+        flipped[0],
+        (normed_low, grad_kv_low, 0, 2 * kv_cols),
+        (hidden_later, context, 1, o_half),
+    )
+    (qo, kvo), _, _ = scatter_sums([qo, kvo], pair)
     query_sum = qo[:, :q_cols]
     key_sum = kvo[:, :kv_cols]
     value_sum = kvo[:, kv_cols : 2 * kv_cols]
     out_sum = jnp.concatenate([qo[:, q_cols:], kvo[:, 2 * kv_cols :]], axis=1).T
+
+    heads_sum = jnp.concatenate([jnp.sum(q_gain_part, axis=0), jnp.sum(k_gain_part, axis=0)])[None, :]
+    for bit in [1] + bits:
+        heads_sum = heads_sum + exchange(heads_sum, bit)
+    head = HD // n
+    heads_sum = lax.dynamic_slice_in_dim(heads_sum.reshape(2, n, head), me, 1, 1).reshape(-1)
 
     def along_rows(weight, grad):
         return jnp.sum(weight.astype(F32) * grad, axis=1)
@@ -460,19 +948,15 @@
     post_gain_part = (
         along_rows(gate_weight, gate_sum) + along_rows(up_weight, up_sum)
     ) / post_gain.astype(F32)
-    mine = (jnp.arange(n) == me)[:, None]
-    widths = jnp.concatenate([input_gain_part, post_gain_part])[None, :]
-    small = jnp.concatenate(
-        [
-            jnp.where(mine, widths, 0.0),
-            jnp.concatenate([q_gain_part.reshape(n, -1), k_gain_part.reshape(n, -1)], axis=1),
-        ],
-        axis=1,
-    )
-    small = lax.dynamic_slice_in_dim(lax.psum(small, ("blk", "fsdp")), me, 1, 0)[0]
-    head = HD // n
-
-    tokens_grad = in_blocks(grad_hidden + norm_back(inputs, scale_in, grad_normed * gain_input))
+    small = jnp.concatenate([input_gain_part, post_gain_part, heads_sum])[None, :]
+    step = 1
+    while step < parts:
+        small = small + lax.ppermute(small, "fsdp", [(i, i ^ step) for i in range(parts)])
+        step *= 2
+    small = small[0]
+
+    tokens_grad = leave("tokens_grad", order, all_parts(my_tokens_grad), F32)
+    layer_out = leave("layer_out", order, all_parts(my_layer_out), BF16)
     return (
         layer_out,
         tokens_grad,
@@ -488,17 +972,6 @@
         up_sum,
         down_sum,
     )
-
-
-def weight_grad_two(first, second, split, order):
-    def side(columns):
-        return jnp.concatenate(
-            [dims(left[:, columns], right, 0, 0) for left, right in (first, second)], axis=1
-        ).astype(BF16)
-
-    away = side(slice(split, None))
-    home = side(slice(0, split))
-    return scatter_sum(home, exchange(away, 1), order)
 
 
 def solution(mesh):

time: 774 us -> 603 us (0.78)
  Pallas kernels: 44.5 us -> 152 us
  matrix products: 98.4 us -> 0 us
  other arithmetic: 124 us -> 42.6 us
  waiting for transfers between devices: 310 us -> 253 us
  blocking collectives: 41.9 us -> 0 us
    psum x3 -> x0, waiting for transfers between devices: 167 us -> none  [the longest x1 64.2 us: shards(): attn = lax.psum(attn_part, 'fsdp').astype(F32)]
    pallas_call x0 -> x29, Pallas kernels: none -> 108 us  [call(): pl.pallas_call(kernel, out_shape=out_shape, compiler_params=pltpu.Compile...]
    dot_general x44 -> x0, matrix products: 98.4 us -> none  [dims(): lax.dot_general(lhs, rhs, (((left,), (right,)), ((), ())), preferred_elem...]
    all_gather x0 -> x4, waiting for transfers between devices: none -> 59.1 us  [all_parts(): return lax.all_gather(mine, 'fsdp', axis=0, tiled=True)]
    psum x1 -> x0, blocking collectives: 41.9 us -> none  [shards(): lax.psum(small, ('blk', 'fsdp'))]
    concatenate x31 -> x16, other arithmetic: 39.3 us -> 7.65 us  [the longest x8 4.32 us: gather_rows(): sent.append(one[0] if len(one) == 1 else jnp.concatenate(one, axis=0))]
    ppermute x51 -> x54, waiting for transfers between devices: 144 us -> 172 us  [exchange(): return lax.ppermute(block, 'blk', [(i, i ^ bit) for i in range(n)])]
    reduce_scatter x0 -> x4, waiting for transfers between devices: none -> 17.4 us  [sum_of_parts(): return lax.psum_scatter(part, 'fsdp', scatter_dimension=0, tiled=True)]
  transfers between devices with their start and end apart: 54 -> 64, of which waited for: 20 -> 42; matrix products, arithmetic and copies ran while one was open for 34% -> 11% of each run, Pallas kernels for 6% -> 20%
where the time goes in v2:
time: 603 us; the launch traced here: 593 us
  waiting for transfers between devices  253 us (42%)
  Pallas kernels  152 us (25%)
  local copies, waits for them, and re-layouts  81.5 us (14%)
  starting transfers between devices  47.8 us (8%)
  other arithmetic  42.6 us (7%)
  between operations  15.9 us (3%)
    ppermute x54, waiting for transfers between devices, exchange(): return lax.ppermute(block, 'blk', [(i, i ^ bit) for i in range(n)])  172 us
    pallas_call x29, Pallas kernels, call(): pl.pallas_call(kernel, out_shape=out_shape, compiler_params=pltpu.Compile...  108 us
    unnamed x257, local copies, waits for them, and re-layouts  68.1 us
    all_gather x4, waiting for transfers between devices, all_parts(): return lax.all_gather(mine, 'fsdp', axis=0, tiled=True)  59.1 us
    ppermute x54, starting transfers between devices, exchange(): return lax.ppermute(block, 'blk', [(i, i ^ bit) for i in range(n)])  45.8 us
    pallas_call x1, Pallas kernels, attend_back(): pl.pallas_call(functools.partial(attend_back_kernel, span), grid_spec=plt...  27.7 us
    reduce_scatter x4, waiting for transfers between devices, sum_of_parts(): return lax.psum_scatter(part, 'fsdp', scatter_dimension=0, tiled=True)  17.4 us
    pallas_call x1, Pallas kernels, attend(): pl.pallas_call(functools.partial(attend_kernel, span), grid_spec=pltpu.Pr...  16 us
  transfers between devices with their start and end apart: 64, of which 42 were waited for; matrix products, arithmetic and copies ran while one was open for 11% of the time, Pallas kernels for 20%

profile of v2, /device:TPU:0, one launch (start us, length us, event | category | flops | bytes accessed | tf_op | source)
XLA Modules:
  0.0 592.6 jit_solution(13276706014926721849)
XLA Ops:
  9.9 3.0 collective-permute-start
  24.5 2.1 enter.1
  28.3 1.9 collective-permute-start.4
  36.3 4.8 collective-permute-done.5
  43.8 2.3 collective-permute-done.6
  49.1 7.7 %projections.1 = (bf16[512,2048]{1,0:T(8,128)(2,1)S(1)}, f32[512,512]{1,0:T(8,128)S(1)}, f32[512,256]{1,0:T(8,128)S(1)}, bf16[512,512]{1,0:T(8,128)(2,1)S(1)}, b...) custom-call(bf16[512,2048]{1,0:T(8,128)(2,1)S(1)} %copy-done.48, f32[1,2048]{1,0:T(1,128)S(1)} %bitcast.24, ...), custom_call_target="tpu_custom_call" | custom-call | tf_op jit(solution)/shard_map/projections/pallas_call | solution.py:157
  60.1 5.2 collective-permute-done.9
  68.9 10.7 %collective-permute-done.11 = bf16[1024,256]{1,0:T(8,128)(2,1)S(1)} collective-permute-done((bf16[1024,256]{1,0:T(8,128)(2,1)S(1)}, bf16[1024,256]{1,0:T(8,128)(2,1)S(1)}, u32[]{:S(2)}, u32[]{:S(2)}) %collective-permute-start.11) | collective-permute-done | bytes 524320 | tf_op jit(solution)/shard_map/ppermute | solution.py:36
  82.8 12.8 %collective-permute-done.15 = bf16[256,1024]{1,0:T(8,128)(2,1)S(1)} collective-permute-done((bf16[256,1024]{1,0:T(8,128)(2,1)S(1)}, bf16[256,1024]{1,0:T(8,128)(2,1)S(1)}, u32[]{:S(2)}, u32[]{:S(2)}) %collective-permute-start.15) | collective-permute-done | bytes 524320 | tf_op jit(solution)/shard_map/ppermute | solution.py:36
  98.7 16.0 %attend.1 = (bf16[512,512]{1,0:T(8,128)(2,1)S(1)}, f32[2,2,512]{2,1,0:T(2,128)S(1)}) custom-call(s32[18]{0:T(128)S(1)} %pad_add_fusion.sc, bf16[512,512]{1,0:T(8,128)(2,1)S(1)} %get-tuple-element.142.q_ref, bf16[2048,256]{1,0:T(8,128)(2,1)S(1)} %constant_dynamic-update-slice_fusion.5.k0, bf16[2048,256]{1,0:T(8,128)(2,1)S(1)} %collective-permute-done.13.k1, ...), custom_call_target="tpu_custom_call" | custom-call | flops 8589934592 | bytes 4194304 | tf_op jit(solution)/shard_map/attend/pallas_call | solution.py:687
  114.7 6.0 %collective-permute-done.17 = bf16[512,1024]{1,0:T(8,128)(2,1)S(1)} collective-permute-done((bf16[512,1024]{1,0:T(8,128)(2,1)S(1)}, bf16[512,1024]{1,0:T(8,128)(2,1)S(1)}, u32[]{:S(2)}, u32[]{:S(2)}) %collective-permute-start.17) | collective-permute-done | bytes 1048608 | tf_op jit(solution)/shard_map/ppermute | solution.py:36
  121.9 4.2 collective-permute-done.19.refs_2_.refs_1_.refs_4_
  126.1 3.2 attention_out.1
  137.4 16.6 %collective-permute-done.20 = bf16[256,1536]{1,0:T(8,128)(2,1)S(1)} collective-permute-done((bf16[256,1536]{1,0:T(8,128)(2,1)S(1)}, bf16[256,1536]{1,0:T(8,128)(2,1)S(1)}, u32[]{:S(2)}, u32[]{:S(2)}) %collective-permute-start.20) | collective-permute-done | bytes 786464 | tf_op jit(solution)/shard_map/ppermute | solution.py:36
  161.2 2.3 constant_dynamic-update-slice_fusion.10
  164.5 29.2 %collective-permute-done.22 = bf16[512,1536]{1,0:T(8,128)(2,1)} collective-permute-done((bf16[512,1536]{1,0:T(8,128)(2,1)}, bf16[512,1536]{1,0:T(8,128)(2,1)}, u32[]{:S(2)}, u32[]{:S(2)}) %collective-permute-start.22) | collective-permute-done | bytes 1572896 | tf_op jit(solution)/shard_map/ppermute | solution.py:36
  194.9 2.7 constant_dynamic-update-slice_fusion.8.wg0.refs_2_
  205.6 5.1 collective-permute-done.26.refs_3_.refs_6_.refs_8_
  210.8 5.5 grad_act.1.grad_ref
  217.4 31.7 %all-gather.5.cloned.1.call-done.post_ref.refs_0_ = bf16[512,2048]{1,0:T(8,128)(2,1)} async-done(((bf16[128,2048]{1,0:T(8,128)(2,1)}), bf16[512,2048]{1,0:T(8,128)(2,1)}) %all-gather.5.cloned.1.call-update) | async-done | bytes 2097168 | tf_op jit(solution)/shard_map/all_gather | solution.py:755
  252.1 10.5 %hidden_units.1 = (bf16[512,1536]{1,0:T(8,128)(2,1)S(1)}, bf16[512,1536]{1,0:T(8,128)(2,1)S(1)}, bf16[512,1536]{1,0:T(8,128)(2,1)S(1)}) custom-call(bf16[512,2048]{1,0:T(8,128)(2,1)S(1)} %copy-done.8, bf16[1024,1536]{1,0:T(8,128)(2,1)} %constant_dynamic-update-slice_fusion.8.wg0.refs_2_, bf16[1024,1536]{1,0:T(8,128)(2,1)} %collective-permute-done.24.wg1.refs_3_, ...), custom_call_target="tpu_custom_call" | custom-call | tf_op jit(solution)/shard_map/hidden_units/pallas_call | solution.py:157
  262.6 11.4 %grad_post.1 = bf16[512,2048]{1,0:T(8,128)(2,1)S(1)} custom-call(bf16[512,1536]{1,0:T(8,128)(2,1)S(1)} %get-tuple-element.175.refs_0_.refs_1_, bf16[512,1536]{1,0:T(8,128)(2,1)S(1)} %get-tuple-element.177.refs_1_, bf16[1024,1536]{1,0:T(8,128)(2,1)} %constant_dynamic-update-slice_fusion.8.wg0.refs_2_, bf16[1024,1536]{1,0:T(8,128)(2,1)} %collective-permute-done.24.wg1.refs_3_, ...), custom_call_target="tpu_custom_call" | custom-call | tf_op jit(solution)/shard_map/grad_post/pallas_call | solution.py:157
  279.6 2.6 gate_grad_away.1
  282.3 2.6 up_grad_away.1
  285.4 2.5 collective-permute-done.27.refs_2_
  287.9 4.3 gate_grad.1
  292.4 4.3 up_grad.1
  301.9 17.3 %reduce-scatter.7.cloned.1.call-done.grad_ref = bf16[128,2048]{1,0:T(8,128)(2,1)} async-done(((bf16[512,2048]{1,0:T(8,128)(2,1)}), bf16[128,2048]{1,0:T(8,128)(2,1)}) %reduce-scatter.7.cloned.1.call-update) | async-done | bytes 524304 | tf_op jit(solution)/shard_map/reduce_scatter | solution.py:751
  325.2 9.5 %collective-permute-done.29 = bf16[512,1536]{1,0:T(8,128)(2,1)} collective-permute-done((bf16[512,1536]{1,0:T(8,128)(2,1)}, bf16[512,1536]{1,0:T(8,128)(2,1)}, u32[]{:S(2)}, u32[]{:S(2)}) %collective-permute-start.29) | collective-permute-done | bytes 1572896 | tf_op jit(solution)/shard_map/ppermute | solution.py:36
  335.9 2.6 add_convert_fusion.3
  338.5 2.4 add_convert_fusion.2
  346.1 6.1 %units_out.1 = bf16[512,2048]{1,0:T(8,128)(2,1)S(1)} custom-call(bf16[512,1536]{1,0:T(8,128)(2,1)S(1)} %get-tuple-element.173.refs_0_.refs_1_.refs_2_, bf16[512,1536]{1,0:T(8,128)(2,1)S(1)} %get-tuple-element.173.refs_0_.refs_1_.refs_2_, bf16[512,1536]{1,0:T(8,128)(2,1)S(1)} %get-tuple-element.173.refs_0_.refs_1_.refs_2_, bf16[1024,1024]{1,0:T(8,128)(2,1)S(1)} %copy-done.6, ...), custom_call_target="tpu_custom_call" | custom-call | tf_op jit(solution)/shard_map/units_out/pallas_call | solution.py:157
  353.5 6.0 %collective-permute-done.31 = bf16[256,1536]{1,0:T(8,128)(2,1)S(1)} collective-permute-done((bf16[256,1536]{1,0:T(8,128)(2,1)}, bf16[256,1536]{1,0:T(8,128)(2,1)S(1)}, u32[]{:S(2)}, u32[]{:S(2)}) %collective-permute-start.31) | collective-permute-done | bytes 786464 | tf_op jit(solution)/shard_map/ppermute | solution.py:36
  360.7 9.8 %all-gather.7.cloned.1.call-done.left_ref.refs_1_ = bf16[512,2048]{1,0:T(8,128)(2,1)} async-done(((bf16[128,2048]{1,0:T(8,128)(2,1)}), bf16[512,2048]{1,0:T(8,128)(2,1)}) %all-gather.7.cloned.1.call-update) | async-done | bytes 2097168 | tf_op jit(solution)/shard_map/all_gather | solution.py:755
  378.2 27.7 %attend_back.1 = (f32[512,512]{1,0:T(8,128)S(1)}, bf16[2048,256]{1,0:T(8,128)(2,1)S(1)}, bf16[2048,256]{1,0:T(8,128)(2,1)S(1)}, bf16[2048,256]{1,0:T(8,128)(2,1)S(1)}, bf16[2048,256]{1,0:T(8,128)(2,1)S(1)}) custom-call(s32[18]{0:T(128)S(1)} %pad_add_fusion.sc, bf16[512,512]{1,0:T(8,128)(2,1)S(1)} %copy-done.89, bf16[512,512]{1,0:T(8,128)(2,1)S(1)} %grad_context.1.do_ref, ...), custom_call_target="tpu_custom_call" | custom-call | flops 21474836480 | bytes 8388608 | tf_op jit(solution)/shard_map/attend_back/pallas_call | solution.py:725
  406.6 2.1 collective-permute-done.33
  413.6 11.0 %collective-permute-done.35 = bf16[1024,256]{1,0:T(8,128)(2,1)S(1)} collective-permute-done((bf16[1024,256]{1,0:T(8,128)(2,1)S(1)}, bf16[1024,256]{1,0:T(8,128)(2,1)S(1)}, u32[]{:S(2)}, u32[]{:S(2)}) %collective-permute-start.35) | collective-permute-done | bytes 524320 | tf_op jit(solution)/shard_map/ppermute | solution.py:36
  429.3 4.0 collective-permute-done.37.refs_1_
  435.2 6.8 %grad_normed.1 = bf16[512,2048]{1,0:T(8,128)(2,1)S(1)} custom-call(bf16[512,512]{1,0:T(8,128)(2,1)S(1)} %get-tuple-element.205.refs_0_.refs_2_, bf16[512,512]{1,0:T(8,128)(2,1)S(1)} %get-tuple-element.213.refs_1_.refs_2_, bf16[1024,512]{1,0:T(8,128)(2,1)} %constant_dynamic-update-slice_fusion.2.wq0.refs_2_, ...), custom_call_target="tpu_custom_call" | custom-call | tf_op jit(solution)/shard_map/grad_normed/pallas_call | solution.py:157
  445.8 1.9 down_a_away.1
  447.8 1.9 down_b_away.1
  451.2 3.5 down_a.1
  455.6 3.5 down_b.1
  465.3 3.0 query_grad_away.1
  468.3 3.1 key_value_grad_away.1
  471.9 8.1 %collective-permute-done.52 = bf16[512,768]{1,0:T(8,128)(2,1)} collective-permute-done((bf16[512,768]{1,0:T(8,128)(2,1)}, bf16[512,768]{1,0:T(8,128)(2,1)}, u32[]{:S(2)}, u32[]{:S(2)}) %collective-permute-start.52) | collective-permute-done | bytes 786464 | tf_op jit(solution)/shard_map/ppermute | solution.py:36
  480.3 1.8 add_convert_fusion.10
  482.1 1.8 add_convert_fusion.9
  486.0 8.3 %collective-permute-done.54 = bf16[256,768]{1,0:T(8,128)(2,1)} collective-permute-done((bf16[256,768]{1,0:T(8,128)(2,1)}, bf16[256,768]{1,0:T(8,128)(2,1)}, u32[]{:S(2)}, u32[]{:S(2)}) %collective-permute-start.54) | collective-permute-done | bytes 393248 | tf_op jit(solution)/shard_map/ppermute | solution.py:36
  497.3 5.1 query_grad.1
  502.4 5.2 key_value_grad.1
  511.3 2.2 convert_add_fusion.2
  513.5 2.2 convert_add_fusion.3
  515.9 3.3 multiply_reduce_fusion.1
  519.8 6.4 %collective-permute-done.41 = bf16[512,768]{1,0:T(8,128)(2,1)} collective-permute-done((bf16[512,768]{1,0:T(8,128)(2,1)}, bf16[512,768]{1,0:T(8,128)(2,1)}, u32[]{:S(2)}, u32[]{:S(2)}) %collective-permute-start.41) | collective-permute-done | bytes 786464 | tf_op jit(solution)/shard_map/ppermute | solution.py:36
  527.2 1.8 add_convert_fusion.14
  529.1 2.0 add_convert_fusion.13
  537.0 3.2 multiply_reduce_fusion
  541.0 2.9 collective-permute-done.47
  545.3 2.0 multiply_reduce_fusion.4
  555.4 2.5 collective-permute-done.49
  560.8 2.4 layer_out.1
  563.2 17.5 %all-gather.11.cloned.1.call-done.refs_0_ = bf16[512,2048]{1,0:T(8,128)(2,1)} async-done(((bf16[128,2048]{1,0:T(8,128)(2,1)}), bf16[512,2048]{1,0:T(8,128)(2,1)}) %all-gather.11.cloned.1.call-update) | async-done | bytes 2097168 | tf_op jit(solution)/shard_map/all_gather | solution.py:755
  582.3 3.0 tokens_grad.1
  (455 shorter events, 161.5 us)
Async XLA Ops:
  7.2 194.3 %reduce-scatter.5.cloned.1.call-start = ((), (), s32[]{:S(2)}) async-start(), calls=%async_computation.4 | async-start | bytes 2621440 | tf_op jit(solution)/shard_map/reduce_scatter | solution.py:751
  9.9 16.8 %collective-permute-start = (bf16[256,512]{1,0:T(8,128)(2,1)}, bf16[256,512]{1,0:T(8,128)(2,1)}, u32[]{:S(2)}, u32[]{:S(2)}) collective-permute-start(bf16[256,512]{1,0:T(8,128)(2,1)} %param.24), channel_id=1, source_target_pairs={{0,8},{4,12},{8,0},{12,4},{16,24},{20,28},{24,16},{28,20},{1,9},{5... | collective-permute-start | bytes 786440 | tf_op jit(solution)/shard_map/ppermute | solution.py:36
  12.9 13.8 %collective-permute-start.1 = (bf16[256,512]{1,0:T(8,128)(2,1)S(1)}, bf16[256,512]{1,0:T(8,128)(2,1)}, u32[]{:S(2)}, u32[]{:S(2)}) collective-permute-start(bf16[256,512]{1,0:T(8,128)(2,1)S(1)} %constant_dynamic-update-slice_fusion), channel_id=1, source_target_pairs={{0,16},{4,20},{8,24},{12,28},{16,0},{20,4},{24,8},{28,12},{1,17},{... | collective-permute-start | bytes 786440 | tf_op jit(solution)/shard_map/ppermute | solution.py:36
  14.4 12.2 %collective-permute-start.2 = (bf16[1,544]{1,0:T(2,128)(2,1)S(1)}, bf16[1,544]{1,0:T(2,128)(2,1)S(1)}, u32[]{:S(2)}, u32[]{:S(2)}) collective-permute-start(bf16[1,544]{1,0:T(2,128)(2,1)S(1)} %reshape.140), channel_id=1, source_target_pairs={{0,8},{4,12},{8,0},{12,4},{16,24},{20,28},{24,16},{28,20},{1,9},{5... | collective-permute-start | bytes 3272 | tf_op jit(solution)/shard_map/ppermute | solution.py:36
  28.2 12.9 %collective-permute-start.3 = (bf16[512,512]{1,0:T(8,128)(2,1)S(1)}, bf16[512,512]{1,0:T(8,128)(2,1)S(1)}, u32[]{:S(2)}, u32[]{:S(2)}) collective-permute-start(bf16[512,512]{1,0:T(8,128)(2,1)S(1)} %get-tuple-element.136), channel_id=1, source_target_pairs={{0,16},{4,20},{8,24},{12,28},{16,0},{20,4},{24,8},{28,12},{1,17},{... | collective-permute-start | bytes 1572872 | tf_op jit(solution)/shard_map/ppermute | solution.py:36
  28.3 12.8 %collective-permute-start.4 = (bf16[512,512]{1,0:T(8,128)(2,1)S(1)}, bf16[512,512]{1,0:T(8,128)(2,1)S(1)}, u32[]{:S(2)}, u32[]{:S(2)}) collective-permute-start(bf16[512,512]{1,0:T(8,128)(2,1)S(1)} %get-tuple-element.137), channel_id=1, source_target_pairs={{0,8},{4,12},{8,0},{12,4},{16,24},{20,28},{24,16},{28,20},{1,9},{5... | collective-permute-start | bytes 1572872 | tf_op jit(solution)/shard_map/ppermute | solution.py:36
  33.1 8.0 %collective-permute-start.5 = (bf16[2,544]{1,0:T(2,128)(2,1)S(1)}, bf16[2,544]{1,0:T(2,128)(2,1)S(1)}, u32[]{:S(2)}, u32[]{:S(2)}) collective-permute-start(bf16[2,544]{1,0:T(2,128)(2,1)S(1)} %pad_maximum_fusion.18), channel_id=1, source_target_pairs={{0,16},{4,20},{8,24},{12,28},{16,0},{20,4},{24,8},{28,12},{1,17},{... | collective-permute-start | bytes 6536 | tf_op jit(solution)/shard_map/ppermute | solution.py:36
  42.0 4.6 collective-permute-start.7
  43.1 3.5 collective-permute-start.8
  43.7 2.5 collective-permute-start.6
  56.8 8.4 %collective-permute-start.9 = (bf16[512,256]{1,0:T(8,128)(2,1)S(1)}, bf16[512,256]{1,0:T(8,128)(2,1)S(1)}, u32[]{:S(2)}, u32[]{:S(2)}) collective-permute-start(bf16[512,256]{1,0:T(8,128)(2,1)S(1)} %get-tuple-element.145), channel_id=1, source_target_pairs={{0,8},{4,12},{8,0},{12,4},{16,24},{20,28},{24,16},{28,20},{1,9},{5... | collective-permute-start | bytes 786440 | tf_op jit(solution)/shard_map/ppermute | solution.py:36
  58.5 8.1 %collective-permute-start.10 = (bf16[512,256]{1,0:T(8,128)(2,1)S(1)}, bf16[512,256]{1,0:T(8,128)(2,1)S(1)}, u32[]{:S(2)}, u32[]{:S(2)}) collective-permute-start(bf16[512,256]{1,0:T(8,128)(2,1)S(1)} %get-tuple-element.146), channel_id=1, source_target_pairs={{0,16},{4,20},{8,24},{12,28},{16,0},{20,4},{24,8},{28,12},{1,17},{... | collective-permute-start | bytes 786440 | tf_op jit(solution)/shard_map/ppermute | solution.py:36
  66.7 12.9 %collective-permute-start.11 = (bf16[1024,256]{1,0:T(8,128)(2,1)S(1)}, bf16[1024,256]{1,0:T(8,128)(2,1)S(1)}, u32[]{:S(2)}, u32[]{:S(2)}) collective-permute-start(bf16[1024,256]{1,0:T(8,128)(2,1)S(1)} %pad_maximum_fusion.12), channel_id=1, source_target_pairs={{0,16},{4,20},{8,24},{12,28},{16,0},{20,4},{24,8},{28,12},{1,17},{... | collective-permute-start | bytes 1572872 | tf_op jit(solution)/shard_map/ppermute | solution.py:36
  68.3 12.5 %collective-permute-start.12 = (bf16[1024,256]{1,0:T(8,128)(2,1)S(1)}, bf16[1024,256]{1,0:T(8,128)(2,1)S(1)}, u32[]{:S(2)}, u32[]{:S(2)}) collective-permute-start(bf16[1024,256]{1,0:T(8,128)(2,1)S(1)} %pad_maximum_fusion.13), channel_id=1, source_target_pairs={{0,8},{4,12},{8,0},{12,4},{16,24},{20,28},{24,16},{28,20},{1,9},{5... | collective-permute-start | bytes 1572872 | tf_op jit(solution)/shard_map/ppermute | solution.py:36
  80.9 17.8 %collective-permute-start.13 = (bf16[2048,256]{1,0:T(8,128)(2,1)S(1)}, bf16[2048,256]{1,0:T(8,128)(2,1)S(1)}, u32[]{:S(2)}, u32[]{:S(2)}) collective-permute-start(bf16[2048,256]{1,0:T(8,128)(2,1)S(1)} %constant_dynamic-update-slice_fusion.5.k0), channel_id=1, source_target_pairs={{0,4},{4,0},{8,12},{12,8},{16,20},{20,16},{24,28},{28,24},{1,5},{5... | collective-permute-start | bytes 3145736 | tf_op jit(solution)/shard_map/ppermute | solution.py:36
  81.1 17.6 %collective-permute-start.14 = (bf16[2048,256]{1,0:T(8,128)(2,1)S(1)}, bf16[2048,256]{1,0:T(8,128)(2,1)S(1)}, u32[]{:S(2)}, u32[]{:S(2)}) collective-permute-start(bf16[2048,256]{1,0:T(8,128)(2,1)S(1)} %pad_maximum_fusion.6.v0), channel_id=1, source_target_pairs={{0,4},{4,0},{8,12},{12,8},{16,20},{20,16},{24,28},{28,24},{1,5},{5... | collective-permute-start | bytes 3145736 | tf_op jit(solution)/shard_map/ppermute | solution.py:36
  81.7 13.9 %collective-permute-start.15 = (bf16[256,1024]{1,0:T(8,128)(2,1)S(1)}, bf16[256,1024]{1,0:T(8,128)(2,1)S(1)}, u32[]{:S(2)}, u32[]{:S(2)}) collective-permute-start(bf16[256,1024]{1,0:T(8,128)(2,1)S(1)} %copy-done.116), channel_id=1, source_target_pairs={{0,8},{4,12},{8,0},{12,4},{16,24},{20,28},{24,16},{28,20},{1,9},{5... | collective-permute-start | bytes 1572872 | tf_op jit(solution)/shard_map/ppermute | solution.py:36
  82.3 13.6 %collective-permute-start.16 = (bf16[256,1024]{1,0:T(8,128)(2,1)S(1)}, bf16[256,1024]{1,0:T(8,128)(2,1)S(1)}, u32[]{:S(2)}, u32[]{:S(2)}) collective-permute-start(bf16[256,1024]{1,0:T(8,128)(2,1)S(1)} %copy-done.93), channel_id=1, source_target_pairs={{0,16},{4,20},{8,24},{12,28},{16,0},{20,4},{24,8},{28,12},{1,17},{... | collective-permute-start | bytes 1572872 | tf_op jit(solution)/shard_map/ppermute | solution.py:36
  96.7 24.0 %collective-permute-start.17 = (bf16[512,1024]{1,0:T(8,128)(2,1)S(1)}, bf16[512,1024]{1,0:T(8,128)(2,1)S(1)}, u32[]{:S(2)}, u32[]{:S(2)}) collective-permute-start(bf16[512,1024]{1,0:T(8,128)(2,1)S(1)} %pad_maximum_fusion.7), channel_id=1, source_target_pairs={{0,16},{4,20},{8,24},{12,28},{16,0},{20,4},{24,8},{28,12},{1,17},{... | collective-permute-start | bytes 3145736 | tf_op jit(solution)/shard_map/ppermute | solution.py:36
  97.3 23.7 %collective-permute-start.18 = (bf16[512,1024]{1,0:T(8,128)(2,1)S(1)}, bf16[512,1024]{1,0:T(8,128)(2,1)S(1)}, u32[]{:S(2)}, u32[]{:S(2)}) collective-permute-start(bf16[512,1024]{1,0:T(8,128)(2,1)S(1)} %pad_maximum_fusion.8), channel_id=1, source_target_pairs={{0,8},{4,12},{8,0},{12,4},{16,24},{20,28},{24,16},{28,20},{1,9},{5... | collective-permute-start | bytes 3145736 | tf_op jit(solution)/shard_map/ppermute | solution.py:36
  121.9 4.2 collective-permute-start.19
  133.3 115.8 %all-gather.5.cloned.1.call-start = ((), (), s32[]{:S(2)}) async-start(), calls=%async_computation.5 | async-start | bytes 2621440 | tf_op jit(solution)/shard_map/all_gather | solution.py:755
  134.4 19.6 %collective-permute-start.20 = (bf16[256,1536]{1,0:T(8,128)(2,1)S(1)}, bf16[256,1536]{1,0:T(8,128)(2,1)S(1)}, u32[]{:S(2)}, u32[]{:S(2)}) collective-permute-start(bf16[256,1536]{1,0:T(8,128)(2,1)S(1)} %copy-done.90), channel_id=1, source_target_pairs={{0,8},{4,12},{8,0},{12,4},{16,24},{20,28},{24,16},{28,20},{1,9},{5... | collective-permute-start | bytes 2359304 | tf_op jit(solution)/shard_map/ppermute | solution.py:36
  135.8 19.5 %collective-permute-start.21 = (bf16[256,1536]{1,0:T(8,128)(2,1)}, bf16[256,1536]{1,0:T(8,128)(2,1)S(1)}, u32[]{:S(2)}, u32[]{:S(2)}) collective-permute-start(bf16[256,1536]{1,0:T(8,128)(2,1)} %param.32), channel_id=1, source_target_pairs={{0,16},{4,20},{8,24},{12,28},{16,0},{20,4},{24,8},{28,12},{1,17},{... | collective-permute-start | bytes 2359304 | tf_op jit(solution)/shard_map/ppermute | solution.py:36
  158.0 35.7 %collective-permute-start.22 = (bf16[512,1536]{1,0:T(8,128)(2,1)}, bf16[512,1536]{1,0:T(8,128)(2,1)}, u32[]{:S(2)}, u32[]{:S(2)}) collective-permute-start(bf16[512,1536]{1,0:T(8,128)(2,1)} %pad_maximum_fusion.3), channel_id=1, source_target_pairs={{0,16},{4,20},{8,24},{12,28},{16,0},{20,4},{24,8},{28,12},{1,17},{... | collective-permute-start | bytes 4718600 | tf_op jit(solution)/shard_map/ppermute | solution.py:36
  159.5 35.4 %collective-permute-start.23 = (bf16[512,1536]{1,0:T(8,128)(2,1)}, bf16[512,1536]{1,0:T(8,128)(2,1)}, u32[]{:S(2)}, u32[]{:S(2)}) collective-permute-start(bf16[512,1536]{1,0:T(8,128)(2,1)} %pad_maximum_fusion.4), channel_id=1, source_target_pairs={{0,8},{4,12},{8,0},{12,4},{16,24},{20,28},{24,16},{28,20},{1,9},{5... | collective-permute-start | bytes 4718600 | tf_op jit(solution)/shard_map/ppermute | solution.py:36
  197.6 19.9 %collective-permute-start.24 = (bf16[1024,1536]{1,0:T(8,128)(2,1)}, bf16[1024,1536]{1,0:T(8,128)(2,1)}, u32[]{:S(2)}, u32[]{:S(2)}) collective-permute-start(bf16[1024,1536]{1,0:T(8,128)(2,1)} %constant_dynamic-update-slice_fusion.8.wg0.refs_2_), channel_id=1, source_target_pairs={{0,4},{4,0},{8,12},{12,8},{16,20},{20,16},{24,28},{28,24},{1,5},{5... | collective-permute-start | bytes 9437192 | tf_op jit(solution)/shard_map/ppermute | solution.py:36
  201.3 16.2 %collective-permute-start.25 = (bf16[1024,1536]{1,0:T(8,128)(2,1)}, bf16[1024,1536]{1,0:T(8,128)(2,1)}, u32[]{:S(2)}, u32[]{:S(2)}) collective-permute-start(bf16[1024,1536]{1,0:T(8,128)(2,1)} %pad_maximum_fusion.wu0.refs_4_), channel_id=1, source_target_pairs={{0,4},{4,0},{8,12},{12,8},{16,20},{20,16},{24,28},{28,24},{1,5},{5... | collective-permute-start | bytes 9437192 | tf_op jit(solution)/shard_map/ppermute | solution.py:36
  203.6 115.6 %reduce-scatter.7.cloned.1.call-start = ((), (), s32[]{:S(2)}) async-start(), calls=%async_computation.6 | async-start | bytes 2621440 | tf_op jit(solution)/shard_map/reduce_scatter | solution.py:751
  205.2 5.5 collective-permute-start.26
  276.5 94.0 %all-gather.7.cloned.1.call-start = ((), (), s32[]{:S(2)}) async-start(), calls=%async_computation.7 | async-start | bytes 2621440 | tf_op jit(solution)/shard_map/all_gather | solution.py:755
  282.2 5.7 collective-permute-start.27
  284.9 7.5 %collective-permute-start.28 = (bf16[1024,1536]{1,0:T(8,128)(2,1)S(1)}, bf16[1024,1536]{1,0:T(8,128)(2,1)S(1)}, u32[]{:S(2)}, u32[]{:S(2)}) collective-permute-start(bf16[1024,1536]{1,0:T(8,128)(2,1)S(1)} %up_grad_away.1), channel_id=1, source_target_pairs={{0,4},{4,0},{8,12},{12,8},{16,20},{20,16},{24,28},{28,24},{1,5},{5... | collective-permute-start | bytes 9437192 | tf_op jit(solution)/shard_map/ppermute | solution.py:36
  297.9 36.8 %collective-permute-start.29 = (bf16[512,1536]{1,0:T(8,128)(2,1)}, bf16[512,1536]{1,0:T(8,128)(2,1)}, u32[]{:S(2)}, u32[]{:S(2)}) collective-permute-start(bf16[512,1536]{1,0:T(8,128)(2,1)} %get-tuple-element.179), channel_id=1, source_target_pairs={{0,8},{4,12},{8,0},{12,4},{16,24},{20,28},{24,16},{28,20},{1,9},{5... | collective-permute-start | bytes 4718600 | tf_op jit(solution)/shard_map/ppermute | solution.py:36
  299.4 36.5 %collective-permute-start.30 = (bf16[512,1536]{1,0:T(8,128)(2,1)}, bf16[512,1536]{1,0:T(8,128)(2,1)}, u32[]{:S(2)}, u32[]{:S(2)}) collective-permute-start(bf16[512,1536]{1,0:T(8,128)(2,1)} %get-tuple-element.180), channel_id=1, source_target_pairs={{0,16},{4,20},{8,24},{12,28},{16,0},{20,4},{24,8},{28,12},{1,17},{... | collective-permute-start | bytes 4718600 | tf_op jit(solution)/shard_map/ppermute | solution.py:36
  325.1 119.0 %reduce-scatter.9.cloned.1.call-start = ((), (), s32[]{:S(2)}) async-start(), calls=%async_computation.8 | async-start | bytes 2621440 | tf_op jit(solution)/shard_map/reduce_scatter | solution.py:751
  340.9 18.6 %collective-permute-start.31 = (bf16[256,1536]{1,0:T(8,128)(2,1)}, bf16[256,1536]{1,0:T(8,128)(2,1)S(1)}, u32[]{:S(2)}, u32[]{:S(2)}) collective-permute-start(bf16[256,1536]{1,0:T(8,128)(2,1)} %add_convert_fusion.3), channel_id=1, source_target_pairs={{0,16},{4,20},{8,24},{12,28},{16,0},{20,4},{24,8},{28,12},{1,17},{... | collective-permute-start | bytes 2359304 | tf_op jit(solution)/shard_map/ppermute | solution.py:36
  342.3 18.4 %collective-permute-start.32 = (bf16[256,1536]{1,0:T(8,128)(2,1)}, bf16[256,1536]{1,0:T(8,128)(2,1)S(1)}, u32[]{:S(2)}, u32[]{:S(2)}) collective-permute-start(bf16[256,1536]{1,0:T(8,128)(2,1)} %add_convert_fusion.2), channel_id=1, source_target_pairs={{0,8},{4,12},{8,0},{12,4},{16,24},{20,28},{24,16},{28,20},{1,9},{5... | collective-permute-start | bytes 2359304 | tf_op jit(solution)/shard_map/ppermute | solution.py:36
  370.6 162.5 %reduce-scatter.11.cloned.1.call-start = ((), (), s32[]{:S(2)}) async-start(), calls=%async_computation.10 | async-start | bytes 2621440 | tf_op jit(solution)/shard_map/reduce_scatter | solution.py:751
  405.9 2.7 collective-permute-start.33
  406.0 4.1 collective-permute-start.34
  410.7 14.0 %collective-permute-start.35 = (bf16[1024,256]{1,0:T(8,128)(2,1)S(1)}, bf16[1024,256]{1,0:T(8,128)(2,1)S(1)}, u32[]{:S(2)}, u32[]{:S(2)}) collective-permute-start(bf16[1024,256]{1,0:T(8,128)(2,1)S(1)} %add_convert_fusion.7), channel_id=1, source_target_pairs={{0,8},{4,12},{8,0},{12,4},{16,24},{20,28},{24,16},{28,20},{1,9},{5... | collective-permute-start | bytes 1572872 | tf_op jit(solution)/shard_map/ppermute | solution.py:36
  412.0 13.7 %collective-permute-start.36 = (bf16[1024,256]{1,0:T(8,128)(2,1)S(1)}, bf16[1024,256]{1,0:T(8,128)(2,1)S(1)}, u32[]{:S(2)}, u32[]{:S(2)}) collective-permute-start(bf16[1024,256]{1,0:T(8,128)(2,1)S(1)} %get-tuple-element.202), channel_id=1, source_target_pairs={{0,16},{4,20},{8,24},{12,28},{16,0},{20,4},{24,8},{28,12},{1,17},{... | collective-permute-start | bytes 1572872 | tf_op jit(solution)/shard_map/ppermute | solution.py:36
  426.0 7.3 %collective-permute-start.37 = (bf16[512,256]{1,0:T(8,128)(2,1)S(1)}, bf16[512,256]{1,0:T(8,128)(2,1)S(1)}, u32[]{:S(2)}, u32[]{:S(2)}) collective-permute-start(bf16[512,256]{1,0:T(8,128)(2,1)S(1)} %get-tuple-element.208), channel_id=1, source_target_pairs={{0,16},{4,20},{8,24},{12,28},{16,0},{20,4},{24,8},{28,12},{1,17},{... | collective-permute-start | bytes 786440 | tf_op jit(solution)/shard_map/ppermute | solution.py:36
  427.5 6.9 %collective-permute-start.38 = (bf16[512,256]{1,0:T(8,128)(2,1)S(1)}, bf16[512,256]{1,0:T(8,128)(2,1)S(1)}, u32[]{:S(2)}, u32[]{:S(2)}) collective-permute-start(bf16[512,256]{1,0:T(8,128)(2,1)S(1)} %get-tuple-element.209), channel_id=1, source_target_pairs={{0,8},{4,12},{8,0},{12,4},{16,24},{20,28},{24,16},{28,20},{1,9},{5... | collective-permute-start | bytes 786440 | tf_op jit(solution)/shard_map/ppermute | solution.py:36
  444.1 115.0 %all-gather.9.cloned.1.call-start = ((), (), s32[]{:S(2)}) async-start(), calls=%async_computation.9 | async-start | bytes 2621440 | tf_op jit(solution)/shard_map/all_gather | solution.py:755
  447.7 3.5 collective-permute-start.50
  449.7 5.9 collective-permute-start.51
  460.1 19.9 %collective-permute-start.52 = (bf16[512,768]{1,0:T(8,128)(2,1)}, bf16[512,768]{1,0:T(8,128)(2,1)}, u32[]{:S(2)}, u32[]{:S(2)}) collective-permute-start(bf16[512,768]{1,0:T(8,128)(2,1)} %get-tuple-element.234), channel_id=1, source_target_pairs={{0,8},{4,12},{8,0},{12,4},{16,24},{20,28},{24,16},{28,20},{1,9},{5... | collective-permute-start | bytes 2359304 | tf_op jit(solution)/shard_map/ppermute | solution.py:36
  460.7 19.6 %collective-permute-start.53 = (bf16[512,768]{1,0:T(8,128)(2,1)}, bf16[512,768]{1,0:T(8,128)(2,1)}, u32[]{:S(2)}, u32[]{:S(2)}) collective-permute-start(bf16[512,768]{1,0:T(8,128)(2,1)} %get-tuple-element.235), channel_id=1, source_target_pairs={{0,16},{4,20},{8,24},{12,28},{16,0},{20,4},{24,8},{28,12},{1,17},{... | collective-permute-start | bytes 2359304 | tf_op jit(solution)/shard_map/ppermute | solution.py:36
  462.3 118.4 %all-gather.11.cloned.1.call-start = ((), (), s32[]{:S(2)}) async-start(), calls=%async_computation.11 | async-start | bytes 2621440 | tf_op jit(solution)/shard_map/all_gather | solution.py:755
  468.3 26.3 %collective-permute-start.39 = (bf16[1024,768]{1,0:T(8,128)(2,1)}, bf16[1024,768]{1,0:T(8,128)(2,1)}, u32[]{:S(2)}, u32[]{:S(2)}) collective-permute-start(bf16[1024,768]{1,0:T(8,128)(2,1)} %query_grad_away.1), channel_id=1, source_target_pairs={{0,4},{4,0},{8,12},{12,8},{16,20},{20,16},{24,28},{28,24},{1,5},{5... | collective-permute-start | bytes 4718600 | tf_op jit(solution)/shard_map/ppermute | solution.py:36
  471.4 31.0 %collective-permute-start.40 = (bf16[1024,768]{1,0:T(8,128)(2,1)}, bf16[1024,768]{1,0:T(8,128)(2,1)}, u32[]{:S(2)}, u32[]{:S(2)}) collective-permute-start(bf16[1024,768]{1,0:T(8,128)(2,1)} %key_value_grad_away.1), channel_id=1, source_target_pairs={{0,4},{4,0},{8,12},{12,8},{16,20},{20,16},{24,28},{28,24},{1,5},{5... | collective-permute-start | bytes 4718600 | tf_op jit(solution)/shard_map/ppermute | solution.py:36
  484.0 10.3 %collective-permute-start.54 = (bf16[256,768]{1,0:T(8,128)(2,1)}, bf16[256,768]{1,0:T(8,128)(2,1)}, u32[]{:S(2)}, u32[]{:S(2)}) collective-permute-start(bf16[256,768]{1,0:T(8,128)(2,1)} %add_convert_fusion.10), channel_id=1, source_target_pairs={{0,16},{4,20},{8,24},{12,28},{16,0},{20,4},{24,8},{28,12},{1,17},{... | collective-permute-start | bytes 1179656 | tf_op jit(solution)/shard_map/ppermute | solution.py:36
  484.6 10.0 %collective-permute-start.55 = (bf16[256,768]{1,0:T(8,128)(2,1)}, bf16[256,768]{1,0:T(8,128)(2,1)}, u32[]{:S(2)}, u32[]{:S(2)}) collective-permute-start(bf16[256,768]{1,0:T(8,128)(2,1)} %add_convert_fusion.9), channel_id=1, source_target_pairs={{0,8},{4,12},{8,0},{12,4},{16,24},{20,28},{24,16},{28,20},{1,9},{5... | collective-permute-start | bytes 1179656 | tf_op jit(solution)/shard_map/ppermute | solution.py:36
  508.4 17.8 %collective-permute-start.41 = (bf16[512,768]{1,0:T(8,128)(2,1)}, bf16[512,768]{1,0:T(8,128)(2,1)}, u32[]{:S(2)}, u32[]{:S(2)}) collective-permute-start(bf16[512,768]{1,0:T(8,128)(2,1)} %get-tuple-element.220), channel_id=1, source_target_pairs={{0,8},{4,12},{8,0},{12,4},{16,24},{20,28},{24,16},{28,20},{1,9},{5... | collective-permute-start | bytes 2359304 | tf_op jit(solution)/shard_map/ppermute | solution.py:36
  509.9 17.3 %collective-permute-start.42 = (bf16[512,768]{1,0:T(8,128)(2,1)}, bf16[512,768]{1,0:T(8,128)(2,1)}, u32[]{:S(2)}, u32[]{:S(2)}) collective-permute-start(bf16[512,768]{1,0:T(8,128)(2,1)} %get-tuple-element.221), channel_id=1, source_target_pairs={{0,16},{4,20},{8,24},{12,28},{16,0},{20,4},{24,8},{28,12},{1,17},{... | collective-permute-start | bytes 2359304 | tf_op jit(solution)/shard_map/ppermute | solution.py:36
  515.8 3.4 collective-permute-start.45
  519.2 21.1 %collective-permute-start.46 = (f32[1,256]{1,0:T(1,128)S(1)}, f32[1,256]{1,0:T(1,128)S(1)}, u32[]{:S(2)}, u32[]{:S(2)}) collective-permute-start(f32[1,256]{1,0:T(1,128)S(1)} %add.163), channel_id=1, source_target_pairs={{0,8},{4,12},{8,0},{12,4},{16,24},{20,28},{24,16},{28,20},{1,9},{5... | collective-permute-start | bytes 3080 | tf_op jit(solution)/shard_map/ppermute | solution.py:36
  531.0 13.0 %collective-permute-start.43 = (bf16[256,768]{1,0:T(8,128)(2,1)}, bf16[256,768]{1,0:T(8,128)(2,1)}, u32[]{:S(2)}, u32[]{:S(2)}) collective-permute-start(bf16[256,768]{1,0:T(8,128)(2,1)} %add_convert_fusion.14), channel_id=1, source_target_pairs={{0,16},{4,20},{8,24},{12,28},{16,0},{20,4},{24,8},{28,12},{1,17},{... | collective-permute-start | bytes 1179656 | tf_op jit(solution)/shard_map/ppermute | solution.py:36
  532.5 11.6 %collective-permute-start.44 = (bf16[256,768]{1,0:T(8,128)(2,1)}, bf16[256,768]{1,0:T(8,128)(2,1)}, u32[]{:S(2)}, u32[]{:S(2)}) collective-permute-start(bf16[256,768]{1,0:T(8,128)(2,1)} %add_convert_fusion.13), channel_id=1, source_target_pairs={{0,8},{4,12},{8,0},{12,4},{16,24},{20,28},{24,16},{28,20},{1,9},{5... | collective-permute-start | bytes 1179656 | tf_op jit(solution)/shard_map/ppermute | solution.py:36
  540.2 3.6 collective-permute-start.47
  549.8 3.6 collective-permute-start.48
  553.4 4.6 collective-permute-start.49
  (122 other events, 954.4 us)
Sparse Core Ops, SparseCore 0:
  133.4 45.0 reduce-scatter.4
  203.8 45.3 all-gather.4
  276.7 42.5 reduce-scatter.6
  325.2 45.2 all-gather.6
  373.2 42.5 reduce-scatter.8
  444.3 40.8 reduce-scatter.10
  486.7 45.2 all-gather.8
  537.1 43.6 all-gather.10

commit v3 on v2

--- a/solution.py
+++ b/solution.py
@@ -44,33 +44,44 @@
     return lax.optimization_barrier((value,) + others)[0]
 
 
-def gather_rows(pieces, orders, before=(), beside=(), closing=()):
-    count = len(pieces)
-    held = [{0: piece} for piece in pieces]
-    gots = []
-    for step in range(len(orders[0])):
-        sent = []
-        for have in held:
-            one = [have[m] for m in sorted(have)]
-            sent.append(one[0] if len(one) == 1 else jnp.concatenate(one, axis=0))
-        sent = together(sent, before[step] if step < len(before) else ())
-        got = [exchange(x, order[step]) for x, order in zip(sent, orders)]
-        gots.append(got)
-        last = step == len(orders[0]) - 1
-        got = together(got, (beside[step] if step < len(beside) else ()) + (tuple(closing) if last else ()))
-        for have, brought, order in zip(held, got, orders):
-            rows = have[0].shape[0]
-            for i, m in enumerate(sorted(have)):
-                have[m | order[step]] = brought[i * rows : (i + 1) * rows]
+def gather_step(held, orders, step, before=(), beside=()):
+    sent = []
+    for have in held:
+        one = [have[m] for m in sorted(have)]
+        sent.append(one[0] if len(one) == 1 else jnp.concatenate(one, axis=0))
+    sent = together(sent, before)
+    raw = [exchange(x, order[step]) for x, order in zip(sent, orders)]
+    got = together(raw, beside)
+    for have, brought, order in zip(held, got, orders):
+        rows = have[0].shape[0]
+        for i, m in enumerate(sorted(have)):
+            have[m | order[step]] = brought[i * rows : (i + 1) * rows]
+    return tuple(raw)
+
+
+def gather_end(held):
     own = [jnp.concatenate([have[m] for m in sorted(have)], axis=0) for have in held]
-    return [(x, exchange(x, 1)) for x in own], gots
+    return [(x, exchange(x, 1)) for x in own]
+
+
+def gather_rest(held, orders, start, before=(), beside=()):
+    raw = ()
+    for step in range(start, len(orders[0])):
+        raw = gather_step(
+            held,
+            orders,
+            step,
+            before if step == start else (),
+            beside if step == len(orders[0]) - 1 else (),
+        )
+    return raw
 
 
 def add_low(a, b):
     return (a.astype(F32) + b.astype(F32)).astype(BF16)
 
 
-def scatter_terms(parts, orders):
+def scatter_terms(parts, orders, beside=()):
     held = []
     sent = [part[0] for part in parts]
     for (leave, stay), order in zip(parts, orders):
@@ -88,8 +99,9 @@
                     have[m] = add_low(*have[m])
         sent = together(sent)
         sends.append(sent)
-        got = together([exchange(x, order[step]) for x, order in zip(sent, orders)])
-        gots.append(got)
+        raw = [exchange(x, order[step]) for x, order in zip(sent, orders)]
+        gots.append(tuple(raw))
+        got = together(raw, beside[step] if step < len(beside) else ())
         for have, back in zip(held, got):
             rows = back.shape[0] // len(have)
             for i, m in enumerate(sorted(have)):
@@ -97,8 +109,8 @@
     return [have[0] for have in held], sends, gots
 
 
-def scatter_sums(parts, orders):
-    terms, sends, gots = scatter_terms(parts, orders)
+def scatter_sums(parts, orders, beside=()):
+    terms, sends, gots = scatter_terms(parts, orders, beside)
     return [a.astype(F32) + b.astype(F32) for a, b in terms], sends, gots
 
 
@@ -140,7 +152,7 @@
     return pltpu.roll(values, HD // 2, 1)
 
 
-def call(kernel, name, grid, in_specs, out_specs, out_shape, args, flops, scratch=(), scalars=None):
+def call(kernel, name, grid, in_specs, out_specs, out_shape, args, flops, scratch=(), scalars=None, near=False):
     if scalars is None:
         spec = {"grid": grid, "in_specs": in_specs, "out_specs": out_specs, "scratch_shapes": scratch}
     else:
@@ -153,7 +165,11 @@
                 scratch_shapes=scratch,
             )
         }
-        args = (scalars,) + tuple(args)
+    if not near:
+        args = in_far(*args)
+        out_shape = [pltpu.HBM(o.shape, o.dtype) for o in out_shape]
+    if scalars is not None:
+        args = (scalars, *args)
     return pl.pallas_call(
         kernel,
         out_shape=out_shape,
@@ -162,6 +178,14 @@
         name=name,
         **spec,
     )(*args)
+
+
+def in_far(*arrays):
+    big = 1 << 17
+    return [
+        pltpu.with_memory_space_constraint(a, pltpu.HBM) if a.size * a.dtype.itemsize >= big else a
+        for a in arrays
+    ]
 
 
 def shape(dims_, dtype):
@@ -199,12 +223,13 @@
         (first, second),
         0,
         scalars=order,
+        near=True,
     )
 
 
 def leave_blocks(sc, out_ref, result):
     width = result.shape[1]
-    n = sc.shape[0]
+    n = len(sc)
     block = width // n
     if block % 128:
         out_ref[...] = result.astype(out_ref.dtype)
@@ -214,19 +239,25 @@
         out_ref[:, at] = result[:, p * block : (p + 1) * block].astype(out_ref.dtype)
 
 
-def leave_kernel(sc, *refs):
-    count = len(refs) // 2
-    for value_ref, out_ref in zip(refs[:count], refs[count:]):
-        leave_blocks(sc, out_ref, value_ref[...])
-
-
-def leave(name, order, value, dtype):
+def leave_kernel(n, sc, value_ref, out_ref):
+    leave_blocks([sc[p] for p in range(n)], out_ref, value_ref[...])
+
+
+def leave(name, order, value, places, dtype):
     rows, width = value.shape
     n = order.shape[0]
-    height = rows // 4
-    spec = pl.BlockSpec((height, width), lambda i, sc: (i, 0))
+    parts = places.shape[0]
+    height = rows // parts
     result = call(
-        leave_kernel, name, (4,), [spec], [spec], [shape((rows, width), dtype)], (value,), 0, scalars=order
+        functools.partial(leave_kernel, n),
+        name,
+        (parts,),
+        [pl.BlockSpec((height, width), lambda i, sc: (sc[n + i], 0))],
+        [pl.BlockSpec((height, width), lambda i, sc: (i, 0))],
+        [shape((rows, width), dtype)],
+        (value,),
+        0,
+        scalars=jnp.concatenate([order, places.astype(jnp.int32)]),
     )[0]
     if width // n % 128:
         index = jnp.arange(n)
@@ -707,7 +738,7 @@
             flops=4 * flops, bytes_accessed=16 * half * HD, transcendentals=rows * half
         ),
         name="attend",
-    )(scalars, queries, *keys, *values)
+    )(scalars, queries, *in_far(*keys, *values))
 
 
 def attend_back(scalars, queries, grad_context, context, lse, keys, values, span):
@@ -721,7 +752,7 @@
     read = pl.BlockSpec((half, HD), lambda h, sc: (0, h), pipeline_mode=slots)
     stacked = across // HD * span
     flops = 10 * rows * half * width
-    grads = jax.ShapeDtypeStruct(keys[0].shape, BF16)
+    grads = pltpu.HBM(keys[0].shape, BF16)
     return pl.pallas_call(
         functools.partial(attend_back_kernel, span),
         grid_spec=pltpu.PrefetchScalarGridSpec(
@@ -738,13 +769,13 @@
                 pltpu.VMEM((stacked, HD), F32),
             ],
         ),
-        out_shape=[jax.ShapeDtypeStruct((rows, width), F32)] + [grads] * 4,
+        out_shape=[pltpu.HBM((rows, width), F32)] + [grads] * 4,
         compiler_params=pltpu.CompilerParams(vmem_limit_bytes=min(60 * MIB, 16 * MIB + 44 * HD * half)),
         cost_estimate=pl.CostEstimate(
             flops=4 * flops, bytes_accessed=32 * half * HD, transcendentals=rows * half
         ),
         name="attend_back",
-    )(scalars, queries, grad_context, context, lse, *keys, *values)
+    )(scalars, *in_far(queries, grad_context, context, lse, *keys, *values))
 
 
 def sum_of_parts(part):
@@ -814,19 +845,17 @@
     def mine(array):
         return lax.dynamic_slice_in_dim(array, my_part, quarter, 0)
 
+    gains = jnp.concatenate([input_gain, post_gain, query_gain, key_gain]).reshape(1, -1)
+    first = [{0: query_weight}, {0: jnp.concatenate([key_weight, value_weight], axis=1)}, {0: gains}]
+    triple = [bits, flipped, bits]
+    out_t = output_weight.T
+    o_half = o_cols // 2
+    gather_step(first, triple, 0, beside=(out_t,))
     tokens, cotangent = enter(order, tokens, cotangent)
     my_tokens = mine(tokens)
     my_cotangent = mine(cotangent)
-    down_t = down_weight.T
-    cut = (units - o_cols) // 2
-    side_a = jnp.concatenate([output_weight.T, down_t[:, :cut]], axis=1)
-    side_b = down_t[:, cut:]
-    gains = jnp.concatenate([input_gain, post_gain, query_gain, key_gain]).reshape(1, -1)
-    (wq, wkv, gains), _ = gather_rows(
-        [query_weight, jnp.concatenate([key_weight, value_weight], axis=1), gains],
-        [bits, flipped, bits],
-        beside=((tokens, cotangent), (side_a, side_b, cosine, sine, scalars)),
-    )
+    late = gather_rest(first, triple, 1, beside=(tokens, cotangent, cosine, sine, scalars))
+    wq, wkv, gains = gather_end(first)
     gains = jnp.concatenate(gains, axis=0).astype(F32)
     gain_input = gains[:, :block].reshape(1, width)
     gain_post = gains[:, block : 2 * block].reshape(1, width)
@@ -839,41 +868,56 @@
     normed_low, q_proj, k_proj, queries, keys, values = projections(
         tokens, gain_input, wq, wkv, cosine, sine, gain_query, gain_key
     )
-    (all_keys, all_values), key_gots = gather_rows([keys, values], pair)
+    outs = [{0: out_t[:, :o_half]}, {0: out_t[:, o_half:]}]
+    out_got = gather_step(outs, pair, 0, before=late)
+    rows_held = [{0: keys}, {0: values}]
+    gather_step(rows_held, pair, 0, before=out_got)
+    gather_rest(outs, pair, 1)
+    key_got = gather_rest(rows_held, pair, 1)
+    all_keys, all_values = gather_end(rows_held)
+    wo_a, wo_b = gather_end(outs)
+    wide = [{0: gate_weight}, {0: up_weight}]
     context, lse = attend(scalars, queries, all_keys, all_values, span)
-
-    (side_a, side_b), _ = gather_rows(
-        [side_a, side_b], pair, before=(tuple(wq[:1]), tuple(key_gots[-1])), closing=[context]
-    )
-    (wg, wu), _ = gather_rows([gate_weight, up_weight], pair, before=((context,),))
-
-    attn_part = to_width("attention_out", (context, 0, side_a, 0, o_cols))
+    wide_got = gather_step(wide, pair, 0, before=key_got, beside=(context,))
+    down_t = down_weight.T
+    middle = units // 2
+    downs = [{0: down_t[:, :middle]}, {0: down_t[:, middle:]}]
+    attn_part = to_width(
+        "attention_out",
+        (after(context, *wide_got), 0, wo_a, 0, o_half),
+        (after(context, *wide_got), 1, wo_b, 0, o_half),
+        tile=512,
+    )
     my_attn = sum_of_parts(attn_part)
     my_post = on_quarter(post_kernel, "post", (my_tokens, my_attn), (gain_post,), (BF16,))[0]
     post_low = all_parts(my_post)
-    grad_act = from_width("grad_act", cotangent, (side_a, o_cols, cut), (side_b, 0, units - cut))
+    wide_got = gather_rest(wide, pair, 1)
+    wg, wu = gather_end(wide)
+    gather_step(downs, pair, 0, before=(my_post, *wide_got))
+    gather_rest(downs, pair, 1)
+    side_a, side_b = gather_end(downs)
+    grad_act = from_width(
+        "grad_act", cotangent, (side_a, 0, middle), (side_b, 0, middle)
+    )
     act, grad_gate, grad_up = hidden_units(post_low, wg, wu, grad_act)
     post_part = to_width("grad_post", (grad_gate, 0, wg, 0, units), (grad_up, 0, wu, 0, units))
     my_grad_post = sum_of_parts(post_part)
 
-    act_later = after(act, post_part)
     gate_later = after(grad_gate, post_part)
     up_later = after(grad_up, post_part)
-    middle = units // 2
-    down_a = weight_grad("down_a", n, bits[0], (cotangent, act_later, 0, middle))
-    down_b = weight_grad("down_b", n, flipped[0], (cotangent, act_later, 1, middle))
     gate_terms = weight_grad("gate_grad", n, bits[0], (post_low, gate_later, 0, units))
     up_terms = weight_grad("up_grad", n, flipped[0], (post_low, up_later, 0, units))
-    (gate_sum, up_sum), sends, gots = scatter_sums([gate_terms, up_terms], pair)
-    (down_a, down_b), _, _ = scatter_sums([down_a, down_b], pair)
-    down_sum = jnp.concatenate([down_a, down_b], axis=1).T
-
+    act_later = after(act, post_part)
+    down_terms = [
+        weight_grad("down_a", n, bits[0], (cotangent, act_later, 0, middle)),
+        weight_grad("down_b", n, flipped[0], (cotangent, act_later, 1, middle)),
+    ]
     mlp_part = to_width(
         "units_out",
-        (act_later, 0, side_a, 1, cut),
-        (act_later, 1, side_b, 0, cut),
-        (act_later, 2, side_b, 1, cut),
-    )
+        (act_later, 0, side_a, 0, middle),
+        (act_later, 1, side_b, 0, middle),
+    )
+    my_grad_post = after(my_grad_post, gate_terms[0], up_terms[0])
     my_grad_hidden, my_hidden_low = on_quarter(
         grad_hidden_kernel,
         "grad_hidden",
@@ -882,17 +926,22 @@
         (F32, BF16),
     )
     hidden_low = all_parts(my_hidden_low)
-    mlp_part, hidden_low = together((mlp_part, hidden_low), tuple(gots[0]))
+    mlp_part, hidden_low = together((mlp_part, hidden_low), (down_terms[0][0], down_terms[1][0]))
     my_mlp = sum_of_parts(mlp_part)
-    my_layer_out = on_quarter(
-        layer_out_kernel, "layer_out_rows", (my_tokens, my_attn, my_mlp), (), (BF16,)
-    )[0]
-
-    grad_context = from_width("grad_context", hidden_low, (side_a, 0, o_cols))
-    grad_context = after(grad_context, *gots[-1])
+
+    grad_context = from_width("grad_context", hidden_low, (wo_a, 0, o_half), (wo_b, 0, o_half))
     dq, dk_own, dk_other, dv_own, dv_other = attend_back(
         scalars, queries, grad_context, context, lse, all_keys, all_values, span
     )
+    (gate_sum, up_sum), _, unit_gots = scatter_sums(
+        [gate_terms, up_terms], pair, beside=((), (dk_own,))
+    )
+    (down_a, down_b), _, down_gots = scatter_sums(down_terms, pair, beside=((dk_own,),))
+    down_sum = jnp.concatenate([down_a, down_b], axis=1).T
+    my_layer_out = on_quarter(
+        layer_out_kernel, "layer_out_rows", (my_tokens, my_attn, after(my_mlp, dk_own, *down_gots[0], *unit_gots[-1])), (), (BF16,)
+    )[0]
+    all_layer_out = all_parts(my_layer_out)
     dk_got, dv_got = together((exchange(dk_other, 1), exchange(dv_other, 1)))
     key_sums = split_sum(dk_own, dk_got, n, bits[0])
     value_sums = split_sum(dv_own, dv_got, n, flipped[0])
@@ -903,9 +952,22 @@
         "keys_back", key_terms, value_terms, k_proj, cosine, sine, gain_key
     )
     normed_part = to_width(
-        "grad_normed", (grad_q_low, 0, wq, 0, q_cols), (grad_kv_low, 0, wkv, 0, 2 * kv_cols)
-    )
-    my_grad_normed = sum_of_parts(after(normed_part, my_mlp))
+        "grad_normed", (grad_q_low, 0, wq, 0, q_cols), (grad_kv_low, 0, wkv, 0, 2 * kv_cols), tile=512
+    )
+    my_grad_normed = sum_of_parts(after(normed_part, all_layer_out))
+    query_terms = [
+        weight_grad(
+            "query_grad", n, bits[0], (normed_low, grad_q_low, 0, q_cols), (hidden_later, context, 0, o_half)
+        ),
+        weight_grad(
+            "key_value_grad",
+            n,
+            flipped[0],
+            (normed_low, after(grad_kv_low, normed_part), 0, 2 * kv_cols),
+            (hidden_later, context, 1, o_half),
+        ),
+    ]
+    my_grad_normed = after(my_grad_normed, *down_gots[-1], query_terms[0][0], query_terms[1][0])
     my_tokens_grad = on_quarter(
         tokens_grad_kernel,
         "tokens_grad_rows",
@@ -914,18 +976,7 @@
         (BF16,),
     )[0]
 
-    o_half = o_cols // 2
-    qo = weight_grad(
-        "query_grad", n, bits[0], (normed_low, grad_q_low, 0, q_cols), (hidden_later, context, 0, o_half)
-    )
-    kvo = weight_grad(
-        "key_value_grad",
-        n,
-        flipped[0],
-        (normed_low, grad_kv_low, 0, 2 * kv_cols),
-        (hidden_later, context, 1, o_half),
-    )
-    (qo, kvo), _, _ = scatter_sums([qo, kvo], pair)
+    (qo, kvo), _, _ = scatter_sums(query_terms, pair, beside=((my_tokens_grad,),))
     query_sum = qo[:, :q_cols]
     key_sum = kvo[:, :kv_cols]
     value_sum = kvo[:, kv_cols : 2 * kv_cols]
@@ -955,8 +1006,8 @@
         step *= 2
     small = small[0]
 
-    tokens_grad = leave("tokens_grad", order, all_parts(my_tokens_grad), F32)
-    layer_out = leave("layer_out", order, all_parts(my_layer_out), BF16)
+    tokens_grad = leave("tokens_grad", order, all_parts(my_tokens_grad), jnp.arange(parts), F32)
+    layer_out = leave("layer_out", order, all_layer_out, jnp.arange(parts), BF16)
     return (
         layer_out,
         tokens_grad,

time: 603 us -> 543 us (0.900)
  waiting for transfers between devices: 253 us -> 166 us
  Pallas kernels: 152 us -> 212 us
  local copies, waits for them, and re-layouts: 81.5 us -> 42.3 us
  starting transfers between devices: 47.8 us -> 54.8 us
    ppermute x54 -> x60, waiting for transfers between devices: 172 us -> 107 us  [exchange(): return lax.ppermute(block, 'blk', [(i, i ^ bit) for i in range(n)])]
    pallas_call x29, Pallas kernels: 108 us -> 167 us  [call(): pl.pallas_call(kernel, out_shape=out_shape, compiler_params=pltpu.Compile...]
    unnamed x257 -> x143, local copies, waits for them, and re-layouts: 68.1 us -> 28.4 us
    all_gather x4, waiting for transfers between devices: 59.1 us -> 31.6 us  [all_parts(): return lax.all_gather(mine, 'fsdp', axis=0, tiled=True)]
    reduce_scatter x4, waiting for transfers between devices: 17.4 us -> 25.6 us  [sum_of_parts(): return lax.psum_scatter(part, 'fsdp', scatter_dimension=0, tiled=True)]
    ppermute x54 -> x60, starting transfers between devices: 45.8 us -> 51.4 us  [exchange(): return lax.ppermute(block, 'blk', [(i, i ^ bit) for i in range(n)])]
    concatenate x15 -> x19, other arithmetic: 8.5 us -> 12.6 us  [the longest x10 8.01 us: gather_step(): sent.append(one[0] if len(one) == 1 else jnp.concatenate(one, axis=0))]
  transfers between devices with their start and end apart: 64 -> 70, of which waited for: 42 -> 33; matrix products, arithmetic and copies ran while one was open for 11% -> 12% of each run, Pallas kernels for 20% -> 32%
where the time goes in v3:
time: 543 us; the launch traced here: 533 us
  Pallas kernels  212 us (39%)
  waiting for transfers between devices  166 us (31%)
  starting transfers between devices  54.8 us (10%)
  local copies, waits for them, and re-layouts  42.3 us (8%)
  other arithmetic  41.8 us (8%)
  between operations  15.5 us (3%)
    pallas_call x29, Pallas kernels, call(): pl.pallas_call(kernel, out_shape=out_shape, compiler_params=pltpu.Compile...  167 us
    ppermute x60, waiting for transfers between devices, exchange(): return lax.ppermute(block, 'blk', [(i, i ^ bit) for i in range(n)])  107 us
    ppermute x60, starting transfers between devices, exchange(): return lax.ppermute(block, 'blk', [(i, i ^ bit) for i in range(n)])  51.4 us
    all_gather x4, waiting for transfers between devices, all_parts(): return lax.all_gather(mine, 'fsdp', axis=0, tiled=True)  31.6 us
    pallas_call x1, Pallas kernels, attend_back(): pl.pallas_call(functools.partial(attend_back_kernel, span), grid_spec=plt...  29 us
    unnamed x143, local copies, waits for them, and re-layouts  28.4 us
    reduce_scatter x4, waiting for transfers between devices, sum_of_parts(): return lax.psum_scatter(part, 'fsdp', scatter_dimension=0, tiled=True)  25.6 us
    pallas_call x1, Pallas kernels, attend(): pl.pallas_call(functools.partial(attend_kernel, span), grid_spec=pltpu.Pr...  16.7 us
  transfers between devices with their start and end apart: 70, of which 33 were waited for; matrix products, arithmetic and copies ran while one was open for 12% of the time, Pallas kernels for 32%

profile of v3, /device:TPU:0, one launch (start us, length us, event | category | flops | bytes accessed | tf_op | source)
XLA Modules:
  0.0 532.6 jit_solution(5565056699314178376)
XLA Ops:
  11.2 2.9 collective-permute-start
  18.3 1.9 fusion
  21.4 1.8 copy.50
  28.1 2.1 enter.1
  35.3 2.0 collective-permute-done.5
  43.2 10.7 %projections.1 = (bf16[512,2048]{1,0:T(8,128)(2,1)}, f32[512,512]{1,0:T(8,128)}, f32[512,256]{1,0:T(8,128)}, bf16[512,512]{1,0:T(8,128)(2,1)}, bf16[512,256]{1,0:T(8,128)(2,1)}, /*index=5*/bf16[512,256]{1,0:T(8,128)(2,1)}) custom-call(bf16[512,2048]{1,0:T(8,128)(2,1)} %copy-done.2, f32[1,2048]{1,0:T(1,128)S(1)} %bitcast.24, bf16[1024,512]{1,0:T(8,128)(2,1)} %copy-done.15, ...), custom_call_target="tpu_custom_call" | custom-call | tf_op jit(solution)/shard_map/projections/pallas_call | solution.py:173
  56.1 6.1 %collective-permute-done.11 = bf16[512,256]{1,0:T(8,128)(2,1)S(1)} collective-permute-done((bf16[512,256]{1,0:T(8,128)(2,1)}, bf16[512,256]{1,0:T(8,128)(2,1)S(1)}, u32[]{:S(2)}, u32[]{:S(2)}) %collective-permute-start.11) | collective-permute-done | bytes 262176 | tf_op jit(solution)/shard_map/ppermute | solution.py:36
  67.1 10.8 %collective-permute-done.13 = bf16[1024,256]{1,0:T(8,128)(2,1)S(1)} collective-permute-done((bf16[1024,256]{1,0:T(8,128)(2,1)S(1)}, bf16[1024,256]{1,0:T(8,128)(2,1)S(1)}, u32[]{:S(2)}, u32[]{:S(2)}) %collective-permute-start.13) | collective-permute-done | bytes 524320 | tf_op jit(solution)/shard_map/ppermute | solution.py:36
  81.4 7.7 %collective-permute-done.19 = bf16[512,256]{1,0:T(8,128)(2,1)S(1)} collective-permute-done((bf16[512,256]{1,0:T(8,128)(2,1)S(1)}, bf16[512,256]{1,0:T(8,128)(2,1)S(1)}, u32[]{:S(2)}, u32[]{:S(2)}) %collective-permute-start.19) | collective-permute-done | bytes 262176 | tf_op jit(solution)/shard_map/ppermute | solution.py:36
  93.3 16.7 %attend.1 = (bf16[512,512]{1,0:T(8,128)(2,1)S(1)}, f32[2,2,512]{2,1,0:T(2,128)S(1)}) custom-call(s32[18]{0:T(128)S(1)} %pad_add_fusion.1.sc, bf16[512,512]{1,0:T(8,128)(2,1)S(1)} %copy-done.7, bf16[2048,256]{1,0:T(8,128)(2,1)} %copy-done.55, bf16[2048,256]{1,0:T(8,128)(2,1)} %copy-done.62, bf16[2048,256]{1,0:T(8,128)(2,1)} %copy-done.33, ...), custom_call_target="tpu_custom_call" | custom-call | flops 8589934592 | bytes 4194304 | tf_op jit(solution)/shard_map/attend/pallas_call | solution.py:718
  112.7 5.0 attention_out.1
  118.0 2.5 pad_maximum_fusion.1
  123.7 2.4 copy.51
  126.2 2.0 constant_dynamic-slice_fusion.1.tokens_ref
  129.2 2.1 constant_dynamic-update-slice_fusion.9
  131.2 26.6 %collective-permute-done.23 = bf16[512,1536]{1,0:T(8,128)(2,1)} collective-permute-done((bf16[512,1536]{1,0:T(8,128)(2,1)}, bf16[512,1536]{1,0:T(8,128)(2,1)}, u32[]{:S(2)}, u32[]{:S(2)}) %collective-permute-start.23) | collective-permute-done | bytes 1572896 | tf_op jit(solution)/shard_map/ppermute | solution.py:36
  158.1 2.7 constant_dynamic-update-slice_fusion.8.wg0.refs_2_
  162.1 2.3 post.1
  168.8 1.8 pad_maximum_fusion.wu0.refs_4_
  170.7 4.5 collective-permute-done.27
  179.5 16.0 %collective-permute-done.29 = bf16[512,768]{1,0:T(8,128)(2,1)S(1)} collective-permute-done((bf16[512,768]{1,0:T(8,128)(2,1)S(1)}, bf16[512,768]{1,0:T(8,128)(2,1)S(1)}, u32[]{:S(2)}, u32[]{:S(2)}) %collective-permute-start.29) | collective-permute-done | bytes 786464 | tf_op jit(solution)/shard_map/ppermute | solution.py:36
  198.9 2.3 collective-permute-done.31.refs_1_.refs_3_
  201.3 2.2 collective-permute-done.32.refs_3_.refs_5_
  204.7 9.0 %grad_act.1.grad_ref = bf16[512,1536]{1,0:T(8,128)(2,1)} custom-call(bf16[512,2048]{1,0:T(8,128)(2,1)} %copy-done, bf16[1024,768]{1,0:T(8,128)(2,1)} %copy-done.8, bf16[1024,768]{1,0:T(8,128)(2,1)} %copy-done.13, bf16[1024,768]{1,0:T(8,128)(2,1)} %copy-done.9, bf16[1024,768]{1,0:T(8,128)(2,1)} %copy-done.14), custom_call_target="tpu_custom_call" | custom-call | tf_op jit(solution)/shard_map/grad_act/pallas_call | solution.py:173
  215.0 13.3 %hidden_units.1 = (bf16[512,1536]{1,0:T(8,128)(2,1)}, bf16[512,1536]{1,0:T(8,128)(2,1)}, bf16[512,1536]{1,0:T(8,128)(2,1)}) custom-call(bf16[512,2048]{1,0:T(8,128)(2,1)} %all-gather.5.cloned.1.call-done.post_ref.refs_0_, bf16[1024,1536]{1,0:T(8,128)(2,1)} %constant_dynamic-update-slice_fusion.8.wg0.refs_2_, ...), custom_call_target="tpu_custom_call" | custom-call | tf_op jit(solution)/shard_map/hidden_units/pallas_call | solution.py:173
  228.3 13.3 %grad_post.1 = bf16[512,2048]{1,0:T(8,128)(2,1)} custom-call(bf16[512,1536]{1,0:T(8,128)(2,1)} %get-tuple-element.195.refs_0_.refs_1_, bf16[512,1536]{1,0:T(8,128)(2,1)} %get-tuple-element.197.refs_1_, bf16[1024,1536]{1,0:T(8,128)(2,1)} %constant_dynamic-update-slice_fusion.8.wg0.refs_2_, bf16[1024,1536]{1,0:T(8,128)(2,1)} %collective-permute-done.25.wg1.refs_3_, ...), custom_call_target="tpu_custom_call" | custom-call | tf_op jit(solution)/shard_map/grad_post/pallas_call | solution.py:173
  241.7 5.5 %gate_grad_away.1 = bf16[1024,1536]{1,0:T(8,128)(2,1)} custom-call(bf16[512,2048]{1,0:T(8,128)(2,1)} %all-gather.5.cloned.1.call-done.post_ref.refs_0_, bf16[512,1536]{1,0:T(8,128)(2,1)} %get-tuple-element.195.refs_0_.refs_1_), custom_call_target="tpu_custom_call" | custom-call | tf_op jit(solution)/shard_map/gate_grad_away/pallas_call | solution.py:173
  247.2 5.5 %up_grad_away.1 = bf16[1024,1536]{1,0:T(8,128)(2,1)} custom-call(bf16[512,2048]{1,0:T(8,128)(2,1)} %all-gather.5.cloned.1.call-done.post_ref.refs_0_, bf16[512,1536]{1,0:T(8,128)(2,1)} %get-tuple-element.197.refs_1_), custom_call_target="tpu_custom_call" | custom-call | tf_op jit(solution)/shard_map/up_grad_away/pallas_call | solution.py:173
  253.1 1.9 constant_dynamic-slice_fusion.cotangent_ref
  255.0 1.7 copy-done.19
  256.7 6.9 %gate_grad.1 = (bf16[512,1536]{1,0:T(8,128)(2,1)}, bf16[512,1536]{1,0:T(8,128)(2,1)}) custom-call(s32[4]{0:T(128)S(1)} %copy-done.6, bf16[512,2048]{1,0:T(8,128)(2,1)} %all-gather.5.cloned.1.call-done.post_ref.refs_0_, bf16[512,1536]{1,0:T(8,128)(2,1)} %get-tuple-element.195.refs_0_.refs_1_, bf16[1024,1536]{1,0:T(8,128)(2,1)} %copy-done.19), custom_call_target="tpu_custom_call" | custom-call | tf_op jit(solution)/shard_map/gate_grad/pallas_call | solution.py:173
  265.2 6.9 %up_grad.1 = (bf16[512,1536]{1,0:T(8,128)(2,1)}, bf16[512,1536]{1,0:T(8,128)(2,1)}) custom-call(s32[4]{0:T(128)S(1)} %copy-done.5, bf16[512,2048]{1,0:T(8,128)(2,1)} %all-gather.5.cloned.1.call-done.post_ref.refs_0_, bf16[512,1536]{1,0:T(8,128)(2,1)} %get-tuple-element.197.refs_1_, bf16[1024,1536]{1,0:T(8,128)(2,1)} %copy-done.18), custom_call_target="tpu_custom_call" | custom-call | tf_op jit(solution)/shard_map/up_grad/pallas_call | solution.py:173
  272.1 12.2 %reduce-scatter.7.cloned.1.call-done.grad_ref = bf16[128,2048]{1,0:T(8,128)(2,1)} async-done(((bf16[512,2048]{1,0:T(8,128)(2,1)}), bf16[128,2048]{1,0:T(8,128)(2,1)}) %reduce-scatter.7.cloned.1.call-update) | async-done | bytes 524304 | tf_op jit(solution)/shard_map/reduce_scatter | solution.py:782
  284.4 3.5 grad_hidden.1
  288.1 4.6 down_a_away.1
  292.7 4.6 down_b_away.1
  300.7 9.4 %units_out.1 = bf16[512,2048]{1,0:T(8,128)(2,1)} custom-call(bf16[512,1536]{1,0:T(8,128)(2,1)} %get-tuple-element.194.refs_0_.refs_1_, bf16[512,1536]{1,0:T(8,128)(2,1)} %get-tuple-element.194.refs_0_.refs_1_, bf16[1024,768]{1,0:T(8,128)(2,1)} %copy-done.8, bf16[1024,768]{1,0:T(8,128)(2,1)} %copy-done.13, bf16[1024,768]{1,0:T(8,128)(2,1)} %copy-done.9, ...), custom_call_target="tpu_custom_call" | custom-call | tf_op jit(solution)/shard_map/units_out/pallas_call | solution.py:173
  310.1 5.6 %down_a.1 = (bf16[512,768]{1,0:T(8,128)(2,1)}, bf16[512,768]{1,0:T(8,128)(2,1)}) custom-call(s32[4]{0:T(128)S(1)} %copy-done.6, bf16[512,2048]{1,0:T(8,128)(2,1)} %copy-done, bf16[512,1536]{1,0:T(8,128)(2,1)} %get-tuple-element.194.refs_0_.refs_1_, bf16[1024,768]{1,0:T(8,128)(2,1)} %collective-permute-done.35.refs_2_), custom_call_target="tpu_custom_call" | custom-call | tf_op jit(solution)/shard_map/down_a/pallas_call | solution.py:173
  315.7 5.6 %down_b.1 = (bf16[512,768]{1,0:T(8,128)(2,1)}, bf16[512,768]{1,0:T(8,128)(2,1)}) custom-call(s32[4]{0:T(128)S(1)} %copy-done.5, bf16[512,2048]{1,0:T(8,128)(2,1)} %copy-done, bf16[512,1536]{1,0:T(8,128)(2,1)} %get-tuple-element.194.refs_0_.refs_1_, bf16[1024,768]{1,0:T(8,128)(2,1)} %collective-permute-done.36.refs_2_), custom_call_target="tpu_custom_call" | custom-call | tf_op jit(solution)/shard_map/down_b/pallas_call | solution.py:173
  321.3 12.0 %all-gather.7.cloned.1.call-done.left_ref.refs_1_ = bf16[512,2048]{1,0:T(8,128)(2,1)} async-done(((bf16[128,2048]{1,0:T(8,128)(2,1)}), bf16[512,2048]{1,0:T(8,128)(2,1)}) %all-gather.7.cloned.1.call-update) | async-done | bytes 2097168 | tf_op jit(solution)/shard_map/all_gather | solution.py:786
  340.5 4.5 grad_context.1.do_ref
  345.0 29.0 %attend_back.1 = (f32[512,512]{1,0:T(8,128)}, bf16[2048,256]{1,0:T(8,128)(2,1)}, bf16[2048,256]{1,0:T(8,128)(2,1)}, bf16[2048,256]{1,0:T(8,128)(2,1)}, bf16[2048,256]{1,0:T(8,128)(2,1)}) custom-call(s32[18]{0:T(128)S(1)} %pad_add_fusion.1.sc, bf16[512,512]{1,0:T(8,128)(2,1)} %get-tuple-element.154.q_ref, bf16[512,512]{1,0:T(8,128)(2,1)} %grad_context.1.do_ref, ...), custom_call_target="tpu_custom_call" | custom-call | flops 21474836480 | bytes 8388608 | tf_op jit(solution)/shard_map/attend_back/pallas_call | solution.py:756
  375.2 3.4 reduce-scatter.9.cloned.1.call-done.mlp_ref
  378.6 2.3 layer_out_rows.1
  389.3 10.9 %collective-permute-done.45 = bf16[1024,256]{1,0:T(8,128)(2,1)S(1)} collective-permute-done((bf16[1024,256]{1,0:T(8,128)(2,1)S(1)}, bf16[1024,256]{1,0:T(8,128)(2,1)S(1)}, u32[]{:S(2)}, u32[]{:S(2)}) %collective-permute-start.45) | collective-permute-done | bytes 524320 | tf_op jit(solution)/shard_map/ppermute | solution.py:36
  405.1 3.5 queries_back.1
  408.6 1.8 collective-permute-done.47.refs_1_
  412.3 3.0 keys_back.1
  415.3 6.4 %grad_normed.1 = bf16[512,2048]{1,0:T(8,128)(2,1)} custom-call(bf16[512,512]{1,0:T(8,128)(2,1)} %get-tuple-element.229.refs_0_.refs_2_, bf16[512,512]{1,0:T(8,128)(2,1)} %get-tuple-element.248.refs_1_.refs_2_, bf16[1024,512]{1,0:T(8,128)(2,1)} %copy-done.15, bf16[1024,512]{1,0:T(8,128)(2,1)} %collective-permute-done.7.wq1.refs_3_, ...), custom_call_target="tpu_custom_call" | custom-call | tf_op jit(solution)/shard_map/grad_normed/pallas_call | solution.py:173
  421.6 4.7 all-gather.9.cloned.1.call-done.value_ref
  426.4 4.7 query_grad_away.1
  431.2 4.8 key_value_grad_away.1
  442.0 5.8 %query_grad.1 = (bf16[512,768]{1,0:T(8,128)(2,1)}, bf16[512,768]{1,0:T(8,128)(2,1)}) custom-call(s32[4]{0:T(128)S(1)} %copy-done.6, bf16[512,2048]{1,0:T(8,128)(2,1)} %get-tuple-element.245.refs_0_, bf16[512,2048]{1,0:T(8,128)(2,1)} %all-gather.7.cloned.1.call-done.left_ref.refs_1_, bf16[512,512]{1,0:T(8,128)(2,1)} %get-tuple-element.229.refs_0_.refs_2_, ...), custom_call_target="tpu_custom_call" | custom-call | tf_op jit(solution)/shard_map/query_grad/pallas_call | solution.py:173
  447.8 5.8 %key_value_grad.1 = (bf16[512,768]{1,0:T(8,128)(2,1)}, bf16[512,768]{1,0:T(8,128)(2,1)}) custom-call(s32[4]{0:T(128)S(1)} %copy-done.5, bf16[512,2048]{1,0:T(8,128)(2,1)} %get-tuple-element.245.refs_0_, bf16[512,2048]{1,0:T(8,128)(2,1)} %all-gather.7.cloned.1.call-done.left_ref.refs_1_, bf16[512,512]{1,0:T(8,128)(2,1)} %get-tuple-element.248.refs_1_.refs_2_, ...), custom_call_target="tpu_custom_call" | custom-call | tf_op jit(solution)/shard_map/key_value_grad/pallas_call | solution.py:173
  454.7 2.9 multiply_reduce_fusion.1
  457.7 2.9 multiply_reduce_fusion
  463.3 8.7 %reduce-scatter.11.cloned.1.call-done.grad_ref = bf16[128,2048]{1,0:T(8,128)(2,1)} async-done(((bf16[512,2048]{1,0:T(8,128)(2,1)}), bf16[128,2048]{1,0:T(8,128)(2,1)}) %reduce-scatter.11.cloned.1.call-update) | async-done | bytes 524304 | tf_op jit(solution)/shard_map/reduce_scatter | solution.py:782
  472.0 3.0 tokens_grad_rows.1
  475.0 1.9 add_convert_fusion.12
  483.8 5.4 %collective-permute-done.59 = f32[1,256]{1,0:T(1,128)S(1)} collective-permute-done((f32[1,256]{1,0:T(1,128)S(1)}, f32[1,256]{1,0:T(1,128)S(1)}, u32[]{:S(2)}, u32[]{:S(2)}) %collective-permute-start.59) | collective-permute-done | bytes 1056 | tf_op jit(solution)/shard_map/ppermute | solution.py:36
  496.7 4.4 layer_out.1
  501.1 2.5 collective-permute-start.61
  507.0 13.5 %all-gather.11.cloned.1.call-done.value_ref = bf16[512,2048]{1,0:T(8,128)(2,1)} async-done(((bf16[128,2048]{1,0:T(8,128)(2,1)}), bf16[512,2048]{1,0:T(8,128)(2,1)}) %all-gather.11.cloned.1.call-update) | async-done | bytes 2097168 | tf_op jit(solution)/shard_map/all_gather | solution.py:786
  520.5 4.8 tokens_grad.1
  (359 shorter events, 120.0 us)
Async XLA Ops:
  7.2 154.9 %reduce-scatter.5.cloned.1.call-start = ((), (), s32[]{:S(2)}) async-start(), calls=%async_computation.4 | async-start | bytes 2621440 | tf_op jit(solution)/shard_map/reduce_scatter | solution.py:782
  11.2 12.0 %collective-permute-start = (bf16[256,512]{1,0:T(8,128)(2,1)}, bf16[256,512]{1,0:T(8,128)(2,1)}, u32[]{:S(2)}, u32[]{:S(2)}) collective-permute-start(bf16[256,512]{1,0:T(8,128)(2,1)} %param.24), channel_id=1, source_target_pairs={{0,8},{4,12},{8,0},{12,4},{16,24},{20,28},{24,16},{28,20},{1,9},{5... | collective-permute-start | bytes 786440 | tf_op jit(solution)/shard_map/ppermute | solution.py:36
  14.1 9.0 %collective-permute-start.1 = (bf16[256,512]{1,0:T(8,128)(2,1)}, bf16[256,512]{1,0:T(8,128)(2,1)}, u32[]{:S(2)}, u32[]{:S(2)}) collective-permute-start(bf16[256,512]{1,0:T(8,128)(2,1)} %constant_dynamic-update-slice_fusion), channel_id=1, source_target_pairs={{0,16},{4,20},{8,24},{12,28},{16,0},{20,4},{24,8},{28,12},{1,17},{... | collective-permute-start | bytes 786440 | tf_op jit(solution)/shard_map/ppermute | solution.py:36
  15.7 7.5 %collective-permute-start.2 = (bf16[1,544]{1,0:T(2,128)(2,1)S(1)}, bf16[1,544]{1,0:T(2,128)(2,1)S(1)}, u32[]{:S(2)}, u32[]{:S(2)}) collective-permute-start(bf16[1,544]{1,0:T(2,128)(2,1)S(1)} %reshape.140), channel_id=1, source_target_pairs={{0,8},{4,12},{8,0},{12,4},{16,24},{20,28},{24,16},{28,20},{1,9},{5... | collective-permute-start | bytes 3272 | tf_op jit(solution)/shard_map/ppermute | solution.py:36
  24.4 12.9 %collective-permute-start.3 = (bf16[512,512]{1,0:T(8,128)(2,1)S(1)}, bf16[512,512]{1,0:T(8,128)(2,1)S(1)}, u32[]{:S(2)}, u32[]{:S(2)}) collective-permute-start(bf16[512,512]{1,0:T(8,128)(2,1)S(1)} %get-tuple-element.147), channel_id=1, source_target_pairs={{0,16},{4,20},{8,24},{12,28},{16,0},{20,4},{24,8},{28,12},{1,17},{... | collective-permute-start | bytes 1572872 | tf_op jit(solution)/shard_map/ppermute | solution.py:36
  25.0 12.4 %collective-permute-start.4 = (bf16[512,512]{1,0:T(8,128)(2,1)S(1)}, bf16[512,512]{1,0:T(8,128)(2,1)S(1)}, u32[]{:S(2)}, u32[]{:S(2)}) collective-permute-start(bf16[512,512]{1,0:T(8,128)(2,1)S(1)} %get-tuple-element.148), channel_id=1, source_target_pairs={{0,8},{4,12},{8,0},{12,4},{16,24},{20,28},{24,16},{28,20},{1,9},{5... | collective-permute-start | bytes 1572872 | tf_op jit(solution)/shard_map/ppermute | solution.py:36
  32.8 4.6 collective-permute-start.5
  37.4 5.8 %collective-permute-start.7 = (bf16[1024,512]{1,0:T(8,128)(2,1)S(1)}, bf16[1024,512]{1,0:T(8,128)(2,1)}, u32[]{:S(2)}, u32[]{:S(2)}) collective-permute-start(bf16[1024,512]{1,0:T(8,128)(2,1)S(1)} %constant_dynamic-update-slice_fusion.2.wq0.refs_2_), channel_id=1, source_target_pairs={{0,4},{4,0},{8,12},{12,8},{16,20},{20,16},{24,28},{28,24},{1,5},{5... | collective-permute-start | bytes 3145736 | tf_op jit(solution)/shard_map/ppermute | solution.py:36
  39.7 14.3 %collective-permute-start.9 = (bf16[256,256]{1,0:T(8,128)(2,1)S(1)}, bf16[256,256]{1,0:T(8,128)(2,1)S(1)}, u32[]{:S(2)}, u32[]{:S(2)}) collective-permute-start(bf16[256,256]{1,0:T(8,128)(2,1)S(1)} %get-tuple-element.157), channel_id=1, source_target_pairs={{0,8},{4,12},{8,0},{12,4},{16,24},{20,28},{24,16},{28,20},{1,9},{5... | collective-permute-start | bytes 393224 | tf_op jit(solution)/shard_map/ppermute | solution.py:36
  41.3 12.7 %collective-permute-start.10 = (bf16[256,256]{1,0:T(8,128)(2,1)S(1)}, bf16[256,256]{1,0:T(8,128)(2,1)S(1)}, u32[]{:S(2)}, u32[]{:S(2)}) collective-permute-start(bf16[256,256]{1,0:T(8,128)(2,1)S(1)} %get-tuple-element.158), channel_id=1, source_target_pairs={{0,16},{4,20},{8,24},{12,28},{16,0},{20,4},{24,8},{28,12},{1,17},{... | collective-permute-start | bytes 393224 | tf_op jit(solution)/shard_map/ppermute | solution.py:36
  54.0 8.2 %collective-permute-start.11 = (bf16[512,256]{1,0:T(8,128)(2,1)}, bf16[512,256]{1,0:T(8,128)(2,1)S(1)}, u32[]{:S(2)}, u32[]{:S(2)}) collective-permute-start(bf16[512,256]{1,0:T(8,128)(2,1)} %get-tuple-element.159), channel_id=1, source_target_pairs={{0,8},{4,12},{8,0},{12,4},{16,24},{20,28},{24,16},{28,20},{1,9},{5... | collective-permute-start | bytes 786440 | tf_op jit(solution)/shard_map/ppermute | solution.py:36
  54.6 8.3 %collective-permute-start.12 = (bf16[512,256]{1,0:T(8,128)(2,1)}, bf16[512,256]{1,0:T(8,128)(2,1)S(1)}, u32[]{:S(2)}, u32[]{:S(2)}) collective-permute-start(bf16[512,256]{1,0:T(8,128)(2,1)} %get-tuple-element.160), channel_id=1, source_target_pairs={{0,16},{4,20},{8,24},{12,28},{16,0},{20,4},{24,8},{28,12},{1,17},{... | collective-permute-start | bytes 786440 | tf_op jit(solution)/shard_map/ppermute | solution.py:36
  64.9 12.9 %collective-permute-start.13 = (bf16[1024,256]{1,0:T(8,128)(2,1)S(1)}, bf16[1024,256]{1,0:T(8,128)(2,1)S(1)}, u32[]{:S(2)}, u32[]{:S(2)}) collective-permute-start(bf16[1024,256]{1,0:T(8,128)(2,1)S(1)} %pad_maximum_fusion.11), channel_id=1, source_target_pairs={{0,16},{4,20},{8,24},{12,28},{16,0},{20,4},{24,8},{28,12},{1,17},{... | collective-permute-start | bytes 1572872 | tf_op jit(solution)/shard_map/ppermute | solution.py:36
  66.5 12.6 %collective-permute-start.14 = (bf16[1024,256]{1,0:T(8,128)(2,1)S(1)}, bf16[1024,256]{1,0:T(8,128)(2,1)S(1)}, u32[]{:S(2)}, u32[]{:S(2)}) collective-permute-start(bf16[1024,256]{1,0:T(8,128)(2,1)S(1)} %pad_maximum_fusion.12), channel_id=1, source_target_pairs={{0,8},{4,12},{8,0},{12,4},{16,24},{20,28},{24,16},{28,20},{1,9},{5... | collective-permute-start | bytes 1572872 | tf_op jit(solution)/shard_map/ppermute | solution.py:36
  79.2 11.4 %collective-permute-start.15 = (bf16[2048,256]{1,0:T(8,128)(2,1)S(1)}, bf16[2048,256]{1,0:T(8,128)(2,1)S(1)}, u32[]{:S(2)}, u32[]{:S(2)}) collective-permute-start(bf16[2048,256]{1,0:T(8,128)(2,1)S(1)} %constant_dynamic-update-slice_fusion.5.k0), channel_id=1, source_target_pairs={{0,4},{4,0},{8,12},{12,8},{16,20},{20,16},{24,28},{28,24},{1,5},{5... | collective-permute-start | bytes 3145736 | tf_op jit(solution)/shard_map/ppermute | solution.py:36
  80.2 12.1 %collective-permute-start.16 = (bf16[2048,256]{1,0:T(8,128)(2,1)S(1)}, bf16[2048,256]{1,0:T(8,128)(2,1)S(1)}, u32[]{:S(2)}, u32[]{:S(2)}) collective-permute-start(bf16[2048,256]{1,0:T(8,128)(2,1)S(1)} %pad_maximum_fusion.6.v0), channel_id=1, source_target_pairs={{0,4},{4,0},{8,12},{12,8},{16,20},{20,16},{24,28},{28,24},{1,5},{5... | collective-permute-start | bytes 3145736 | tf_op jit(solution)/shard_map/ppermute | solution.py:36
  80.3 8.8 %collective-permute-start.19 = (bf16[512,256]{1,0:T(8,128)(2,1)S(1)}, bf16[512,256]{1,0:T(8,128)(2,1)S(1)}, u32[]{:S(2)}, u32[]{:S(2)}) collective-permute-start(bf16[512,256]{1,0:T(8,128)(2,1)S(1)} %pad_maximum_fusion.17), channel_id=1, source_target_pairs={{0,16},{4,20},{8,24},{12,28},{16,0},{20,4},{24,8},{28,12},{1,17},{... | collective-permute-start | bytes 786440 | tf_op jit(solution)/shard_map/ppermute | solution.py:36
  80.8 8.4 %collective-permute-start.20 = (bf16[512,256]{1,0:T(8,128)(2,1)S(1)}, bf16[512,256]{1,0:T(8,128)(2,1)S(1)}, u32[]{:S(2)}, u32[]{:S(2)}) collective-permute-start(bf16[512,256]{1,0:T(8,128)(2,1)S(1)} %pad_maximum_fusion.18), channel_id=1, source_target_pairs={{0,8},{4,12},{8,0},{12,4},{16,24},{20,28},{24,16},{28,20},{1,9},{5... | collective-permute-start | bytes 786440 | tf_op jit(solution)/shard_map/ppermute | solution.py:36
  89.3 21.6 %collective-permute-start.21 = (bf16[1024,256]{1,0:T(8,128)(2,1)S(1)}, bf16[1024,256]{1,0:T(8,128)(2,1)S(1)}, u32[]{:S(2)}, u32[]{:S(2)}) collective-permute-start(bf16[1024,256]{1,0:T(8,128)(2,1)S(1)} %pad_maximum_fusion.13.refs_2_.refs_0_), channel_id=1, source_target_pairs={{0,4},{4,0},{8,12},{12,8},{16,20},{20,16},{24,28},{28,24},{1,5},{5... | collective-permute-start | bytes 1572872 | tf_op jit(solution)/shard_map/ppermute | solution.py:36
  89.4 21.5 %collective-permute-start.22 = (bf16[1024,256]{1,0:T(8,128)(2,1)S(1)}, bf16[1024,256]{1,0:T(8,128)(2,1)S(1)}, u32[]{:S(2)}, u32[]{:S(2)}) collective-permute-start(bf16[1024,256]{1,0:T(8,128)(2,1)S(1)} %pad_maximum_fusion.14.refs_4_.refs_2_), channel_id=1, source_target_pairs={{0,4},{4,0},{8,12},{12,8},{16,20},{20,16},{24,28},{28,24},{1,5},{5... | collective-permute-start | bytes 1572872 | tf_op jit(solution)/shard_map/ppermute | solution.py:36
  90.0 20.9 %collective-permute-start.17 = (bf16[256,1536]{1,0:T(8,128)(2,1)S(1)}, bf16[256,1536]{1,0:T(8,128)(2,1)}, u32[]{:S(2)}, u32[]{:S(2)}) collective-permute-start(bf16[256,1536]{1,0:T(8,128)(2,1)S(1)} %copy-done.11), channel_id=1, source_target_pairs={{0,8},{4,12},{8,0},{12,4},{16,24},{20,28},{24,16},{28,20},{1,9},{5... | collective-permute-start | bytes 2359304 | tf_op jit(solution)/shard_map/ppermute | solution.py:36
  90.6 20.3 %collective-permute-start.18 = (bf16[256,1536]{1,0:T(8,128)(2,1)S(1)}, bf16[256,1536]{1,0:T(8,128)(2,1)S(1)}, u32[]{:S(2)}, u32[]{:S(2)}) collective-permute-start(bf16[256,1536]{1,0:T(8,128)(2,1)S(1)} %copy-done.12), channel_id=1, source_target_pairs={{0,16},{4,20},{8,24},{12,28},{16,0},{20,4},{24,8},{28,12},{1,17},{... | collective-permute-start | bytes 2359304 | tf_op jit(solution)/shard_map/ppermute | solution.py:36
  117.8 97.2 %all-gather.5.cloned.1.call-start = ((), (), s32[]{:S(2)}) async-start(), calls=%async_computation.5 | async-start | bytes 2621440 | tf_op jit(solution)/shard_map/all_gather | solution.py:786
  121.7 36.1 %collective-permute-start.23 = (bf16[512,1536]{1,0:T(8,128)(2,1)}, bf16[512,1536]{1,0:T(8,128)(2,1)}, u32[]{:S(2)}, u32[]{:S(2)}) collective-permute-start(bf16[512,1536]{1,0:T(8,128)(2,1)} %pad_maximum_fusion.1), channel_id=1, source_target_pairs={{0,16},{4,20},{8,24},{12,28},{16,0},{20,4},{24,8},{28,12},{1,17},{... | collective-permute-start | bytes 4718600 | tf_op jit(solution)/shard_map/ppermute | solution.py:36
  122.3 35.8 %collective-permute-start.24 = (bf16[512,1536]{1,0:T(8,128)(2,1)}, bf16[512,1536]{1,0:T(8,128)(2,1)}, u32[]{:S(2)}, u32[]{:S(2)}) collective-permute-start(bf16[512,1536]{1,0:T(8,128)(2,1)} %pad_maximum_fusion.2), channel_id=1, source_target_pairs={{0,8},{4,12},{8,0},{12,4},{16,24},{20,28},{24,16},{28,20},{1,9},{5... | collective-permute-start | bytes 4718600 | tf_op jit(solution)/shard_map/ppermute | solution.py:36
  160.8 52.9 %collective-permute-start.25 = (bf16[1024,1536]{1,0:T(8,128)(2,1)}, bf16[1024,1536]{1,0:T(8,128)(2,1)}, u32[]{:S(2)}, u32[]{:S(2)}) collective-permute-start(bf16[1024,1536]{1,0:T(8,128)(2,1)} %constant_dynamic-update-slice_fusion.8.wg0.refs_2_), channel_id=1, source_target_pairs={{0,4},{4,0},{8,12},{12,8},{16,20},{20,16},{24,28},{28,24},{1,5},{5... | collective-permute-start | bytes 9437192 | tf_op jit(solution)/shard_map/ppermute | solution.py:36
  164.4 10.8 %collective-permute-start.27 = (bf16[256,768]{1,0:T(8,128)(2,1)S(1)}, bf16[256,768]{1,0:T(8,128)(2,1)}, u32[]{:S(2)}, u32[]{:S(2)}) collective-permute-start(bf16[256,768]{1,0:T(8,128)(2,1)S(1)} %get-tuple-element.183), channel_id=1, source_target_pairs={{0,8},{4,12},{8,0},{12,4},{16,24},{20,28},{24,16},{28,20},{1,9},{5... | collective-permute-start | bytes 1179656 | tf_op jit(solution)/shard_map/ppermute | solution.py:36
  165.9 10.4 %collective-permute-start.28 = (bf16[256,768]{1,0:T(8,128)(2,1)S(1)}, bf16[256,768]{1,0:T(8,128)(2,1)S(1)}, u32[]{:S(2)}, u32[]{:S(2)}) collective-permute-start(bf16[256,768]{1,0:T(8,128)(2,1)S(1)} %get-tuple-element.184), channel_id=1, source_target_pairs={{0,16},{4,20},{8,24},{12,28},{16,0},{20,4},{24,8},{28,12},{1,17},{... | collective-permute-start | bytes 1179656 | tf_op jit(solution)/shard_map/ppermute | solution.py:36
  170.7 43.0 %collective-permute-start.26 = (bf16[1024,1536]{1,0:T(8,128)(2,1)}, bf16[1024,1536]{1,0:T(8,128)(2,1)}, u32[]{:S(2)}, u32[]{:S(2)}) collective-permute-start(bf16[1024,1536]{1,0:T(8,128)(2,1)} %pad_maximum_fusion.wu0.refs_4_), channel_id=1, source_target_pairs={{0,4},{4,0},{8,12},{12,8},{16,20},{20,16},{24,28},{28,24},{1,5},{5... | collective-permute-start | bytes 9437192 | tf_op jit(solution)/shard_map/ppermute | solution.py:36
  170.7 113.7 %reduce-scatter.7.cloned.1.call-start = ((), (), s32[]{:S(2)}) async-start(), calls=%async_computation.6 | async-start | bytes 2621440 | tf_op jit(solution)/shard_map/reduce_scatter | solution.py:782
  177.4 18.1 %collective-permute-start.29 = (bf16[512,768]{1,0:T(8,128)(2,1)S(1)}, bf16[512,768]{1,0:T(8,128)(2,1)S(1)}, u32[]{:S(2)}, u32[]{:S(2)}) collective-permute-start(bf16[512,768]{1,0:T(8,128)(2,1)S(1)} %pad_maximum_fusion.7), channel_id=1, source_target_pairs={{0,16},{4,20},{8,24},{12,28},{16,0},{20,4},{24,8},{28,12},{1,17},{... | collective-permute-start | bytes 2359304 | tf_op jit(solution)/shard_map/ppermute | solution.py:36
  179.0 17.7 %collective-permute-start.30 = (bf16[512,768]{1,0:T(8,128)(2,1)S(1)}, bf16[512,768]{1,0:T(8,128)(2,1)S(1)}, u32[]{:S(2)}, u32[]{:S(2)}) collective-permute-start(bf16[512,768]{1,0:T(8,128)(2,1)S(1)} %pad_maximum_fusion.8), channel_id=1, source_target_pairs={{0,8},{4,12},{8,0},{12,4},{16,24},{20,28},{24,16},{28,20},{1,9},{5... | collective-permute-start | bytes 2359304 | tf_op jit(solution)/shard_map/ppermute | solution.py:36
  198.9 4.6 collective-permute-start.32
  241.6 91.6 %all-gather.7.cloned.1.call-start = ((), (), s32[]{:S(2)}) async-start(), calls=%async_computation.7 | async-start | bytes 2621440 | tf_op jit(solution)/shard_map/all_gather | solution.py:786
  247.2 7.9 %collective-permute-start.33 = (bf16[1024,1536]{1,0:T(8,128)(2,1)}, bf16[1024,1536]{1,0:T(8,128)(2,1)S(1)}, u32[]{:S(2)}, u32[]{:S(2)}) collective-permute-start(bf16[1024,1536]{1,0:T(8,128)(2,1)} %gate_grad_away.1), channel_id=1, source_target_pairs={{0,4},{4,0},{8,12},{12,8},{16,20},{20,16},{24,28},{28,24},{1,5},{5... | collective-permute-start | bytes 9437192 | tf_op jit(solution)/shard_map/ppermute | solution.py:36
  252.6 10.9 %collective-permute-start.34 = (bf16[1024,1536]{1,0:T(8,128)(2,1)}, bf16[1024,1536]{1,0:T(8,128)(2,1)S(1)}, u32[]{:S(2)}, u32[]{:S(2)}) collective-permute-start(bf16[1024,1536]{1,0:T(8,128)(2,1)} %up_grad_away.1), channel_id=1, source_target_pairs={{0,4},{4,0},{8,12},{12,8},{16,20},{20,16},{24,28},{28,24},{1,5},{5... | collective-permute-start | bytes 9437192 | tf_op jit(solution)/shard_map/ppermute | solution.py:36
  287.9 90.7 %reduce-scatter.9.cloned.1.call-start = ((), (), s32[]{:S(2)}) async-start(), calls=%async_computation.8 | async-start | bytes 2621440 | tf_op jit(solution)/shard_map/reduce_scatter | solution.py:782
  292.7 17.5 %collective-permute-start.35 = (bf16[1024,768]{1,0:T(8,128)(2,1)}, bf16[1024,768]{1,0:T(8,128)(2,1)}, u32[]{:S(2)}, u32[]{:S(2)}) collective-permute-start(bf16[1024,768]{1,0:T(8,128)(2,1)} %down_a_away.1), channel_id=1, source_target_pairs={{0,4},{4,0},{8,12},{12,8},{16,20},{20,16},{24,28},{28,24},{1,5},{5... | collective-permute-start | bytes 4718600 | tf_op jit(solution)/shard_map/ppermute | solution.py:36
  297.3 18.4 %collective-permute-start.36 = (bf16[1024,768]{1,0:T(8,128)(2,1)}, bf16[1024,768]{1,0:T(8,128)(2,1)}, u32[]{:S(2)}, u32[]{:S(2)}) collective-permute-start(bf16[1024,768]{1,0:T(8,128)(2,1)} %down_b_away.1), channel_id=1, source_target_pairs={{0,4},{4,0},{8,12},{12,8},{16,20},{20,16},{24,28},{28,24},{1,5},{5... | collective-permute-start | bytes 4718600 | tf_op jit(solution)/shard_map/ppermute | solution.py:36
  297.8 38.6 %collective-permute-start.39 = (bf16[512,1536]{1,0:T(8,128)(2,1)}, bf16[512,1536]{1,0:T(8,128)(2,1)}, u32[]{:S(2)}, u32[]{:S(2)}) collective-permute-start(bf16[512,1536]{1,0:T(8,128)(2,1)} %get-tuple-element.210), channel_id=1, source_target_pairs={{0,8},{4,12},{8,0},{12,4},{16,24},{20,28},{24,16},{28,20},{1,9},{5... | collective-permute-start | bytes 4718600 | tf_op jit(solution)/shard_map/ppermute | solution.py:36
  299.2 37.1 %collective-permute-start.40 = (bf16[512,1536]{1,0:T(8,128)(2,1)}, bf16[512,1536]{1,0:T(8,128)(2,1)}, u32[]{:S(2)}, u32[]{:S(2)}) collective-permute-start(bf16[512,1536]{1,0:T(8,128)(2,1)} %get-tuple-element.211), channel_id=1, source_target_pairs={{0,16},{4,20},{8,24},{12,28},{16,0},{20,4},{24,8},{28,12},{1,17},{... | collective-permute-start | bytes 4718600 | tf_op jit(solution)/shard_map/ppermute | solution.py:36
  333.3 93.1 %all-gather.9.cloned.1.call-start = ((), (), s32[]{:S(2)}) async-start(), calls=%async_computation.9 | async-start | bytes 2621440 | tf_op jit(solution)/shard_map/all_gather | solution.py:786
  333.4 40.7 %collective-permute-start.37 = (bf16[512,768]{1,0:T(8,128)(2,1)}, bf16[512,768]{1,0:T(8,128)(2,1)S(1)}, u32[]{:S(2)}, u32[]{:S(2)}) collective-permute-start(bf16[512,768]{1,0:T(8,128)(2,1)} %get-tuple-element.207), channel_id=1, source_target_pairs={{0,8},{4,12},{8,0},{12,4},{16,24},{20,28},{24,16},{28,20},{1,9},{5... | collective-permute-start | bytes 2359304 | tf_op jit(solution)/shard_map/ppermute | solution.py:36
  334.9 39.1 %collective-permute-start.38 = (bf16[512,768]{1,0:T(8,128)(2,1)}, bf16[512,768]{1,0:T(8,128)(2,1)S(1)}, u32[]{:S(2)}, u32[]{:S(2)}) collective-permute-start(bf16[512,768]{1,0:T(8,128)(2,1)} %get-tuple-element.208), channel_id=1, source_target_pairs={{0,16},{4,20},{8,24},{12,28},{16,0},{20,4},{24,8},{28,12},{1,17},{... | collective-permute-start | bytes 2359304 | tf_op jit(solution)/shard_map/ppermute | solution.py:36
  339.2 34.8 %collective-permute-start.41 = (bf16[256,1536]{1,0:T(8,128)(2,1)S(1)}, bf16[256,1536]{1,0:T(8,128)(2,1)}, u32[]{:S(2)}, u32[]{:S(2)}) collective-permute-start(bf16[256,1536]{1,0:T(8,128)(2,1)S(1)} %add_convert_fusion.3), channel_id=1, source_target_pairs={{0,16},{4,20},{8,24},{12,28},{16,0},{20,4},{24,8},{28,12},{1,17},{... | collective-permute-start | bytes 2359304 | tf_op jit(solution)/shard_map/ppermute | solution.py:36
  340.0 35.2 %collective-permute-start.42 = (bf16[256,1536]{1,0:T(8,128)(2,1)S(1)}, bf16[256,1536]{1,0:T(8,128)(2,1)}, u32[]{:S(2)}, u32[]{:S(2)}) collective-permute-start(bf16[256,1536]{1,0:T(8,128)(2,1)S(1)} %add_convert_fusion.2), channel_id=1, source_target_pairs={{0,8},{4,12},{8,0},{12,4},{16,24},{20,28},{24,16},{28,20},{1,9},{5... | collective-permute-start | bytes 2359304 | tf_op jit(solution)/shard_map/ppermute | solution.py:36
  380.9 91.0 %reduce-scatter.11.cloned.1.call-start = ((), (), s32[]{:S(2)}) async-start(), calls=%async_computation.10 | async-start | bytes 2621440 | tf_op jit(solution)/shard_map/reduce_scatter | solution.py:782
  386.2 14.0 %collective-permute-start.45 = (bf16[1024,256]{1,0:T(8,128)(2,1)S(1)}, bf16[1024,256]{1,0:T(8,128)(2,1)S(1)}, u32[]{:S(2)}, u32[]{:S(2)}) collective-permute-start(bf16[1024,256]{1,0:T(8,128)(2,1)S(1)} %add_convert_fusion.7), channel_id=1, source_target_pairs={{0,8},{4,12},{8,0},{12,4},{16,24},{20,28},{24,16},{28,20},{1,9},{5... | collective-permute-start | bytes 1572872 | tf_op jit(solution)/shard_map/ppermute | solution.py:36
  387.7 13.7 %collective-permute-start.46 = (bf16[1024,256]{1,0:T(8,128)(2,1)S(1)}, bf16[1024,256]{1,0:T(8,128)(2,1)S(1)}, u32[]{:S(2)}, u32[]{:S(2)}) collective-permute-start(bf16[1024,256]{1,0:T(8,128)(2,1)S(1)} %get-tuple-element.226), channel_id=1, source_target_pairs={{0,16},{4,20},{8,24},{12,28},{16,0},{20,4},{24,8},{28,12},{1,17},{... | collective-permute-start | bytes 1572872 | tf_op jit(solution)/shard_map/ppermute | solution.py:36
  403.1 7.3 %collective-permute-start.47 = (bf16[512,256]{1,0:T(8,128)(2,1)S(1)}, bf16[512,256]{1,0:T(8,128)(2,1)S(1)}, u32[]{:S(2)}, u32[]{:S(2)}) collective-permute-start(bf16[512,256]{1,0:T(8,128)(2,1)S(1)} %get-tuple-element.232), channel_id=1, source_target_pairs={{0,16},{4,20},{8,24},{12,28},{16,0},{20,4},{24,8},{28,12},{1,17},{... | collective-permute-start | bytes 786440 | tf_op jit(solution)/shard_map/ppermute | solution.py:36
  404.6 7.0 %collective-permute-start.48 = (bf16[512,256]{1,0:T(8,128)(2,1)S(1)}, bf16[512,256]{1,0:T(8,128)(2,1)S(1)}, u32[]{:S(2)}, u32[]{:S(2)}) collective-permute-start(bf16[512,256]{1,0:T(8,128)(2,1)S(1)} %get-tuple-element.233), channel_id=1, source_target_pairs={{0,8},{4,12},{8,0},{12,4},{16,24},{20,28},{24,16},{28,20},{1,9},{5... | collective-permute-start | bytes 786440 | tf_op jit(solution)/shard_map/ppermute | solution.py:36
  426.4 94.1 %all-gather.11.cloned.1.call-start = ((), (), s32[]{:S(2)}) async-start(), calls=%async_computation.11 | async-start | bytes 2621440 | tf_op jit(solution)/shard_map/all_gather | solution.py:786
  431.2 10.8 %collective-permute-start.51 = (bf16[1024,768]{1,0:T(8,128)(2,1)}, bf16[1024,768]{1,0:T(8,128)(2,1)}, u32[]{:S(2)}, u32[]{:S(2)}) collective-permute-start(bf16[1024,768]{1,0:T(8,128)(2,1)} %query_grad_away.1), channel_id=1, source_target_pairs={{0,4},{4,0},{8,12},{12,8},{16,20},{20,16},{24,28},{28,24},{1,5},{5... | collective-permute-start | bytes 4718600 | tf_op jit(solution)/shard_map/ppermute | solution.py:36
  436.0 11.8 %collective-permute-start.52 = (bf16[1024,768]{1,0:T(8,128)(2,1)}, bf16[1024,768]{1,0:T(8,128)(2,1)}, u32[]{:S(2)}, u32[]{:S(2)}) collective-permute-start(bf16[1024,768]{1,0:T(8,128)(2,1)} %key_value_grad_away.1), channel_id=1, source_target_pairs={{0,4},{4,0},{8,12},{12,8},{16,20},{20,16},{24,28},{28,24},{1,5},{5... | collective-permute-start | bytes 4718600 | tf_op jit(solution)/shard_map/ppermute | solution.py:36
  438.9 22.4 %collective-permute-start.49 = (bf16[256,768]{1,0:T(8,128)(2,1)S(1)}, bf16[256,768]{1,0:T(8,128)(2,1)S(1)}, u32[]{:S(2)}, u32[]{:S(2)}) collective-permute-start(bf16[256,768]{1,0:T(8,128)(2,1)S(1)} %add_convert_fusion.15), channel_id=1, source_target_pairs={{0,16},{4,20},{8,24},{12,28},{16,0},{20,4},{24,8},{28,12},{1,17},{... | collective-permute-start | bytes 1179656 | tf_op jit(solution)/shard_map/ppermute | solution.py:36
  440.5 20.8 %collective-permute-start.50 = (bf16[256,768]{1,0:T(8,128)(2,1)S(1)}, bf16[256,768]{1,0:T(8,128)(2,1)}, u32[]{:S(2)}, u32[]{:S(2)}) collective-permute-start(bf16[256,768]{1,0:T(8,128)(2,1)S(1)} %add_convert_fusion.14), channel_id=1, source_target_pairs={{0,8},{4,12},{8,0},{12,4},{16,24},{20,28},{24,16},{28,20},{1,9},{5... | collective-permute-start | bytes 1179656 | tf_op jit(solution)/shard_map/ppermute | solution.py:36
  453.6 21.4 %collective-permute-start.53 = (bf16[512,768]{1,0:T(8,128)(2,1)}, bf16[512,768]{1,0:T(8,128)(2,1)}, u32[]{:S(2)}, u32[]{:S(2)}) collective-permute-start(bf16[512,768]{1,0:T(8,128)(2,1)} %get-tuple-element.252), channel_id=1, source_target_pairs={{0,8},{4,12},{8,0},{12,4},{16,24},{20,28},{24,16},{28,20},{1,9},{5... | collective-permute-start | bytes 2359304 | tf_op jit(solution)/shard_map/ppermute | solution.py:36
  454.1 20.9 %collective-permute-start.54 = (bf16[512,768]{1,0:T(8,128)(2,1)}, bf16[512,768]{1,0:T(8,128)(2,1)}, u32[]{:S(2)}, u32[]{:S(2)}) collective-permute-start(bf16[512,768]{1,0:T(8,128)(2,1)} %get-tuple-element.253), channel_id=1, source_target_pairs={{0,16},{4,20},{8,24},{12,28},{16,0},{20,4},{24,8},{28,12},{1,17},{... | collective-permute-start | bytes 2359304 | tf_op jit(solution)/shard_map/ppermute | solution.py:36
  461.9 20.5 %collective-permute-start.58 = (f32[1,256]{1,0:T(1,128)S(1)}, f32[1,256]{1,0:T(1,128)}, u32[]{:S(2)}, u32[]{:S(2)}) collective-permute-start(f32[1,256]{1,0:T(1,128)S(1)} %add.165), channel_id=1, source_target_pairs={{0,8},{4,12},{8,0},{12,4},{16,24},{20,28},{24,16},{28,20},{1,9},{5... | collective-permute-start | bytes 3080 | tf_op jit(solution)/shard_map/ppermute | solution.py:36
  478.2 11.3 %collective-permute-start.55 = (bf16[256,768]{1,0:T(8,128)(2,1)}, bf16[256,768]{1,0:T(8,128)(2,1)}, u32[]{:S(2)}, u32[]{:S(2)}) collective-permute-start(bf16[256,768]{1,0:T(8,128)(2,1)} %add_convert_fusion.12), channel_id=1, source_target_pairs={{0,16},{4,20},{8,24},{12,28},{16,0},{20,4},{24,8},{28,12},{1,17},{... | collective-permute-start | bytes 1179656 | tf_op jit(solution)/shard_map/ppermute | solution.py:36
  479.7 10.5 %collective-permute-start.56 = (bf16[256,768]{1,0:T(8,128)(2,1)S(1)}, bf16[256,768]{1,0:T(8,128)(2,1)}, u32[]{:S(2)}, u32[]{:S(2)}) collective-permute-start(bf16[256,768]{1,0:T(8,128)(2,1)S(1)} %add_convert_fusion.11), channel_id=1, source_target_pairs={{0,8},{4,12},{8,0},{12,4},{16,24},{20,28},{24,16},{28,20},{1,9},{5... | collective-permute-start | bytes 1179656 | tf_op jit(solution)/shard_map/ppermute | solution.py:36
  483.1 6.2 %collective-permute-start.59 = (f32[1,256]{1,0:T(1,128)S(1)}, f32[1,256]{1,0:T(1,128)S(1)}, u32[]{:S(2)}, u32[]{:S(2)}) collective-permute-start(f32[1,256]{1,0:T(1,128)S(1)} %add.166), channel_id=1, source_target_pairs={{0,16},{4,20},{8,24},{12,28},{16,0},{20,4},{24,8},{28,12},{1,17},{... | collective-permute-start | bytes 3080 | tf_op jit(solution)/shard_map/ppermute | solution.py:36
  494.9 6.2 %collective-permute-start.60 = (f32[1,544]{1,0:T(1,128)S(1)}, f32[1,544]{1,0:T(1,128)S(1)}, u32[]{:S(2)}, u32[]{:S(2)}) collective-permute-start(f32[1,544]{1,0:T(1,128)S(1)} %broadcast_in_dim.82), channel_id=1, source_target_pairs={{0,1},{1,0},{2,3},{3,2},{4,5},{5,4},{6,7},{7,6},{8,9},{9,8},{10,11... | collective-permute-start | bytes 6536 | tf_op jit(solution)/shard_map/ppermute | solution.py:1005
  501.1 4.7 collective-permute-start.61
  (71 other events, 351.7 us)
Sparse Core Ops, SparseCore 0:
  117.9 44.1 reduce-scatter.4
  170.8 44.1 all-gather.4
  241.8 42.5 reduce-scatter.6
  288.0 45.2 all-gather.6
  336.0 42.5 reduce-scatter.8
  381.1 45.2 all-gather.8
  429.3 42.6 reduce-scatter.10
  475.1 45.3 all-gather.10

commit v4 on v3

--- a/solution.py
+++ b/solution.py
@@ -152,7 +152,7 @@
     return pltpu.roll(values, HD // 2, 1)
 
 
-def call(kernel, name, grid, in_specs, out_specs, out_shape, args, flops, scratch=(), scalars=None, near=False):
+def call(kernel, name, grid, in_specs, out_specs, out_shape, args, flops, scratch=(), scalars=None, near=(), near_out=False):
     if scalars is None:
         spec = {"grid": grid, "in_specs": in_specs, "out_specs": out_specs, "scratch_shapes": scratch}
     else:
@@ -165,8 +165,8 @@
                 scratch_shapes=scratch,
             )
         }
-    if not near:
-        args = in_far(*args)
+    args = [a if i in near else in_far(a)[0] for i, a in enumerate(args)]
+    if not near_out:
         out_shape = [pltpu.HBM(o.shape, o.dtype) for o in out_shape]
     if scalars is not None:
         args = (scalars, *args)
@@ -223,7 +223,8 @@
         (first, second),
         0,
         scalars=order,
-        near=True,
+        near=(0, 1),
+        near_out=True,
     )
 
 
@@ -307,73 +308,85 @@
     )
 
 
-def project_kernel(
-    q_steps, split, tokens_ref, gain_ref, wq0, wq1, wkv0, wkv1, cos_ref, sin_ref, gq_ref, gk_ref,
-    normed_ref, q_proj, k_proj, queries, keys, values,
+def head_outputs(product, proj_ref, out_ref, cos_ref, sin_ref, gain_ref, factor):
+    proj_ref[...] = product
+    for h in range(product.shape[1] // HD):
+        one = slice(h * HD, (h + 1) * HD)
+        u = product[:, one]
+        u = u * norm_scale(u) * gain_ref[...]
+        u = u * cos_ref[...] + turned(u) * sin_ref[...]
+        out_ref[:, one] = (u * factor if factor else u).astype(BF16)
+
+
+def halves_product(left_ref, split, w0, w1):
+    return dims(left_ref[:, :split], w0[...], 1, 0) + dims(left_ref[:, split:], w1[...], 1, 0)
+
+
+def keys_kernel(
+    split, tokens_ref, gain_ref, w0, w1, cos_ref, sin_ref, head_gain, normed_ref, proj_ref, keys, values
 ):
-    j = pl.program_id(0)
-
-    @pl.when(j == 0)
+    @pl.when(pl.program_id(0) == 0)
     def _():
         inputs = tokens_ref[...].astype(F32)
         normed_ref[...] = (inputs * norm_scale(inputs) * gain_ref[...]).astype(BF16)
-
-    def product(w0, w1):
-        return dims(normed_ref[:, :split], w0[...], 1, 0) + dims(normed_ref[:, split:], w1[...], 1, 0)
-
-    def heads(proj, proj_ref, out_ref, gain, factor):
-        proj_ref[...] = proj
-        for h in range(proj.shape[1] // HD):
-            one = slice(h * HD, (h + 1) * HD)
-            u = proj[:, one]
-            u = u * norm_scale(u) * gain
-            u = u * cos_ref[...] + turned(u) * sin_ref[...]
-            out_ref[:, one] = (u * factor if factor else u).astype(BF16)
-
-    @pl.when(j < q_steps)
+        product = halves_product(normed_ref, split, w0, w1)
+        head_outputs(product, proj_ref, keys, cos_ref, sin_ref, head_gain, None)
+
+    @pl.when(pl.program_id(0) == 1)
     def _():
-        heads(product(wq0, wq1), q_proj, queries, gq_ref[...], HD**-0.5 * LOG2E)
-
-    @pl.when(j == q_steps)
-    def _():
-        heads(product(wkv0, wkv1), k_proj, keys, gk_ref[...], None)
-
-    @pl.when(j == q_steps + 1)
-    def _():
-        values[...] = product(wkv0, wkv1).astype(BF16)
-
-
-def projections(tokens, gain, wq, wkv, cosine, sine, gain_query, gain_key):
+        values[...] = halves_product(normed_ref, split, w0, w1).astype(BF16)
+
+
+def queries_kernel(split, normed_ref, w0, w1, cos_ref, sin_ref, head_gain, proj_ref, queries):
+    product = halves_product(normed_ref, split, w0, w1)
+    head_outputs(product, proj_ref, queries, cos_ref, sin_ref, head_gain, HD**-0.5 * LOG2E)
+
+
+def whole_block(array):
+    return pl.BlockSpec(array.shape, lambda *i: (0, 0))
+
+
+def project_keys(tokens, gain, pair, cosine, sine, head_gain):
     rows, width = tokens.shape
-    q_cols = wq[0].shape[1]
-    kv_cols = wkv[0].shape[1] // 2
-    steps = q_cols // kv_cols
+    columns = pair[0].shape[1] // 2
     split = width // 2
-
-    def whole(array):
-        return pl.BlockSpec(array.shape, lambda j: (0, 0))
-
-    q_tile = pl.BlockSpec((split, kv_cols), lambda j: (0, jnp.minimum(j, steps - 1)))
-    kv_tile = pl.BlockSpec((split, kv_cols), lambda j: (0, jnp.maximum(j - steps, 0)))
-    q_out = pl.BlockSpec((rows, kv_cols), lambda j: (0, jnp.minimum(j, steps - 1)))
-    kv_out = pl.BlockSpec((rows, kv_cols), lambda j: (0, 0))
-    small = [cosine, sine, gain_query, gain_key]
+    side = pl.BlockSpec((split, columns), lambda j: (0, j))
+    out = pl.BlockSpec((rows, columns), lambda j: (0, 0))
+    small = [cosine, sine, head_gain]
     return call(
-        functools.partial(project_kernel, steps, split),
-        "projections",
-        (steps + 2,),
-        [whole(tokens), whole(gain), q_tile, q_tile, kv_tile, kv_tile] + [whole(a) for a in small],
-        [whole(tokens), q_out, kv_out, q_out, kv_out, kv_out],
+        functools.partial(keys_kernel, split),
+        "project_keys",
+        (2,),
+        [whole_block(tokens), whole_block(gain), side, side] + [whole_block(a) for a in small],
+        [whole_block(tokens), out, out, out],
         [
             shape((rows, width), BF16),
-            shape((rows, q_cols), F32),
-            shape((rows, kv_cols), F32),
-            shape((rows, q_cols), BF16),
-            shape((rows, kv_cols), BF16),
-            shape((rows, kv_cols), BF16),
+            shape((rows, columns), F32),
+            shape((rows, columns), BF16),
+            shape((rows, columns), BF16),
         ],
-        (tokens, gain, *wq, *wkv, *small),
-        2 * rows * width * (q_cols + 2 * kv_cols),
+        (tokens, gain, *pair, *small),
+        4 * rows * width * columns,
+        near=range(7),
+    )
+
+
+def project_queries(normed, pair, cosine, sine, head_gain, tile=256):
+    rows, width = normed.shape
+    columns = pair[0].shape[1]
+    split = width // 2
+    side = pl.BlockSpec((split, tile), lambda j: (0, j))
+    out = pl.BlockSpec((rows, tile), lambda j: (0, j))
+    small = [cosine, sine, head_gain]
+    return call(
+        functools.partial(queries_kernel, split),
+        "project_queries",
+        (columns // tile,),
+        [whole_block(normed), side, side] + [whole_block(a) for a in small],
+        [out, out],
+        [shape((rows, columns), F32), shape((rows, columns), BF16)],
+        (normed, *pair, *small),
+        2 * rows * width * columns,
     )
 
 
@@ -393,7 +406,7 @@
             out_ref[...] = total.astype(out_ref.dtype)
 
 
-def to_width(name, *terms, tile=256):
+def to_width(name, *terms, tile=256, near=()):
     rows = terms[0][0].shape[0]
     split = terms[0][2][0].shape[0]
     half = split // tile
@@ -420,6 +433,7 @@
         [shape((rows, 2 * split), BF16)],
         tuple(args),
         flops,
+        near=near,
     )[0]
 
 
@@ -491,88 +505,119 @@
         [unit, unit, unit],
         (post, *wg, *wu, grad_act),
         4 * rows * width * units,
-    )
-
-
-def away_kernel(count, *refs):
-    out_ref = refs[-1]
-    start = 0
-    for left, right in zip(refs[:count], refs[count : 2 * count]):
-        columns = right.shape[1]
-        out_ref[:, start : start + columns] = dims(left[...].T, right[...], 1, 0).astype(BF16)
-        start += columns
-
-
-def home_kernel(count, leaving, sc, *refs):
-    got_ref, leave_ref, stay_ref = refs[2 * count :]
+        near=(1, 2, 3, 4),
+    )
+
+
+def side_products(count, sides, refs):
+    turned_lefts = [left[...].T for left in refs[:count]]
+    at = count
+    for side in sides:
+        start = 0
+        terms = []
+        for which in side:
+            right = refs[at]
+            at += 1
+            columns = slice(start, start + right.shape[1])
+            terms.append((columns, dims(turned_lefts[which], right[...], 1, 0)))
+            start = columns.stop
+        yield terms
+
+
+def away_kernel(count, sides, *refs):
+    outs = refs[-len(sides) :]
+    for out_ref, terms in zip(outs, side_products(count, sides, refs)):
+        for columns, term in terms:
+            out_ref[:, columns] = term.astype(BF16)
+
+
+def home_kernel(count, sides, steps, sc, *refs):
+    inputs = count + sum(len(side) for side in sides)
+    gots = refs[inputs : inputs + len(sides)]
+    outs = refs[inputs + len(sides) :]
     step = pl.program_id(0)
-    for out_ref, here in ((leave_ref, step < leaving), (stay_ref, step >= leaving)):
-
-        @pl.when(here)
-        def _(out_ref=out_ref):
-            start = 0
-            for left, right in zip(refs[:count], refs[count : 2 * count]):
-                columns = right.shape[1]
-                at = slice(start, start + columns)
-                term = dims(left[...].T, right[...], 1, 0) + got_ref[:, at].astype(F32)
-                out_ref[:, at] = term.astype(BF16)
-                start += columns
-
-
-def weight_grad(name, n, bit, *pairs):
-    rows, width = pairs[0][0].shape
+    for i, terms in enumerate(side_products(count, sides, refs)):
+        leaves = sc[(5 * i + 1) * steps + step] == 1
+        for columns, term in terms:
+            total = (term + gots[i][:, columns].astype(F32)).astype(BF16)
+
+            @pl.when(leaves)
+            def _(i=i, columns=columns, total=total):
+                outs[2 * i][:, columns] = total
+
+            @pl.when(jnp.logical_not(leaves))
+            def _(i=i, columns=columns, total=total):
+                outs[2 * i + 1][:, columns] = total
+
+
+def visits(places, wanted):
+    held = []
+    for step, (place, own) in enumerate(zip(places, wanted)):
+        if own:
+            held.append(place)
+        elif any(wanted[:step]):
+            held.append(held[-1])
+        else:
+            held.append(next(p for p, o in zip(places[step:], wanted[step:]) if o))
+    return held
+
+
+def weight_grads(name, n, bits_of, lefts, *sides, tile=512):
+    rows, width = lefts[0].shape
     split = width // 2
-    total = sum(p[3] for p in pairs)
-    flops = rows * width * total
-    right_specs = [(p[2], p[3]) for p in pairs]
-    lefts = [p[0] for p in pairs]
-    rights = [p[1] for p in pairs]
-    tile = 256
-    tiles = split // tile
-    away = call(
-        functools.partial(away_kernel, len(pairs)),
-        name + "_away",
-        (tiles,),
-        [pl.BlockSpec((rows, tile), lambda i: (0, tiles + i))] * len(pairs)
-        + [pl.BlockSpec((rows, c), lambda i, w=w: (0, w)) for w, c in right_specs],
-        [pl.BlockSpec((tile, total), lambda i: (i, 0))],
-        [shape((split, total), BF16)],
-        (*lefts, *rights),
-        flops,
-    )[0]
-    got = exchange(away, 1)
+    count = len(lefts)
+    kinds = [[term[0] for term in side] for side in sides]
+    rights = [(term[1], term[2], term[3]) for side in sides for term in side]
+    totals = [sum(term[3] for term in side) for side in sides]
+    args = (*lefts, *[r[0] for r in rights])
+
+    def products(first):
+        tiles = split // tile
+        return call(
+            functools.partial(away_kernel, count, kinds),
+            name + "_away" if first else name,
+            (tiles,),
+            [pl.BlockSpec((rows, tile), lambda i, f=first: (0, f + i))] * count
+            + [pl.BlockSpec((rows, c), lambda i, w=w: (0, w)) for _, w, c in rights],
+            [pl.BlockSpec((tile, total), lambda i: (i, 0)) for total in totals],
+            [shape((split, total), BF16) for total in totals],
+            args,
+            0,
+        )
+
+    gots = together([exchange(away, 1) for away in products(split // tile)])
     block = width // n
-    order = leaving_first(n, bit)
-    leaving = len(order) // 2
     if block % 128:
-        home = call(
-            functools.partial(away_kernel, len(pairs)),
-            name,
-            (tiles,),
-            [pl.BlockSpec((rows, tile), lambda i: (0, i))] * len(pairs)
-            + [pl.BlockSpec((rows, c), lambda i, w=w: (0, w)) for w, c in right_specs],
-            [pl.BlockSpec((tile, total), lambda i: (i, 0))],
-            [shape((split, total), BF16)],
-            (*lefts, *rights),
-            flops,
-        )[0]
-        return split_sum(home, got, n, bit)
-    return call(
-        functools.partial(home_kernel, len(pairs), leaving),
+        return [split_sum(home, got, n, bit) for home, got, bit in zip(products(0), gots, bits_of)]
+    steps = n // 2
+    order = leaving_first(n, bits_of[0])
+    table = []
+    for bit in bits_of:
+        masks = [2 * i for i in range(steps)]
+        gone = [i for i, m in enumerate(masks) if m & bit]
+        kept = [i for i, m in enumerate(masks) if not m & bit]
+        leaves = [i in gone for i in order]
+        places = [(gone if i in gone else kept).index(i) for i in order]
+        table += order + [int(x) for x in leaves]
+        table += visits(places, leaves) + visits(places, [not x for x in leaves]) + [0] * steps
+    outs = call(
+        functools.partial(home_kernel, count, kinds, steps),
         name,
-        (len(order),),
-        [pl.BlockSpec((rows, block), lambda i, sc: (0, sc[i]))] * len(pairs)
-        + [pl.BlockSpec((rows, c), lambda i, sc, w=w: (0, w)) for w, c in right_specs]
-        + [pl.BlockSpec((block, total), lambda i, sc: (sc[i], 0))],
+        (steps,),
+        [pl.BlockSpec((rows, block), lambda i, sc: (0, sc[i]))] * count
+        + [pl.BlockSpec((rows, c), lambda i, sc, w=w: (0, w)) for _, w, c in rights]
+        + [pl.BlockSpec((block, total), lambda i, sc: (sc[i], 0)) for total in totals],
         [
-            pl.BlockSpec((block, total), lambda i, sc: (jnp.minimum(i, leaving - 1), 0)),
-            pl.BlockSpec((block, total), lambda i, sc: (jnp.maximum(i - leaving, 0), 0)),
+            pl.BlockSpec((block, total), lambda i, sc, at=(5 * k + 2 + part) * steps: (sc[at + i], 0))
+            for k, total in enumerate(totals)
+            for part in range(2)
         ],
-        [shape((split // 2, total), BF16)] * 2,
-        (*lefts, *rights, got),
-        flops,
-        scalars=jnp.array(order, jnp.int32),
-    )
+        [shape((split // 2, total), BF16) for total in totals for part in range(2)],
+        (*args, *gots),
+        0,
+        scalars=jnp.array(table, jnp.int32),
+    )
+    return list(zip(outs[::2], outs[1::2]))
 
 
 def heads_back_kernel(terms, passed, *refs):
@@ -616,166 +661,224 @@
     )
 
 
-def attend_kernel(span, sc, q_ref, k0, k1, v0, v1, ctx_ref, lse_ref, k_s, v_s, acc_s, sum_s):
-    half = k0.shape[0]
-    k_s[:half] = k0[...]
-    k_s[half:] = k1[...]
-    v_s[:half] = v0[...]
-    v_s[half:] = v1[...]
-    group = q_ref.shape[1] // HD
+def fetch(halves, columns, scratch, sems):
+    copies = []
+    for i, half in enumerate(halves):
+        rows = half.shape[0]
+        at = pl.ds((i % 2) * rows, rows)
+        copy = pltpu.make_async_copy(half.at[:, columns], scratch[i // 2].at[at], sems.at[i])
+        copy.start()
+        copies.append(copy)
+    return copies
+
+
+def attend_kernel(
+    span, head, heads, sc, q_ref, k0, k1, v0, v1, ctx_ref, lse_ref, k_s, v_s, acc_s, sum_s, sems
+):
+    columns = slice(head * HD, (head + heads) * HD)
+    copies = fetch((k0, k1, v0, v1), columns, (k_s, v_s), sems)
+    group = q_ref.shape[1] // HD // heads
     rows = span * group
+    for copy in copies:
+        copy.wait()
     for s in range(2):
         top = slice(s * span, (s + 1) * span)
-        q = jnp.concatenate([q_ref[top, g * HD : (g + 1) * HD] for g in range(group)], axis=0)
+
+        def stacked(h):
+            parts = range(h * group, (h + 1) * group)
+            return jnp.concatenate([q_ref[top, g * HD : (g + 1) * HD] for g in parts], axis=0)
+
+        qs = [stacked(h) for h in range(heads)]
         acc_s[...] = jnp.zeros_like(acc_s)
         sum_s[...] = jnp.zeros_like(sum_s)
 
         def step(p, masked):
             at = pl.ds(pl.multiple_of(sc[2 + p] * span, span), span)
-            e = jnp.exp2(dims(q, k_s[at, :], 1, 1))
+            es = [jnp.exp2(dims(qs[h], k_s[at, h * HD : (h + 1) * HD], 1, 1)) for h in range(heads)]
             if masked:
                 row = lax.broadcasted_iota(jnp.int32, (rows, span), 0) % span
                 col = lax.broadcasted_iota(jnp.int32, (rows, span), 1)
-                e = jnp.where(row >= col, e, 0.0)
-            part = e[:, :HD]
-            for c in range(HD, span, HD):
-                part = part + e[:, c : c + HD]
-            sum_s[...] += part
-            acc_s[...] += dims(e.astype(BF16), v_s[at, :], 1, 0)
+                es = [jnp.where(row >= col, e, 0.0) for e in es]
+            for h, e in enumerate(es):
+                part = e[:, :HD]
+                for c in range(HD, span, HD):
+                    part = part + e[:, c : c + HD]
+                sum_s[h] += part
+                acc_s[h] += dims(e.astype(BF16), v_s[at, h * HD : (h + 1) * HD], 1, 0)
 
         pl.loop(0, sc[s])(lambda p: step(p, False))
         step(sc[s], True)
-        total = jnp.sum(sum_s[...], axis=1, keepdims=True)
-        ctx = (acc_s[...] / total).astype(BF16)
-        for g in range(group):
-            ctx_ref[top, g * HD : (g + 1) * HD] = ctx[g * span : (g + 1) * span]
-        wide = jnp.broadcast_to(jnp.log2(total), (rows, HD))
-        lse_ref[0, s : s + 1, :] = wide.T[0:1]
+        for h in range(heads):
+            total = jnp.sum(sum_s[h], axis=1, keepdims=True)
+            ctx = (acc_s[h] / total).astype(BF16)
+            for g in range(group):
+                at = slice((h * group + g) * HD, (h * group + g + 1) * HD)
+                ctx_ref[top, at] = ctx[g * span : (g + 1) * span]
+            wide = jnp.broadcast_to(jnp.log2(total), (rows, HD))
+            lse_ref[h, s : s + 1, :] = wide.T[0:1]
 
 
 def attend_back_kernel(
-    span, sc, q_ref, do_ref, ctx_ref, lse_ref, k0, k1, v0, v1, dq_ref, dk0, dk1, dv0, dv1, k_s, v_s, dk_s, dv_s, dq_s
+    span, head, heads, sc, q_ref, do_ref, ctx_ref, lse_ref, k0, k1, v0, v1,
+    dq_ref, dk0, dk1, dv0, dv1, k_s, v_s, dk_s, dv_s, dq_s, sems,
 ):
     half = k0.shape[0]
-    k_s[:half] = k0[...]
-    k_s[half:] = k1[...]
-    v_s[:half] = v0[...]
-    v_s[half:] = v1[...]
-    dk_s[...] = jnp.zeros_like(dk_s)
-    dv_s[...] = jnp.zeros_like(dv_s)
-    group = q_ref.shape[1] // HD
+    columns = slice(head * HD, (head + heads) * HD)
+    copies = fetch((k0, k1, v0, v1), columns, (k_s, v_s), sems)
+    group = q_ref.shape[1] // HD // heads
     rows = span * group
-    for s in range(2):
-        top = slice(s * span, (s + 1) * span)
-
-        def stacked(ref):
-            return jnp.concatenate([ref[top, g * HD : (g + 1) * HD] for g in range(group)], axis=0)
-
-        q = stacked(q_ref)
-        do = stacked(do_ref)
-        q_t = q.T
-        do_t = do.T
-        product = do.astype(F32) * stacked(ctx_ref).astype(F32)
-        delta = jnp.sum(product.T, axis=0, keepdims=True)
-        lse = lse_ref[0, s : s + 1, :]
+    chunks = 2 * half // span
+    cols = [slice(h * HD, (h + 1) * HD) for h in range(heads)]
+    later = (sc[1] > sc[0]).astype(jnp.int32)
+
+    def clear(p):
+        at = pl.ds(pl.multiple_of(sc[2 + p] * span, span), span)
+        dk_s[at] = jnp.zeros((span, heads * HD), F32)
+        dv_s[at] = jnp.zeros((span, heads * HD), F32)
+
+    pl.loop(jnp.maximum(sc[0], sc[1]) + 1, chunks)(clear)
+    for first in (True, False):
+        which = later if first else 1 - later
+        top = pl.ds(pl.multiple_of(which * span, span), span)
+
+        def stacked(ref, h):
+            parts = range(h * group, (h + 1) * group)
+            return jnp.concatenate([ref[top, g * HD : (g + 1) * HD] for g in parts], axis=0)
+
+        qs = [stacked(q_ref, h) for h in range(heads)]
+        dos = [stacked(do_ref, h) for h in range(heads)]
+        q_ts = [q.T for q in qs]
+        do_ts = [do.T for do in dos]
+        products = [dos[h].astype(F32) * stacked(ctx_ref, h).astype(F32) for h in range(heads)]
+        deltas = [jnp.sum(product.T, axis=0, keepdims=True) for product in products]
+        lses = [lse_ref[h, pl.ds(which, 1), :] for h in range(heads)]
         dq_s[...] = jnp.zeros_like(dq_s)
+        if first:
+            for copy in copies:
+                copy.wait()
 
         def step(p, masked):
             at = pl.ds(pl.multiple_of(sc[2 + p] * span, span), span)
-            k = k_s[at, :]
-            probs = jnp.exp2(dims(k, q_t, 1, 0) - lse)
+            ks = [k_s[at, c] for c in cols]
+            scores = [dims(ks[h], q_ts[h], 1, 0) for h in range(heads)]
+            grad_probs = [dims(v_s[at, cols[h]], do_ts[h], 1, 0) for h in range(heads)]
+            probs = [jnp.exp2(scores[h] - lses[h]) for h in range(heads)]
             if masked:
                 key = lax.broadcasted_iota(jnp.int32, (span, rows), 0)
                 query = lax.broadcasted_iota(jnp.int32, (span, rows), 1) % span
-                probs = jnp.where(query >= key, probs, 0.0)
-            dv_s[at, :] += dims(probs.astype(BF16), do, 1, 0)
-            grad = (probs * (dims(v_s[at, :], do_t, 1, 0) - delta)).astype(BF16)
-            dk_s[at, :] += dims(grad, q, 1, 0)
-            dq_s[...] += dims(grad, k, 0, 0)
-
-        pl.loop(0, sc[s])(lambda p: step(p, False))
-        step(sc[s], True)
-        dq = dq_s[...] * (HD**-0.5)
-        for g in range(group):
-            dq_ref[top, g * HD : (g + 1) * HD] = dq[g * span : (g + 1) * span]
+                probs = [jnp.where(query >= key, p, 0.0) for p in probs]
+            grads = [(probs[h] * (grad_probs[h] - deltas[h])).astype(BF16) for h in range(heads)]
+            for h in range(heads):
+                dv = dims(probs[h].astype(BF16), dos[h], 1, 0)
+                dk = dims(grads[h], qs[h], 1, 0)
+                if first:
+                    dv_s[at, cols[h]] = dv
+                    dk_s[at, cols[h]] = dk
+                else:
+                    dv_s[at, cols[h]] += dv
+                    dk_s[at, cols[h]] += dk
+                dq_s[h] += dims(ks[h], grads[h], 0, 0)
+
+        pl.loop(0, sc[which])(lambda p: step(p, False))
+        step(sc[which], True)
+        for h in range(heads):
+            dq = dq_s[h].T * (HD**-0.5)
+            for g in range(group):
+                at = slice((h * group + g) * HD, (h * group + g + 1) * HD)
+                dq_ref[top, at] = dq[g * span : (g + 1) * span]
     dk0[...] = (dk_s[:half] * LN2).astype(BF16)
     dk1[...] = (dk_s[half:] * LN2).astype(BF16)
     dv0[...] = dv_s[:half].astype(BF16)
     dv1[...] = dv_s[half:].astype(BF16)
 
 
+def head_groups(kv_local, half):
+    heads = kv_local if half <= 4096 else 1
+    return heads, range(0, kv_local, heads)
+
+
 def attend(scalars, queries, keys, values, span):
     rows, width = queries.shape
+    half = keys[0].shape[0]
     kv_local = keys[0].shape[1] // HD
-    across = width // kv_local
-    half = keys[0].shape[0]
-    wide = pl.BlockSpec((rows, across), lambda h, sc: (0, h))
-    slots = pl.Buffered(2 if half <= 4096 else 1)
-    tall = pl.BlockSpec((half, HD), lambda h, sc: (0, h))
-    read = pl.BlockSpec((half, HD), lambda h, sc: (0, h), pipeline_mode=slots)
-    stacked = across // HD * span
-    flops = 4 * rows * half * width
-    return pl.pallas_call(
-        functools.partial(attend_kernel, span),
-        grid_spec=pltpu.PrefetchScalarGridSpec(
-            num_scalar_prefetch=1,
-            grid=(kv_local,),
-            in_specs=[wide, read, read, read, read],
-            out_specs=[wide, pl.BlockSpec((1, 2, stacked), lambda h, sc: (h, 0, 0))],
-            scratch_shapes=[
-                pltpu.VMEM((2 * half, HD), BF16),
-                pltpu.VMEM((2 * half, HD), BF16),
-                pltpu.VMEM((stacked, HD), F32),
-                pltpu.VMEM((stacked, HD), F32),
-            ],
-        ),
-        out_shape=[
-            jax.ShapeDtypeStruct((rows, width), BF16),
-            jax.ShapeDtypeStruct((kv_local, 2, stacked), F32),
-        ],
-        compiler_params=pltpu.CompilerParams(vmem_limit_bytes=min(60 * MIB, 16 * MIB + 44 * HD * half)),
-        cost_estimate=pl.CostEstimate(
-            flops=4 * flops, bytes_accessed=16 * half * HD, transcendentals=rows * half
-        ),
-        name="attend",
-    )(scalars, queries, *in_far(*keys, *values))
+    heads, firsts = head_groups(kv_local, half)
+    across = width // kv_local * heads
+    stacked = width // kv_local // HD * span
+    far = pl.BlockSpec(memory_space=pl.ANY)
+    results = []
+    for head in firsts:
+        results.append(
+            pl.pallas_call(
+                functools.partial(attend_kernel, span, head, heads),
+                grid_spec=pltpu.PrefetchScalarGridSpec(
+                    num_scalar_prefetch=1,
+                    grid=(1,),
+                    in_specs=[pl.BlockSpec((rows, across), lambda i, sc, at=head // heads: (0, at))]
+                    + [far] * 4,
+                    out_specs=[
+                        pl.BlockSpec((rows, across), lambda i, sc: (0, 0)),
+                        pl.BlockSpec((heads, 2, stacked), lambda i, sc: (0, 0, 0)),
+                    ],
+                    scratch_shapes=[pltpu.VMEM((2 * half, heads * HD), BF16)] * 2
+                    + [pltpu.VMEM((heads, stacked, HD), F32)] * 2
+                    + [pltpu.SemaphoreType.DMA((4,))],
+                ),
+                out_shape=[shape((rows, across), BF16), shape((heads, 2, stacked), F32)],
+                compiler_params=pltpu.CompilerParams(
+                    vmem_limit_bytes=min(60 * MIB, 16 * MIB + 44 * HD * half)
+                ),
+                cost_estimate=pl.CostEstimate(
+                    flops=16 * rows * half * across, bytes_accessed=8 * half * HD, transcendentals=0
+                ),
+                name="attend",
+            )(scalars, queries, *in_far(*keys, *values))
+        )
+    if len(results) == 1:
+        return results[0]
+    return [jnp.concatenate(both, axis=1 - i) for i, both in enumerate(zip(*results))]
 
 
 def attend_back(scalars, queries, grad_context, context, lse, keys, values, span):
     rows, width = queries.shape
+    half = keys[0].shape[0]
     kv_local = keys[0].shape[1] // HD
-    across = width // kv_local
-    half = keys[0].shape[0]
-    wide = pl.BlockSpec((rows, across), lambda h, sc: (0, h))
-    slots = pl.Buffered(2 if half <= 4096 else 1)
-    tall = pl.BlockSpec((half, HD), lambda h, sc: (0, h))
-    read = pl.BlockSpec((half, HD), lambda h, sc: (0, h), pipeline_mode=slots)
-    stacked = across // HD * span
-    flops = 10 * rows * half * width
-    grads = pltpu.HBM(keys[0].shape, BF16)
-    return pl.pallas_call(
-        functools.partial(attend_back_kernel, span),
-        grid_spec=pltpu.PrefetchScalarGridSpec(
-            num_scalar_prefetch=1,
-            grid=(kv_local,),
-            in_specs=[wide, wide, wide, pl.BlockSpec((1, 2, stacked), lambda h, sc: (h, 0, 0))]
-            + [read] * 4,
-            out_specs=[wide] + [tall] * 4,
-            scratch_shapes=[
-                pltpu.VMEM((2 * half, HD), BF16),
-                pltpu.VMEM((2 * half, HD), BF16),
-                pltpu.VMEM((2 * half, HD), F32),
-                pltpu.VMEM((2 * half, HD), F32),
-                pltpu.VMEM((stacked, HD), F32),
-            ],
-        ),
-        out_shape=[pltpu.HBM((rows, width), F32)] + [grads] * 4,
-        compiler_params=pltpu.CompilerParams(vmem_limit_bytes=min(60 * MIB, 16 * MIB + 44 * HD * half)),
-        cost_estimate=pl.CostEstimate(
-            flops=4 * flops, bytes_accessed=32 * half * HD, transcendentals=rows * half
-        ),
-        name="attend_back",
-    )(scalars, *in_far(queries, grad_context, context, lse, *keys, *values))
+    heads, firsts = head_groups(kv_local, half)
+    across = width // kv_local * heads
+    stacked = width // kv_local // HD * span
+    far = pl.BlockSpec(memory_space=pl.ANY)
+    tall = pl.BlockSpec((half, heads * HD), lambda i, sc: (0, 0))
+    grads = pltpu.HBM((half, heads * HD), BF16)
+    results = []
+    for head in firsts:
+        at = head // heads
+        wide = pl.BlockSpec((rows, across), lambda i, sc, at=at: (0, at))
+        results.append(
+            pl.pallas_call(
+                functools.partial(attend_back_kernel, span, head, heads),
+                grid_spec=pltpu.PrefetchScalarGridSpec(
+                    num_scalar_prefetch=1,
+                    grid=(1,),
+                    in_specs=[wide] * 3
+                    + [pl.BlockSpec((heads, 2, stacked), lambda i, sc, at=at: (at, 0, 0))]
+                    + [far] * 4,
+                    out_specs=[pl.BlockSpec((rows, across), lambda i, sc: (0, 0))] + [tall] * 4,
+                    scratch_shapes=[pltpu.VMEM((2 * half, heads * HD), BF16)] * 2
+                    + [pltpu.VMEM((2 * half, heads * HD), F32)] * 2
+                    + [pltpu.VMEM((heads, HD, stacked), F32), pltpu.SemaphoreType.DMA((4,))],
+                ),
+                out_shape=[pltpu.HBM((rows, across), F32)] + [grads] * 4,
+                compiler_params=pltpu.CompilerParams(
+                    vmem_limit_bytes=min(60 * MIB, 16 * MIB + 44 * HD * half)
+                ),
+                cost_estimate=pl.CostEstimate(
+                    flops=40 * rows * half * across, bytes_accessed=32 * half * HD, transcendentals=0
+                ),
+                name="attend_back",
+            )(scalars, *in_far(queries, grad_context, context, lse, *keys, *values))
+        )
+    if len(results) == 1:
+        return results[0]
+    return [jnp.concatenate(parts, axis=1) for parts in zip(*results)]
 
 
 def sum_of_parts(part):
@@ -865,59 +968,63 @@
     gain_query = head_gains[:, :part].reshape(1, HD)
     gain_key = head_gains[:, part:].reshape(1, HD)
 
-    normed_low, q_proj, k_proj, queries, keys, values = projections(
-        tokens, gain_input, wq, wkv, cosine, sine, gain_query, gain_key
+    normed_low, k_proj, keys, values = project_keys(
+        tokens, gain_input, wkv, cosine, sine, gain_key
     )
     outs = [{0: out_t[:, :o_half]}, {0: out_t[:, o_half:]}]
     out_got = gather_step(outs, pair, 0, before=late)
     rows_held = [{0: keys}, {0: values}]
-    gather_step(rows_held, pair, 0, before=out_got)
-    gather_rest(outs, pair, 1)
+    q_proj, queries = project_queries(after(normed_low, keys), wq, cosine, sine, gain_query)
+    gather_step(rows_held, pair, 0, before=out_got, beside=(queries,))
     key_got = gather_rest(rows_held, pair, 1)
     all_keys, all_values = gather_end(rows_held)
+    context, lse = attend(scalars, queries, all_keys, all_values, span)
+    out_got = gather_rest(outs, pair, 1, before=key_got, beside=(context,))
     wo_a, wo_b = gather_end(outs)
     wide = [{0: gate_weight}, {0: up_weight}]
-    context, lse = attend(scalars, queries, all_keys, all_values, span)
-    wide_got = gather_step(wide, pair, 0, before=key_got, beside=(context,))
     down_t = down_weight.T
     middle = units // 2
     downs = [{0: down_t[:, :middle]}, {0: down_t[:, middle:]}]
+    gather_step(downs, pair, 0, before=out_got, beside=(context,))
+    down_got = gather_rest(downs, pair, 1)
+
     attn_part = to_width(
         "attention_out",
-        (after(context, *wide_got), 0, wo_a, 0, o_half),
-        (after(context, *wide_got), 1, wo_b, 0, o_half),
+        (context, 0, wo_a, 0, o_half),
+        (context, 1, wo_b, 0, o_half),
         tile=512,
     )
     my_attn = sum_of_parts(attn_part)
     my_post = on_quarter(post_kernel, "post", (my_tokens, my_attn), (gain_post,), (BF16,))[0]
     post_low = all_parts(my_post)
-    wide_got = gather_rest(wide, pair, 1)
-    wg, wu = gather_end(wide)
-    gather_step(downs, pair, 0, before=(my_post, *wide_got))
-    gather_rest(downs, pair, 1)
+    gather_step(wide, pair, 0, before=down_got)
     side_a, side_b = gather_end(downs)
     grad_act = from_width(
-        "grad_act", cotangent, (side_a, 0, middle), (side_b, 0, middle)
-    )
+        "grad_act", after(cotangent, my_post), (side_a, 0, middle), (side_b, 0, middle)
+    )
+    gather_rest(wide, pair, 1, beside=(my_post, grad_act))
+    wg, wu = gather_end(wide)
     act, grad_gate, grad_up = hidden_units(post_low, wg, wu, grad_act)
-    post_part = to_width("grad_post", (grad_gate, 0, wg, 0, units), (grad_up, 0, wu, 0, units))
+    post_part = to_width("grad_post", (grad_gate, 0, wg, 0, units), (grad_up, 0, wu, 0, units), near=(2, 3, 4, 5))
     my_grad_post = sum_of_parts(post_part)
 
-    gate_later = after(grad_gate, post_part)
-    up_later = after(grad_up, post_part)
-    gate_terms = weight_grad("gate_grad", n, bits[0], (post_low, gate_later, 0, units))
-    up_terms = weight_grad("up_grad", n, flipped[0], (post_low, up_later, 0, units))
-    act_later = after(act, post_part)
-    down_terms = [
-        weight_grad("down_a", n, bits[0], (cotangent, act_later, 0, middle)),
-        weight_grad("down_b", n, flipped[0], (cotangent, act_later, 1, middle)),
-    ]
+    starts = bits[0], flipped[0]
+    act_now, gate_later, up_later = together((act, grad_gate, grad_up), (post_part,))
+    unit_terms = weight_grads(
+        "units_grad", n, starts, [post_low], [(0, gate_later, 0, units)], [(0, up_later, 0, units)]
+    )
+    (gate_sum, up_sum), unit_sends, unit_gots = scatter_sums(unit_terms, pair, beside=((), (post_part,)))
     mlp_part = to_width(
         "units_out",
-        (act_later, 0, side_a, 0, middle),
-        (act_later, 1, side_b, 0, middle),
-    )
-    my_grad_post = after(my_grad_post, gate_terms[0], up_terms[0])
+        (act_now, 0, side_a, 0, middle),
+        (act_now, 1, side_b, 0, middle),
+        tile=512,
+    )
+    act_later = after(act, mlp_part, *unit_gots[0])
+    down_terms = weight_grads(
+        "down_grad", n, starts, [cotangent], [(0, act_later, 0, middle)], [(0, act_later, 1, middle)]
+    )
+    my_grad_post = after(my_grad_post, *[leave for leave, _ in unit_terms])
     my_grad_hidden, my_hidden_low = on_quarter(
         grad_hidden_kernel,
         "grad_hidden",
@@ -926,26 +1033,26 @@
         (F32, BF16),
     )
     hidden_low = all_parts(my_hidden_low)
-    mlp_part, hidden_low = together((mlp_part, hidden_low), (down_terms[0][0], down_terms[1][0]))
+    mlp_part, hidden_low = together(
+        (mlp_part, hidden_low), (*unit_sends[-1], *[leave for leave, _ in down_terms])
+    )
     my_mlp = sum_of_parts(mlp_part)
 
     grad_context = from_width("grad_context", hidden_low, (wo_a, 0, o_half), (wo_b, 0, o_half))
     dq, dk_own, dk_other, dv_own, dv_other = attend_back(
         scalars, queries, grad_context, context, lse, all_keys, all_values, span
     )
-    (gate_sum, up_sum), _, unit_gots = scatter_sums(
-        [gate_terms, up_terms], pair, beside=((), (dk_own,))
-    )
     (down_a, down_b), _, down_gots = scatter_sums(down_terms, pair, beside=((dk_own,),))
     down_sum = jnp.concatenate([down_a, down_b], axis=1).T
-    my_layer_out = on_quarter(
-        layer_out_kernel, "layer_out_rows", (my_tokens, my_attn, after(my_mlp, dk_own, *down_gots[0], *unit_gots[-1])), (), (BF16,)
-    )[0]
-    all_layer_out = all_parts(my_layer_out)
+    dk_other, dv_other = together((dk_other, dv_other), (*unit_gots[-1], *down_gots[0]))
     dk_got, dv_got = together((exchange(dk_other, 1), exchange(dv_other, 1)))
     key_sums = split_sum(dk_own, dk_got, n, bits[0])
     value_sums = split_sum(dv_own, dv_got, n, flipped[0])
     (key_terms, value_terms), sends, _ = scatter_terms([key_sums, value_sums], pair)
+    my_layer_out = on_quarter(
+        layer_out_kernel, "layer_out_rows", (my_tokens, my_attn, after(my_mlp, *sends[0])), (), (BF16,)
+    )[0]
+    all_layer_out = all_parts(my_layer_out)
     dq, hidden_later = together((dq, hidden_low), tuple(sends[0]))
     grad_q_low, q_gain_part = heads_back("queries_back", [dq], [], q_proj, cosine, sine, gain_query)
     grad_kv_low, k_gain_part = heads_back(
@@ -955,19 +1062,15 @@
         "grad_normed", (grad_q_low, 0, wq, 0, q_cols), (grad_kv_low, 0, wkv, 0, 2 * kv_cols), tile=512
     )
     my_grad_normed = sum_of_parts(after(normed_part, all_layer_out))
-    query_terms = [
-        weight_grad(
-            "query_grad", n, bits[0], (normed_low, grad_q_low, 0, q_cols), (hidden_later, context, 0, o_half)
-        ),
-        weight_grad(
-            "key_value_grad",
-            n,
-            flipped[0],
-            (normed_low, after(grad_kv_low, normed_part), 0, 2 * kv_cols),
-            (hidden_later, context, 1, o_half),
-        ),
-    ]
-    my_grad_normed = after(my_grad_normed, *down_gots[-1], query_terms[0][0], query_terms[1][0])
+    query_terms = weight_grads(
+        "attention_grad",
+        n,
+        starts,
+        [normed_low, hidden_later],
+        [(0, grad_q_low, 0, q_cols), (1, context, 0, o_half)],
+        [(0, after(grad_kv_low, normed_part, *down_gots[-1]), 0, 2 * kv_cols), (1, context, 1, o_half)],
+    )
+    my_grad_normed = after(my_grad_normed, query_terms[0][0], query_terms[1][0])
     my_tokens_grad = on_quarter(
         tokens_grad_kernel,
         "tokens_grad_rows",

time: 543 us -> 525 us (0.967)
  Pallas kernels: 212 us -> 174 us
  waiting for transfers between devices: 166 us -> 195 us
  other arithmetic: 41.8 us -> 35.8 us
    ppermute x60, waiting for transfers between devices: 107 us -> 146 us  [exchange(): return lax.ppermute(block, 'blk', [(i, i ^ bit) for i in range(n)])]
    pallas_call x29 -> x24, Pallas kernels: 167 us -> 142 us  [call(): pl.pallas_call(kernel, out_shape=out_shape, compiler_params=pltpu.Compile...]
    reduce_scatter x4, waiting for transfers between devices: 25.6 us -> 10.8 us  [sum_of_parts(): return lax.psum_scatter(part, 'fsdp', scatter_dimension=0, tiled=True)]
    pallas_call x2, Pallas kernels: 45.7 us -> 31.2 us  [the longest x1 20.4 us: attend_back(): pl.pallas_call(functools.partial(attend_back_kernel, span, head, heads),...]
    unnamed x143 -> x187, local copies, waits for them, and re-layouts: 28.4 us -> 26.8 us
  transfers between devices with their start and end apart: 70 -> 70, of which waited for: 33 -> 44; matrix products, arithmetic and copies ran while one was open for 12% -> 11% of each run, Pallas kernels for 32% -> 27%
where the time goes in v4:
time: 525 us; the launch traced here: 515 us
  waiting for transfers between devices  195 us (37%)
  Pallas kernels  174 us (33%)
  starting transfers between devices  52.4 us (10%)
  local copies, waits for them, and re-layouts  42.5 us (8%)
  other arithmetic  35.8 us (7%)
  between operations  15.7 us (3%)
    ppermute x60, waiting for transfers between devices, exchange(): return lax.ppermute(block, 'blk', [(i, i ^ bit) for i in range(n)])  146 us
    pallas_call x24, Pallas kernels, call(): pl.pallas_call(kernel, out_shape=out_shape, compiler_params=pltpu.Compile...  142 us
    ppermute x60, starting transfers between devices, exchange(): return lax.ppermute(block, 'blk', [(i, i ^ bit) for i in range(n)])  49.6 us
    all_gather x4, waiting for transfers between devices, all_parts(): return lax.all_gather(mine, 'fsdp', axis=0, tiled=True)  35.4 us
    unnamed x187, local copies, waits for them, and re-layouts  26.8 us
    pallas_call x1, Pallas kernels, attend_back(): pl.pallas_call(functools.partial(attend_back_kernel, span, head, heads),...  20.4 us
    convert_element_type x11, other arithmetic, add_low(): return (a.astype(F32) + b.astype(F32)).astype(BF16)  12.6 us
    reduce_scatter x4, waiting for transfers between devices, sum_of_parts(): return lax.psum_scatter(part, 'fsdp', scatter_dimension=0, tiled=True)  10.8 us
  transfers between devices with their start and end apart: 70, of which 44 were waited for; matrix products, arithmetic and copies ran while one was open for 11% of the time, Pallas kernels for 27%

profile of v4, /device:TPU:0, one launch (start us, length us, event | category | flops | bytes accessed | tf_op | source)
XLA Modules:
  0.0 514.7 jit_solution(5105387450404784081)
XLA Ops:
  9.9 3.0 collective-permute-start
  25.9 2.1 enter.1
  29.3 4.1 collective-permute-done.5
  40.1 2.0 copy-done.7
  42.0 4.5 project_keys.1
  48.8 5.9 %project_queries.1 = (f32[512,512]{1,0:T(8,128)}, bf16[512,512]{1,0:T(8,128)(2,1)}) custom-call(bf16[512,2048]{1,0:T(8,128)(2,1)} %get-tuple-element.171.normed_ref.refs_0_, bf16[1024,512]{1,0:T(8,128)(2,1)} %constant_dynamic-update-slice_fusion.2.w0.refs_2_, bf16[1024,512]{1,0:T(8,128)(2,1)} %collective-permute-done.8.w1.refs_3_, f32[512,128]{1,0:T(8,128)} %copy-done.3, ...), custom_call_target="tpu_custom_call" | custom-call | tf_op jit(solution)/shard_map/project_queries/pallas_call | solution.py:173
  57.4 10.2 %collective-permute-done.13 = bf16[1024,256]{1,0:T(8,128)(2,1)S(1)} collective-permute-done((bf16[1024,256]{1,0:T(8,128)(2,1)S(1)}, bf16[1024,256]{1,0:T(8,128)(2,1)S(1)}, u32[]{:S(2)}, u32[]{:S(2)}) %collective-permute-start.13) | collective-permute-done | bytes 524320 | tf_op jit(solution)/shard_map/ppermute | solution.py:36
  73.7 10.8 %attend.1 = (bf16[512,512]{1,0:T(8,128)(2,1)S(1)}, f32[2,2,512]{2,1,0:T(2,128)S(1)}) custom-call(s32[18]{0:T(128)S(1)} %pad_add_fusion.1.sc, bf16[512,512]{1,0:T(8,128)(2,1)S(1)} %copy-done.11, bf16[2048,256]{1,0:T(8,128)(2,1)} %copy-done.78, bf16[2048,256]{1,0:T(8,128)(2,1)} %copy-done.84, bf16[2048,256]{1,0:T(8,128)(2,1)} %copy-done.41, ...), custom_call_target="tpu_custom_call" | custom-call | flops 8589934592 | bytes 2097152 | tf_op jit(solution)/shard_map/attend/pallas_call | solution.py:811
  89.7 5.0 attention_out.1
  94.9 3.9 collective-permute-done.21
  102.4 16.4 %collective-permute-done.23 = bf16[512,768]{1,0:T(8,128)(2,1)S(1)} collective-permute-done((bf16[512,768]{1,0:T(8,128)(2,1)S(1)}, bf16[512,768]{1,0:T(8,128)(2,1)S(1)}, u32[]{:S(2)}, u32[]{:S(2)}) %collective-permute-start.23) | collective-permute-done | bytes 786464 | tf_op jit(solution)/shard_map/ppermute | solution.py:36
  123.5 13.5 %collective-permute-done.25 = bf16[256,1536]{1,0:T(8,128)(2,1)S(1)} collective-permute-done((bf16[256,1536]{1,0:T(8,128)(2,1)}, bf16[256,1536]{1,0:T(8,128)(2,1)S(1)}, u32[]{:S(2)}, u32[]{:S(2)}) %collective-permute-start.25) | collective-permute-done | bytes 786464 | tf_op jit(solution)/shard_map/ppermute | solution.py:36
  137.8 2.7 pad_maximum_fusion.1
  140.5 2.4 pad_maximum_fusion.2
  144.8 2.0 constant_dynamic-slice_fusion.1.tokens_ref
  146.8 2.1 constant_dynamic-update-slice_fusion.10
  149.8 2.3 post.1
  152.3 9.1 %grad_act.1.grad_ref = bf16[512,1536]{1,0:T(8,128)(2,1)} custom-call(bf16[512,2048]{1,0:T(8,128)(2,1)} %copy-done, bf16[1024,768]{1,0:T(8,128)(2,1)} %copy-done.12, bf16[1024,768]{1,0:T(8,128)(2,1)} %collective-permute-done.29.refs_1_.refs_3_, bf16[1024,768]{1,0:T(8,128)(2,1)} %copy-done.13, bf16[1024,768]{1,0:T(8,128)(2,1)} %collective-permute-done.30.refs_3_.refs_5_), custom_call_target="tpu_custom_call" | custom-call | tf_op jit(solution)/shard_map/grad_act/pallas_call | solution.py:173
  161.3 14.9 %collective-permute-done.27 = bf16[512,1536]{1,0:T(8,128)(2,1)} collective-permute-done((bf16[512,1536]{1,0:T(8,128)(2,1)}, bf16[512,1536]{1,0:T(8,128)(2,1)}, u32[]{:S(2)}, u32[]{:S(2)}) %collective-permute-start.27) | collective-permute-done | bytes 1572896 | tf_op jit(solution)/shard_map/ppermute | solution.py:36
  176.9 2.7 constant_dynamic-update-slice_fusion.8.wg0.refs_2_
  182.9 15.7 %all-gather.5.cloned.1.call-done.post_ref.refs_0_ = bf16[512,2048]{1,0:T(8,128)(2,1)} async-done(((bf16[128,2048]{1,0:T(8,128)(2,1)}), bf16[512,2048]{1,0:T(8,128)(2,1)}) %all-gather.5.cloned.1.call-update) | async-done | bytes 2097168 | tf_op jit(solution)/shard_map/all_gather | solution.py:889
  198.6 12.3 %hidden_units.1 = (bf16[512,1536]{1,0:T(8,128)(2,1)}, bf16[512,1536]{1,0:T(8,128)(2,1)}, bf16[512,1536]{1,0:T(8,128)(2,1)}) custom-call(bf16[512,2048]{1,0:T(8,128)(2,1)} %all-gather.5.cloned.1.call-done.post_ref.refs_0_, bf16[1024,1536]{1,0:T(8,128)(2,1)} %constant_dynamic-update-slice_fusion.8.wg0.refs_2_, ...), custom_call_target="tpu_custom_call" | custom-call | tf_op jit(solution)/shard_map/hidden_units/pallas_call | solution.py:173
  210.9 12.7 %grad_post.1 = bf16[512,2048]{1,0:T(8,128)(2,1)} custom-call(bf16[512,1536]{1,0:T(8,128)(2,1)} %get-tuple-element.213.refs_0_.refs_1_, bf16[512,1536]{1,0:T(8,128)(2,1)} %get-tuple-element.214.refs_1_.refs_2_, bf16[1024,1536]{1,0:T(8,128)(2,1)} %constant_dynamic-update-slice_fusion.8.wg0.refs_2_, bf16[1024,1536]{1,0:T(8,128)(2,1)} %collective-permute-done.31.wg1.refs_3_, ...), custom_call_target="tpu_custom_call" | custom-call | tf_op jit(solution)/shard_map/grad_post/pallas_call | solution.py:173
  223.7 6.9 %units_grad_away.1 = (bf16[1024,1536]{1,0:T(8,128)(2,1)}, bf16[1024,1536]{1,0:T(8,128)(2,1)}) custom-call(bf16[512,2048]{1,0:T(8,128)(2,1)} %all-gather.5.cloned.1.call-done.post_ref.refs_0_, bf16[512,1536]{1,0:T(8,128)(2,1)} %get-tuple-element.213.refs_0_.refs_1_, bf16[512,1536]{1,0:T(8,128)(2,1)} %get-tuple-element.214.refs_1_.refs_2_), custom_call_target="tpu_custom_call" | custom-call | tf_op jit(solution)/shard_map/units_grad_away/pallas_call | solution.py:173
  231.2 5.4 %collective-permute-done.33.refs_3_ = bf16[1024,1536]{1,0:T(8,128)(2,1)S(1)} collective-permute-done((bf16[1024,1536]{1,0:T(8,128)(2,1)}, bf16[1024,1536]{1,0:T(8,128)(2,1)S(1)}, u32[]{:S(2)}, u32[]{:S(2)}) %collective-permute-start.33) | collective-permute-done | bytes 3145760 | tf_op jit(solution)/shard_map/ppermute | solution.py:36
  236.6 4.5 collective-permute-done.34.refs_4_
  242.8 10.9 %units_grad.1 = (bf16[512,1536]{1,0:T(8,128)(2,1)}, bf16[512,1536]{1,0:T(8,128)(2,1)}, bf16[512,1536]{1,0:T(8,128)(2,1)}, bf16[512,1536]{1,0:T(8,128)(2,1)}) custom-call(s32[40]{0:T(128)S(1)} %copy-done.10, bf16[512,2048]{1,0:T(8,128)(2,1)} %all-gather.5.cloned.1.call-done.post_ref.refs_0_, bf16[512,1536]{1,0:T(8,128)(2,1)} %get-tuple-element.213.refs_0_.refs_1_, ...), custom_call_target="tpu_custom_call" | custom-call | tf_op jit(solution)/shard_map/units_grad/pallas_call | solution.py:173
  258.6 7.9 %reduce-scatter.7.cloned.1.call-done.grad_ref = bf16[128,2048]{1,0:T(8,128)(2,1)} async-done(((bf16[512,2048]{1,0:T(8,128)(2,1)}), bf16[128,2048]{1,0:T(8,128)(2,1)}) %reduce-scatter.7.cloned.1.call-update) | async-done | bytes 524304 | tf_op jit(solution)/shard_map/reduce_scatter | solution.py:885
  266.4 3.6 grad_hidden.1
  270.3 7.9 %units_out.1 = bf16[512,2048]{1,0:T(8,128)(2,1)} custom-call(bf16[512,1536]{1,0:T(8,128)(2,1)} %get-tuple-element.231.refs_0_.refs_1_.refs_2_, bf16[512,1536]{1,0:T(8,128)(2,1)} %get-tuple-element.231.refs_0_.refs_1_.refs_2_, bf16[1024,768]{1,0:T(8,128)(2,1)} %copy-done.12, bf16[1024,768]{1,0:T(8,128)(2,1)} %collective-permute-done.29.refs_1_.refs_3_, ...), custom_call_target="tpu_custom_call" | custom-call | tf_op jit(solution)/shard_map/units_out/pallas_call | solution.py:173
  278.2 12.1 %collective-permute-done.35 = bf16[512,1536]{1,0:T(8,128)(2,1)S(1)} collective-permute-done((bf16[512,1536]{1,0:T(8,128)(2,1)}, bf16[512,1536]{1,0:T(8,128)(2,1)S(1)}, u32[]{:S(2)}, u32[]{:S(2)}) %collective-permute-start.35) | collective-permute-done | bytes 1572896 | tf_op jit(solution)/shard_map/ppermute | solution.py:36
  291.5 5.1 down_grad_away.1
  297.2 2.2 add_convert_fusion.3
  299.4 2.3 add_convert_fusion.2
  304.0 8.0 %down_grad.1 = (bf16[512,768]{1,0:T(8,128)(2,1)}, bf16[512,768]{1,0:T(8,128)(2,1)}, bf16[512,768]{1,0:T(8,128)(2,1)}, bf16[512,768]{1,0:T(8,128)(2,1)}) custom-call(s32[40]{0:T(128)S(1)} %copy-done.10, bf16[512,2048]{1,0:T(8,128)(2,1)} %copy-done, bf16[512,1536]{1,0:T(8,128)(2,1)} %get-tuple-element.231.refs_0_.refs_1_.refs_2_, ...), custom_call_target="tpu_custom_call" | custom-call | tf_op jit(solution)/shard_map/down_grad/pallas_call | solution.py:173
  312.1 3.4 all-gather.7.cloned.1.call-done.left_ref.refs_1_
  319.7 4.4 grad_context.1.do_ref
  324.1 20.4 %attend_back.1 = (f32[512,512]{1,0:T(8,128)}, bf16[2048,256]{1,0:T(8,128)(2,1)}, bf16[2048,256]{1,0:T(8,128)(2,1)}, bf16[2048,256]{1,0:T(8,128)(2,1)}, bf16[2048,256]{1,0:T(8,128)(2,1)}) custom-call(s32[18]{0:T(128)S(1)} %pad_add_fusion.1.sc, bf16[512,512]{1,0:T(8,128)(2,1)} %get-tuple-element.173.q_ref, bf16[512,512]{1,0:T(8,128)(2,1)} %grad_context.1.do_ref, ...), custom_call_target="tpu_custom_call" | custom-call | flops 21474836480 | bytes 8388608 | tf_op jit(solution)/shard_map/attend_back/pallas_call | solution.py:856
  344.6 8.4 %collective-permute-done.41 = bf16[512,768]{1,0:T(8,128)(2,1)S(1)} collective-permute-done((bf16[512,768]{1,0:T(8,128)(2,1)}, bf16[512,768]{1,0:T(8,128)(2,1)S(1)}, u32[]{:S(2)}, u32[]{:S(2)}) %collective-permute-start.41) | collective-permute-done | bytes 786464 | tf_op jit(solution)/shard_map/ppermute | solution.py:36
  353.6 2.0 fusion.3
  360.8 2.3 layer_out_rows.1
  366.6 10.9 %collective-permute-done.45 = bf16[1024,256]{1,0:T(8,128)(2,1)S(1)} collective-permute-done((bf16[1024,256]{1,0:T(8,128)(2,1)}, bf16[1024,256]{1,0:T(8,128)(2,1)S(1)}, u32[]{:S(2)}, u32[]{:S(2)}) %collective-permute-start.45) | collective-permute-done | bytes 524320 | tf_op jit(solution)/shard_map/ppermute | solution.py:36
  382.2 3.5 queries_back.1
  388.8 3.0 keys_back.1
  391.8 6.4 %grad_normed.1 = bf16[512,2048]{1,0:T(8,128)(2,1)} custom-call(bf16[512,512]{1,0:T(8,128)(2,1)} %get-tuple-element.258.refs_0_.refs_2_, bf16[512,512]{1,0:T(8,128)(2,1)} %get-tuple-element.275.refs_1_.refs_4_, bf16[1024,512]{1,0:T(8,128)(2,1)} %constant_dynamic-update-slice_fusion.2.w0.refs_2_, bf16[1024,512]{1,0:T(8,128)(2,1)} %collective-permute-done.8.w1.refs_3_, ...), custom_call_target="tpu_custom_call" | custom-call | tf_op jit(solution)/shard_map/grad_normed/pallas_call | solution.py:173
  398.3 10.3 %all-gather.9.cloned.1.call-done.value_ref = bf16[512,2048]{1,0:T(8,128)(2,1)} async-done(((bf16[128,2048]{1,0:T(8,128)(2,1)}), bf16[512,2048]{1,0:T(8,128)(2,1)}) %all-gather.9.cloned.1.call-update) | async-done | bytes 2097168 | tf_op jit(solution)/shard_map/all_gather | solution.py:889
  411.9 7.9 %collective-permute-done.49 = bf16[256,768]{1,0:T(8,128)(2,1)S(1)} collective-permute-done((bf16[256,768]{1,0:T(8,128)(2,1)S(1)}, bf16[256,768]{1,0:T(8,128)(2,1)S(1)}, u32[]{:S(2)}, u32[]{:S(2)}) %collective-permute-start.49) | collective-permute-done | bytes 393248 | tf_op jit(solution)/shard_map/ppermute | solution.py:36
  421.0 4.8 attention_grad_away.1
  426.5 3.0 collective-permute-done.51.refs_6_
  429.5 2.2 collective-permute-done.52.refs_7_
  432.9 9.4 %attention_grad.1 = (bf16[512,768]{1,0:T(8,128)(2,1)}, bf16[512,768]{1,0:T(8,128)(2,1)}, bf16[512,768]{1,0:T(8,128)(2,1)}, bf16[512,768]{1,0:T(8,128)(2,1)}) custom-call(s32[40]{0:T(128)S(1)} %copy-done.10, bf16[512,2048]{1,0:T(8,128)(2,1)} %get-tuple-element.171.normed_ref.refs_0_, bf16[512,2048]{1,0:T(8,128)(2,1)} %all-gather.7.cloned.1.call-done.left_ref.refs_1_, ...), custom_call_target="tpu_custom_call" | custom-call | tf_op jit(solution)/shard_map/attention_grad/pallas_call | solution.py:173
  444.3 2.7 multiply_reduce_fusion.1
  447.0 2.7 multiply_reduce_fusion
  451.6 2.6 reduce-scatter.11.cloned.1.call-done.grad_ref
  454.2 2.9 tokens_grad_rows.1
  457.1 5.1 collective-permute-done.53
  463.4 1.9 add_convert_fusion.12
  465.3 2.1 add_convert_fusion.11
  471.5 6.2 %collective-permute-done.59 = f32[1,256]{1,0:T(1,128)S(1)} collective-permute-done((f32[1,256]{1,0:T(1,128)S(1)}, f32[1,256]{1,0:T(1,128)S(1)}, u32[]{:S(2)}, u32[]{:S(2)}) %collective-permute-start.59) | collective-permute-done | bytes 1056 | tf_op jit(solution)/shard_map/ppermute | solution.py:36
  479.5 1.9 multiply_reduce_fusion.4
  485.6 4.4 layer_out.1
  492.9 2.6 collective-permute-done.61
  496.7 6.0 %all-gather.11.cloned.1.call-done.value_ref = bf16[512,2048]{1,0:T(8,128)(2,1)} async-done(((bf16[128,2048]{1,0:T(8,128)(2,1)}), bf16[512,2048]{1,0:T(8,128)(2,1)}) %all-gather.11.cloned.1.call-update) | async-done | bytes 2097168 | tf_op jit(solution)/shard_map/all_gather | solution.py:889
  502.6 4.8 tokens_grad.1
  (398 shorter events, 113.7 us)
Async XLA Ops:
  7.2 142.7 %reduce-scatter.5.cloned.1.call-start = ((), (), s32[]{:S(2)}) async-start(), calls=%async_computation.4 | async-start | bytes 2621440 | tf_op jit(solution)/shard_map/reduce_scatter | solution.py:885
  9.9 10.4 %collective-permute-start = (bf16[256,512]{1,0:T(8,128)(2,1)}, bf16[256,512]{1,0:T(8,128)(2,1)S(1)}, u32[]{:S(2)}, u32[]{:S(2)}) collective-permute-start(bf16[256,512]{1,0:T(8,128)(2,1)} %param.21), channel_id=1, source_target_pairs={{0,8},{4,12},{8,0},{12,4},{16,24},{20,28},{24,16},{28,20},{1,9},{5... | collective-permute-start | bytes 786440 | tf_op jit(solution)/shard_map/ppermute | solution.py:36
  12.9 7.8 %collective-permute-start.1 = (bf16[256,512]{1,0:T(8,128)(2,1)S(1)}, bf16[256,512]{1,0:T(8,128)(2,1)S(1)}, u32[]{:S(2)}, u32[]{:S(2)}) collective-permute-start(bf16[256,512]{1,0:T(8,128)(2,1)S(1)} %constant_dynamic-update-slice_fusion), channel_id=1, source_target_pairs={{0,16},{4,20},{8,24},{12,28},{16,0},{20,4},{24,8},{28,12},{1,17},{... | collective-permute-start | bytes 786440 | tf_op jit(solution)/shard_map/ppermute | solution.py:36
  14.4 5.9 %collective-permute-start.2 = (bf16[1,544]{1,0:T(2,128)(2,1)S(1)}, bf16[1,544]{1,0:T(2,128)(2,1)S(1)}, u32[]{:S(2)}, u32[]{:S(2)}) collective-permute-start(bf16[1,544]{1,0:T(2,128)(2,1)S(1)} %reshape.140), channel_id=1, source_target_pairs={{0,8},{4,12},{8,0},{12,4},{16,24},{20,28},{24,16},{28,20},{1,9},{5... | collective-permute-start | bytes 3272 | tf_op jit(solution)/shard_map/ppermute | solution.py:36
  20.8 12.6 %collective-permute-start.3 = (bf16[512,512]{1,0:T(8,128)(2,1)S(1)}, bf16[512,512]{1,0:T(8,128)(2,1)S(1)}, u32[]{:S(2)}, u32[]{:S(2)}) collective-permute-start(bf16[512,512]{1,0:T(8,128)(2,1)S(1)} %get-tuple-element.163), channel_id=1, source_target_pairs={{0,16},{4,20},{8,24},{12,28},{16,0},{20,4},{24,8},{28,12},{1,17},{... | collective-permute-start | bytes 1572872 | tf_op jit(solution)/shard_map/ppermute | solution.py:36
  22.4 12.2 %collective-permute-start.4 = (bf16[512,512]{1,0:T(8,128)(2,1)S(1)}, bf16[512,512]{1,0:T(8,128)(2,1)S(1)}, u32[]{:S(2)}, u32[]{:S(2)}) collective-permute-start(bf16[512,512]{1,0:T(8,128)(2,1)S(1)} %get-tuple-element.164), channel_id=1, source_target_pairs={{0,8},{4,12},{8,0},{12,4},{16,24},{20,28},{24,16},{28,20},{1,9},{5... | collective-permute-start | bytes 1572872 | tf_op jit(solution)/shard_map/ppermute | solution.py:36
  23.0 10.4 %collective-permute-start.5 = (bf16[2,544]{1,0:T(2,128)(2,1)S(1)}, bf16[2,544]{1,0:T(2,128)(2,1)S(1)}, u32[]{:S(2)}, u32[]{:S(2)}) collective-permute-start(bf16[2,544]{1,0:T(2,128)(2,1)S(1)} %pad_maximum_fusion.21), channel_id=1, source_target_pairs={{0,16},{4,20},{8,24},{12,28},{16,0},{20,4},{24,8},{28,12},{1,17},{... | collective-permute-start | bytes 6536 | tf_op jit(solution)/shard_map/ppermute | solution.py:36
  34.7 5.4 %collective-permute-start.7 = (bf16[1024,512]{1,0:T(8,128)(2,1)S(1)}, bf16[1024,512]{1,0:T(8,128)(2,1)S(1)}, u32[]{:S(2)}, u32[]{:S(2)}) collective-permute-start(bf16[1024,512]{1,0:T(8,128)(2,1)S(1)} %pad_maximum_fusion.5.w0.refs_4_), channel_id=1, source_target_pairs={{0,4},{4,0},{8,12},{12,8},{16,20},{20,16},{24,28},{28,24},{1,5},{5... | collective-permute-start | bytes 3145736 | tf_op jit(solution)/shard_map/ppermute | solution.py:36
  37.2 11.6 %collective-permute-start.8 = (bf16[1024,512]{1,0:T(8,128)(2,1)}, bf16[1024,512]{1,0:T(8,128)(2,1)}, u32[]{:S(2)}, u32[]{:S(2)}) collective-permute-start(bf16[1024,512]{1,0:T(8,128)(2,1)} %constant_dynamic-update-slice_fusion.2.w0.refs_2_), channel_id=1, source_target_pairs={{0,4},{4,0},{8,12},{12,8},{16,20},{20,16},{24,28},{28,24},{1,5},{5... | collective-permute-start | bytes 3145736 | tf_op jit(solution)/shard_map/ppermute | solution.py:36
  37.7 8.9 %collective-permute-start.9 = (bf16[256,256]{1,0:T(8,128)(2,1)S(1)}, bf16[256,256]{1,0:T(8,128)(2,1)S(1)}, u32[]{:S(2)}, u32[]{:S(2)}) collective-permute-start(bf16[256,256]{1,0:T(8,128)(2,1)S(1)} %get-tuple-element.175), channel_id=1, source_target_pairs={{0,8},{4,12},{8,0},{12,4},{16,24},{20,28},{24,16},{28,20},{1,9},{5... | collective-permute-start | bytes 393224 | tf_op jit(solution)/shard_map/ppermute | solution.py:36
  38.5 8.0 %collective-permute-start.10 = (bf16[256,256]{1,0:T(8,128)(2,1)S(1)}, bf16[256,256]{1,0:T(8,128)(2,1)S(1)}, u32[]{:S(2)}, u32[]{:S(2)}) collective-permute-start(bf16[256,256]{1,0:T(8,128)(2,1)S(1)} %get-tuple-element.176), channel_id=1, source_target_pairs={{0,16},{4,20},{8,24},{12,28},{16,0},{20,4},{24,8},{28,12},{1,17},{... | collective-permute-start | bytes 393224 | tf_op jit(solution)/shard_map/ppermute | solution.py:36
  46.6 8.1 %collective-permute-start.11 = (bf16[512,256]{1,0:T(8,128)(2,1)}, bf16[512,256]{1,0:T(8,128)(2,1)S(1)}, u32[]{:S(2)}, u32[]{:S(2)}) collective-permute-start(bf16[512,256]{1,0:T(8,128)(2,1)} %get-tuple-element.177), channel_id=1, source_target_pairs={{0,8},{4,12},{8,0},{12,4},{16,24},{20,28},{24,16},{28,20},{1,9},{5... | collective-permute-start | bytes 786440 | tf_op jit(solution)/shard_map/ppermute | solution.py:36
  47.2 7.6 %collective-permute-start.12 = (bf16[512,256]{1,0:T(8,128)(2,1)}, bf16[512,256]{1,0:T(8,128)(2,1)S(1)}, u32[]{:S(2)}, u32[]{:S(2)}) collective-permute-start(bf16[512,256]{1,0:T(8,128)(2,1)} %get-tuple-element.178), channel_id=1, source_target_pairs={{0,16},{4,20},{8,24},{12,28},{16,0},{20,4},{24,8},{28,12},{1,17},{... | collective-permute-start | bytes 786440 | tf_op jit(solution)/shard_map/ppermute | solution.py:36
  54.9 12.7 %collective-permute-start.13 = (bf16[1024,256]{1,0:T(8,128)(2,1)S(1)}, bf16[1024,256]{1,0:T(8,128)(2,1)S(1)}, u32[]{:S(2)}, u32[]{:S(2)}) collective-permute-start(bf16[1024,256]{1,0:T(8,128)(2,1)S(1)} %pad_maximum_fusion.11), channel_id=1, source_target_pairs={{0,16},{4,20},{8,24},{12,28},{16,0},{20,4},{24,8},{28,12},{1,17},{... | collective-permute-start | bytes 1572872 | tf_op jit(solution)/shard_map/ppermute | solution.py:36
  56.4 11.8 %collective-permute-start.14 = (bf16[1024,256]{1,0:T(8,128)(2,1)S(1)}, bf16[1024,256]{1,0:T(8,128)(2,1)S(1)}, u32[]{:S(2)}, u32[]{:S(2)}) collective-permute-start(bf16[1024,256]{1,0:T(8,128)(2,1)S(1)} %pad_maximum_fusion.12), channel_id=1, source_target_pairs={{0,8},{4,12},{8,0},{12,4},{16,24},{20,28},{24,16},{28,20},{1,9},{5... | collective-permute-start | bytes 1572872 | tf_op jit(solution)/shard_map/ppermute | solution.py:36
  69.6 15.7 %collective-permute-start.17 = (bf16[512,256]{1,0:T(8,128)(2,1)S(1)}, bf16[512,256]{1,0:T(8,128)(2,1)S(1)}, u32[]{:S(2)}, u32[]{:S(2)}) collective-permute-start(bf16[512,256]{1,0:T(8,128)(2,1)S(1)} %pad_maximum_fusion.17), channel_id=1, source_target_pairs={{0,16},{4,20},{8,24},{12,28},{16,0},{20,4},{24,8},{28,12},{1,17},{... | collective-permute-start | bytes 786440 | tf_op jit(solution)/shard_map/ppermute | solution.py:36
  70.8 14.5 %collective-permute-start.18 = (bf16[512,256]{1,0:T(8,128)(2,1)S(1)}, bf16[512,256]{1,0:T(8,128)(2,1)S(1)}, u32[]{:S(2)}, u32[]{:S(2)}) collective-permute-start(bf16[512,256]{1,0:T(8,128)(2,1)S(1)} %pad_maximum_fusion.18), channel_id=1, source_target_pairs={{0,8},{4,12},{8,0},{12,4},{16,24},{20,28},{24,16},{28,20},{1,9},{5... | collective-permute-start | bytes 786440 | tf_op jit(solution)/shard_map/ppermute | solution.py:36
  85.3 4.3 collective-permute-start.19
  85.5 4.1 collective-permute-start.20
  87.6 11.2 %collective-permute-start.21 = (bf16[256,768]{1,0:T(8,128)(2,1)S(1)}, bf16[256,768]{1,0:T(8,128)(2,1)S(1)}, u32[]{:S(2)}, u32[]{:S(2)}) collective-permute-start(bf16[256,768]{1,0:T(8,128)(2,1)S(1)} %get-tuple-element.192), channel_id=1, source_target_pairs={{0,8},{4,12},{8,0},{12,4},{16,24},{20,28},{24,16},{28,20},{1,9},{5... | collective-permute-start | bytes 1179656 | tf_op jit(solution)/shard_map/ppermute | solution.py:36
  88.7 10.9 %collective-permute-start.22 = (bf16[256,768]{1,0:T(8,128)(2,1)S(1)}, bf16[256,768]{1,0:T(8,128)(2,1)S(1)}, u32[]{:S(2)}, u32[]{:S(2)}) collective-permute-start(bf16[256,768]{1,0:T(8,128)(2,1)S(1)} %get-tuple-element.193), channel_id=1, source_target_pairs={{0,16},{4,20},{8,24},{12,28},{16,0},{20,4},{24,8},{28,12},{1,17},{... | collective-permute-start | bytes 1179656 | tf_op jit(solution)/shard_map/ppermute | solution.py:36
  94.7 103.9 %all-gather.5.cloned.1.call-start = ((), (), s32[]{:S(2)}) async-start(), calls=%async_computation.5 | async-start | bytes 2621440 | tf_op jit(solution)/shard_map/all_gather | solution.py:889
  100.3 18.4 %collective-permute-start.23 = (bf16[512,768]{1,0:T(8,128)(2,1)S(1)}, bf16[512,768]{1,0:T(8,128)(2,1)S(1)}, u32[]{:S(2)}, u32[]{:S(2)}) collective-permute-start(bf16[512,768]{1,0:T(8,128)(2,1)S(1)} %pad_maximum_fusion.7), channel_id=1, source_target_pairs={{0,16},{4,20},{8,24},{12,28},{16,0},{20,4},{24,8},{28,12},{1,17},{... | collective-permute-start | bytes 2359304 | tf_op jit(solution)/shard_map/ppermute | solution.py:36
  101.3 18.1 %collective-permute-start.24 = (bf16[512,768]{1,0:T(8,128)(2,1)S(1)}, bf16[512,768]{1,0:T(8,128)(2,1)S(1)}, u32[]{:S(2)}, u32[]{:S(2)}) collective-permute-start(bf16[512,768]{1,0:T(8,128)(2,1)S(1)} %pad_maximum_fusion.8), channel_id=1, source_target_pairs={{0,8},{4,12},{8,0},{12,4},{16,24},{20,28},{24,16},{28,20},{1,9},{5... | collective-permute-start | bytes 2359304 | tf_op jit(solution)/shard_map/ppermute | solution.py:36
  119.4 17.5 %collective-permute-start.25 = (bf16[256,1536]{1,0:T(8,128)(2,1)}, bf16[256,1536]{1,0:T(8,128)(2,1)S(1)}, u32[]{:S(2)}, u32[]{:S(2)}) collective-permute-start(bf16[256,1536]{1,0:T(8,128)(2,1)} %param.28), channel_id=1, source_target_pairs={{0,8},{4,12},{8,0},{12,4},{16,24},{20,28},{24,16},{28,20},{1,9},{5... | collective-permute-start | bytes 2359304 | tf_op jit(solution)/shard_map/ppermute | solution.py:36
  120.5 17.3 %collective-permute-start.26 = (bf16[256,1536]{1,0:T(8,128)(2,1)}, bf16[256,1536]{1,0:T(8,128)(2,1)S(1)}, u32[]{:S(2)}, u32[]{:S(2)}) collective-permute-start(bf16[256,1536]{1,0:T(8,128)(2,1)} %param.29), channel_id=1, source_target_pairs={{0,16},{4,20},{8,24},{12,28},{16,0},{20,4},{24,8},{28,12},{1,17},{... | collective-permute-start | bytes 2359304 | tf_op jit(solution)/shard_map/ppermute | solution.py:36
  121.6 30.7 %collective-permute-start.29 = (bf16[1024,768]{1,0:T(8,128)(2,1)S(1)}, bf16[1024,768]{1,0:T(8,128)(2,1)}, u32[]{:S(2)}, u32[]{:S(2)}) collective-permute-start(bf16[1024,768]{1,0:T(8,128)(2,1)S(1)} %pad_maximum_fusion.3.refs_0_.refs_2_), channel_id=1, source_target_pairs={{0,4},{4,0},{8,12},{12,8},{16,20},{20,16},{24,28},{28,24},{1,5},{5... | collective-permute-start | bytes 4718600 | tf_op jit(solution)/shard_map/ppermute | solution.py:36
  123.4 28.9 %collective-permute-start.30 = (bf16[1024,768]{1,0:T(8,128)(2,1)S(1)}, bf16[1024,768]{1,0:T(8,128)(2,1)}, u32[]{:S(2)}, u32[]{:S(2)}) collective-permute-start(bf16[1024,768]{1,0:T(8,128)(2,1)S(1)} %pad_maximum_fusion.4.refs_2_.refs_4_), channel_id=1, source_target_pairs={{0,4},{4,0},{8,12},{12,8},{16,20},{20,16},{24,28},{28,24},{1,5},{5... | collective-permute-start | bytes 4718600 | tf_op jit(solution)/shard_map/ppermute | solution.py:36
  142.8 33.4 %collective-permute-start.27 = (bf16[512,1536]{1,0:T(8,128)(2,1)}, bf16[512,1536]{1,0:T(8,128)(2,1)}, u32[]{:S(2)}, u32[]{:S(2)}) collective-permute-start(bf16[512,1536]{1,0:T(8,128)(2,1)} %pad_maximum_fusion.1), channel_id=1, source_target_pairs={{0,16},{4,20},{8,24},{12,28},{16,0},{20,4},{24,8},{28,12},{1,17},{... | collective-permute-start | bytes 4718600 | tf_op jit(solution)/shard_map/ppermute | solution.py:36
  143.7 33.1 %collective-permute-start.28 = (bf16[512,1536]{1,0:T(8,128)(2,1)}, bf16[512,1536]{1,0:T(8,128)(2,1)}, u32[]{:S(2)}, u32[]{:S(2)}) collective-permute-start(bf16[512,1536]{1,0:T(8,128)(2,1)} %pad_maximum_fusion.2), channel_id=1, source_target_pairs={{0,8},{4,12},{8,0},{12,4},{16,24},{20,28},{24,16},{28,20},{1,9},{5... | collective-permute-start | bytes 4718600 | tf_op jit(solution)/shard_map/ppermute | solution.py:36
  152.2 114.2 %reduce-scatter.7.cloned.1.call-start = ((), (), s32[]{:S(2)}) async-start(), calls=%async_computation.6 | async-start | bytes 2621440 | tf_op jit(solution)/shard_map/reduce_scatter | solution.py:885
  179.5 19.1 %collective-permute-start.31 = (bf16[1024,1536]{1,0:T(8,128)(2,1)}, bf16[1024,1536]{1,0:T(8,128)(2,1)}, u32[]{:S(2)}, u32[]{:S(2)}) collective-permute-start(bf16[1024,1536]{1,0:T(8,128)(2,1)} %constant_dynamic-update-slice_fusion.8.wg0.refs_2_), channel_id=1, source_target_pairs={{0,4},{4,0},{8,12},{12,8},{16,20},{20,16},{24,28},{28,24},{1,5},{5... | collective-permute-start | bytes 9437192 | tf_op jit(solution)/shard_map/ppermute | solution.py:36
  182.4 16.2 %collective-permute-start.32 = (bf16[1024,1536]{1,0:T(8,128)(2,1)S(1)}, bf16[1024,1536]{1,0:T(8,128)(2,1)}, u32[]{:S(2)}, u32[]{:S(2)}) collective-permute-start(bf16[1024,1536]{1,0:T(8,128)(2,1)S(1)} %pad_maximum_fusion.wu0.refs_4_), channel_id=1, source_target_pairs={{0,4},{4,0},{8,12},{12,8},{16,20},{20,16},{24,28},{28,24},{1,5},{5... | collective-permute-start | bytes 9437192 | tf_op jit(solution)/shard_map/ppermute | solution.py:36
  223.7 91.8 %all-gather.7.cloned.1.call-start = ((), (), s32[]{:S(2)}) async-start(), calls=%async_computation.7 | async-start | bytes 2621440 | tf_op jit(solution)/shard_map/all_gather | solution.py:889
  230.7 5.9 %collective-permute-start.33 = (bf16[1024,1536]{1,0:T(8,128)(2,1)}, bf16[1024,1536]{1,0:T(8,128)(2,1)S(1)}, u32[]{:S(2)}, u32[]{:S(2)}) collective-permute-start(bf16[1024,1536]{1,0:T(8,128)(2,1)} %get-tuple-element.215), channel_id=1, source_target_pairs={{0,4},{4,0},{8,12},{12,8},{16,20},{20,16},{24,28},{28,24},{1,5},{5... | collective-permute-start | bytes 9437192 | tf_op jit(solution)/shard_map/ppermute | solution.py:36
  230.7 10.4 %collective-permute-start.34 = (bf16[1024,1536]{1,0:T(8,128)(2,1)}, bf16[1024,1536]{1,0:T(8,128)(2,1)S(1)}, u32[]{:S(2)}, u32[]{:S(2)}) collective-permute-start(bf16[1024,1536]{1,0:T(8,128)(2,1)} %get-tuple-element.216), channel_id=1, source_target_pairs={{0,4},{4,0},{8,12},{12,8},{16,20},{20,16},{24,28},{28,24},{1,5},{5... | collective-permute-start | bytes 9437192 | tf_op jit(solution)/shard_map/ppermute | solution.py:36
  253.7 36.6 %collective-permute-start.35 = (bf16[512,1536]{1,0:T(8,128)(2,1)}, bf16[512,1536]{1,0:T(8,128)(2,1)S(1)}, u32[]{:S(2)}, u32[]{:S(2)}) collective-permute-start(bf16[512,1536]{1,0:T(8,128)(2,1)} %get-tuple-element.224), channel_id=1, source_target_pairs={{0,8},{4,12},{8,0},{12,4},{16,24},{20,28},{24,16},{28,20},{1,9},{5... | collective-permute-start | bytes 4718600 | tf_op jit(solution)/shard_map/ppermute | solution.py:36
  255.2 36.3 %collective-permute-start.36 = (bf16[512,1536]{1,0:T(8,128)(2,1)}, bf16[512,1536]{1,0:T(8,128)(2,1)S(1)}, u32[]{:S(2)}, u32[]{:S(2)}) collective-permute-start(bf16[512,1536]{1,0:T(8,128)(2,1)} %get-tuple-element.225), channel_id=1, source_target_pairs={{0,16},{4,20},{8,24},{12,28},{16,0},{20,4},{24,8},{28,12},{1,17},{... | collective-permute-start | bytes 4718600 | tf_op jit(solution)/shard_map/ppermute | solution.py:36
  270.1 90.8 %reduce-scatter.9.cloned.1.call-start = ((), (), s32[]{:S(2)}) async-start(), calls=%async_computation.8 | async-start | bytes 2621440 | tf_op jit(solution)/shard_map/reduce_scatter | solution.py:885
  296.6 5.1 collective-permute-start.37
  296.7 5.9 %collective-permute-start.38 = (bf16[1024,768]{1,0:T(8,128)(2,1)}, bf16[1024,768]{1,0:T(8,128)(2,1)S(1)}, u32[]{:S(2)}, u32[]{:S(2)}) collective-permute-start(bf16[1024,768]{1,0:T(8,128)(2,1)} %get-tuple-element.233), channel_id=1, source_target_pairs={{0,4},{4,0},{8,12},{12,8},{16,20},{20,16},{24,28},{28,24},{1,5},{5... | collective-permute-start | bytes 4718600 | tf_op jit(solution)/shard_map/ppermute | solution.py:36
  315.5 93.1 %all-gather.9.cloned.1.call-start = ((), (), s32[]{:S(2)}) async-start(), calls=%async_computation.9 | async-start | bytes 2621440 | tf_op jit(solution)/shard_map/all_gather | solution.py:889
  315.6 29.0 %collective-permute-start.39 = (bf16[256,1536]{1,0:T(8,128)(2,1)S(1)}, bf16[256,1536]{1,0:T(8,128)(2,1)S(1)}, u32[]{:S(2)}, u32[]{:S(2)}) collective-permute-start(bf16[256,1536]{1,0:T(8,128)(2,1)S(1)} %copy-done.56), channel_id=1, source_target_pairs={{0,16},{4,20},{8,24},{12,28},{16,0},{20,4},{24,8},{28,12},{1,17},{... | collective-permute-start | bytes 2359304 | tf_op jit(solution)/shard_map/ppermute | solution.py:36
  317.1 27.5 %collective-permute-start.40 = (bf16[256,1536]{1,0:T(8,128)(2,1)S(1)}, bf16[256,1536]{1,0:T(8,128)(2,1)S(1)}, u32[]{:S(2)}, u32[]{:S(2)}) collective-permute-start(bf16[256,1536]{1,0:T(8,128)(2,1)S(1)} %copy-done.55), channel_id=1, source_target_pairs={{0,8},{4,12},{8,0},{12,4},{16,24},{20,28},{24,16},{28,20},{1,9},{5... | collective-permute-start | bytes 2359304 | tf_op jit(solution)/shard_map/ppermute | solution.py:36
  318.6 34.4 %collective-permute-start.41 = (bf16[512,768]{1,0:T(8,128)(2,1)}, bf16[512,768]{1,0:T(8,128)(2,1)S(1)}, u32[]{:S(2)}, u32[]{:S(2)}) collective-permute-start(bf16[512,768]{1,0:T(8,128)(2,1)} %get-tuple-element.244), channel_id=1, source_target_pairs={{0,8},{4,12},{8,0},{12,4},{16,24},{20,28},{24,16},{28,20},{1,9},{5... | collective-permute-start | bytes 2359304 | tf_op jit(solution)/shard_map/ppermute | solution.py:36
  319.1 33.8 %collective-permute-start.42 = (bf16[512,768]{1,0:T(8,128)(2,1)}, bf16[512,768]{1,0:T(8,128)(2,1)S(1)}, u32[]{:S(2)}, u32[]{:S(2)}) collective-permute-start(bf16[512,768]{1,0:T(8,128)(2,1)} %get-tuple-element.245), channel_id=1, source_target_pairs={{0,16},{4,20},{8,24},{12,28},{16,0},{20,4},{24,8},{28,12},{1,17},{... | collective-permute-start | bytes 2359304 | tf_op jit(solution)/shard_map/ppermute | solution.py:36
  353.1 4.4 collective-permute-start.44
  363.2 91.0 %reduce-scatter.11.cloned.1.call-start = ((), (), s32[]{:S(2)}) async-start(), calls=%async_computation.10 | async-start | bytes 2621440 | tf_op jit(solution)/shard_map/reduce_scatter | solution.py:885
  363.5 14.0 %collective-permute-start.45 = (bf16[1024,256]{1,0:T(8,128)(2,1)}, bf16[1024,256]{1,0:T(8,128)(2,1)S(1)}, u32[]{:S(2)}, u32[]{:S(2)}) collective-permute-start(bf16[1024,256]{1,0:T(8,128)(2,1)} %add_convert_fusion.7), channel_id=1, source_target_pairs={{0,8},{4,12},{8,0},{12,4},{16,24},{20,28},{24,16},{28,20},{1,9},{5... | collective-permute-start | bytes 1572872 | tf_op jit(solution)/shard_map/ppermute | solution.py:36
  365.0 13.7 %collective-permute-start.46 = (bf16[1024,256]{1,0:T(8,128)(2,1)}, bf16[1024,256]{1,0:T(8,128)(2,1)S(1)}, u32[]{:S(2)}, u32[]{:S(2)}) collective-permute-start(bf16[1024,256]{1,0:T(8,128)(2,1)} %get-tuple-element.252), channel_id=1, source_target_pairs={{0,16},{4,20},{8,24},{12,28},{16,0},{20,4},{24,8},{28,12},{1,17},{... | collective-permute-start | bytes 1572872 | tf_op jit(solution)/shard_map/ppermute | solution.py:36
  380.4 7.1 %collective-permute-start.47 = (bf16[512,256]{1,0:T(8,128)(2,1)S(1)}, bf16[512,256]{1,0:T(8,128)(2,1)S(1)}, u32[]{:S(2)}, u32[]{:S(2)}) collective-permute-start(bf16[512,256]{1,0:T(8,128)(2,1)S(1)} %get-tuple-element.261), channel_id=1, source_target_pairs={{0,16},{4,20},{8,24},{12,28},{16,0},{20,4},{24,8},{28,12},{1,17},{... | collective-permute-start | bytes 786440 | tf_op jit(solution)/shard_map/ppermute | solution.py:36
  381.6 6.5 %collective-permute-start.48 = (bf16[512,256]{1,0:T(8,128)(2,1)S(1)}, bf16[512,256]{1,0:T(8,128)(2,1)S(1)}, u32[]{:S(2)}, u32[]{:S(2)}) collective-permute-start(bf16[512,256]{1,0:T(8,128)(2,1)S(1)} %get-tuple-element.262), channel_id=1, source_target_pairs={{0,8},{4,12},{8,0},{12,4},{16,24},{20,28},{24,16},{28,20},{1,9},{5... | collective-permute-start | bytes 786440 | tf_op jit(solution)/shard_map/ppermute | solution.py:36
  408.6 94.0 %all-gather.11.cloned.1.call-start = ((), (), s32[]{:S(2)}) async-start(), calls=%async_computation.11 | async-start | bytes 2621440 | tf_op jit(solution)/shard_map/all_gather | solution.py:889
  408.9 10.9 %collective-permute-start.49 = (bf16[256,768]{1,0:T(8,128)(2,1)S(1)}, bf16[256,768]{1,0:T(8,128)(2,1)S(1)}, u32[]{:S(2)}, u32[]{:S(2)}) collective-permute-start(bf16[256,768]{1,0:T(8,128)(2,1)S(1)} %add_convert_fusion.15), channel_id=1, source_target_pairs={{0,16},{4,20},{8,24},{12,28},{16,0},{20,4},{24,8},{28,12},{1,17},{... | collective-permute-start | bytes 1179656 | tf_op jit(solution)/shard_map/ppermute | solution.py:36
  410.4 10.6 %collective-permute-start.50 = (bf16[256,768]{1,0:T(8,128)(2,1)S(1)}, bf16[256,768]{1,0:T(8,128)(2,1)S(1)}, u32[]{:S(2)}, u32[]{:S(2)}) collective-permute-start(bf16[256,768]{1,0:T(8,128)(2,1)S(1)} %add_convert_fusion.14), channel_id=1, source_target_pairs={{0,8},{4,12},{8,0},{12,4},{16,24},{20,28},{24,16},{28,20},{1,9},{5... | collective-permute-start | bytes 1179656 | tf_op jit(solution)/shard_map/ppermute | solution.py:36
  425.9 5.9 %collective-permute-start.52 = (bf16[1024,768]{1,0:T(8,128)(2,1)}, bf16[1024,768]{1,0:T(8,128)(2,1)S(1)}, u32[]{:S(2)}, u32[]{:S(2)}) collective-permute-start(bf16[1024,768]{1,0:T(8,128)(2,1)} %get-tuple-element.277), channel_id=1, source_target_pairs={{0,4},{4,0},{8,12},{12,8},{16,20},{20,16},{24,28},{28,24},{1,5},{5... | collective-permute-start | bytes 4718600 | tf_op jit(solution)/shard_map/ppermute | solution.py:36
  442.3 20.0 %collective-permute-start.53 = (bf16[512,768]{1,0:T(8,128)(2,1)}, bf16[512,768]{1,0:T(8,128)(2,1)}, u32[]{:S(2)}, u32[]{:S(2)}) collective-permute-start(bf16[512,768]{1,0:T(8,128)(2,1)} %get-tuple-element.284), channel_id=1, source_target_pairs={{0,8},{4,12},{8,0},{12,4},{16,24},{20,28},{24,16},{28,20},{1,9},{5... | collective-permute-start | bytes 2359304 | tf_op jit(solution)/shard_map/ppermute | solution.py:36
  443.8 19.6 %collective-permute-start.54 = (bf16[512,768]{1,0:T(8,128)(2,1)}, bf16[512,768]{1,0:T(8,128)(2,1)}, u32[]{:S(2)}, u32[]{:S(2)}) collective-permute-start(bf16[512,768]{1,0:T(8,128)(2,1)} %get-tuple-element.285), channel_id=1, source_target_pairs={{0,16},{4,20},{8,24},{12,28},{16,0},{20,4},{24,8},{28,12},{1,17},{... | collective-permute-start | bytes 2359304 | tf_op jit(solution)/shard_map/ppermute | solution.py:36
  451.0 18.8 %collective-permute-start.58 = (f32[1,256]{1,0:T(1,128)S(1)}, f32[1,256]{1,0:T(1,128)S(1)}, u32[]{:S(2)}, u32[]{:S(2)}) collective-permute-start(f32[1,256]{1,0:T(1,128)S(1)} %add.165), channel_id=1, source_target_pairs={{0,8},{4,12},{8,0},{12,4},{16,24},{20,28},{24,16},{28,20},{1,9},{5... | collective-permute-start | bytes 3080 | tf_op jit(solution)/shard_map/ppermute | solution.py:36
  467.4 10.5 %collective-permute-start.55 = (bf16[256,768]{1,0:T(8,128)(2,1)}, bf16[256,768]{1,0:T(8,128)(2,1)}, u32[]{:S(2)}, u32[]{:S(2)}) collective-permute-start(bf16[256,768]{1,0:T(8,128)(2,1)} %add_convert_fusion.12), channel_id=1, source_target_pairs={{0,16},{4,20},{8,24},{12,28},{16,0},{20,4},{24,8},{28,12},{1,17},{... | collective-permute-start | bytes 1179656 | tf_op jit(solution)/shard_map/ppermute | solution.py:36
  467.9 10.1 %collective-permute-start.56 = (bf16[256,768]{1,0:T(8,128)(2,1)}, bf16[256,768]{1,0:T(8,128)(2,1)}, u32[]{:S(2)}, u32[]{:S(2)}) collective-permute-start(bf16[256,768]{1,0:T(8,128)(2,1)} %add_convert_fusion.11), channel_id=1, source_target_pairs={{0,8},{4,12},{8,0},{12,4},{16,24},{20,28},{24,16},{28,20},{1,9},{5... | collective-permute-start | bytes 1179656 | tf_op jit(solution)/shard_map/ppermute | solution.py:36
  469.8 7.9 %collective-permute-start.59 = (f32[1,256]{1,0:T(1,128)S(1)}, f32[1,256]{1,0:T(1,128)S(1)}, u32[]{:S(2)}, u32[]{:S(2)}) collective-permute-start(f32[1,256]{1,0:T(1,128)S(1)} %add.166), channel_id=1, source_target_pairs={{0,16},{4,20},{8,24},{12,28},{16,0},{20,4},{24,8},{28,12},{1,17},{... | collective-permute-start | bytes 3080 | tf_op jit(solution)/shard_map/ppermute | solution.py:36
  483.7 6.2 %collective-permute-start.60 = (f32[1,544]{1,0:T(1,128)S(1)}, f32[1,544]{1,0:T(1,128)S(1)}, u32[]{:S(2)}, u32[]{:S(2)}) collective-permute-start(f32[1,544]{1,0:T(1,128)S(1)} %broadcast_in_dim.82), channel_id=1, source_target_pairs={{0,1},{1,0},{2,3},{3,2},{4,5},{5,4},{6,7},{7,6},{8,9},{9,8},{10,11... | collective-permute-start | bytes 6536 | tf_op jit(solution)/shard_map/ppermute | solution.py:1108
  490.0 5.5 %collective-permute-start.61 = (f32[1,544]{1,0:T(1,128)S(1)}, f32[1,544]{1,0:T(1,128)S(1)}, u32[]{:S(2)}, u32[]{:S(2)}) collective-permute-start(f32[1,544]{1,0:T(1,128)S(1)} %reshape_add_fusion), channel_id=1, source_target_pairs={{0,2},{1,3},{2,0},{3,1},{4,6},{5,7},{6,4},{7,5},{8,10},{9,11},{10,... | collective-permute-start | bytes 6536 | tf_op jit(solution)/shard_map/ppermute | solution.py:1108
  (93 other events, 516.7 us)
Sparse Core Ops, SparseCore 0:
  94.8 44.1 reduce-scatter.4
  152.3 46.2 all-gather.4
  223.8 42.5 reduce-scatter.6
  270.2 45.2 all-gather.6
  318.2 42.5 reduce-scatter.8
  363.3 45.2 all-gather.8
  411.6 42.5 reduce-scatter.10
  457.2 45.3 all-gather.10

commit v5 on v4

--- a/solution.py
+++ b/solution.py
@@ -997,10 +997,10 @@
     my_attn = sum_of_parts(attn_part)
     my_post = on_quarter(post_kernel, "post", (my_tokens, my_attn), (gain_post,), (BF16,))[0]
     post_low = all_parts(my_post)
-    gather_step(wide, pair, 0, before=down_got)
+    gather_step(wide, pair, 0, before=down_got, beside=(my_tokens,))
     side_a, side_b = gather_end(downs)
     grad_act = from_width(
-        "grad_act", after(cotangent, my_post), (side_a, 0, middle), (side_b, 0, middle)
+        "grad_act", after(cotangent, my_post), (side_a, 0, middle), (side_b, 0, middle), tile=middle
     )
     gather_rest(wide, pair, 1, beside=(my_post, grad_act))
     wg, wu = gather_end(wide)

time: 525 us -> 522 us (level)
    unnamed x187 -> x193, local copies, waits for them, and re-layouts: 26.8 us -> 24.9 us
  transfers between devices with their start and end apart: 70 -> 70, of which waited for: 44 -> 45; matrix products, arithmetic and copies ran while one was open for 11% -> 11% of each run, Pallas kernels for 27% -> 27%
where the time goes in v5:
time: 522 us; the launch traced here: 512 us
  waiting for transfers between devices  198 us (38%)
  Pallas kernels  172 us (33%)
  starting transfers between devices  53 us (10%)
  local copies, waits for them, and re-layouts  39.6 us (8%)
  other arithmetic  33.9 us (6%)
  between operations  15.7 us (3%)
    ppermute x60, waiting for transfers between devices, exchange(): return lax.ppermute(block, 'blk', [(i, i ^ bit) for i in range(n)])  148 us
    pallas_call x24, Pallas kernels, call(): pl.pallas_call(kernel, out_shape=out_shape, compiler_params=pltpu.Compile...  141 us
    ppermute x60, starting transfers between devices, exchange(): return lax.ppermute(block, 'blk', [(i, i ^ bit) for i in range(n)])  50.1 us
    all_gather x4, waiting for transfers between devices, all_parts(): return lax.all_gather(mine, 'fsdp', axis=0, tiled=True)  36.6 us
    unnamed x193, local copies, waits for them, and re-layouts  24.9 us
    pallas_call x1, Pallas kernels, attend_back(): pl.pallas_call(functools.partial(attend_back_kernel, span, head, heads),...  20.4 us
    reduce_scatter x4, waiting for transfers between devices, sum_of_parts(): return lax.psum_scatter(part, 'fsdp', scatter_dimension=0, tiled=True)  11 us
    pallas_call x1, Pallas kernels, attend(): pl.pallas_call(functools.partial(attend_kernel, span, head, heads), grid_...  10.7 us
  transfers between devices with their start and end apart: 70, of which 45 were waited for; matrix products, arithmetic and copies ran while one was open for 11% of the time, Pallas kernels for 27%

profile of v5, /device:TPU:0, one launch (start us, length us, event | category | flops | bytes accessed | tf_op | source)
XLA Modules:
  0.0 512.2 jit_solution(1664816807955540323)
XLA Ops:
  9.9 3.0 collective-permute-start
  16.9 1.7 constant_dynamic-update-slice_fusion.4
  25.9 2.1 enter.1
  29.3 4.1 collective-permute-done.5
  39.4 2.0 copy-done.7
  41.4 4.5 project_keys.1
  48.1 5.9 %project_queries.1 = (f32[512,512]{1,0:T(8,128)}, bf16[512,512]{1,0:T(8,128)(2,1)}) custom-call(bf16[512,2048]{1,0:T(8,128)(2,1)} %get-tuple-element.171.normed_ref.refs_0_, bf16[1024,512]{1,0:T(8,128)(2,1)} %constant_dynamic-update-slice_fusion.2.w0.refs_2_, bf16[1024,512]{1,0:T(8,128)(2,1)} %collective-permute-done.8.w1.refs_3_, f32[512,128]{1,0:T(8,128)} %copy-done.3, ...), custom_call_target="tpu_custom_call" | custom-call | tf_op jit(solution)/shard_map/project_queries/pallas_call | solution.py:173
  57.1 10.2 %collective-permute-done.13 = bf16[1024,256]{1,0:T(8,128)(2,1)S(1)} collective-permute-done((bf16[1024,256]{1,0:T(8,128)(2,1)S(1)}, bf16[1024,256]{1,0:T(8,128)(2,1)S(1)}, u32[]{:S(2)}, u32[]{:S(2)}) %collective-permute-start.13) | collective-permute-done | bytes 524320 | tf_op jit(solution)/shard_map/ppermute | solution.py:36
  73.8 10.7 %attend.1 = (bf16[512,512]{1,0:T(8,128)(2,1)S(1)}, f32[2,2,512]{2,1,0:T(2,128)S(1)}) custom-call(s32[18]{0:T(128)S(1)} %pad_add_fusion.1.sc, bf16[512,512]{1,0:T(8,128)(2,1)S(1)} %copy-done.11, bf16[2048,256]{1,0:T(8,128)(2,1)} %copy-done.79, bf16[2048,256]{1,0:T(8,128)(2,1)} %copy-done.86, bf16[2048,256]{1,0:T(8,128)(2,1)} %copy-done.40, ...), custom_call_target="tpu_custom_call" | custom-call | flops 8589934592 | bytes 2097152 | tf_op jit(solution)/shard_map/attend/pallas_call | solution.py:811
  89.3 5.0 attention_out.1
  94.6 3.5 collective-permute-done.21
  102.5 16.6 %collective-permute-done.23 = bf16[512,768]{1,0:T(8,128)(2,1)S(1)} collective-permute-done((bf16[512,768]{1,0:T(8,128)(2,1)}, bf16[512,768]{1,0:T(8,128)(2,1)S(1)}, u32[]{:S(2)}, u32[]{:S(2)}) %collective-permute-start.23) | collective-permute-done | bytes 786464 | tf_op jit(solution)/shard_map/ppermute | solution.py:36
  121.8 1.9 constant_dynamic-slice_fusion.1.tokens_ref
  126.9 10.1 %collective-permute-done.25 = bf16[256,1536]{1,0:T(8,128)(2,1)S(1)} collective-permute-done((bf16[256,1536]{1,0:T(8,128)(2,1)}, bf16[256,1536]{1,0:T(8,128)(2,1)S(1)}, u32[]{:S(2)}, u32[]{:S(2)}) %collective-permute-start.25) | collective-permute-done | bytes 786464 | tf_op jit(solution)/shard_map/ppermute | solution.py:36
  137.2 2.7 pad_maximum_fusion.1
  139.9 2.4 pad_maximum_fusion.2
  145.0 2.1 constant_dynamic-update-slice_fusion.10
  148.0 2.3 post.1
  150.4 8.0 %grad_act.1.grad_ref = bf16[512,1536]{1,0:T(8,128)(2,1)} custom-call(bf16[512,2048]{1,0:T(8,128)(2,1)} %copy-done, bf16[1024,768]{1,0:T(8,128)(2,1)} %copy-done.12, bf16[1024,768]{1,0:T(8,128)(2,1)} %collective-permute-done.29.refs_1_.refs_3_, bf16[1024,768]{1,0:T(8,128)(2,1)} %copy-done.13, bf16[1024,768]{1,0:T(8,128)(2,1)} %collective-permute-done.30.refs_3_.refs_5_), custom_call_target="tpu_custom_call" | custom-call | tf_op jit(solution)/shard_map/grad_act/pallas_call | solution.py:173
  158.4 16.9 %collective-permute-done.27 = bf16[512,1536]{1,0:T(8,128)(2,1)} collective-permute-done((bf16[512,1536]{1,0:T(8,128)(2,1)}, bf16[512,1536]{1,0:T(8,128)(2,1)}, u32[]{:S(2)}, u32[]{:S(2)}) %collective-permute-start.27) | collective-permute-done | bytes 1572896 | tf_op jit(solution)/shard_map/ppermute | solution.py:36
  176.4 2.7 constant_dynamic-update-slice_fusion.8.wg0.refs_2_
  182.4 13.7 %all-gather.5.cloned.1.call-done.post_ref.refs_0_ = bf16[512,2048]{1,0:T(8,128)(2,1)} async-done(((bf16[128,2048]{1,0:T(8,128)(2,1)}), bf16[512,2048]{1,0:T(8,128)(2,1)}) %all-gather.5.cloned.1.call-update) | async-done | bytes 2097168 | tf_op jit(solution)/shard_map/all_gather | solution.py:889
  196.1 12.3 %hidden_units.1 = (bf16[512,1536]{1,0:T(8,128)(2,1)}, bf16[512,1536]{1,0:T(8,128)(2,1)}, bf16[512,1536]{1,0:T(8,128)(2,1)}) custom-call(bf16[512,2048]{1,0:T(8,128)(2,1)} %all-gather.5.cloned.1.call-done.post_ref.refs_0_, bf16[1024,1536]{1,0:T(8,128)(2,1)} %constant_dynamic-update-slice_fusion.8.wg0.refs_2_, ...), custom_call_target="tpu_custom_call" | custom-call | tf_op jit(solution)/shard_map/hidden_units/pallas_call | solution.py:173
  208.4 12.7 %grad_post.1 = bf16[512,2048]{1,0:T(8,128)(2,1)} custom-call(bf16[512,1536]{1,0:T(8,128)(2,1)} %get-tuple-element.213.refs_0_.refs_1_, bf16[512,1536]{1,0:T(8,128)(2,1)} %get-tuple-element.214.refs_1_.refs_2_, bf16[1024,1536]{1,0:T(8,128)(2,1)} %constant_dynamic-update-slice_fusion.8.wg0.refs_2_, bf16[1024,1536]{1,0:T(8,128)(2,1)} %collective-permute-done.31.wg1.refs_3_, ...), custom_call_target="tpu_custom_call" | custom-call | tf_op jit(solution)/shard_map/grad_post/pallas_call | solution.py:173
  221.3 7.0 %units_grad_away.1 = (bf16[1024,1536]{1,0:T(8,128)(2,1)}, bf16[1024,1536]{1,0:T(8,128)(2,1)}) custom-call(bf16[512,2048]{1,0:T(8,128)(2,1)} %all-gather.5.cloned.1.call-done.post_ref.refs_0_, bf16[512,1536]{1,0:T(8,128)(2,1)} %get-tuple-element.213.refs_0_.refs_1_, bf16[512,1536]{1,0:T(8,128)(2,1)} %get-tuple-element.214.refs_1_.refs_2_), custom_call_target="tpu_custom_call" | custom-call | tf_op jit(solution)/shard_map/units_grad_away/pallas_call | solution.py:173
  228.7 5.4 %collective-permute-done.33.refs_3_ = bf16[1024,1536]{1,0:T(8,128)(2,1)S(1)} collective-permute-done((bf16[1024,1536]{1,0:T(8,128)(2,1)}, bf16[1024,1536]{1,0:T(8,128)(2,1)S(1)}, u32[]{:S(2)}, u32[]{:S(2)}) %collective-permute-start.33) | collective-permute-done | bytes 3145760 | tf_op jit(solution)/shard_map/ppermute | solution.py:36
  234.1 4.5 collective-permute-done.34.refs_4_
  240.3 10.9 %units_grad.1 = (bf16[512,1536]{1,0:T(8,128)(2,1)}, bf16[512,1536]{1,0:T(8,128)(2,1)}, bf16[512,1536]{1,0:T(8,128)(2,1)}, bf16[512,1536]{1,0:T(8,128)(2,1)}) custom-call(s32[40]{0:T(128)S(1)} %copy-done.10, bf16[512,2048]{1,0:T(8,128)(2,1)} %all-gather.5.cloned.1.call-done.post_ref.refs_0_, bf16[512,1536]{1,0:T(8,128)(2,1)} %get-tuple-element.213.refs_0_.refs_1_, ...), custom_call_target="tpu_custom_call" | custom-call | tf_op jit(solution)/shard_map/units_grad/pallas_call | solution.py:173
  254.2 1.9 constant_dynamic-slice_fusion.cotangent_ref
  256.1 7.9 %reduce-scatter.7.cloned.1.call-done.grad_ref = bf16[128,2048]{1,0:T(8,128)(2,1)} async-done(((bf16[512,2048]{1,0:T(8,128)(2,1)}), bf16[128,2048]{1,0:T(8,128)(2,1)}) %reduce-scatter.7.cloned.1.call-update) | async-done | bytes 524304 | tf_op jit(solution)/shard_map/reduce_scatter | solution.py:885
  264.0 3.6 grad_hidden.1
  267.8 7.9 %units_out.1 = bf16[512,2048]{1,0:T(8,128)(2,1)} custom-call(bf16[512,1536]{1,0:T(8,128)(2,1)} %get-tuple-element.231.refs_0_.refs_1_.refs_2_, bf16[512,1536]{1,0:T(8,128)(2,1)} %get-tuple-element.231.refs_0_.refs_1_.refs_2_, bf16[1024,768]{1,0:T(8,128)(2,1)} %copy-done.12, bf16[1024,768]{1,0:T(8,128)(2,1)} %collective-permute-done.29.refs_1_.refs_3_, ...), custom_call_target="tpu_custom_call" | custom-call | tf_op jit(solution)/shard_map/units_out/pallas_call | solution.py:173
  275.7 12.1 %collective-permute-done.35 = bf16[512,1536]{1,0:T(8,128)(2,1)S(1)} collective-permute-done((bf16[512,1536]{1,0:T(8,128)(2,1)}, bf16[512,1536]{1,0:T(8,128)(2,1)S(1)}, u32[]{:S(2)}, u32[]{:S(2)}) %collective-permute-start.35) | collective-permute-done | bytes 1572896 | tf_op jit(solution)/shard_map/ppermute | solution.py:36
  289.1 5.0 down_grad_away.1
  295.9 1.8 collective-permute-done.37.refs_3_
  297.8 2.2 collective-permute-done.38.refs_4_
  301.2 8.0 %down_grad.1 = (bf16[512,768]{1,0:T(8,128)(2,1)}, bf16[512,768]{1,0:T(8,128)(2,1)}, bf16[512,768]{1,0:T(8,128)(2,1)}, bf16[512,768]{1,0:T(8,128)(2,1)}) custom-call(s32[40]{0:T(128)S(1)} %copy-done.10, bf16[512,2048]{1,0:T(8,128)(2,1)} %copy-done, bf16[512,1536]{1,0:T(8,128)(2,1)} %get-tuple-element.231.refs_0_.refs_1_.refs_2_, ...), custom_call_target="tpu_custom_call" | custom-call | tf_op jit(solution)/shard_map/down_grad/pallas_call | solution.py:173
  309.2 3.8 all-gather.7.cloned.1.call-done.left_ref.refs_1_
  317.2 4.4 grad_context.1.do_ref
  321.6 20.4 %attend_back.1 = (f32[512,512]{1,0:T(8,128)}, bf16[2048,256]{1,0:T(8,128)(2,1)}, bf16[2048,256]{1,0:T(8,128)(2,1)}, bf16[2048,256]{1,0:T(8,128)(2,1)}, bf16[2048,256]{1,0:T(8,128)(2,1)}) custom-call(s32[18]{0:T(128)S(1)} %pad_add_fusion.1.sc, bf16[512,512]{1,0:T(8,128)(2,1)} %get-tuple-element.173.q_ref, bf16[512,512]{1,0:T(8,128)(2,1)} %grad_context.1.do_ref, ...), custom_call_target="tpu_custom_call" | custom-call | flops 21474836480 | bytes 8388608 | tf_op jit(solution)/shard_map/attend_back/pallas_call | solution.py:856
  342.1 8.4 %collective-permute-done.41 = bf16[512,768]{1,0:T(8,128)(2,1)S(1)} collective-permute-done((bf16[512,768]{1,0:T(8,128)(2,1)}, bf16[512,768]{1,0:T(8,128)(2,1)S(1)}, u32[]{:S(2)}, u32[]{:S(2)}) %collective-permute-start.41) | collective-permute-done | bytes 786464 | tf_op jit(solution)/shard_map/ppermute | solution.py:36
  358.3 2.3 layer_out_rows.1
  364.1 10.5 %collective-permute-done.45 = bf16[1024,256]{1,0:T(8,128)(2,1)S(1)} collective-permute-done((bf16[1024,256]{1,0:T(8,128)(2,1)S(1)}, bf16[1024,256]{1,0:T(8,128)(2,1)S(1)}, u32[]{:S(2)}, u32[]{:S(2)}) %collective-permute-start.45) | collective-permute-done | bytes 524320 | tf_op jit(solution)/shard_map/ppermute | solution.py:36
  379.6 3.5 queries_back.1
  386.3 3.0 keys_back.1
  389.3 6.4 %grad_normed.1 = bf16[512,2048]{1,0:T(8,128)(2,1)} custom-call(bf16[512,512]{1,0:T(8,128)(2,1)} %get-tuple-element.258.refs_0_.refs_2_, bf16[512,512]{1,0:T(8,128)(2,1)} %get-tuple-element.275.refs_1_.refs_4_, bf16[1024,512]{1,0:T(8,128)(2,1)} %constant_dynamic-update-slice_fusion.2.w0.refs_2_, bf16[1024,512]{1,0:T(8,128)(2,1)} %collective-permute-done.8.w1.refs_3_, ...), custom_call_target="tpu_custom_call" | custom-call | tf_op jit(solution)/shard_map/grad_normed/pallas_call | solution.py:173
  395.7 10.4 %all-gather.9.cloned.1.call-done.value_ref = bf16[512,2048]{1,0:T(8,128)(2,1)} async-done(((bf16[128,2048]{1,0:T(8,128)(2,1)}), bf16[512,2048]{1,0:T(8,128)(2,1)}) %all-gather.9.cloned.1.call-update) | async-done | bytes 2097168 | tf_op jit(solution)/shard_map/all_gather | solution.py:889
  409.4 7.9 %collective-permute-done.49 = bf16[256,768]{1,0:T(8,128)(2,1)S(1)} collective-permute-done((bf16[256,768]{1,0:T(8,128)(2,1)S(1)}, bf16[256,768]{1,0:T(8,128)(2,1)S(1)}, u32[]{:S(2)}, u32[]{:S(2)}) %collective-permute-start.49) | collective-permute-done | bytes 393248 | tf_op jit(solution)/shard_map/ppermute | solution.py:36
  418.5 4.8 attention_grad_away.1
  424.0 3.0 collective-permute-done.51.refs_6_
  427.0 2.2 collective-permute-done.52.refs_7_
  430.4 9.3 %attention_grad.1 = (bf16[512,768]{1,0:T(8,128)(2,1)}, bf16[512,768]{1,0:T(8,128)(2,1)}, bf16[512,768]{1,0:T(8,128)(2,1)}, bf16[512,768]{1,0:T(8,128)(2,1)}) custom-call(s32[40]{0:T(128)S(1)} %copy-done.10, bf16[512,2048]{1,0:T(8,128)(2,1)} %get-tuple-element.171.normed_ref.refs_0_, bf16[512,2048]{1,0:T(8,128)(2,1)} %all-gather.7.cloned.1.call-done.left_ref.refs_1_, ...), custom_call_target="tpu_custom_call" | custom-call | tf_op jit(solution)/shard_map/attention_grad/pallas_call | solution.py:173
  441.8 2.7 multiply_reduce_fusion.1
  444.5 2.7 multiply_reduce_fusion
  449.0 2.7 reduce-scatter.11.cloned.1.call-done.grad_ref
  451.7 2.9 tokens_grad_rows.1
  454.7 5.0 collective-permute-done.53
  460.9 1.9 add_convert_fusion.12
  468.0 6.3 %collective-permute-done.59 = f32[1,256]{1,0:T(1,128)S(1)} collective-permute-done((f32[1,256]{1,0:T(1,128)S(1)}, f32[1,256]{1,0:T(1,128)S(1)}, u32[]{:S(2)}, u32[]{:S(2)}) %collective-permute-start.59) | collective-permute-done | bytes 1056 | tf_op jit(solution)/shard_map/ppermute | solution.py:36
  481.0 4.4 layer_out.1
  485.4 1.9 collective-permute-start.61
  488.4 1.8 collective-permute-done.61
  491.4 8.7 %all-gather.11.cloned.1.call-done.value_ref = bf16[512,2048]{1,0:T(8,128)(2,1)} async-done(((bf16[128,2048]{1,0:T(8,128)(2,1)}), bf16[512,2048]{1,0:T(8,128)(2,1)}) %all-gather.11.cloned.1.call-update) | async-done | bytes 2097168 | tf_op jit(solution)/shard_map/all_gather | solution.py:889
  500.1 4.8 tokens_grad.1
  (404 shorter events, 114.8 us)
Async XLA Ops:
  7.2 140.8 %reduce-scatter.5.cloned.1.call-start = ((), (), s32[]{:S(2)}) async-start(), calls=%async_computation.4 | async-start | bytes 2621440 | tf_op jit(solution)/shard_map/reduce_scatter | solution.py:885
  9.9 10.5 %collective-permute-start = (bf16[256,512]{1,0:T(8,128)(2,1)}, bf16[256,512]{1,0:T(8,128)(2,1)S(1)}, u32[]{:S(2)}, u32[]{:S(2)}) collective-permute-start(bf16[256,512]{1,0:T(8,128)(2,1)} %param.21), channel_id=1, source_target_pairs={{0,8},{4,12},{8,0},{12,4},{16,24},{20,28},{24,16},{28,20},{1,9},{5... | collective-permute-start | bytes 786440 | tf_op jit(solution)/shard_map/ppermute | solution.py:36
  12.9 7.8 %collective-permute-start.1 = (bf16[256,512]{1,0:T(8,128)(2,1)S(1)}, bf16[256,512]{1,0:T(8,128)(2,1)S(1)}, u32[]{:S(2)}, u32[]{:S(2)}) collective-permute-start(bf16[256,512]{1,0:T(8,128)(2,1)S(1)} %constant_dynamic-update-slice_fusion), channel_id=1, source_target_pairs={{0,16},{4,20},{8,24},{12,28},{16,0},{20,4},{24,8},{28,12},{1,17},{... | collective-permute-start | bytes 786440 | tf_op jit(solution)/shard_map/ppermute | solution.py:36
  14.4 5.9 %collective-permute-start.2 = (bf16[1,544]{1,0:T(2,128)(2,1)S(1)}, bf16[1,544]{1,0:T(2,128)(2,1)S(1)}, u32[]{:S(2)}, u32[]{:S(2)}) collective-permute-start(bf16[1,544]{1,0:T(2,128)(2,1)S(1)} %reshape.140), channel_id=1, source_target_pairs={{0,8},{4,12},{8,0},{12,4},{16,24},{20,28},{24,16},{28,20},{1,9},{5... | collective-permute-start | bytes 3272 | tf_op jit(solution)/shard_map/ppermute | solution.py:36
  20.8 12.7 %collective-permute-start.3 = (bf16[512,512]{1,0:T(8,128)(2,1)S(1)}, bf16[512,512]{1,0:T(8,128)(2,1)S(1)}, u32[]{:S(2)}, u32[]{:S(2)}) collective-permute-start(bf16[512,512]{1,0:T(8,128)(2,1)S(1)} %get-tuple-element.163), channel_id=1, source_target_pairs={{0,16},{4,20},{8,24},{12,28},{16,0},{20,4},{24,8},{28,12},{1,17},{... | collective-permute-start | bytes 1572872 | tf_op jit(solution)/shard_map/ppermute | solution.py:36
  22.4 12.2 %collective-permute-start.4 = (bf16[512,512]{1,0:T(8,128)(2,1)S(1)}, bf16[512,512]{1,0:T(8,128)(2,1)S(1)}, u32[]{:S(2)}, u32[]{:S(2)}) collective-permute-start(bf16[512,512]{1,0:T(8,128)(2,1)S(1)} %get-tuple-element.164), channel_id=1, source_target_pairs={{0,8},{4,12},{8,0},{12,4},{16,24},{20,28},{24,16},{28,20},{1,9},{5... | collective-permute-start | bytes 1572872 | tf_op jit(solution)/shard_map/ppermute | solution.py:36
  23.0 10.4 %collective-permute-start.5 = (bf16[2,544]{1,0:T(2,128)(2,1)S(1)}, bf16[2,544]{1,0:T(2,128)(2,1)S(1)}, u32[]{:S(2)}, u32[]{:S(2)}) collective-permute-start(bf16[2,544]{1,0:T(2,128)(2,1)S(1)} %pad_maximum_fusion.21), channel_id=1, source_target_pairs={{0,16},{4,20},{8,24},{12,28},{16,0},{20,4},{24,8},{28,12},{1,17},{... | collective-permute-start | bytes 6536 | tf_op jit(solution)/shard_map/ppermute | solution.py:36
  34.7 4.7 collective-permute-start.7
  36.9 11.2 %collective-permute-start.8 = (bf16[1024,512]{1,0:T(8,128)(2,1)}, bf16[1024,512]{1,0:T(8,128)(2,1)}, u32[]{:S(2)}, u32[]{:S(2)}) collective-permute-start(bf16[1024,512]{1,0:T(8,128)(2,1)} %constant_dynamic-update-slice_fusion.2.w0.refs_2_), channel_id=1, source_target_pairs={{0,4},{4,0},{8,12},{12,8},{16,20},{20,16},{24,28},{28,24},{1,5},{5... | collective-permute-start | bytes 3145736 | tf_op jit(solution)/shard_map/ppermute | solution.py:36
  37.0 8.9 %collective-permute-start.9 = (bf16[256,256]{1,0:T(8,128)(2,1)S(1)}, bf16[256,256]{1,0:T(8,128)(2,1)S(1)}, u32[]{:S(2)}, u32[]{:S(2)}) collective-permute-start(bf16[256,256]{1,0:T(8,128)(2,1)S(1)} %get-tuple-element.175), channel_id=1, source_target_pairs={{0,8},{4,12},{8,0},{12,4},{16,24},{20,28},{24,16},{28,20},{1,9},{5... | collective-permute-start | bytes 393224 | tf_op jit(solution)/shard_map/ppermute | solution.py:36
  37.9 8.0 %collective-permute-start.10 = (bf16[256,256]{1,0:T(8,128)(2,1)S(1)}, bf16[256,256]{1,0:T(8,128)(2,1)S(1)}, u32[]{:S(2)}, u32[]{:S(2)}) collective-permute-start(bf16[256,256]{1,0:T(8,128)(2,1)S(1)} %get-tuple-element.176), channel_id=1, source_target_pairs={{0,16},{4,20},{8,24},{12,28},{16,0},{20,4},{24,8},{28,12},{1,17},{... | collective-permute-start | bytes 393224 | tf_op jit(solution)/shard_map/ppermute | solution.py:36
  45.9 8.4 %collective-permute-start.11 = (bf16[512,256]{1,0:T(8,128)(2,1)}, bf16[512,256]{1,0:T(8,128)(2,1)S(1)}, u32[]{:S(2)}, u32[]{:S(2)}) collective-permute-start(bf16[512,256]{1,0:T(8,128)(2,1)} %get-tuple-element.177), channel_id=1, source_target_pairs={{0,8},{4,12},{8,0},{12,4},{16,24},{20,28},{24,16},{28,20},{1,9},{5... | collective-permute-start | bytes 786440 | tf_op jit(solution)/shard_map/ppermute | solution.py:36
  46.5 8.0 %collective-permute-start.12 = (bf16[512,256]{1,0:T(8,128)(2,1)}, bf16[512,256]{1,0:T(8,128)(2,1)S(1)}, u32[]{:S(2)}, u32[]{:S(2)}) collective-permute-start(bf16[512,256]{1,0:T(8,128)(2,1)} %get-tuple-element.178), channel_id=1, source_target_pairs={{0,16},{4,20},{8,24},{12,28},{16,0},{20,4},{24,8},{28,12},{1,17},{... | collective-permute-start | bytes 786440 | tf_op jit(solution)/shard_map/ppermute | solution.py:36
  54.6 12.7 %collective-permute-start.13 = (bf16[1024,256]{1,0:T(8,128)(2,1)S(1)}, bf16[1024,256]{1,0:T(8,128)(2,1)S(1)}, u32[]{:S(2)}, u32[]{:S(2)}) collective-permute-start(bf16[1024,256]{1,0:T(8,128)(2,1)S(1)} %pad_maximum_fusion.11), channel_id=1, source_target_pairs={{0,16},{4,20},{8,24},{12,28},{16,0},{20,4},{24,8},{28,12},{1,17},{... | collective-permute-start | bytes 1572872 | tf_op jit(solution)/shard_map/ppermute | solution.py:36
  56.2 12.2 %collective-permute-start.14 = (bf16[1024,256]{1,0:T(8,128)(2,1)S(1)}, bf16[1024,256]{1,0:T(8,128)(2,1)S(1)}, u32[]{:S(2)}, u32[]{:S(2)}) collective-permute-start(bf16[1024,256]{1,0:T(8,128)(2,1)S(1)} %pad_maximum_fusion.12), channel_id=1, source_target_pairs={{0,8},{4,12},{8,0},{12,4},{16,24},{20,28},{24,16},{28,20},{1,9},{5... | collective-permute-start | bytes 1572872 | tf_op jit(solution)/shard_map/ppermute | solution.py:36
  69.7 15.6 %collective-permute-start.17 = (bf16[512,256]{1,0:T(8,128)(2,1)S(1)}, bf16[512,256]{1,0:T(8,128)(2,1)S(1)}, u32[]{:S(2)}, u32[]{:S(2)}) collective-permute-start(bf16[512,256]{1,0:T(8,128)(2,1)S(1)} %pad_maximum_fusion.17), channel_id=1, source_target_pairs={{0,16},{4,20},{8,24},{12,28},{16,0},{20,4},{24,8},{28,12},{1,17},{... | collective-permute-start | bytes 786440 | tf_op jit(solution)/shard_map/ppermute | solution.py:36
  70.5 14.9 %collective-permute-start.18 = (bf16[512,256]{1,0:T(8,128)(2,1)S(1)}, bf16[512,256]{1,0:T(8,128)(2,1)S(1)}, u32[]{:S(2)}, u32[]{:S(2)}) collective-permute-start(bf16[512,256]{1,0:T(8,128)(2,1)S(1)} %pad_maximum_fusion.18), channel_id=1, source_target_pairs={{0,8},{4,12},{8,0},{12,4},{16,24},{20,28},{24,16},{28,20},{1,9},{5... | collective-permute-start | bytes 786440 | tf_op jit(solution)/shard_map/ppermute | solution.py:36
  85.4 3.9 collective-permute-start.19
  85.6 3.7 collective-permute-start.20
  87.2 10.9 %collective-permute-start.21 = (bf16[256,768]{1,0:T(8,128)(2,1)S(1)}, bf16[256,768]{1,0:T(8,128)(2,1)S(1)}, u32[]{:S(2)}, u32[]{:S(2)}) collective-permute-start(bf16[256,768]{1,0:T(8,128)(2,1)S(1)} %get-tuple-element.192), channel_id=1, source_target_pairs={{0,8},{4,12},{8,0},{12,4},{16,24},{20,28},{24,16},{28,20},{1,9},{5... | collective-permute-start | bytes 1179656 | tf_op jit(solution)/shard_map/ppermute | solution.py:36
  88.0 10.7 %collective-permute-start.22 = (bf16[256,768]{1,0:T(8,128)(2,1)S(1)}, bf16[256,768]{1,0:T(8,128)(2,1)S(1)}, u32[]{:S(2)}, u32[]{:S(2)}) collective-permute-start(bf16[256,768]{1,0:T(8,128)(2,1)S(1)} %get-tuple-element.193), channel_id=1, source_target_pairs={{0,16},{4,20},{8,24},{12,28},{16,0},{20,4},{24,8},{28,12},{1,17},{... | collective-permute-start | bytes 1179656 | tf_op jit(solution)/shard_map/ppermute | solution.py:36
  94.4 101.7 %all-gather.5.cloned.1.call-start = ((), (), s32[]{:S(2)}) async-start(), calls=%async_computation.5 | async-start | bytes 2621440 | tf_op jit(solution)/shard_map/all_gather | solution.py:889
  100.7 18.4 %collective-permute-start.23 = (bf16[512,768]{1,0:T(8,128)(2,1)}, bf16[512,768]{1,0:T(8,128)(2,1)S(1)}, u32[]{:S(2)}, u32[]{:S(2)}) collective-permute-start(bf16[512,768]{1,0:T(8,128)(2,1)} %pad_maximum_fusion.7), channel_id=1, source_target_pairs={{0,16},{4,20},{8,24},{12,28},{16,0},{20,4},{24,8},{28,12},{1,17},{... | collective-permute-start | bytes 2359304 | tf_op jit(solution)/shard_map/ppermute | solution.py:36
  101.8 18.0 %collective-permute-start.24 = (bf16[512,768]{1,0:T(8,128)(2,1)}, bf16[512,768]{1,0:T(8,128)(2,1)S(1)}, u32[]{:S(2)}, u32[]{:S(2)}) collective-permute-start(bf16[512,768]{1,0:T(8,128)(2,1)} %pad_maximum_fusion.8), channel_id=1, source_target_pairs={{0,8},{4,12},{8,0},{12,4},{16,24},{20,28},{24,16},{28,20},{1,9},{5... | collective-permute-start | bytes 2359304 | tf_op jit(solution)/shard_map/ppermute | solution.py:36
  119.8 17.2 %collective-permute-start.25 = (bf16[256,1536]{1,0:T(8,128)(2,1)}, bf16[256,1536]{1,0:T(8,128)(2,1)S(1)}, u32[]{:S(2)}, u32[]{:S(2)}) collective-permute-start(bf16[256,1536]{1,0:T(8,128)(2,1)} %param.28), channel_id=1, source_target_pairs={{0,8},{4,12},{8,0},{12,4},{16,24},{20,28},{24,16},{28,20},{1,9},{5... | collective-permute-start | bytes 2359304 | tf_op jit(solution)/shard_map/ppermute | solution.py:36
  120.4 16.8 %collective-permute-start.26 = (bf16[256,1536]{1,0:T(8,128)(2,1)}, bf16[256,1536]{1,0:T(8,128)(2,1)S(1)}, u32[]{:S(2)}, u32[]{:S(2)}) collective-permute-start(bf16[256,1536]{1,0:T(8,128)(2,1)} %param.29), channel_id=1, source_target_pairs={{0,16},{4,20},{8,24},{12,28},{16,0},{20,4},{24,8},{28,12},{1,17},{... | collective-permute-start | bytes 2359304 | tf_op jit(solution)/shard_map/ppermute | solution.py:36
  125.0 25.4 %collective-permute-start.29 = (bf16[1024,768]{1,0:T(8,128)(2,1)S(1)}, bf16[1024,768]{1,0:T(8,128)(2,1)}, u32[]{:S(2)}, u32[]{:S(2)}) collective-permute-start(bf16[1024,768]{1,0:T(8,128)(2,1)S(1)} %pad_maximum_fusion.3.refs_0_.refs_2_), channel_id=1, source_target_pairs={{0,4},{4,0},{8,12},{12,8},{16,20},{20,16},{24,28},{28,24},{1,5},{5... | collective-permute-start | bytes 4718600 | tf_op jit(solution)/shard_map/ppermute | solution.py:36
  126.8 23.6 %collective-permute-start.30 = (bf16[1024,768]{1,0:T(8,128)(2,1)S(1)}, bf16[1024,768]{1,0:T(8,128)(2,1)}, u32[]{:S(2)}, u32[]{:S(2)}) collective-permute-start(bf16[1024,768]{1,0:T(8,128)(2,1)S(1)} %pad_maximum_fusion.4.refs_2_.refs_4_), channel_id=1, source_target_pairs={{0,4},{4,0},{8,12},{12,8},{16,20},{20,16},{24,28},{28,24},{1,5},{5... | collective-permute-start | bytes 4718600 | tf_op jit(solution)/shard_map/ppermute | solution.py:36
  142.3 33.1 %collective-permute-start.27 = (bf16[512,1536]{1,0:T(8,128)(2,1)}, bf16[512,1536]{1,0:T(8,128)(2,1)}, u32[]{:S(2)}, u32[]{:S(2)}) collective-permute-start(bf16[512,1536]{1,0:T(8,128)(2,1)} %pad_maximum_fusion.1), channel_id=1, source_target_pairs={{0,16},{4,20},{8,24},{12,28},{16,0},{20,4},{24,8},{28,12},{1,17},{... | collective-permute-start | bytes 4718600 | tf_op jit(solution)/shard_map/ppermute | solution.py:36
  143.7 32.8 %collective-permute-start.28 = (bf16[512,1536]{1,0:T(8,128)(2,1)}, bf16[512,1536]{1,0:T(8,128)(2,1)}, u32[]{:S(2)}, u32[]{:S(2)}) collective-permute-start(bf16[512,1536]{1,0:T(8,128)(2,1)} %pad_maximum_fusion.2), channel_id=1, source_target_pairs={{0,8},{4,12},{8,0},{12,4},{16,24},{20,28},{24,16},{28,20},{1,9},{5... | collective-permute-start | bytes 4718600 | tf_op jit(solution)/shard_map/ppermute | solution.py:36
  150.4 113.6 %reduce-scatter.7.cloned.1.call-start = ((), (), s32[]{:S(2)}) async-start(), calls=%async_computation.6 | async-start | bytes 2621440 | tf_op jit(solution)/shard_map/reduce_scatter | solution.py:885
  179.1 17.1 %collective-permute-start.31 = (bf16[1024,1536]{1,0:T(8,128)(2,1)}, bf16[1024,1536]{1,0:T(8,128)(2,1)}, u32[]{:S(2)}, u32[]{:S(2)}) collective-permute-start(bf16[1024,1536]{1,0:T(8,128)(2,1)} %constant_dynamic-update-slice_fusion.8.wg0.refs_2_), channel_id=1, source_target_pairs={{0,4},{4,0},{8,12},{12,8},{16,20},{20,16},{24,28},{28,24},{1,5},{5... | collective-permute-start | bytes 9437192 | tf_op jit(solution)/shard_map/ppermute | solution.py:36
  181.9 14.2 %collective-permute-start.32 = (bf16[1024,1536]{1,0:T(8,128)(2,1)S(1)}, bf16[1024,1536]{1,0:T(8,128)(2,1)}, u32[]{:S(2)}, u32[]{:S(2)}) collective-permute-start(bf16[1024,1536]{1,0:T(8,128)(2,1)S(1)} %pad_maximum_fusion.wu0.refs_4_), channel_id=1, source_target_pairs={{0,4},{4,0},{8,12},{12,8},{16,20},{20,16},{24,28},{28,24},{1,5},{5... | collective-permute-start | bytes 9437192 | tf_op jit(solution)/shard_map/ppermute | solution.py:36
  221.2 91.8 %all-gather.7.cloned.1.call-start = ((), (), s32[]{:S(2)}) async-start(), calls=%async_computation.7 | async-start | bytes 2621440 | tf_op jit(solution)/shard_map/all_gather | solution.py:889
  228.2 5.9 %collective-permute-start.33 = (bf16[1024,1536]{1,0:T(8,128)(2,1)}, bf16[1024,1536]{1,0:T(8,128)(2,1)S(1)}, u32[]{:S(2)}, u32[]{:S(2)}) collective-permute-start(bf16[1024,1536]{1,0:T(8,128)(2,1)} %get-tuple-element.215), channel_id=1, source_target_pairs={{0,4},{4,0},{8,12},{12,8},{16,20},{20,16},{24,28},{28,24},{1,5},{5... | collective-permute-start | bytes 9437192 | tf_op jit(solution)/shard_map/ppermute | solution.py:36
  228.2 10.4 %collective-permute-start.34 = (bf16[1024,1536]{1,0:T(8,128)(2,1)}, bf16[1024,1536]{1,0:T(8,128)(2,1)S(1)}, u32[]{:S(2)}, u32[]{:S(2)}) collective-permute-start(bf16[1024,1536]{1,0:T(8,128)(2,1)} %get-tuple-element.216), channel_id=1, source_target_pairs={{0,4},{4,0},{8,12},{12,8},{16,20},{20,16},{24,28},{28,24},{1,5},{5... | collective-permute-start | bytes 9437192 | tf_op jit(solution)/shard_map/ppermute | solution.py:36
  251.3 36.6 %collective-permute-start.35 = (bf16[512,1536]{1,0:T(8,128)(2,1)}, bf16[512,1536]{1,0:T(8,128)(2,1)S(1)}, u32[]{:S(2)}, u32[]{:S(2)}) collective-permute-start(bf16[512,1536]{1,0:T(8,128)(2,1)} %get-tuple-element.224), channel_id=1, source_target_pairs={{0,8},{4,12},{8,0},{12,4},{16,24},{20,28},{24,16},{28,20},{1,9},{5... | collective-permute-start | bytes 4718600 | tf_op jit(solution)/shard_map/ppermute | solution.py:36
  252.8 36.3 %collective-permute-start.36 = (bf16[512,1536]{1,0:T(8,128)(2,1)}, bf16[512,1536]{1,0:T(8,128)(2,1)S(1)}, u32[]{:S(2)}, u32[]{:S(2)}) collective-permute-start(bf16[512,1536]{1,0:T(8,128)(2,1)} %get-tuple-element.225), channel_id=1, source_target_pairs={{0,16},{4,20},{8,24},{12,28},{16,0},{20,4},{24,8},{28,12},{1,17},{... | collective-permute-start | bytes 4718600 | tf_op jit(solution)/shard_map/ppermute | solution.py:36
  267.6 90.8 %reduce-scatter.9.cloned.1.call-start = ((), (), s32[]{:S(2)}) async-start(), calls=%async_computation.8 | async-start | bytes 2621440 | tf_op jit(solution)/shard_map/reduce_scatter | solution.py:885
  294.1 5.9 %collective-permute-start.38 = (bf16[1024,768]{1,0:T(8,128)(2,1)}, bf16[1024,768]{1,0:T(8,128)(2,1)S(1)}, u32[]{:S(2)}, u32[]{:S(2)}) collective-permute-start(bf16[1024,768]{1,0:T(8,128)(2,1)} %get-tuple-element.233), channel_id=1, source_target_pairs={{0,4},{4,0},{8,12},{12,8},{16,20},{20,16},{24,28},{28,24},{1,5},{5... | collective-permute-start | bytes 4718600 | tf_op jit(solution)/shard_map/ppermute | solution.py:36
  313.0 93.1 %all-gather.9.cloned.1.call-start = ((), (), s32[]{:S(2)}) async-start(), calls=%async_computation.9 | async-start | bytes 2621440 | tf_op jit(solution)/shard_map/all_gather | solution.py:889
  313.1 29.0 %collective-permute-start.39 = (bf16[256,1536]{1,0:T(8,128)(2,1)S(1)}, bf16[256,1536]{1,0:T(8,128)(2,1)S(1)}, u32[]{:S(2)}, u32[]{:S(2)}) collective-permute-start(bf16[256,1536]{1,0:T(8,128)(2,1)S(1)} %copy-done.52), channel_id=1, source_target_pairs={{0,16},{4,20},{8,24},{12,28},{16,0},{20,4},{24,8},{28,12},{1,17},{... | collective-permute-start | bytes 2359304 | tf_op jit(solution)/shard_map/ppermute | solution.py:36
  314.6 27.5 %collective-permute-start.40 = (bf16[256,1536]{1,0:T(8,128)(2,1)S(1)}, bf16[256,1536]{1,0:T(8,128)(2,1)S(1)}, u32[]{:S(2)}, u32[]{:S(2)}) collective-permute-start(bf16[256,1536]{1,0:T(8,128)(2,1)S(1)} %add_convert_fusion.2), channel_id=1, source_target_pairs={{0,8},{4,12},{8,0},{12,4},{16,24},{20,28},{24,16},{28,20},{1,9},{5... | collective-permute-start | bytes 2359304 | tf_op jit(solution)/shard_map/ppermute | solution.py:36
  316.1 34.4 %collective-permute-start.41 = (bf16[512,768]{1,0:T(8,128)(2,1)}, bf16[512,768]{1,0:T(8,128)(2,1)S(1)}, u32[]{:S(2)}, u32[]{:S(2)}) collective-permute-start(bf16[512,768]{1,0:T(8,128)(2,1)} %get-tuple-element.244), channel_id=1, source_target_pairs={{0,8},{4,12},{8,0},{12,4},{16,24},{20,28},{24,16},{28,20},{1,9},{5... | collective-permute-start | bytes 2359304 | tf_op jit(solution)/shard_map/ppermute | solution.py:36
  316.6 33.8 %collective-permute-start.42 = (bf16[512,768]{1,0:T(8,128)(2,1)S(1)}, bf16[512,768]{1,0:T(8,128)(2,1)S(1)}, u32[]{:S(2)}, u32[]{:S(2)}) collective-permute-start(bf16[512,768]{1,0:T(8,128)(2,1)S(1)} %copy-done.88), channel_id=1, source_target_pairs={{0,16},{4,20},{8,24},{12,28},{16,0},{20,4},{24,8},{28,12},{1,17},{... | collective-permute-start | bytes 2359304 | tf_op jit(solution)/shard_map/ppermute | solution.py:36
  350.5 4.4 collective-permute-start.44
  360.7 91.0 %reduce-scatter.11.cloned.1.call-start = ((), (), s32[]{:S(2)}) async-start(), calls=%async_computation.10 | async-start | bytes 2621440 | tf_op jit(solution)/shard_map/reduce_scatter | solution.py:885
  361.0 13.6 %collective-permute-start.45 = (bf16[1024,256]{1,0:T(8,128)(2,1)S(1)}, bf16[1024,256]{1,0:T(8,128)(2,1)S(1)}, u32[]{:S(2)}, u32[]{:S(2)}) collective-permute-start(bf16[1024,256]{1,0:T(8,128)(2,1)S(1)} %copy-done.66), channel_id=1, source_target_pairs={{0,8},{4,12},{8,0},{12,4},{16,24},{20,28},{24,16},{28,20},{1,9},{5... | collective-permute-start | bytes 1572872 | tf_op jit(solution)/shard_map/ppermute | solution.py:36
  362.5 13.5 %collective-permute-start.46 = (bf16[1024,256]{1,0:T(8,128)(2,1)}, bf16[1024,256]{1,0:T(8,128)(2,1)S(1)}, u32[]{:S(2)}, u32[]{:S(2)}) collective-permute-start(bf16[1024,256]{1,0:T(8,128)(2,1)} %get-tuple-element.252), channel_id=1, source_target_pairs={{0,16},{4,20},{8,24},{12,28},{16,0},{20,4},{24,8},{28,12},{1,17},{... | collective-permute-start | bytes 1572872 | tf_op jit(solution)/shard_map/ppermute | solution.py:36
  377.7 6.9 %collective-permute-start.47 = (bf16[512,256]{1,0:T(8,128)(2,1)S(1)}, bf16[512,256]{1,0:T(8,128)(2,1)S(1)}, u32[]{:S(2)}, u32[]{:S(2)}) collective-permute-start(bf16[512,256]{1,0:T(8,128)(2,1)S(1)} %get-tuple-element.261), channel_id=1, source_target_pairs={{0,16},{4,20},{8,24},{12,28},{16,0},{20,4},{24,8},{28,12},{1,17},{... | collective-permute-start | bytes 786440 | tf_op jit(solution)/shard_map/ppermute | solution.py:36
  379.1 6.5 %collective-permute-start.48 = (bf16[512,256]{1,0:T(8,128)(2,1)S(1)}, bf16[512,256]{1,0:T(8,128)(2,1)S(1)}, u32[]{:S(2)}, u32[]{:S(2)}) collective-permute-start(bf16[512,256]{1,0:T(8,128)(2,1)S(1)} %get-tuple-element.262), channel_id=1, source_target_pairs={{0,8},{4,12},{8,0},{12,4},{16,24},{20,28},{24,16},{28,20},{1,9},{5... | collective-permute-start | bytes 786440 | tf_op jit(solution)/shard_map/ppermute | solution.py:36
  406.1 94.0 %all-gather.11.cloned.1.call-start = ((), (), s32[]{:S(2)}) async-start(), calls=%async_computation.11 | async-start | bytes 2621440 | tf_op jit(solution)/shard_map/all_gather | solution.py:889
  406.4 10.9 %collective-permute-start.49 = (bf16[256,768]{1,0:T(8,128)(2,1)S(1)}, bf16[256,768]{1,0:T(8,128)(2,1)S(1)}, u32[]{:S(2)}, u32[]{:S(2)}) collective-permute-start(bf16[256,768]{1,0:T(8,128)(2,1)S(1)} %add_convert_fusion.15), channel_id=1, source_target_pairs={{0,16},{4,20},{8,24},{12,28},{16,0},{20,4},{24,8},{28,12},{1,17},{... | collective-permute-start | bytes 1179656 | tf_op jit(solution)/shard_map/ppermute | solution.py:36
  407.9 10.6 %collective-permute-start.50 = (bf16[256,768]{1,0:T(8,128)(2,1)S(1)}, bf16[256,768]{1,0:T(8,128)(2,1)S(1)}, u32[]{:S(2)}, u32[]{:S(2)}) collective-permute-start(bf16[256,768]{1,0:T(8,128)(2,1)S(1)} %add_convert_fusion.14), channel_id=1, source_target_pairs={{0,8},{4,12},{8,0},{12,4},{16,24},{20,28},{24,16},{28,20},{1,9},{5... | collective-permute-start | bytes 1179656 | tf_op jit(solution)/shard_map/ppermute | solution.py:36
  423.3 3.7 collective-permute-start.51
  423.4 5.9 %collective-permute-start.52 = (bf16[1024,768]{1,0:T(8,128)(2,1)}, bf16[1024,768]{1,0:T(8,128)(2,1)S(1)}, u32[]{:S(2)}, u32[]{:S(2)}) collective-permute-start(bf16[1024,768]{1,0:T(8,128)(2,1)} %get-tuple-element.277), channel_id=1, source_target_pairs={{0,4},{4,0},{8,12},{12,8},{16,20},{20,16},{24,28},{28,24},{1,5},{5... | collective-permute-start | bytes 4718600 | tf_op jit(solution)/shard_map/ppermute | solution.py:36
  439.7 19.9 %collective-permute-start.53 = (bf16[512,768]{1,0:T(8,128)(2,1)}, bf16[512,768]{1,0:T(8,128)(2,1)}, u32[]{:S(2)}, u32[]{:S(2)}) collective-permute-start(bf16[512,768]{1,0:T(8,128)(2,1)} %get-tuple-element.284), channel_id=1, source_target_pairs={{0,8},{4,12},{8,0},{12,4},{16,24},{20,28},{24,16},{28,20},{1,9},{5... | collective-permute-start | bytes 2359304 | tf_op jit(solution)/shard_map/ppermute | solution.py:36
  441.2 19.6 %collective-permute-start.54 = (bf16[512,768]{1,0:T(8,128)(2,1)}, bf16[512,768]{1,0:T(8,128)(2,1)}, u32[]{:S(2)}, u32[]{:S(2)}) collective-permute-start(bf16[512,768]{1,0:T(8,128)(2,1)} %get-tuple-element.285), channel_id=1, source_target_pairs={{0,16},{4,20},{8,24},{12,28},{16,0},{20,4},{24,8},{28,12},{1,17},{... | collective-permute-start | bytes 2359304 | tf_op jit(solution)/shard_map/ppermute | solution.py:36
  448.5 17.8 %collective-permute-start.58 = (f32[1,256]{1,0:T(1,128)S(1)}, f32[1,256]{1,0:T(1,128)S(1)}, u32[]{:S(2)}, u32[]{:S(2)}) collective-permute-start(f32[1,256]{1,0:T(1,128)S(1)} %add.165), channel_id=1, source_target_pairs={{0,8},{4,12},{8,0},{12,4},{16,24},{20,28},{24,16},{28,20},{1,9},{5... | collective-permute-start | bytes 3080 | tf_op jit(solution)/shard_map/ppermute | solution.py:36
  464.0 10.6 %collective-permute-start.55 = (bf16[256,768]{1,0:T(8,128)(2,1)}, bf16[256,768]{1,0:T(8,128)(2,1)}, u32[]{:S(2)}, u32[]{:S(2)}) collective-permute-start(bf16[256,768]{1,0:T(8,128)(2,1)} %add_convert_fusion.12), channel_id=1, source_target_pairs={{0,16},{4,20},{8,24},{12,28},{16,0},{20,4},{24,8},{28,12},{1,17},{... | collective-permute-start | bytes 1179656 | tf_op jit(solution)/shard_map/ppermute | solution.py:36
  464.6 10.0 %collective-permute-start.56 = (bf16[256,768]{1,0:T(8,128)(2,1)S(1)}, bf16[256,768]{1,0:T(8,128)(2,1)}, u32[]{:S(2)}, u32[]{:S(2)}) collective-permute-start(bf16[256,768]{1,0:T(8,128)(2,1)S(1)} %add_convert_fusion.11), channel_id=1, source_target_pairs={{0,8},{4,12},{8,0},{12,4},{16,24},{20,28},{24,16},{28,20},{1,9},{5... | collective-permute-start | bytes 1179656 | tf_op jit(solution)/shard_map/ppermute | solution.py:36
  466.3 8.0 %collective-permute-start.59 = (f32[1,256]{1,0:T(1,128)S(1)}, f32[1,256]{1,0:T(1,128)S(1)}, u32[]{:S(2)}, u32[]{:S(2)}) collective-permute-start(f32[1,256]{1,0:T(1,128)S(1)} %add.166), channel_id=1, source_target_pairs={{0,16},{4,20},{8,24},{12,28},{16,0},{20,4},{24,8},{28,12},{1,17},{... | collective-permute-start | bytes 3080 | tf_op jit(solution)/shard_map/ppermute | solution.py:36
  479.2 6.2 %collective-permute-start.60 = (f32[1,544]{1,0:T(1,128)S(1)}, f32[1,544]{1,0:T(1,128)S(1)}, u32[]{:S(2)}, u32[]{:S(2)}) collective-permute-start(f32[1,544]{1,0:T(1,128)S(1)} %broadcast_in_dim.82), channel_id=1, source_target_pairs={{0,1},{1,0},{2,3},{3,2},{4,5},{5,4},{6,7},{7,6},{8,9},{9,8},{10,11... | collective-permute-start | bytes 6536 | tf_op jit(solution)/shard_map/ppermute | solution.py:1108
  485.4 4.8 collective-permute-start.61
  (96 other events, 543.1 us)
Sparse Core Ops, SparseCore 0:
  94.5 44.1 reduce-scatter.4
  150.5 45.5 all-gather.4
  221.3 42.6 reduce-scatter.6
  267.7 45.2 all-gather.6
  315.7 42.5 reduce-scatter.8
  360.8 45.2 all-gather.8
  409.1 42.5 reduce-scatter.10
  454.8 45.3 all-gather.10

commit v6 on v5

--- a/solution.py
+++ b/solution.py
@@ -1005,7 +1005,7 @@
     gather_rest(wide, pair, 1, beside=(my_post, grad_act))
     wg, wu = gather_end(wide)
     act, grad_gate, grad_up = hidden_units(post_low, wg, wu, grad_act)
-    post_part = to_width("grad_post", (grad_gate, 0, wg, 0, units), (grad_up, 0, wu, 0, units), near=(2, 3, 4, 5))
+    post_part = to_width("grad_post", (grad_gate, 0, wg, 0, units), (grad_up, 0, wu, 0, units), tile=512, near=(2, 3, 4, 5))
     my_grad_post = sum_of_parts(post_part)
 
     starts = bits[0], flipped[0]

time: 522 us -> 521 us (level)
  no operation moved by 1% of the time
where the time goes in v6:
time: 521 us; the launch traced here: 511 us
  waiting for transfers between devices  198 us (38%)
  Pallas kernels  171 us (33%)
  starting transfers between devices  53.1 us (10%)
  local copies, waits for them, and re-layouts  39.6 us (8%)
  other arithmetic  33.9 us (7%)
  between operations  15.7 us (3%)
    ppermute x60, waiting for transfers between devices, exchange(): return lax.ppermute(block, 'blk', [(i, i ^ bit) for i in range(n)])  148 us
    pallas_call x24, Pallas kernels, call(): pl.pallas_call(kernel, out_shape=out_shape, compiler_params=pltpu.Compile...  140 us
    ppermute x60, starting transfers between devices, exchange(): return lax.ppermute(block, 'blk', [(i, i ^ bit) for i in range(n)])  50.1 us
    all_gather x4, waiting for transfers between devices, all_parts(): return lax.all_gather(mine, 'fsdp', axis=0, tiled=True)  36.5 us
    unnamed x193, local copies, waits for them, and re-layouts  24.9 us
    pallas_call x1, Pallas kernels, attend_back(): pl.pallas_call(functools.partial(attend_back_kernel, span, head, heads),...  20.4 us
    reduce_scatter x4, waiting for transfers between devices, sum_of_parts(): return lax.psum_scatter(part, 'fsdp', scatter_dimension=0, tiled=True)  11 us
    pallas_call x1, Pallas kernels, attend(): pl.pallas_call(functools.partial(attend_kernel, span, head, heads), grid_...  10.7 us
  transfers between devices with their start and end apart: 70, of which 45 were waited for; matrix products, arithmetic and copies ran while one was open for 11% of the time, Pallas kernels for 27%

profile of v6, /device:TPU:0, one launch (start us, length us, event | category | flops | bytes accessed | tf_op | source)
XLA Modules:
  0.0 511.2 jit_solution(18296532063338014497)
XLA Ops:
  9.9 3.0 collective-permute-start
  16.9 1.7 constant_dynamic-update-slice_fusion.4
  25.9 2.1 enter.1
  29.3 4.1 collective-permute-done.5
  39.4 2.0 copy-done.7
  41.4 4.5 project_keys.1
  48.1 5.9 %project_queries.1 = (f32[512,512]{1,0:T(8,128)}, bf16[512,512]{1,0:T(8,128)(2,1)}) custom-call(bf16[512,2048]{1,0:T(8,128)(2,1)} %get-tuple-element.171.normed_ref.refs_0_, bf16[1024,512]{1,0:T(8,128)(2,1)} %constant_dynamic-update-slice_fusion.2.w0.refs_2_, bf16[1024,512]{1,0:T(8,128)(2,1)} %collective-permute-done.8.w1.refs_3_, f32[512,128]{1,0:T(8,128)} %copy-done.3, ...), custom_call_target="tpu_custom_call" | custom-call | tf_op jit(solution)/shard_map/project_queries/pallas_call | solution.py:173
  57.1 10.2 %collective-permute-done.13 = bf16[1024,256]{1,0:T(8,128)(2,1)S(1)} collective-permute-done((bf16[1024,256]{1,0:T(8,128)(2,1)S(1)}, bf16[1024,256]{1,0:T(8,128)(2,1)S(1)}, u32[]{:S(2)}, u32[]{:S(2)}) %collective-permute-start.13) | collective-permute-done | bytes 524320 | tf_op jit(solution)/shard_map/ppermute | solution.py:36
  73.8 10.7 %attend.1 = (bf16[512,512]{1,0:T(8,128)(2,1)S(1)}, f32[2,2,512]{2,1,0:T(2,128)S(1)}) custom-call(s32[18]{0:T(128)S(1)} %pad_add_fusion.1.sc, bf16[512,512]{1,0:T(8,128)(2,1)S(1)} %copy-done.11, bf16[2048,256]{1,0:T(8,128)(2,1)} %copy-done.79, bf16[2048,256]{1,0:T(8,128)(2,1)} %copy-done.86, bf16[2048,256]{1,0:T(8,128)(2,1)} %copy-done.40, ...), custom_call_target="tpu_custom_call" | custom-call | flops 8589934592 | bytes 2097152 | tf_op jit(solution)/shard_map/attend/pallas_call | solution.py:811
  89.3 5.0 attention_out.1
  94.6 3.5 collective-permute-done.21
  102.5 16.6 %collective-permute-done.23 = bf16[512,768]{1,0:T(8,128)(2,1)S(1)} collective-permute-done((bf16[512,768]{1,0:T(8,128)(2,1)}, bf16[512,768]{1,0:T(8,128)(2,1)S(1)}, u32[]{:S(2)}, u32[]{:S(2)}) %collective-permute-start.23) | collective-permute-done | bytes 786464 | tf_op jit(solution)/shard_map/ppermute | solution.py:36
  121.8 1.9 constant_dynamic-slice_fusion.1.tokens_ref
  126.9 10.1 %collective-permute-done.25 = bf16[256,1536]{1,0:T(8,128)(2,1)S(1)} collective-permute-done((bf16[256,1536]{1,0:T(8,128)(2,1)}, bf16[256,1536]{1,0:T(8,128)(2,1)S(1)}, u32[]{:S(2)}, u32[]{:S(2)}) %collective-permute-start.25) | collective-permute-done | bytes 786464 | tf_op jit(solution)/shard_map/ppermute | solution.py:36
  137.3 2.7 pad_maximum_fusion.1
  140.0 2.4 pad_maximum_fusion.2
  145.0 2.1 constant_dynamic-update-slice_fusion.10
  148.0 2.3 post.1
  150.5 8.0 %grad_act.1.grad_ref = bf16[512,1536]{1,0:T(8,128)(2,1)} custom-call(bf16[512,2048]{1,0:T(8,128)(2,1)} %copy-done, bf16[1024,768]{1,0:T(8,128)(2,1)} %copy-done.12, bf16[1024,768]{1,0:T(8,128)(2,1)} %collective-permute-done.29.refs_1_.refs_3_, bf16[1024,768]{1,0:T(8,128)(2,1)} %copy-done.13, bf16[1024,768]{1,0:T(8,128)(2,1)} %collective-permute-done.30.refs_3_.refs_5_), custom_call_target="tpu_custom_call" | custom-call | tf_op jit(solution)/shard_map/grad_act/pallas_call | solution.py:173
  158.5 16.9 %collective-permute-done.27 = bf16[512,1536]{1,0:T(8,128)(2,1)} collective-permute-done((bf16[512,1536]{1,0:T(8,128)(2,1)}, bf16[512,1536]{1,0:T(8,128)(2,1)}, u32[]{:S(2)}, u32[]{:S(2)}) %collective-permute-start.27) | collective-permute-done | bytes 1572896 | tf_op jit(solution)/shard_map/ppermute | solution.py:36
  176.5 2.7 constant_dynamic-update-slice_fusion.8.wg0.refs_2_
  182.5 13.7 %all-gather.5.cloned.1.call-done.post_ref.refs_0_ = bf16[512,2048]{1,0:T(8,128)(2,1)} async-done(((bf16[128,2048]{1,0:T(8,128)(2,1)}), bf16[512,2048]{1,0:T(8,128)(2,1)}) %all-gather.5.cloned.1.call-update) | async-done | bytes 2097168 | tf_op jit(solution)/shard_map/all_gather | solution.py:889
  196.1 12.3 %hidden_units.1 = (bf16[512,1536]{1,0:T(8,128)(2,1)}, bf16[512,1536]{1,0:T(8,128)(2,1)}, bf16[512,1536]{1,0:T(8,128)(2,1)}) custom-call(bf16[512,2048]{1,0:T(8,128)(2,1)} %all-gather.5.cloned.1.call-done.post_ref.refs_0_, bf16[1024,1536]{1,0:T(8,128)(2,1)} %constant_dynamic-update-slice_fusion.8.wg0.refs_2_, ...), custom_call_target="tpu_custom_call" | custom-call | tf_op jit(solution)/shard_map/hidden_units/pallas_call | solution.py:173
  208.5 11.7 %grad_post.1 = bf16[512,2048]{1,0:T(8,128)(2,1)} custom-call(bf16[512,1536]{1,0:T(8,128)(2,1)} %get-tuple-element.213.refs_0_.refs_1_, bf16[512,1536]{1,0:T(8,128)(2,1)} %get-tuple-element.214.refs_1_.refs_2_, bf16[1024,1536]{1,0:T(8,128)(2,1)} %constant_dynamic-update-slice_fusion.8.wg0.refs_2_, bf16[1024,1536]{1,0:T(8,128)(2,1)} %collective-permute-done.31.wg1.refs_3_, ...), custom_call_target="tpu_custom_call" | custom-call | tf_op jit(solution)/shard_map/grad_post/pallas_call | solution.py:173
  220.3 7.0 %units_grad_away.1 = (bf16[1024,1536]{1,0:T(8,128)(2,1)}, bf16[1024,1536]{1,0:T(8,128)(2,1)}) custom-call(bf16[512,2048]{1,0:T(8,128)(2,1)} %all-gather.5.cloned.1.call-done.post_ref.refs_0_, bf16[512,1536]{1,0:T(8,128)(2,1)} %get-tuple-element.213.refs_0_.refs_1_, bf16[512,1536]{1,0:T(8,128)(2,1)} %get-tuple-element.214.refs_1_.refs_2_), custom_call_target="tpu_custom_call" | custom-call | tf_op jit(solution)/shard_map/units_grad_away/pallas_call | solution.py:173
  227.7 5.4 %collective-permute-done.33.refs_3_ = bf16[1024,1536]{1,0:T(8,128)(2,1)S(1)} collective-permute-done((bf16[1024,1536]{1,0:T(8,128)(2,1)}, bf16[1024,1536]{1,0:T(8,128)(2,1)S(1)}, u32[]{:S(2)}, u32[]{:S(2)}) %collective-permute-start.33) | collective-permute-done | bytes 3145760 | tf_op jit(solution)/shard_map/ppermute | solution.py:36
  233.1 4.5 collective-permute-done.34.refs_4_
  239.3 11.0 %units_grad.1 = (bf16[512,1536]{1,0:T(8,128)(2,1)}, bf16[512,1536]{1,0:T(8,128)(2,1)}, bf16[512,1536]{1,0:T(8,128)(2,1)}, bf16[512,1536]{1,0:T(8,128)(2,1)}) custom-call(s32[40]{0:T(128)S(1)} %copy-done.10, bf16[512,2048]{1,0:T(8,128)(2,1)} %all-gather.5.cloned.1.call-done.post_ref.refs_0_, bf16[512,1536]{1,0:T(8,128)(2,1)} %get-tuple-element.213.refs_0_.refs_1_, ...), custom_call_target="tpu_custom_call" | custom-call | tf_op jit(solution)/shard_map/units_grad/pallas_call | solution.py:173
  253.3 1.9 constant_dynamic-slice_fusion.cotangent_ref
  255.2 7.8 %reduce-scatter.7.cloned.1.call-done.grad_ref = bf16[128,2048]{1,0:T(8,128)(2,1)} async-done(((bf16[512,2048]{1,0:T(8,128)(2,1)}), bf16[128,2048]{1,0:T(8,128)(2,1)}) %reduce-scatter.7.cloned.1.call-update) | async-done | bytes 524304 | tf_op jit(solution)/shard_map/reduce_scatter | solution.py:885
  263.0 3.6 grad_hidden.1
  266.9 7.9 %units_out.1 = bf16[512,2048]{1,0:T(8,128)(2,1)} custom-call(bf16[512,1536]{1,0:T(8,128)(2,1)} %get-tuple-element.231.refs_0_.refs_1_.refs_2_, bf16[512,1536]{1,0:T(8,128)(2,1)} %get-tuple-element.231.refs_0_.refs_1_.refs_2_, bf16[1024,768]{1,0:T(8,128)(2,1)} %copy-done.12, bf16[1024,768]{1,0:T(8,128)(2,1)} %collective-permute-done.29.refs_1_.refs_3_, ...), custom_call_target="tpu_custom_call" | custom-call | tf_op jit(solution)/shard_map/units_out/pallas_call | solution.py:173
  274.8 12.1 %collective-permute-done.35 = bf16[512,1536]{1,0:T(8,128)(2,1)S(1)} collective-permute-done((bf16[512,1536]{1,0:T(8,128)(2,1)}, bf16[512,1536]{1,0:T(8,128)(2,1)S(1)}, u32[]{:S(2)}, u32[]{:S(2)}) %collective-permute-start.35) | collective-permute-done | bytes 1572896 | tf_op jit(solution)/shard_map/ppermute | solution.py:36
  288.1 5.1 down_grad_away.1
  295.0 1.8 collective-permute-done.37.refs_3_
  296.8 2.2 collective-permute-done.38.refs_4_
  300.2 8.0 %down_grad.1 = (bf16[512,768]{1,0:T(8,128)(2,1)}, bf16[512,768]{1,0:T(8,128)(2,1)}, bf16[512,768]{1,0:T(8,128)(2,1)}, bf16[512,768]{1,0:T(8,128)(2,1)}) custom-call(s32[40]{0:T(128)S(1)} %copy-done.10, bf16[512,2048]{1,0:T(8,128)(2,1)} %copy-done, bf16[512,1536]{1,0:T(8,128)(2,1)} %get-tuple-element.231.refs_0_.refs_1_.refs_2_, ...), custom_call_target="tpu_custom_call" | custom-call | tf_op jit(solution)/shard_map/down_grad/pallas_call | solution.py:173
  308.2 3.8 all-gather.7.cloned.1.call-done.left_ref.refs_1_
  316.2 4.4 grad_context.1.do_ref
  320.6 20.4 %attend_back.1 = (f32[512,512]{1,0:T(8,128)}, bf16[2048,256]{1,0:T(8,128)(2,1)}, bf16[2048,256]{1,0:T(8,128)(2,1)}, bf16[2048,256]{1,0:T(8,128)(2,1)}, bf16[2048,256]{1,0:T(8,128)(2,1)}) custom-call(s32[18]{0:T(128)S(1)} %pad_add_fusion.1.sc, bf16[512,512]{1,0:T(8,128)(2,1)} %get-tuple-element.173.q_ref, bf16[512,512]{1,0:T(8,128)(2,1)} %grad_context.1.do_ref, ...), custom_call_target="tpu_custom_call" | custom-call | flops 21474836480 | bytes 8388608 | tf_op jit(solution)/shard_map/attend_back/pallas_call | solution.py:856
  341.1 8.4 %collective-permute-done.41 = bf16[512,768]{1,0:T(8,128)(2,1)S(1)} collective-permute-done((bf16[512,768]{1,0:T(8,128)(2,1)}, bf16[512,768]{1,0:T(8,128)(2,1)S(1)}, u32[]{:S(2)}, u32[]{:S(2)}) %collective-permute-start.41) | collective-permute-done | bytes 786464 | tf_op jit(solution)/shard_map/ppermute | solution.py:36
  357.3 2.3 layer_out_rows.1
  363.2 10.5 %collective-permute-done.45 = bf16[1024,256]{1,0:T(8,128)(2,1)S(1)} collective-permute-done((bf16[1024,256]{1,0:T(8,128)(2,1)S(1)}, bf16[1024,256]{1,0:T(8,128)(2,1)S(1)}, u32[]{:S(2)}, u32[]{:S(2)}) %collective-permute-start.45) | collective-permute-done | bytes 524320 | tf_op jit(solution)/shard_map/ppermute | solution.py:36
  378.7 3.5 queries_back.1
  385.3 3.0 keys_back.1
  388.3 6.4 %grad_normed.1 = bf16[512,2048]{1,0:T(8,128)(2,1)} custom-call(bf16[512,512]{1,0:T(8,128)(2,1)} %get-tuple-element.258.refs_0_.refs_2_, bf16[512,512]{1,0:T(8,128)(2,1)} %get-tuple-element.275.refs_1_.refs_4_, bf16[1024,512]{1,0:T(8,128)(2,1)} %constant_dynamic-update-slice_fusion.2.w0.refs_2_, bf16[1024,512]{1,0:T(8,128)(2,1)} %collective-permute-done.8.w1.refs_3_, ...), custom_call_target="tpu_custom_call" | custom-call | tf_op jit(solution)/shard_map/grad_normed/pallas_call | solution.py:173
  394.7 10.4 %all-gather.9.cloned.1.call-done.value_ref = bf16[512,2048]{1,0:T(8,128)(2,1)} async-done(((bf16[128,2048]{1,0:T(8,128)(2,1)}), bf16[512,2048]{1,0:T(8,128)(2,1)}) %all-gather.9.cloned.1.call-update) | async-done | bytes 2097168 | tf_op jit(solution)/shard_map/all_gather | solution.py:889
  408.4 7.9 %collective-permute-done.49 = bf16[256,768]{1,0:T(8,128)(2,1)S(1)} collective-permute-done((bf16[256,768]{1,0:T(8,128)(2,1)S(1)}, bf16[256,768]{1,0:T(8,128)(2,1)S(1)}, u32[]{:S(2)}, u32[]{:S(2)}) %collective-permute-start.49) | collective-permute-done | bytes 393248 | tf_op jit(solution)/shard_map/ppermute | solution.py:36
  417.5 4.8 attention_grad_away.1
  423.0 3.0 collective-permute-done.51.refs_6_
  426.0 2.2 collective-permute-done.52.refs_7_
  429.4 9.3 %attention_grad.1 = (bf16[512,768]{1,0:T(8,128)(2,1)}, bf16[512,768]{1,0:T(8,128)(2,1)}, bf16[512,768]{1,0:T(8,128)(2,1)}, bf16[512,768]{1,0:T(8,128)(2,1)}) custom-call(s32[40]{0:T(128)S(1)} %copy-done.10, bf16[512,2048]{1,0:T(8,128)(2,1)} %get-tuple-element.171.normed_ref.refs_0_, bf16[512,2048]{1,0:T(8,128)(2,1)} %all-gather.7.cloned.1.call-done.left_ref.refs_1_, ...), custom_call_target="tpu_custom_call" | custom-call | tf_op jit(solution)/shard_map/attention_grad/pallas_call | solution.py:173
  440.8 2.7 multiply_reduce_fusion.1
  443.5 2.7 multiply_reduce_fusion
  448.0 2.7 reduce-scatter.11.cloned.1.call-done.grad_ref
  450.7 2.9 tokens_grad_rows.1
  453.7 5.0 collective-permute-done.53
  459.9 1.9 add_convert_fusion.12
  467.0 6.3 %collective-permute-done.59 = f32[1,256]{1,0:T(1,128)S(1)} collective-permute-done((f32[1,256]{1,0:T(1,128)S(1)}, f32[1,256]{1,0:T(1,128)S(1)}, u32[]{:S(2)}, u32[]{:S(2)}) %collective-permute-start.59) | collective-permute-done | bytes 1056 | tf_op jit(solution)/shard_map/ppermute | solution.py:36
  480.0 4.4 layer_out.1
  484.4 2.0 collective-permute-start.61
  487.5 1.8 collective-permute-done.61
  490.4 8.7 %all-gather.11.cloned.1.call-done.value_ref = bf16[512,2048]{1,0:T(8,128)(2,1)} async-done(((bf16[128,2048]{1,0:T(8,128)(2,1)}), bf16[512,2048]{1,0:T(8,128)(2,1)}) %all-gather.11.cloned.1.call-update) | async-done | bytes 2097168 | tf_op jit(solution)/shard_map/all_gather | solution.py:889
  499.1 4.8 tokens_grad.1
  (404 shorter events, 114.9 us)
Async XLA Ops:
  7.2 140.8 %reduce-scatter.5.cloned.1.call-start = ((), (), s32[]{:S(2)}) async-start(), calls=%async_computation.4 | async-start | bytes 2621440 | tf_op jit(solution)/shard_map/reduce_scatter | solution.py:885
  9.9 10.5 %collective-permute-start = (bf16[256,512]{1,0:T(8,128)(2,1)}, bf16[256,512]{1,0:T(8,128)(2,1)S(1)}, u32[]{:S(2)}, u32[]{:S(2)}) collective-permute-start(bf16[256,512]{1,0:T(8,128)(2,1)} %param.21), channel_id=1, source_target_pairs={{0,8},{4,12},{8,0},{12,4},{16,24},{20,28},{24,16},{28,20},{1,9},{5... | collective-permute-start | bytes 786440 | tf_op jit(solution)/shard_map/ppermute | solution.py:36
  12.9 7.8 %collective-permute-start.1 = (bf16[256,512]{1,0:T(8,128)(2,1)S(1)}, bf16[256,512]{1,0:T(8,128)(2,1)S(1)}, u32[]{:S(2)}, u32[]{:S(2)}) collective-permute-start(bf16[256,512]{1,0:T(8,128)(2,1)S(1)} %constant_dynamic-update-slice_fusion), channel_id=1, source_target_pairs={{0,16},{4,20},{8,24},{12,28},{16,0},{20,4},{24,8},{28,12},{1,17},{... | collective-permute-start | bytes 786440 | tf_op jit(solution)/shard_map/ppermute | solution.py:36
  14.4 5.9 %collective-permute-start.2 = (bf16[1,544]{1,0:T(2,128)(2,1)S(1)}, bf16[1,544]{1,0:T(2,128)(2,1)S(1)}, u32[]{:S(2)}, u32[]{:S(2)}) collective-permute-start(bf16[1,544]{1,0:T(2,128)(2,1)S(1)} %reshape.140), channel_id=1, source_target_pairs={{0,8},{4,12},{8,0},{12,4},{16,24},{20,28},{24,16},{28,20},{1,9},{5... | collective-permute-start | bytes 3272 | tf_op jit(solution)/shard_map/ppermute | solution.py:36
  20.8 12.7 %collective-permute-start.3 = (bf16[512,512]{1,0:T(8,128)(2,1)S(1)}, bf16[512,512]{1,0:T(8,128)(2,1)S(1)}, u32[]{:S(2)}, u32[]{:S(2)}) collective-permute-start(bf16[512,512]{1,0:T(8,128)(2,1)S(1)} %get-tuple-element.163), channel_id=1, source_target_pairs={{0,16},{4,20},{8,24},{12,28},{16,0},{20,4},{24,8},{28,12},{1,17},{... | collective-permute-start | bytes 1572872 | tf_op jit(solution)/shard_map/ppermute | solution.py:36
  22.4 12.2 %collective-permute-start.4 = (bf16[512,512]{1,0:T(8,128)(2,1)S(1)}, bf16[512,512]{1,0:T(8,128)(2,1)S(1)}, u32[]{:S(2)}, u32[]{:S(2)}) collective-permute-start(bf16[512,512]{1,0:T(8,128)(2,1)S(1)} %get-tuple-element.164), channel_id=1, source_target_pairs={{0,8},{4,12},{8,0},{12,4},{16,24},{20,28},{24,16},{28,20},{1,9},{5... | collective-permute-start | bytes 1572872 | tf_op jit(solution)/shard_map/ppermute | solution.py:36
  23.0 10.4 %collective-permute-start.5 = (bf16[2,544]{1,0:T(2,128)(2,1)S(1)}, bf16[2,544]{1,0:T(2,128)(2,1)S(1)}, u32[]{:S(2)}, u32[]{:S(2)}) collective-permute-start(bf16[2,544]{1,0:T(2,128)(2,1)S(1)} %pad_maximum_fusion.21), channel_id=1, source_target_pairs={{0,16},{4,20},{8,24},{12,28},{16,0},{20,4},{24,8},{28,12},{1,17},{... | collective-permute-start | bytes 6536 | tf_op jit(solution)/shard_map/ppermute | solution.py:36
  34.7 4.7 collective-permute-start.7
  36.9 11.2 %collective-permute-start.8 = (bf16[1024,512]{1,0:T(8,128)(2,1)}, bf16[1024,512]{1,0:T(8,128)(2,1)}, u32[]{:S(2)}, u32[]{:S(2)}) collective-permute-start(bf16[1024,512]{1,0:T(8,128)(2,1)} %constant_dynamic-update-slice_fusion.2.w0.refs_2_), channel_id=1, source_target_pairs={{0,4},{4,0},{8,12},{12,8},{16,20},{20,16},{24,28},{28,24},{1,5},{5... | collective-permute-start | bytes 3145736 | tf_op jit(solution)/shard_map/ppermute | solution.py:36
  37.0 8.9 %collective-permute-start.9 = (bf16[256,256]{1,0:T(8,128)(2,1)S(1)}, bf16[256,256]{1,0:T(8,128)(2,1)S(1)}, u32[]{:S(2)}, u32[]{:S(2)}) collective-permute-start(bf16[256,256]{1,0:T(8,128)(2,1)S(1)} %get-tuple-element.175), channel_id=1, source_target_pairs={{0,8},{4,12},{8,0},{12,4},{16,24},{20,28},{24,16},{28,20},{1,9},{5... | collective-permute-start | bytes 393224 | tf_op jit(solution)/shard_map/ppermute | solution.py:36
  37.9 8.0 %collective-permute-start.10 = (bf16[256,256]{1,0:T(8,128)(2,1)S(1)}, bf16[256,256]{1,0:T(8,128)(2,1)S(1)}, u32[]{:S(2)}, u32[]{:S(2)}) collective-permute-start(bf16[256,256]{1,0:T(8,128)(2,1)S(1)} %get-tuple-element.176), channel_id=1, source_target_pairs={{0,16},{4,20},{8,24},{12,28},{16,0},{20,4},{24,8},{28,12},{1,17},{... | collective-permute-start | bytes 393224 | tf_op jit(solution)/shard_map/ppermute | solution.py:36
  45.9 8.4 %collective-permute-start.11 = (bf16[512,256]{1,0:T(8,128)(2,1)}, bf16[512,256]{1,0:T(8,128)(2,1)S(1)}, u32[]{:S(2)}, u32[]{:S(2)}) collective-permute-start(bf16[512,256]{1,0:T(8,128)(2,1)} %get-tuple-element.177), channel_id=1, source_target_pairs={{0,8},{4,12},{8,0},{12,4},{16,24},{20,28},{24,16},{28,20},{1,9},{5... | collective-permute-start | bytes 786440 | tf_op jit(solution)/shard_map/ppermute | solution.py:36
  46.5 8.0 %collective-permute-start.12 = (bf16[512,256]{1,0:T(8,128)(2,1)}, bf16[512,256]{1,0:T(8,128)(2,1)S(1)}, u32[]{:S(2)}, u32[]{:S(2)}) collective-permute-start(bf16[512,256]{1,0:T(8,128)(2,1)} %get-tuple-element.178), channel_id=1, source_target_pairs={{0,16},{4,20},{8,24},{12,28},{16,0},{20,4},{24,8},{28,12},{1,17},{... | collective-permute-start | bytes 786440 | tf_op jit(solution)/shard_map/ppermute | solution.py:36
  54.6 12.7 %collective-permute-start.13 = (bf16[1024,256]{1,0:T(8,128)(2,1)S(1)}, bf16[1024,256]{1,0:T(8,128)(2,1)S(1)}, u32[]{:S(2)}, u32[]{:S(2)}) collective-permute-start(bf16[1024,256]{1,0:T(8,128)(2,1)S(1)} %pad_maximum_fusion.11), channel_id=1, source_target_pairs={{0,16},{4,20},{8,24},{12,28},{16,0},{20,4},{24,8},{28,12},{1,17},{... | collective-permute-start | bytes 1572872 | tf_op jit(solution)/shard_map/ppermute | solution.py:36
  56.2 12.2 %collective-permute-start.14 = (bf16[1024,256]{1,0:T(8,128)(2,1)S(1)}, bf16[1024,256]{1,0:T(8,128)(2,1)S(1)}, u32[]{:S(2)}, u32[]{:S(2)}) collective-permute-start(bf16[1024,256]{1,0:T(8,128)(2,1)S(1)} %pad_maximum_fusion.12), channel_id=1, source_target_pairs={{0,8},{4,12},{8,0},{12,4},{16,24},{20,28},{24,16},{28,20},{1,9},{5... | collective-permute-start | bytes 1572872 | tf_op jit(solution)/shard_map/ppermute | solution.py:36
  69.7 15.6 %collective-permute-start.17 = (bf16[512,256]{1,0:T(8,128)(2,1)S(1)}, bf16[512,256]{1,0:T(8,128)(2,1)S(1)}, u32[]{:S(2)}, u32[]{:S(2)}) collective-permute-start(bf16[512,256]{1,0:T(8,128)(2,1)S(1)} %pad_maximum_fusion.17), channel_id=1, source_target_pairs={{0,16},{4,20},{8,24},{12,28},{16,0},{20,4},{24,8},{28,12},{1,17},{... | collective-permute-start | bytes 786440 | tf_op jit(solution)/shard_map/ppermute | solution.py:36
  70.5 14.9 %collective-permute-start.18 = (bf16[512,256]{1,0:T(8,128)(2,1)S(1)}, bf16[512,256]{1,0:T(8,128)(2,1)S(1)}, u32[]{:S(2)}, u32[]{:S(2)}) collective-permute-start(bf16[512,256]{1,0:T(8,128)(2,1)S(1)} %pad_maximum_fusion.18), channel_id=1, source_target_pairs={{0,8},{4,12},{8,0},{12,4},{16,24},{20,28},{24,16},{28,20},{1,9},{5... | collective-permute-start | bytes 786440 | tf_op jit(solution)/shard_map/ppermute | solution.py:36
  85.4 3.9 collective-permute-start.19
  85.6 3.7 collective-permute-start.20
  87.3 10.9 %collective-permute-start.21 = (bf16[256,768]{1,0:T(8,128)(2,1)S(1)}, bf16[256,768]{1,0:T(8,128)(2,1)S(1)}, u32[]{:S(2)}, u32[]{:S(2)}) collective-permute-start(bf16[256,768]{1,0:T(8,128)(2,1)S(1)} %get-tuple-element.192), channel_id=1, source_target_pairs={{0,8},{4,12},{8,0},{12,4},{16,24},{20,28},{24,16},{28,20},{1,9},{5... | collective-permute-start | bytes 1179656 | tf_op jit(solution)/shard_map/ppermute | solution.py:36
  88.0 10.7 %collective-permute-start.22 = (bf16[256,768]{1,0:T(8,128)(2,1)S(1)}, bf16[256,768]{1,0:T(8,128)(2,1)S(1)}, u32[]{:S(2)}, u32[]{:S(2)}) collective-permute-start(bf16[256,768]{1,0:T(8,128)(2,1)S(1)} %get-tuple-element.193), channel_id=1, source_target_pairs={{0,16},{4,20},{8,24},{12,28},{16,0},{20,4},{24,8},{28,12},{1,17},{... | collective-permute-start | bytes 1179656 | tf_op jit(solution)/shard_map/ppermute | solution.py:36
  94.4 101.7 %all-gather.5.cloned.1.call-start = ((), (), s32[]{:S(2)}) async-start(), calls=%async_computation.5 | async-start | bytes 2621440 | tf_op jit(solution)/shard_map/all_gather | solution.py:889
  100.6 18.5 %collective-permute-start.23 = (bf16[512,768]{1,0:T(8,128)(2,1)}, bf16[512,768]{1,0:T(8,128)(2,1)S(1)}, u32[]{:S(2)}, u32[]{:S(2)}) collective-permute-start(bf16[512,768]{1,0:T(8,128)(2,1)} %pad_maximum_fusion.7), channel_id=1, source_target_pairs={{0,16},{4,20},{8,24},{12,28},{16,0},{20,4},{24,8},{28,12},{1,17},{... | collective-permute-start | bytes 2359304 | tf_op jit(solution)/shard_map/ppermute | solution.py:36
  101.8 18.0 %collective-permute-start.24 = (bf16[512,768]{1,0:T(8,128)(2,1)}, bf16[512,768]{1,0:T(8,128)(2,1)S(1)}, u32[]{:S(2)}, u32[]{:S(2)}) collective-permute-start(bf16[512,768]{1,0:T(8,128)(2,1)} %pad_maximum_fusion.8), channel_id=1, source_target_pairs={{0,8},{4,12},{8,0},{12,4},{16,24},{20,28},{24,16},{28,20},{1,9},{5... | collective-permute-start | bytes 2359304 | tf_op jit(solution)/shard_map/ppermute | solution.py:36
  119.8 17.2 %collective-permute-start.25 = (bf16[256,1536]{1,0:T(8,128)(2,1)}, bf16[256,1536]{1,0:T(8,128)(2,1)S(1)}, u32[]{:S(2)}, u32[]{:S(2)}) collective-permute-start(bf16[256,1536]{1,0:T(8,128)(2,1)} %param.28), channel_id=1, source_target_pairs={{0,8},{4,12},{8,0},{12,4},{16,24},{20,28},{24,16},{28,20},{1,9},{5... | collective-permute-start | bytes 2359304 | tf_op jit(solution)/shard_map/ppermute | solution.py:36
  120.4 16.8 %collective-permute-start.26 = (bf16[256,1536]{1,0:T(8,128)(2,1)}, bf16[256,1536]{1,0:T(8,128)(2,1)S(1)}, u32[]{:S(2)}, u32[]{:S(2)}) collective-permute-start(bf16[256,1536]{1,0:T(8,128)(2,1)} %param.29), channel_id=1, source_target_pairs={{0,16},{4,20},{8,24},{12,28},{16,0},{20,4},{24,8},{28,12},{1,17},{... | collective-permute-start | bytes 2359304 | tf_op jit(solution)/shard_map/ppermute | solution.py:36
  125.0 25.4 %collective-permute-start.29 = (bf16[1024,768]{1,0:T(8,128)(2,1)S(1)}, bf16[1024,768]{1,0:T(8,128)(2,1)}, u32[]{:S(2)}, u32[]{:S(2)}) collective-permute-start(bf16[1024,768]{1,0:T(8,128)(2,1)S(1)} %pad_maximum_fusion.3.refs_0_.refs_2_), channel_id=1, source_target_pairs={{0,4},{4,0},{8,12},{12,8},{16,20},{20,16},{24,28},{28,24},{1,5},{5... | collective-permute-start | bytes 4718600 | tf_op jit(solution)/shard_map/ppermute | solution.py:36
  126.8 23.6 %collective-permute-start.30 = (bf16[1024,768]{1,0:T(8,128)(2,1)S(1)}, bf16[1024,768]{1,0:T(8,128)(2,1)}, u32[]{:S(2)}, u32[]{:S(2)}) collective-permute-start(bf16[1024,768]{1,0:T(8,128)(2,1)S(1)} %pad_maximum_fusion.4.refs_2_.refs_4_), channel_id=1, source_target_pairs={{0,4},{4,0},{8,12},{12,8},{16,20},{20,16},{24,28},{28,24},{1,5},{5... | collective-permute-start | bytes 4718600 | tf_op jit(solution)/shard_map/ppermute | solution.py:36
  142.3 33.1 %collective-permute-start.27 = (bf16[512,1536]{1,0:T(8,128)(2,1)}, bf16[512,1536]{1,0:T(8,128)(2,1)}, u32[]{:S(2)}, u32[]{:S(2)}) collective-permute-start(bf16[512,1536]{1,0:T(8,128)(2,1)} %pad_maximum_fusion.1), channel_id=1, source_target_pairs={{0,16},{4,20},{8,24},{12,28},{16,0},{20,4},{24,8},{28,12},{1,17},{... | collective-permute-start | bytes 4718600 | tf_op jit(solution)/shard_map/ppermute | solution.py:36
  143.7 32.8 %collective-permute-start.28 = (bf16[512,1536]{1,0:T(8,128)(2,1)}, bf16[512,1536]{1,0:T(8,128)(2,1)}, u32[]{:S(2)}, u32[]{:S(2)}) collective-permute-start(bf16[512,1536]{1,0:T(8,128)(2,1)} %pad_maximum_fusion.2), channel_id=1, source_target_pairs={{0,8},{4,12},{8,0},{12,4},{16,24},{20,28},{24,16},{28,20},{1,9},{5... | collective-permute-start | bytes 4718600 | tf_op jit(solution)/shard_map/ppermute | solution.py:36
  150.4 112.6 %reduce-scatter.7.cloned.1.call-start = ((), (), s32[]{:S(2)}) async-start(), calls=%async_computation.6 | async-start | bytes 2621440 | tf_op jit(solution)/shard_map/reduce_scatter | solution.py:885
  179.1 17.0 %collective-permute-start.31 = (bf16[1024,1536]{1,0:T(8,128)(2,1)}, bf16[1024,1536]{1,0:T(8,128)(2,1)}, u32[]{:S(2)}, u32[]{:S(2)}) collective-permute-start(bf16[1024,1536]{1,0:T(8,128)(2,1)} %constant_dynamic-update-slice_fusion.8.wg0.refs_2_), channel_id=1, source_target_pairs={{0,4},{4,0},{8,12},{12,8},{16,20},{20,16},{24,28},{28,24},{1,5},{5... | collective-permute-start | bytes 9437192 | tf_op jit(solution)/shard_map/ppermute | solution.py:36
  182.0 14.1 %collective-permute-start.32 = (bf16[1024,1536]{1,0:T(8,128)(2,1)S(1)}, bf16[1024,1536]{1,0:T(8,128)(2,1)}, u32[]{:S(2)}, u32[]{:S(2)}) collective-permute-start(bf16[1024,1536]{1,0:T(8,128)(2,1)S(1)} %pad_maximum_fusion.wu0.refs_4_), channel_id=1, source_target_pairs={{0,4},{4,0},{8,12},{12,8},{16,20},{20,16},{24,28},{28,24},{1,5},{5... | collective-permute-start | bytes 9437192 | tf_op jit(solution)/shard_map/ppermute | solution.py:36
  220.2 91.8 %all-gather.7.cloned.1.call-start = ((), (), s32[]{:S(2)}) async-start(), calls=%async_computation.7 | async-start | bytes 2621440 | tf_op jit(solution)/shard_map/all_gather | solution.py:889
  227.2 5.9 %collective-permute-start.33 = (bf16[1024,1536]{1,0:T(8,128)(2,1)}, bf16[1024,1536]{1,0:T(8,128)(2,1)S(1)}, u32[]{:S(2)}, u32[]{:S(2)}) collective-permute-start(bf16[1024,1536]{1,0:T(8,128)(2,1)} %get-tuple-element.215), channel_id=1, source_target_pairs={{0,4},{4,0},{8,12},{12,8},{16,20},{20,16},{24,28},{28,24},{1,5},{5... | collective-permute-start | bytes 9437192 | tf_op jit(solution)/shard_map/ppermute | solution.py:36
  227.2 10.4 %collective-permute-start.34 = (bf16[1024,1536]{1,0:T(8,128)(2,1)}, bf16[1024,1536]{1,0:T(8,128)(2,1)S(1)}, u32[]{:S(2)}, u32[]{:S(2)}) collective-permute-start(bf16[1024,1536]{1,0:T(8,128)(2,1)} %get-tuple-element.216), channel_id=1, source_target_pairs={{0,4},{4,0},{8,12},{12,8},{16,20},{20,16},{24,28},{28,24},{1,5},{5... | collective-permute-start | bytes 9437192 | tf_op jit(solution)/shard_map/ppermute | solution.py:36
  250.3 36.6 %collective-permute-start.35 = (bf16[512,1536]{1,0:T(8,128)(2,1)}, bf16[512,1536]{1,0:T(8,128)(2,1)S(1)}, u32[]{:S(2)}, u32[]{:S(2)}) collective-permute-start(bf16[512,1536]{1,0:T(8,128)(2,1)} %get-tuple-element.224), channel_id=1, source_target_pairs={{0,8},{4,12},{8,0},{12,4},{16,24},{20,28},{24,16},{28,20},{1,9},{5... | collective-permute-start | bytes 4718600 | tf_op jit(solution)/shard_map/ppermute | solution.py:36
  251.8 36.3 %collective-permute-start.36 = (bf16[512,1536]{1,0:T(8,128)(2,1)}, bf16[512,1536]{1,0:T(8,128)(2,1)S(1)}, u32[]{:S(2)}, u32[]{:S(2)}) collective-permute-start(bf16[512,1536]{1,0:T(8,128)(2,1)} %get-tuple-element.225), channel_id=1, source_target_pairs={{0,16},{4,20},{8,24},{12,28},{16,0},{20,4},{24,8},{28,12},{1,17},{... | collective-permute-start | bytes 4718600 | tf_op jit(solution)/shard_map/ppermute | solution.py:36
  266.6 90.7 %reduce-scatter.9.cloned.1.call-start = ((), (), s32[]{:S(2)}) async-start(), calls=%async_computation.8 | async-start | bytes 2621440 | tf_op jit(solution)/shard_map/reduce_scatter | solution.py:885
  293.2 5.9 %collective-permute-start.38 = (bf16[1024,768]{1,0:T(8,128)(2,1)}, bf16[1024,768]{1,0:T(8,128)(2,1)S(1)}, u32[]{:S(2)}, u32[]{:S(2)}) collective-permute-start(bf16[1024,768]{1,0:T(8,128)(2,1)} %get-tuple-element.233), channel_id=1, source_target_pairs={{0,4},{4,0},{8,12},{12,8},{16,20},{20,16},{24,28},{28,24},{1,5},{5... | collective-permute-start | bytes 4718600 | tf_op jit(solution)/shard_map/ppermute | solution.py:36
  312.0 93.1 %all-gather.9.cloned.1.call-start = ((), (), s32[]{:S(2)}) async-start(), calls=%async_computation.9 | async-start | bytes 2621440 | tf_op jit(solution)/shard_map/all_gather | solution.py:889
  312.1 29.0 %collective-permute-start.39 = (bf16[256,1536]{1,0:T(8,128)(2,1)S(1)}, bf16[256,1536]{1,0:T(8,128)(2,1)S(1)}, u32[]{:S(2)}, u32[]{:S(2)}) collective-permute-start(bf16[256,1536]{1,0:T(8,128)(2,1)S(1)} %copy-done.52), channel_id=1, source_target_pairs={{0,16},{4,20},{8,24},{12,28},{16,0},{20,4},{24,8},{28,12},{1,17},{... | collective-permute-start | bytes 2359304 | tf_op jit(solution)/shard_map/ppermute | solution.py:36
  313.6 27.4 %collective-permute-start.40 = (bf16[256,1536]{1,0:T(8,128)(2,1)S(1)}, bf16[256,1536]{1,0:T(8,128)(2,1)S(1)}, u32[]{:S(2)}, u32[]{:S(2)}) collective-permute-start(bf16[256,1536]{1,0:T(8,128)(2,1)S(1)} %add_convert_fusion.2), channel_id=1, source_target_pairs={{0,8},{4,12},{8,0},{12,4},{16,24},{20,28},{24,16},{28,20},{1,9},{5... | collective-permute-start | bytes 2359304 | tf_op jit(solution)/shard_map/ppermute | solution.py:36
  315.1 34.4 %collective-permute-start.41 = (bf16[512,768]{1,0:T(8,128)(2,1)}, bf16[512,768]{1,0:T(8,128)(2,1)S(1)}, u32[]{:S(2)}, u32[]{:S(2)}) collective-permute-start(bf16[512,768]{1,0:T(8,128)(2,1)} %get-tuple-element.244), channel_id=1, source_target_pairs={{0,8},{4,12},{8,0},{12,4},{16,24},{20,28},{24,16},{28,20},{1,9},{5... | collective-permute-start | bytes 2359304 | tf_op jit(solution)/shard_map/ppermute | solution.py:36
  315.7 33.8 %collective-permute-start.42 = (bf16[512,768]{1,0:T(8,128)(2,1)S(1)}, bf16[512,768]{1,0:T(8,128)(2,1)S(1)}, u32[]{:S(2)}, u32[]{:S(2)}) collective-permute-start(bf16[512,768]{1,0:T(8,128)(2,1)S(1)} %copy-done.88), channel_id=1, source_target_pairs={{0,16},{4,20},{8,24},{12,28},{16,0},{20,4},{24,8},{28,12},{1,17},{... | collective-permute-start | bytes 2359304 | tf_op jit(solution)/shard_map/ppermute | solution.py:36
  349.6 4.4 collective-permute-start.44
  359.7 91.0 %reduce-scatter.11.cloned.1.call-start = ((), (), s32[]{:S(2)}) async-start(), calls=%async_computation.10 | async-start | bytes 2621440 | tf_op jit(solution)/shard_map/reduce_scatter | solution.py:885
  360.0 13.7 %collective-permute-start.45 = (bf16[1024,256]{1,0:T(8,128)(2,1)S(1)}, bf16[1024,256]{1,0:T(8,128)(2,1)S(1)}, u32[]{:S(2)}, u32[]{:S(2)}) collective-permute-start(bf16[1024,256]{1,0:T(8,128)(2,1)S(1)} %copy-done.66), channel_id=1, source_target_pairs={{0,8},{4,12},{8,0},{12,4},{16,24},{20,28},{24,16},{28,20},{1,9},{5... | collective-permute-start | bytes 1572872 | tf_op jit(solution)/shard_map/ppermute | solution.py:36
  361.5 13.5 %collective-permute-start.46 = (bf16[1024,256]{1,0:T(8,128)(2,1)}, bf16[1024,256]{1,0:T(8,128)(2,1)S(1)}, u32[]{:S(2)}, u32[]{:S(2)}) collective-permute-start(bf16[1024,256]{1,0:T(8,128)(2,1)} %get-tuple-element.252), channel_id=1, source_target_pairs={{0,16},{4,20},{8,24},{12,28},{16,0},{20,4},{24,8},{28,12},{1,17},{... | collective-permute-start | bytes 1572872 | tf_op jit(solution)/shard_map/ppermute | solution.py:36
  376.7 6.9 %collective-permute-start.47 = (bf16[512,256]{1,0:T(8,128)(2,1)S(1)}, bf16[512,256]{1,0:T(8,128)(2,1)S(1)}, u32[]{:S(2)}, u32[]{:S(2)}) collective-permute-start(bf16[512,256]{1,0:T(8,128)(2,1)S(1)} %get-tuple-element.261), channel_id=1, source_target_pairs={{0,16},{4,20},{8,24},{12,28},{16,0},{20,4},{24,8},{28,12},{1,17},{... | collective-permute-start | bytes 786440 | tf_op jit(solution)/shard_map/ppermute | solution.py:36
  378.1 6.5 %collective-permute-start.48 = (bf16[512,256]{1,0:T(8,128)(2,1)S(1)}, bf16[512,256]{1,0:T(8,128)(2,1)S(1)}, u32[]{:S(2)}, u32[]{:S(2)}) collective-permute-start(bf16[512,256]{1,0:T(8,128)(2,1)S(1)} %get-tuple-element.262), channel_id=1, source_target_pairs={{0,8},{4,12},{8,0},{12,4},{16,24},{20,28},{24,16},{28,20},{1,9},{5... | collective-permute-start | bytes 786440 | tf_op jit(solution)/shard_map/ppermute | solution.py:36
  405.1 94.0 %all-gather.11.cloned.1.call-start = ((), (), s32[]{:S(2)}) async-start(), calls=%async_computation.11 | async-start | bytes 2621440 | tf_op jit(solution)/shard_map/all_gather | solution.py:889
  405.4 10.9 %collective-permute-start.49 = (bf16[256,768]{1,0:T(8,128)(2,1)S(1)}, bf16[256,768]{1,0:T(8,128)(2,1)S(1)}, u32[]{:S(2)}, u32[]{:S(2)}) collective-permute-start(bf16[256,768]{1,0:T(8,128)(2,1)S(1)} %add_convert_fusion.15), channel_id=1, source_target_pairs={{0,16},{4,20},{8,24},{12,28},{16,0},{20,4},{24,8},{28,12},{1,17},{... | collective-permute-start | bytes 1179656 | tf_op jit(solution)/shard_map/ppermute | solution.py:36
  407.0 10.6 %collective-permute-start.50 = (bf16[256,768]{1,0:T(8,128)(2,1)S(1)}, bf16[256,768]{1,0:T(8,128)(2,1)S(1)}, u32[]{:S(2)}, u32[]{:S(2)}) collective-permute-start(bf16[256,768]{1,0:T(8,128)(2,1)S(1)} %add_convert_fusion.14), channel_id=1, source_target_pairs={{0,8},{4,12},{8,0},{12,4},{16,24},{20,28},{24,16},{28,20},{1,9},{5... | collective-permute-start | bytes 1179656 | tf_op jit(solution)/shard_map/ppermute | solution.py:36
  422.3 3.7 collective-permute-start.51
  422.4 5.9 %collective-permute-start.52 = (bf16[1024,768]{1,0:T(8,128)(2,1)}, bf16[1024,768]{1,0:T(8,128)(2,1)S(1)}, u32[]{:S(2)}, u32[]{:S(2)}) collective-permute-start(bf16[1024,768]{1,0:T(8,128)(2,1)} %get-tuple-element.277), channel_id=1, source_target_pairs={{0,4},{4,0},{8,12},{12,8},{16,20},{20,16},{24,28},{28,24},{1,5},{5... | collective-permute-start | bytes 4718600 | tf_op jit(solution)/shard_map/ppermute | solution.py:36
  438.8 20.0 %collective-permute-start.53 = (bf16[512,768]{1,0:T(8,128)(2,1)}, bf16[512,768]{1,0:T(8,128)(2,1)}, u32[]{:S(2)}, u32[]{:S(2)}) collective-permute-start(bf16[512,768]{1,0:T(8,128)(2,1)} %get-tuple-element.284), channel_id=1, source_target_pairs={{0,8},{4,12},{8,0},{12,4},{16,24},{20,28},{24,16},{28,20},{1,9},{5... | collective-permute-start | bytes 2359304 | tf_op jit(solution)/shard_map/ppermute | solution.py:36
  440.3 19.6 %collective-permute-start.54 = (bf16[512,768]{1,0:T(8,128)(2,1)}, bf16[512,768]{1,0:T(8,128)(2,1)}, u32[]{:S(2)}, u32[]{:S(2)}) collective-permute-start(bf16[512,768]{1,0:T(8,128)(2,1)} %get-tuple-element.285), channel_id=1, source_target_pairs={{0,16},{4,20},{8,24},{12,28},{16,0},{20,4},{24,8},{28,12},{1,17},{... | collective-permute-start | bytes 2359304 | tf_op jit(solution)/shard_map/ppermute | solution.py:36
  447.5 17.8 %collective-permute-start.58 = (f32[1,256]{1,0:T(1,128)S(1)}, f32[1,256]{1,0:T(1,128)S(1)}, u32[]{:S(2)}, u32[]{:S(2)}) collective-permute-start(f32[1,256]{1,0:T(1,128)S(1)} %add.165), channel_id=1, source_target_pairs={{0,8},{4,12},{8,0},{12,4},{16,24},{20,28},{24,16},{28,20},{1,9},{5... | collective-permute-start | bytes 3080 | tf_op jit(solution)/shard_map/ppermute | solution.py:36
  463.0 10.6 %collective-permute-start.55 = (bf16[256,768]{1,0:T(8,128)(2,1)}, bf16[256,768]{1,0:T(8,128)(2,1)}, u32[]{:S(2)}, u32[]{:S(2)}) collective-permute-start(bf16[256,768]{1,0:T(8,128)(2,1)} %add_convert_fusion.12), channel_id=1, source_target_pairs={{0,16},{4,20},{8,24},{12,28},{16,0},{20,4},{24,8},{28,12},{1,17},{... | collective-permute-start | bytes 1179656 | tf_op jit(solution)/shard_map/ppermute | solution.py:36
  463.6 10.0 %collective-permute-start.56 = (bf16[256,768]{1,0:T(8,128)(2,1)S(1)}, bf16[256,768]{1,0:T(8,128)(2,1)}, u32[]{:S(2)}, u32[]{:S(2)}) collective-permute-start(bf16[256,768]{1,0:T(8,128)(2,1)S(1)} %add_convert_fusion.11), channel_id=1, source_target_pairs={{0,8},{4,12},{8,0},{12,4},{16,24},{20,28},{24,16},{28,20},{1,9},{5... | collective-permute-start | bytes 1179656 | tf_op jit(solution)/shard_map/ppermute | solution.py:36
  465.3 8.0 %collective-permute-start.59 = (f32[1,256]{1,0:T(1,128)S(1)}, f32[1,256]{1,0:T(1,128)S(1)}, u32[]{:S(2)}, u32[]{:S(2)}) collective-permute-start(f32[1,256]{1,0:T(1,128)S(1)} %add.166), channel_id=1, source_target_pairs={{0,16},{4,20},{8,24},{12,28},{16,0},{20,4},{24,8},{28,12},{1,17},{... | collective-permute-start | bytes 3080 | tf_op jit(solution)/shard_map/ppermute | solution.py:36
  478.2 6.2 %collective-permute-start.60 = (f32[1,544]{1,0:T(1,128)S(1)}, f32[1,544]{1,0:T(1,128)S(1)}, u32[]{:S(2)}, u32[]{:S(2)}) collective-permute-start(f32[1,544]{1,0:T(1,128)S(1)} %broadcast_in_dim.82), channel_id=1, source_target_pairs={{0,1},{1,0},{2,3},{3,2},{4,5},{5,4},{6,7},{7,6},{8,9},{9,8},{10,11... | collective-permute-start | bytes 6536 | tf_op jit(solution)/shard_map/ppermute | solution.py:1108
  484.4 4.8 collective-permute-start.61
  (96 other events, 543.3 us)
Sparse Core Ops, SparseCore 0:
  94.5 44.1 reduce-scatter.4
  150.5 45.5 all-gather.4
  220.3 42.6 reduce-scatter.6
  266.7 45.2 all-gather.6
  314.7 42.5 reduce-scatter.8
  359.8 45.2 all-gather.8
  408.1 42.5 reduce-scatter.10
  453.8 45.3 all-gather.10
